TPU v7x, 32 devices: a whole 2x2x4 slice. The times are simulated.
32 devices in a mesh: dp: 16 (over z, x, core), tensor: 2 (over y).
Axes of the slice: x: 2, y: 2, z: 4, core: 2. Of those that a mesh axis runs over, the one named last changes fastest.
Arguments:
- block_in: bfloat16 [32768, 1024], P(('dp', 'tensor')), may hold values from -6 to 6
- ln1_scale: bfloat16 [1024], replicated, may hold values from 0.5 to 1.5
- ln1_shift: bfloat16 [1024], replicated, may hold values from -0.5 to 0.5
- qkv_weight: bfloat16 [1024, 3, 1024], P(None, None, 'tensor'), may hold values from -0.1875 to 0.1875
- qkv_bias: bfloat16 [3, 1024], P(None, 'tensor'), may hold values from -0.5 to 0.5
- out_weight: bfloat16 [1024, 1024], P('tensor'), may hold values from -1.5 to 1.5
- out_bias: bfloat16 [1024], replicated, may hold values from -1.5 to 1.5
- ln2_scale: bfloat16 [1024], replicated, may hold values from 0.5 to 1.5
- ln2_shift: bfloat16 [1024], replicated, may hold values from -0.5 to 0.5
- up_weight: bfloat16 [1024, 4096], P(None, 'tensor'), may hold values from -0.1875 to 0.1875
- up_bias: bfloat16 [4096], P('tensor'), may hold values from -1.5 to 1.5
- down_weight: bfloat16 [4096, 1024], P('tensor'), may hold values from -0.09375 to 0.09375
- down_bias: bfloat16 [1024], replicated, may hold values from -1.5 to 1.5
- out_grad: bfloat16 [32768, 1024], P(('dp', 'tensor')), may hold values from -6 to 6
Outputs:
- block_out: bfloat16 [32768, 1024], P(('dp', 'tensor'))
- in_grad: bfloat16 [32768, 1024], P(('dp', 'tensor'))
- ln1_scale_grad: float32 [1024], P('tensor')
- ln1_shift_grad: float32 [1024], P('tensor')
- qkv_weight_grad: float32 [1024, 3, 1024], P(None, None, 'tensor')
- qkv_bias_grad: float32 [3, 1024], P(None, 'tensor')
- out_weight_grad: float32 [1024, 1024], P('tensor')
- out_bias_grad: float32 [1024], P('tensor')
- ln2_scale_grad: float32 [1024], P('tensor')
- ln2_shift_grad: float32 [1024], P('tensor')
- up_weight_grad: float32 [1024, 4096], P(None, 'tensor')
- up_bias_grad: float32 [4096], P('tensor')
- down_weight_grad: float32 [4096, 1024], P('tensor')
- down_bias_grad: float32 [1024], P('tensor')
All inputs are finite; a program needn't handle non-finite values.
Results may differ from a plain program's by a relative error of at most 0.02.
Values may be sent and summed in bfloat16 or wider, within the bound.
A program may use at most 320 MiB of HBM per device.

v0:
```python
import math

import jax
import jax.numpy as jnp
import numpy as np
from jax import lax
from jax.sharding import PartitionSpec as P

HD = 64
GH = 16
GW = 16
SEQ = 2048


epsilon = 1e-06


def rotary_tables():
    rot_dims = 2 * (HD // 3 // 2)
    half_dims = rot_dims // 2
    index = jnp.arange(SEQ, dtype=jnp.int32)
    places = (index // (GH * GW), index // GW % GH, index % GW)
    freqs = jnp.float32(10000.0) ** (
        -jnp.arange(half_dims, dtype=jnp.float32) / jnp.float32(half_dims)
    )
    cos_parts = []
    sin_parts = []
    for which in range(3):
        angle = places[which].astype(jnp.float32)[:, None] * freqs[None, :]
        cos_parts = cos_parts + [jnp.cos(angle), jnp.cos(angle)]
        sin_parts = sin_parts + [-jnp.sin(angle), jnp.sin(angle)]
    remain = HD - 3 * rot_dims
    cos_parts.append(jnp.ones((SEQ, remain), jnp.float32))
    sin_parts.append(jnp.zeros((SEQ, remain), jnp.float32))
    return (jnp.concatenate(cos_parts, 1), jnp.concatenate(sin_parts, 1))


def partner_order():
    rot_dims = 2 * (HD // 3 // 2)
    half_dims = rot_dims // 2
    order = np.arange(HD)
    for which in range(3):
        first = which * rot_dims
        order[first : first + half_dims] = np.arange(first + half_dims, first + rot_dims)
        order[first + half_dims : first + rot_dims] = np.arange(first, first + half_dims)
    return order


def rotate(values, cos_table, sin_table):
    partner = jnp.take(values, partner_order(), axis=-1)
    return values * cos_table[:, None, :] + partner * sin_table[:, None, :]


def unrotate(grads, cos_table, sin_table):
    turned = grads * sin_table[:, None, :]
    return grads * cos_table[:, None, :] + jnp.take(turned, partner_order(), axis=-1)


def norm_parts(values, scale_vec, shift_vec):
    centred = values - jnp.mean(values, axis=-1, keepdims=True)
    inv_dev = lax.rsqrt(jnp.mean(centred * centred, axis=-1, keepdims=True) + epsilon)
    normal = centred * inv_dev
    return (normal * scale_vec + shift_vec, normal, inv_dev)


def norm_back(upstream, normal, inv_dev, scale_vec):
    scaled = upstream * scale_vec
    mean_first = jnp.mean(scaled, axis=-1, keepdims=True)
    mean_second = jnp.mean(scaled * normal, axis=-1, keepdims=True)
    back = inv_dev * (scaled - mean_first - normal * mean_second)
    return (back, jnp.sum(upstream * normal, 0), jnp.sum(upstream, 0))


def gelu_slope(hidden):
    normal_cdf = 0.5 * (1.0 + jax.scipy.special.erf(hidden * (1.0 / math.sqrt(2.0))))
    density = jnp.exp(-0.5 * hidden * hidden) * (1.0 / math.sqrt(2.0 * math.pi))
    return normal_cdf + hidden * density


def inner_rows(left, right):
    return lax.dot_general(
        left, right, (((0,), (0,)), ((), ())), preferred_element_type=jnp.float32
    )


def outer_cols(left, right):
    return lax.dot_general(
        left, right, (((1,), (1,)), ((), ())), preferred_element_type=jnp.float32
    )


def attention_forward(queries, key_rows, value_rows):
    scale_factor = 1.0 / math.sqrt(HD)
    block_rows = min(512, SEQ)

    def one_clip(clip_parts):
        clip_q, clip_k, clip_v = clip_parts
        blocks_q = clip_q.reshape(SEQ // block_rows, block_rows, clip_q.shape[1], HD)

        def one_block(query_blk):
            scores = (
                jnp.einsum("qhd,khd->hqk", query_blk, clip_k, preferred_element_type=jnp.float32)
                * scale_factor
            )
            row_peak = jnp.max(scores, axis=-1, keepdims=True)
            weights = jnp.exp(scores - row_peak)
            row_total = jnp.sum(weights, axis=-1, keepdims=True)
            shares_low = (weights / row_total).astype(jnp.bfloat16)
            output = jnp.einsum(
                "hqk,khd->qhd", shares_low, clip_v, preferred_element_type=jnp.float32
            )
            return (output, (row_peak + jnp.log(row_total))[..., 0])

        outputs, log_totals = lax.map(one_block, blocks_q)
        return (outputs.reshape(SEQ, clip_q.shape[1], HD), log_totals)

    return lax.map(one_clip, (queries, key_rows, value_rows))


def attention_backward(queries, key_rows, value_rows, log_totals, attended_grad):
    scale_factor = 1.0 / math.sqrt(HD)
    block_rows = min(512, SEQ)

    def one_clip(clip_parts):
        clip_q, clip_k, clip_v, clip_lse, clip_dout = clip_parts
        local_heads = clip_q.shape[1]
        block_count = SEQ // block_rows
        block_items = (
            clip_q.reshape(block_count, block_rows, local_heads, HD),
            clip_lse,
            clip_dout.reshape(block_count, block_rows, local_heads, HD),
        )

        def one_block(carry, items):
            key_acc, value_acc = carry
            query_blk, lse_blk, dout_blk = items
            scores = (
                jnp.einsum("qhd,khd->hqk", query_blk, clip_k, preferred_element_type=jnp.float32)
                * scale_factor
            )
            shares = jnp.exp(scores - lse_blk[..., None])
            share_grad = jnp.einsum(
                "qhd,khd->hqk", dout_blk, clip_v, preferred_element_type=jnp.float32
            )
            centre = jnp.sum(shares * share_grad, axis=-1, keepdims=True)
            score_grad = (shares * (share_grad - centre)).astype(jnp.bfloat16)
            query_grad = (
                jnp.einsum("hqk,khd->qhd", score_grad, clip_k, preferred_element_type=jnp.float32)
                * scale_factor
            )
            key_acc = (
                key_acc
                + jnp.einsum(
                    "hqk,qhd->khd", score_grad, query_blk, preferred_element_type=jnp.float32
                )
                * scale_factor
            )
            value_acc = value_acc + jnp.einsum(
                "hqk,qhd->khd",
                shares.astype(jnp.bfloat16),
                dout_blk,
                preferred_element_type=jnp.float32,
            )
            return ((key_acc, value_acc), query_grad)

        empty = jnp.zeros((SEQ, local_heads, HD), jnp.float32)
        (key_grad, value_grad), query_grads = lax.scan(one_block, (empty, empty), block_items)
        return (query_grads.reshape(SEQ, local_heads, HD), key_grad, value_grad)

    return lax.map(one_clip, (queries, key_rows, value_rows, log_totals, attended_grad))


def on_device(
    block_in,
    ln1_scale,
    ln1_shift,
    qkv_weight,
    qkv_bias,
    out_weight,
    out_bias,
    ln2_scale,
    ln2_shift,
    up_weight,
    up_bias,
    down_weight,
    down_bias,
    out_grad,
):
    tok_dev, width = block_in.shape
    tok_group = tok_dev * lax.axis_size("tensor")
    local_width = qkv_weight.shape[2]
    local_heads = local_width // HD
    clip_count = tok_group // SEQ
    cos_table, sin_table = rotary_tables()
    ln1_gain = ln1_scale.astype(jnp.float32)
    ln2_gain = ln2_scale.astype(jnp.float32)
    qkv_flat = qkv_weight.reshape(width, 3 * local_width)
    x_rows = block_in.astype(jnp.float32)
    normed1_f, normal1, inv_one = norm_parts(x_rows, ln1_gain, ln1_shift.astype(jnp.float32))
    normed1 = normed1_f.astype(jnp.bfloat16)
    normed1_all = lax.all_gather(normed1, "tensor", axis=0, tiled=True)
    qkv_rows = jnp.dot(normed1_all, qkv_flat, preferred_element_type=jnp.float32) + qkv_bias.astype(
        jnp.float32
    ).reshape(3 * local_width)
    qkv_rows = qkv_rows.reshape(clip_count, SEQ, 3, local_heads, HD)
    queries = rotate(qkv_rows[:, :, 0], cos_table, sin_table).astype(jnp.bfloat16)
    key_rows = rotate(qkv_rows[:, :, 1], cos_table, sin_table).astype(jnp.bfloat16)
    value_rows = qkv_rows[:, :, 2].astype(jnp.bfloat16)
    attended_f, log_totals = attention_forward(queries, key_rows, value_rows)
    attended = attended_f.reshape(tok_group, local_width).astype(jnp.bfloat16)
    branch_one = lax.psum_scatter(
        jnp.dot(attended, out_weight, preferred_element_type=jnp.float32).astype(jnp.bfloat16),
        "tensor",
        scatter_dimension=0,
        tiled=True,
    ).astype(jnp.float32) + out_bias.astype(jnp.float32)
    resid = x_rows + branch_one
    normed2_f, normal2, inv_two = norm_parts(resid, ln2_gain, ln2_shift.astype(jnp.float32))
    normed2 = normed2_f.astype(jnp.bfloat16)
    normed2_all = lax.all_gather(normed2, "tensor", axis=0, tiled=True)
    hidden = jnp.dot(normed2_all, up_weight, preferred_element_type=jnp.float32) + up_bias.astype(
        jnp.float32
    )
    acted = jax.nn.gelu(hidden, approximate=False).astype(jnp.bfloat16)
    branch_two = lax.psum_scatter(
        jnp.dot(acted, down_weight, preferred_element_type=jnp.float32).astype(jnp.bfloat16),
        "tensor",
        scatter_dimension=0,
        tiled=True,
    ).astype(jnp.float32) + down_bias.astype(jnp.float32)
    block_out = (resid + branch_two).astype(jnp.bfloat16)
    grad_rows = out_grad.astype(jnp.float32)
    down_bias_part = jnp.sum(grad_rows, 0)
    piece = lax.all_gather(out_grad, "tensor", axis=0, tiled=True)
    weight_acc = inner_rows(acted, piece)
    rows_buffer = outer_cols(piece, down_weight)
    down_grad = weight_acc
    acted_grad = rows_buffer
    hidden_grad = (acted_grad * gelu_slope(hidden)).astype(jnp.bfloat16)
    up_grad = inner_rows(normed2_all, hidden_grad)
    up_bias_grad = jnp.sum(hidden_grad, 0, dtype=jnp.float32)
    normed2_grad = lax.psum_scatter(
        outer_cols(hidden_grad, up_weight).astype(jnp.bfloat16),
        "tensor",
        scatter_dimension=0,
        tiled=True,
    ).astype(jnp.float32)
    resid_part, ln2_scale_part, ln2_shift_part = norm_back(normed2_grad, normal2, inv_two, ln2_gain)
    resid_grad = grad_rows + resid_part
    branch_grad = resid_grad.astype(jnp.bfloat16)
    out_bias_part = jnp.sum(branch_grad, 0, dtype=jnp.float32)
    piece = lax.all_gather(branch_grad, "tensor", axis=0, tiled=True)
    weight_acc = inner_rows(attended, piece)
    rows_buffer = outer_cols(piece, out_weight)
    out_weight_grad = weight_acc
    attended_grad = rows_buffer
    attended_grad = attended_grad.astype(jnp.bfloat16).reshape(clip_count, SEQ, local_heads, HD)
    query_grad, key_grad, value_grad = attention_backward(
        queries, key_rows, value_rows, log_totals, attended_grad
    )
    query_grad = unrotate(query_grad, cos_table, sin_table)
    key_grad = unrotate(key_grad, cos_table, sin_table)
    qkv_grad = (
        jnp.stack([query_grad, key_grad, value_grad], axis=2)
        .reshape(tok_group, 3 * local_width)
        .astype(jnp.bfloat16)
    )
    qkv_weight_grad = inner_rows(normed1_all, qkv_grad).reshape(width, 3, local_width)
    qkv_bias_grad = jnp.sum(qkv_grad, 0, dtype=jnp.float32).reshape(3, local_width)
    normed1_grad = lax.psum_scatter(
        outer_cols(qkv_grad, qkv_flat).astype(jnp.bfloat16),
        "tensor",
        scatter_dimension=0,
        tiled=True,
    ).astype(jnp.float32)
    input_part, ln1_scale_part, ln1_shift_part = norm_back(normed1_grad, normal1, inv_one, ln1_gain)
    in_grad = (resid_grad + input_part).astype(jnp.bfloat16)
    vector_parts = jnp.stack(
        [
            ln1_scale_part,
            ln1_shift_part,
            out_bias_part,
            ln2_scale_part,
            ln2_shift_part,
            down_bias_part,
        ]
    )
    vector_parts = lax.psum_scatter(vector_parts, "tensor", scatter_dimension=1, tiled=True)
    (
        qkv_weight_grad,
        qkv_bias_grad,
        out_weight_grad,
        up_grad,
        up_bias_grad,
        down_grad,
        vector_parts,
    ) = (
        lax.psum(qkv_weight_grad.astype(jnp.bfloat16), "dp").astype(jnp.float32),
        lax.psum(qkv_bias_grad.astype(jnp.bfloat16), "dp").astype(jnp.float32),
        lax.psum(out_weight_grad.astype(jnp.bfloat16), "dp").astype(jnp.float32),
        lax.psum(up_grad.astype(jnp.bfloat16), "dp").astype(jnp.float32),
        lax.psum(up_bias_grad.astype(jnp.bfloat16), "dp").astype(jnp.float32),
        lax.psum(down_grad.astype(jnp.bfloat16), "dp").astype(jnp.float32),
        lax.psum(vector_parts.astype(jnp.bfloat16), "dp").astype(jnp.float32),
    )
    return (
        block_out,
        in_grad,
        vector_parts[0],
        vector_parts[1],
        qkv_weight_grad,
        qkv_bias_grad,
        out_weight_grad,
        vector_parts[2],
        vector_parts[3],
        vector_parts[4],
        up_grad,
        up_bias_grad,
        down_grad,
        vector_parts[5],
    )


def solution(mesh):
    placed = (
        P(("dp", "tensor"), None),
        P(),
        P(),
        P(None, None, "tensor"),
        P(None, "tensor"),
        P("tensor", None),
        P(),
        P(),
        P(),
        P(None, "tensor"),
        P("tensor"),
        P("tensor", None),
        P(),
        P(("dp", "tensor"), None),
    )
    return jax.shard_map(
        on_device,
        mesh=mesh,
        in_specs=placed,
        out_specs=(
            P(("dp", "tensor"), None),
            P(("dp", "tensor"), None),
            P("tensor"),
            P("tensor"),
            P(None, None, "tensor"),
            P(None, "tensor"),
            P("tensor", None),
            P("tensor"),
            P("tensor"),
            P("tensor"),
            P(None, "tensor"),
            P("tensor"),
            P("tensor", None),
            P("tensor"),
        ),
        check_vma=False,
    )
```

profile of v0, /device:TPU:0, one launch (start us, length us, event | category | flops | bytes accessed | tf_op | source)
XLA Modules:
  0.0 1640.2 jit_solution(8438572377253438690)
XLA Ops:
  22.1 9.1 concatenate.15
  32.0 43.5 %all-gather.5.cloned.1.call-done = bf16[2048,1024]{1,0:T(8,128)(2,1)} async-done(((bf16[1024,1024]{1,0:T(8,128)(2,1)}), bf16[2048,1024]{1,0:T(8,128)(2,1)}) %all-gather.5.cloned.1.call-update) | async-done | bytes 4194320 | tf_op jit(solution)/shard_map/all_gather | solution.py:201
  75.5 10.2 convolution_add_fusion
  88.4 8.2 copy_bitcast_fusion.1
  106.7 10.5 fusion.82
  120.9 177.5 %while.47 = (s32[]{:T(128)}, bf16[4,512,8,64]{1,3,2,0:T(8,128)(2,1)}, f32[4,8,512]{2,1,0:T(8,128)}, bf16[4,512,8,64]{1,3,2,0:T(8,128)(2,1)}, bf16[2048,8,64]{0,2...) while((s32[]{:T(128)}, bf16[4,512,8,64]{1,3,2,0:T(8,128)(2,1)}, f32[4,8,512]{2,1,0:T(8,128)}, ...), condition=%wide.region_5.7_spmd, body=%wide.region_2.6_spmd.sunk | while | flops 2222977024 | bytes 106561632 | solution.py:114
  120.9 14.1 multiply_reduce_fusion.5
  135.1 14.0 fusion.150
  149.1 15.5 fusion.151
  165.2 14.1 multiply_reduce_fusion.5
  179.4 14.0 fusion.150
  193.4 15.6 fusion.151
  209.6 14.1 multiply_reduce_fusion.5
  223.7 14.0 fusion.150
  237.7 15.6 fusion.151
  253.9 14.1 multiply_reduce_fusion.5
  268.0 14.0 fusion.150
  282.0 15.6 fusion.151
  309.4 53.8 %reduce-scatter.6.cloned.1.call-done = bf16[1024,1024]{1,0:T(8,128)(2,1)} async-done(((bf16[2048,1024]{1,0:T(8,128)(2,1)}), bf16[1024,1024]{1,0:T(8,128)(2,1)}) %reduce-scatter.6.cloned.1.call-update) | async-done | bytes 2097168 | tf_op jit(solution)/shard_map/reduce_scatter | solution.py:211
  370.6 56.2 %all-gather.7.cloned.1.call-done = bf16[2048,1024]{1,0:T(8,128)(2,1)} async-done(((bf16[1024,1024]{1,0:T(8,128)(2,1)}), bf16[2048,1024]{1,0:T(8,128)(2,1)}) %all-gather.7.cloned.1.call-update) | async-done | bytes 4194320 | tf_op jit(solution)/shard_map/all_gather | solution.py:220
  426.8 48.2 %fusion.34 = (bf16[2048,2048]{1,0:T(8,128)(2,1)}, f32[2048,2048]{1,0:T(8,128)}) fusion(f32[2048]{0:T(1024)S(1)} %convert_element_type.237, bf16[2048,1024]{1,0:T(8,128)(2,1)} %all-gather.7.cloned.1.call-done, bf16[1024,2048]{1,0:T(8,128)(2,1)} %param.33), kind=kOutput, calls=%fused_computation.48 | convolution fusion | flops 8866758656 | bytes 33562624 | tf_op jit(solution)/shard_map/dot_general | solution.py:221
  475.1 10.0 all-gather.9.cloned.1.call-done
  485.1 20.6 %fusion.102 = (bf16[2048]{0:T(1024)(128)(2,1)}, bf16[2048,2048]{1,0:T(8,128)(2,1)S(1)}) fusion(f32[2048,2048]{1,0:T(8,128)} %get-tuple-element.336, f32[2048]{0:T(1024)S(1)} %convert_element_type.237, bf16[2048,1024]{1,0:T(8,128)(2,1)} %all-gather.9.cloned.1.call-done, bf16[2048,1024]{1,0:T(8,128)(2,1)} %param.35), kind=kOutput, calls=%fused_computation.187 | convolution fusion | flops 8640264192 | bytes 33566720 | tf_op jit(solution)/shard_map/dot_general | solution.py:87
  509.0 10.6 convolution_convert_fusion.2
  519.7 13.8 convolution_convert_fusion.3
  534.3 39.9 %reduce-scatter.10.cloned.1.call-done = bf16[1024,1024]{1,0:T(8,128)(2,1)} async-done(((bf16[2048,1024]{1,0:T(8,128)(2,1)}), bf16[1024,1024]{1,0:T(8,128)(2,1)}) %reduce-scatter.10.cloned.1.call-update) | async-done | bytes 2097168 | tf_op jit(solution)/shard_map/reduce_scatter | solution.py:242
  579.0 51.6 %reduce-scatter.8.cloned.1.call-done = bf16[1024,1024]{1,0:T(8,128)(2,1)} async-done(((bf16[2048,1024]{1,0:T(8,128)(2,1)}), bf16[1024,1024]{1,0:T(8,128)(2,1)}) %reduce-scatter.8.cloned.1.call-update) | async-done | bytes 2097168 | tf_op jit(solution)/shard_map/reduce_scatter | solution.py:225
  630.6 7.8 convert_reduce_fusion.4
  638.5 14.6 convolution_convert_fusion.5
  653.1 13.1 convolution_convert_fusion.1
  666.2 29.1 %all-gather.11.cloned.1.call-done = bf16[2048,1024]{1,0:T(8,128)(2,1)} async-done(((bf16[1024,1024]{1,0:T(8,128)(2,1)}), bf16[2048,1024]{1,0:T(8,128)(2,1)}) %all-gather.11.cloned.1.call-update) | async-done | bytes 4194320 | tf_op jit(solution)/shard_map/all_gather | solution.py:252
  709.1 495.7 %while.48 = (s32[]{:T(128)}, f32[2048,8,64]{0,2,1:T(8,128)}, f32[2048,8,64]{0,2,1:T(8,128)}, f32[4,512,8,64]{1,0,2,3:T(4,128)}, bf16[4,512,8,64]{1,3,2,0:T(8,128...) while((s32[]{:T(128)}, f32[2048,8,64]{0,2,1:T(8,128)}, ...), condition=%wide.region_15.17_spmd.clone, body=%wide.region_13.16_spmd.clone.sunk | while | flops 5474873344 | bytes 370262304 | solution.py:167
  710.0 14.1 fusion.161
  724.1 16.1 bitcast_add_fusion.7
  740.2 23.6 %multiply_reduce_fusion.6 = (f32[8,512]{1,0:T(8,128)S(1)}, f32[8,512,2048]{2,1,0:T(8,128)}) fusion(f32[8,512,2048]{2,1,0:T(8,128)} %fusion.161, f32[8,512]{1,0:T(8,128)S(1)} %dynamic-slice_bitcast_fusion.2, bf16[2048,8,64]{0,2,1:T(8,128)(2,1)S(1)} %copy-done.10, bf16[4,512,8,64]{1,3,2,0:T(8,128)(2,1)} %get-tuple-element.493, s32[]{:T(128)S(6)} %copy.161), kind=kOutput, calls=%fused_computation.18.clone.1 | convolution fusion | flops 1107292160 | bytes 69763072 | tf_op jit(solution)/shard_map/while/body/eval_jaxpr/while/body/eval_jaxpr/qhd,khd->hqk/dot_general | solution.py:142
  763.8 27.9 %multiply_convert_fusion.2 = bf16[8,512,2048]{2,1,0:T(8,128)(2,1)} fusion(f32[8,512,2048]{2,1,0:T(8,128)} %get-tuple-element.441, f32[8,512,2048]{2,1,0:T(8,128)} %fusion.161, f32[8,512]{1,0:T(8,128)S(1)} %get-tuple-element.442, f32[8,512]{1,0:T(8,128)S(1)} %dynamic-slice_bitcast_fusion.2), kind=kLoop, calls=%fused_computation.17.clone.1 | loop fusion | flops 41943040 | bytes 83918848 | tf_op jit(solution)/shard_map/while/body/eval_jaxpr/while/body/eval_jaxpr/convert_element_type | solution.py:146
  791.7 10.3 fusion.162
  810.6 20.7 %dynamic_update_slice.31 = f32[4,512,8,64]{1,0,2,3:T(4,128)} dynamic-update-slice(f32[4,512,8,64]{1,0,2,3:T(4,128)} %get-tuple-element.478, f32[1,512,8,64]{1,0,2,3:T(1,128)S(1)} %copy.144, s32[]{:T(128)S(6)} %copy.161, s32[]{:T(128)} %constant.172.clone.1..sunk, s32[]{:T(128)} %constant.172.clone.1..sunk, s32[]{:T(128)} %constant.172.clone.1..sunk) | dynamic-update-slice | bytes 2097156 | tf_op jit(solution)/shard_map/while/body/eval_jaxpr/while/body/jit(dynamic_update_index_in_dim)/dynamic_update_slice | solution.py:114
  831.9 14.1 fusion.161
  846.1 17.3 %bitcast_add_fusion.7 = f32[2048,8,64]{0,2,1:T(8,128)} fusion(f32[2048,8,64]{0,2,1:T(8,128)} %get-tuple-element.477, f32[8,512,2048]{2,1,0:T(8,128)} %fusion.161, f32[8,512]{1,0:T(8,128)S(1)} %dynamic-slice_bitcast_fusion.2, pred[]{:T(512)S(6)} %compare.16, bf16[4,512,8,64]{1,3,2,0:T(8,128)(2,1)} %get-tuple-element.493, s32[]{:T(128)S(6)} %copy.161), kind=kOutput, calls=%fused_computation.24.clone.1 | convolution fusion | flops 1101004800 | bytes 42483716 | tf_op jit(solution)/shard_map/while/body/eval_jaxpr/while/body/eval_jaxpr/hqk,qhd->khd/dot_general | solution.py:158
  863.3 23.6 %multiply_reduce_fusion.6 = (f32[8,512]{1,0:T(8,128)S(1)}, f32[8,512,2048]{2,1,0:T(8,128)}) fusion(f32[8,512,2048]{2,1,0:T(8,128)} %fusion.161, f32[8,512]{1,0:T(8,128)S(1)} %dynamic-slice_bitcast_fusion.2, bf16[2048,8,64]{0,2,1:T(8,128)(2,1)S(1)} %copy-done.10, bf16[4,512,8,64]{1,3,2,0:T(8,128)(2,1)} %get-tuple-element.493, s32[]{:T(128)S(6)} %copy.161), kind=kOutput, calls=%fused_computation.18.clone.1 | convolution fusion | flops 1107292160 | bytes 69763072 | tf_op jit(solution)/shard_map/while/body/eval_jaxpr/while/body/eval_jaxpr/qhd,khd->hqk/dot_general | solution.py:142
  887.0 27.9 %multiply_convert_fusion.2 = bf16[8,512,2048]{2,1,0:T(8,128)(2,1)} fusion(f32[8,512,2048]{2,1,0:T(8,128)} %get-tuple-element.441, f32[8,512,2048]{2,1,0:T(8,128)} %fusion.161, f32[8,512]{1,0:T(8,128)S(1)} %get-tuple-element.442, f32[8,512]{1,0:T(8,128)S(1)} %dynamic-slice_bitcast_fusion.2), kind=kLoop, calls=%fused_computation.17.clone.1 | loop fusion | flops 41943040 | bytes 83918848 | tf_op jit(solution)/shard_map/while/body/eval_jaxpr/while/body/eval_jaxpr/convert_element_type | solution.py:146
  914.8 10.3 fusion.162
  926.3 7.6 bitcast_add_fusion.6
  935.0 20.7 %dynamic_update_slice.31 = f32[4,512,8,64]{1,0,2,3:T(4,128)} dynamic-update-slice(f32[4,512,8,64]{1,0,2,3:T(4,128)} %get-tuple-element.478, f32[1,512,8,64]{1,0,2,3:T(1,128)S(1)} %copy.144, s32[]{:T(128)S(6)} %copy.161, s32[]{:T(128)} %constant.172.clone.1..sunk, s32[]{:T(128)} %constant.172.clone.1..sunk, s32[]{:T(128)} %constant.172.clone.1..sunk) | dynamic-update-slice | bytes 2097156 | tf_op jit(solution)/shard_map/while/body/eval_jaxpr/while/body/jit(dynamic_update_index_in_dim)/dynamic_update_slice | solution.py:114
  956.4 14.1 fusion.161
  970.5 17.3 %bitcast_add_fusion.7 = f32[2048,8,64]{0,2,1:T(8,128)} fusion(f32[2048,8,64]{0,2,1:T(8,128)} %get-tuple-element.477, f32[8,512,2048]{2,1,0:T(8,128)} %fusion.161, f32[8,512]{1,0:T(8,128)S(1)} %dynamic-slice_bitcast_fusion.2, pred[]{:T(512)S(6)} %compare.16, bf16[4,512,8,64]{1,3,2,0:T(8,128)(2,1)} %get-tuple-element.493, s32[]{:T(128)S(6)} %copy.161), kind=kOutput, calls=%fused_computation.24.clone.1 | convolution fusion | flops 1101004800 | bytes 42483716 | tf_op jit(solution)/shard_map/while/body/eval_jaxpr/while/body/eval_jaxpr/hqk,qhd->khd/dot_general | solution.py:158
  987.8 23.6 %multiply_reduce_fusion.6 = (f32[8,512]{1,0:T(8,128)S(1)}, f32[8,512,2048]{2,1,0:T(8,128)}) fusion(f32[8,512,2048]{2,1,0:T(8,128)} %fusion.161, f32[8,512]{1,0:T(8,128)S(1)} %dynamic-slice_bitcast_fusion.2, bf16[2048,8,64]{0,2,1:T(8,128)(2,1)S(1)} %copy-done.10, bf16[4,512,8,64]{1,3,2,0:T(8,128)(2,1)} %get-tuple-element.493, s32[]{:T(128)S(6)} %copy.161), kind=kOutput, calls=%fused_computation.18.clone.1 | convolution fusion | flops 1107292160 | bytes 69763072 | tf_op jit(solution)/shard_map/while/body/eval_jaxpr/while/body/eval_jaxpr/qhd,khd->hqk/dot_general | solution.py:142
  1011.4 27.9 %multiply_convert_fusion.2 = bf16[8,512,2048]{2,1,0:T(8,128)(2,1)} fusion(f32[8,512,2048]{2,1,0:T(8,128)} %get-tuple-element.441, f32[8,512,2048]{2,1,0:T(8,128)} %fusion.161, f32[8,512]{1,0:T(8,128)S(1)} %get-tuple-element.442, f32[8,512]{1,0:T(8,128)S(1)} %dynamic-slice_bitcast_fusion.2), kind=kLoop, calls=%fused_computation.17.clone.1 | loop fusion | flops 41943040 | bytes 83918848 | tf_op jit(solution)/shard_map/while/body/eval_jaxpr/while/body/eval_jaxpr/convert_element_type | solution.py:146
  1039.3 10.3 fusion.162
  1059.5 20.7 %dynamic_update_slice.31 = f32[4,512,8,64]{1,0,2,3:T(4,128)} dynamic-update-slice(f32[4,512,8,64]{1,0,2,3:T(4,128)} %get-tuple-element.478, f32[1,512,8,64]{1,0,2,3:T(1,128)S(1)} %copy.144, s32[]{:T(128)S(6)} %copy.161, s32[]{:T(128)} %constant.172.clone.1..sunk, s32[]{:T(128)} %constant.172.clone.1..sunk, s32[]{:T(128)} %constant.172.clone.1..sunk) | dynamic-update-slice | bytes 2097156 | tf_op jit(solution)/shard_map/while/body/eval_jaxpr/while/body/jit(dynamic_update_index_in_dim)/dynamic_update_slice | solution.py:114
  1080.9 14.1 fusion.161
  1095.0 17.3 %bitcast_add_fusion.7 = f32[2048,8,64]{0,2,1:T(8,128)} fusion(f32[2048,8,64]{0,2,1:T(8,128)} %get-tuple-element.477, f32[8,512,2048]{2,1,0:T(8,128)} %fusion.161, f32[8,512]{1,0:T(8,128)S(1)} %dynamic-slice_bitcast_fusion.2, pred[]{:T(512)S(6)} %compare.16, bf16[4,512,8,64]{1,3,2,0:T(8,128)(2,1)} %get-tuple-element.493, s32[]{:T(128)S(6)} %copy.161), kind=kOutput, calls=%fused_computation.24.clone.1 | convolution fusion | flops 1101004800 | bytes 42483716 | tf_op jit(solution)/shard_map/while/body/eval_jaxpr/while/body/eval_jaxpr/hqk,qhd->khd/dot_general | solution.py:158
  1112.3 23.6 %multiply_reduce_fusion.6 = (f32[8,512]{1,0:T(8,128)S(1)}, f32[8,512,2048]{2,1,0:T(8,128)}) fusion(f32[8,512,2048]{2,1,0:T(8,128)} %fusion.161, f32[8,512]{1,0:T(8,128)S(1)} %dynamic-slice_bitcast_fusion.2, bf16[2048,8,64]{0,2,1:T(8,128)(2,1)S(1)} %copy-done.10, bf16[4,512,8,64]{1,3,2,0:T(8,128)(2,1)} %get-tuple-element.493, s32[]{:T(128)S(6)} %copy.161), kind=kOutput, calls=%fused_computation.18.clone.1 | convolution fusion | flops 1107292160 | bytes 69763072 | tf_op jit(solution)/shard_map/while/body/eval_jaxpr/while/body/eval_jaxpr/qhd,khd->hqk/dot_general | solution.py:142
  1135.9 27.9 %multiply_convert_fusion.2 = bf16[8,512,2048]{2,1,0:T(8,128)(2,1)} fusion(f32[8,512,2048]{2,1,0:T(8,128)} %get-tuple-element.441, f32[8,512,2048]{2,1,0:T(8,128)} %fusion.161, f32[8,512]{1,0:T(8,128)S(1)} %get-tuple-element.442, f32[8,512]{1,0:T(8,128)S(1)} %dynamic-slice_bitcast_fusion.2), kind=kLoop, calls=%fused_computation.17.clone.1 | loop fusion | flops 41943040 | bytes 83918848 | tf_op jit(solution)/shard_map/while/body/eval_jaxpr/while/body/eval_jaxpr/convert_element_type | solution.py:146
  1163.7 10.3 fusion.162
  1183.9 20.7 %dynamic_update_slice.31 = f32[4,512,8,64]{1,0,2,3:T(4,128)} dynamic-update-slice(f32[4,512,8,64]{1,0,2,3:T(4,128)} %get-tuple-element.478, f32[1,512,8,64]{1,0,2,3:T(1,128)S(1)} %copy.144, s32[]{:T(128)S(6)} %copy.161, s32[]{:T(128)} %constant.172.clone.1..sunk, s32[]{:T(128)} %constant.172.clone.1..sunk, s32[]{:T(128)} %constant.172.clone.1..sunk) | dynamic-update-slice | bytes 2097156 | tf_op jit(solution)/shard_map/while/body/eval_jaxpr/while/body/jit(dynamic_update_index_in_dim)/dynamic_update_slice | solution.py:114
  1235.0 7.6 fusion.72
  1248.1 7.8 convolution_convert_fusion.7
  1255.9 8.2 fusion.79
  1264.2 11.2 convolution_convert_fusion
  1275.8 223.1 %all-reduce.4.cloned.1.call-done = (bf16[1024,3,512]{2,0,1:T(8,128)(2,1)}, bf16[512,1024]{1,0:T(8,128)(2,1)}, bf16[1024,2048]{1,0:T(8,128)(2,1)}, bf16[2048,1024]{1,0:T(8,128)(2,1)}) async-done(((bf16[1024,3,512]{2,0,1:T(8,128)(2,1)}, bf16[512,1024]{1,0:T(8,128)(2,1)}, bf16[1024,2048]{1,0:T(8,128)(2,1)}, bf16[2048,1024]{1,0:T(8,128)(2,1)}), (bf16[1024,3,512]{2,0,1:T(8,128)(2,1)}, ...) | async-done | bytes 12582928 | tf_op jit(solution)/shard_map/psum | solution.py:298
  1514.4 41.3 %reduce-scatter.12.cloned.1.call-done = bf16[1024,1024]{1,0:T(8,128)(2,1)} async-done(((bf16[2048,1024]{1,0:T(8,128)(2,1)}), bf16[1024,1024]{1,0:T(8,128)(2,1)}) %reduce-scatter.12.cloned.1.call-update) | async-done | bytes 2097168 | tf_op jit(solution)/shard_map/reduce_scatter | solution.py:270
  1570.6 60.7 %all-reduce = (bf16[6,512]{1,0:T(8,128)(2,1)S(1)}, bf16[3,512]{1,0:T(4,128)(2,1)S(1)}, bf16[2048]{0:T(1024)(128)(2,1)S(1)}) all-reduce(bf16[6,512]{1,0:T(8,128)(2,1)S(1)} %convert_element_type.255, bf16[3,512]{1,0:T(4,128)(2,1)S(1)} %convert_element_type.259, ...), channel_id=1, replica_groups=mesh['dp'=16,'tensor'=2] {'dp'}, use_global_device_ids=true, to_apply=%region_26.28 | all-reduce | flops 6656 | bytes 26624 | tf_op jit(solution)/shard_map/psum | solution.py:304
  (244 shorter events, 177.3 us)
Async XLA Ops:
  7.2 297.1 %copy-start = (bf16[512,1024]{1,0:T(8,128)(2,1)S(1)}, bf16[512,1024]{1,0:T(8,128)(2,1)}, u32[]{:S(2)}) copy-start(bf16[512,1024]{1,0:T(8,128)(2,1)} %param.29) | copy-start | bytes 3145732
  7.2 6.5 copy-start.6
  7.2 68.3 %all-gather.5.cloned.1.call-start = ((), (), s32[]{:S(2)}) async-start(), calls=%async_computation.5 | async-start | bytes 6291456 | tf_op jit(solution)/shard_map/all_gather | solution.py:201
  8.1 5.0 copy-start.32
  10.8 5.2 copy-start.45
  15.9 347.4 %reduce-scatter.6.cloned.1.call-start = ((), (), s32[]{:S(2)}) async-start(), calls=%async_computation.6 | async-start | bytes 6291456 | tf_op jit(solution)/shard_map/reduce_scatter | solution.py:211
  15.9 16.0 copy-start.52
  31.9 74.8 %copy-start.16 = (f32[2048,64]{0,1:T(8,128)}, f32[2048,64]{0,1:T(8,128)S(1)}, u32[]{:S(2)}) copy-start(f32[2048,64]{0,1:T(8,128)S(1)} %concatenate.16) | copy-start | bytes 1572868
  32.0 69.7 %copy-start.44 = (s32[1024]{0:T(1024)}, s32[1024]{0:T(1024)S(1)}, u32[]{:S(2)}) copy-start(s32[1024]{0:T(1024)S(1)} %pad_clamp_fusion) | copy-start | bytes 12292
  88.4 8.3 copy-start.13
  88.4 8.3 copy-start.14
  101.7 5.1 copy-start.18
  298.4 4.6 copy-start.3
  308.7 54.5 %copy-start.7 = (bf16[1024,1024]{1,0:T(8,128)(2,1)S(1)}, bf16[1024,1024]{1,0:T(8,128)(2,1)}, u32[]{:S(2)}) copy-start(bf16[1024,1024]{1,0:T(8,128)(2,1)} %param.24) | copy-start | bytes 6291460
  308.8 118.1 %all-gather.7.cloned.1.call-start = ((), (), s32[]{:S(2)}) async-start(), calls=%async_computation.7 | async-start | bytes 6291456 | tf_op jit(solution)/shard_map/all_gather | solution.py:220
  309.4 57.4 %copy-start.26 = (f32[1024]{0:T(1024)}, f32[1024]{0:T(1024)S(1)}, u32[]{:S(2)}) copy-start(f32[1024]{0:T(1024)S(1)} %convert_element_type.233) | copy-start | bytes 12292
  309.4 57.4 %copy-start.36 = (f32[1024]{0:T(1024)}, f32[1024]{0:T(1024)S(1)}, u32[]{:S(2)}) copy-start(f32[1024]{0:T(1024)S(1)} %convert_element_type.234) | copy-start | bytes 12292
  369.9 115.1 %all-gather.9.cloned.1.call-start = ((), (), s32[]{:S(2)}) async-start(), calls=%async_computation.9 | async-start | bytes 6291456 | tf_op jit(solution)/shard_map/all_gather | solution.py:234
  370.5 203.7 %reduce-scatter.10.cloned.1.call-start = ((), (), s32[]{:S(2)}) async-start(), calls=%async_computation.10 | async-start | bytes 6291456 | tf_op jit(solution)/shard_map/reduce_scatter | solution.py:242
  485.1 24.0 %copy-start.53 = (bf16[1024,2048]{1,0:T(8,128)(2,1)S(1)}, bf16[1024,2048]{1,0:T(8,128)(2,1)}, u32[]{:S(2)}) copy-start(bf16[1024,2048]{1,0:T(8,128)(2,1)} %param.33) | copy-start | bytes 12582916
  519.7 110.9 %reduce-scatter.8.cloned.1.call-start = ((), (), s32[]{:S(2)}) async-start(), calls=%async_computation.8 | async-start | bytes 6291456 | tf_op jit(solution)/shard_map/reduce_scatter | solution.py:225
  533.6 40.6 %copy-start.8 = (bf16[1024,1024]{1,0:T(8,128)(2,1)S(1)}, bf16[1024,1024]{1,0:T(8,128)(2,1)}, u32[]{:S(2)}) copy-start(bf16[1024,1024]{1,0:T(8,128)(2,1)} %param.24) | copy-start | bytes 6291460
  533.6 40.6 %copy-start.27 = (f32[1024]{0:T(1024)S(1)}, f32[1024]{0:T(1024)}, u32[]{:S(2)}) copy-start(f32[1024]{0:T(1024)} %copy-done.26) | copy-start | bytes 12292
  533.6 40.6 %copy-start.31 = (f32[1024]{0:T(1024)S(1)}, f32[1024]{0:T(1024)}, u32[]{:S(2)}) copy-start(f32[1024]{0:T(1024)} %copy-done.30) | copy-start | bytes 12292
  533.6 40.6 %copy-start.37 = (f32[1024]{0:T(1024)S(1)}, f32[1024]{0:T(1024)}, u32[]{:S(2)}) copy-start(f32[1024]{0:T(1024)} %copy-done.36) | copy-start | bytes 12292
  533.6 40.6 %copy-start.39 = (f32[1024]{0:T(1024)S(1)}, f32[1024]{0:T(1024)}, u32[]{:S(2)}) copy-start(f32[1024]{0:T(1024)} %copy-done.38) | copy-start | bytes 12292
  533.7 161.7 %all-gather.11.cloned.1.call-start = ((), (), s32[]{:S(2)}) async-start(), calls=%async_computation.11 | async-start | bytes 6291456 | tf_op jit(solution)/shard_map/all_gather | solution.py:252
  638.4 860.5 %all-reduce.4.cloned.1.call-start = ((), (), s32[]{:S(2)}) async-start(), calls=%async_computation.14 | async-start | bytes 25165824 | tf_op jit(solution)/shard_map/psum | solution.py:298
  638.5 14.6 copy-start.55
  703.5 5.6 copy-start.4
  724.1 16.1 copy-start.10
  791.7 11.5 copy-start.2
  803.2 6.3 copy-start.15
  809.5 21.8 %copy-start.5 = (bf16[2048,8,64]{0,2,1:T(8,128)(2,1)S(1)}, bf16[2048,8,64]{0,2,1:T(8,128)(2,1)}, u32[]{:S(2)}) copy-start(bf16[2048,8,64]{0,2,1:T(8,128)(2,1)} %get-tuple-element.526) | copy-start | bytes 6291460 | tf_op jit(solution)/shard_map/while/body/eval_jaxpr/while
  846.1 17.3 %copy-start.10 = (bf16[2048,8,64]{0,2,1:T(8,128)(2,1)S(1)}, bf16[2048,8,64]{0,2,1:T(8,128)(2,1)}, u32[]{:S(2)}) copy-start(bf16[2048,8,64]{0,2,1:T(8,128)(2,1)} %get-tuple-element.494) | copy-start | bytes 6291460 | tf_op jit(solution)/shard_map/while/body/eval_jaxpr/while
  914.8 11.5 copy-start.2
  926.3 7.6 copy-start.15
  933.9 21.8 %copy-start.5 = (bf16[2048,8,64]{0,2,1:T(8,128)(2,1)S(1)}, bf16[2048,8,64]{0,2,1:T(8,128)(2,1)}, u32[]{:S(2)}) copy-start(bf16[2048,8,64]{0,2,1:T(8,128)(2,1)} %get-tuple-element.526) | copy-start | bytes 6291460 | tf_op jit(solution)/shard_map/while/body/eval_jaxpr/while
  970.5 17.3 %copy-start.10 = (bf16[2048,8,64]{0,2,1:T(8,128)(2,1)S(1)}, bf16[2048,8,64]{0,2,1:T(8,128)(2,1)}, u32[]{:S(2)}) copy-start(bf16[2048,8,64]{0,2,1:T(8,128)(2,1)} %get-tuple-element.494) | copy-start | bytes 6291460 | tf_op jit(solution)/shard_map/while/body/eval_jaxpr/while
  1039.3 11.5 copy-start.2
  1050.8 7.6 copy-start.15
  1058.4 21.8 %copy-start.5 = (bf16[2048,8,64]{0,2,1:T(8,128)(2,1)S(1)}, bf16[2048,8,64]{0,2,1:T(8,128)(2,1)}, u32[]{:S(2)}) copy-start(bf16[2048,8,64]{0,2,1:T(8,128)(2,1)} %get-tuple-element.526) | copy-start | bytes 6291460 | tf_op jit(solution)/shard_map/while/body/eval_jaxpr/while
  1095.0 17.3 %copy-start.10 = (bf16[2048,8,64]{0,2,1:T(8,128)(2,1)S(1)}, bf16[2048,8,64]{0,2,1:T(8,128)(2,1)}, u32[]{:S(2)}) copy-start(bf16[2048,8,64]{0,2,1:T(8,128)(2,1)} %get-tuple-element.494) | copy-start | bytes 6291460 | tf_op jit(solution)/shard_map/while/body/eval_jaxpr/while
  1163.7 11.5 copy-start.2
  1175.3 7.6 copy-start.15
  1182.8 21.8 %copy-start.5 = (bf16[2048,8,64]{0,2,1:T(8,128)(2,1)S(1)}, bf16[2048,8,64]{0,2,1:T(8,128)(2,1)}, u32[]{:S(2)}) copy-start(bf16[2048,8,64]{0,2,1:T(8,128)(2,1)} %get-tuple-element.526) | copy-start | bytes 6291460 | tf_op jit(solution)/shard_map/while/body/eval_jaxpr/while
  1210.8 4.6 copy-start.12
  1210.8 4.6 copy-start.17
  1229.8 5.2 copy-start.19
  1248.1 7.8 copy-start.20
  1248.1 7.8 copy-start.54
  1264.2 291.5 %reduce-scatter.12.cloned.1.call-start = ((), (), s32[]{:S(2)}) async-start(), calls=%async_computation.12 | async-start | bytes 6291456 | tf_op jit(solution)/shard_map/reduce_scatter | solution.py:270
  1275.4 294.5 %reduce-scatter.14.cloned.1.call-start = ((), (), s32[]{:S(2)}) async-start(), calls=%async_computation.13 | async-start | bytes 49152 | tf_op jit(solution)/shard_map/reduce_scatter | solution.py:288
  1505.5 4.5 copy-start.21
  1509.9 45.7 %copy-start.9 = (bf16[1024,1024]{1,0:T(8,128)(2,1)S(1)}, bf16[1024,1024]{1,0:T(8,128)(2,1)}, u32[]{:S(2)}) copy-start(bf16[1024,1024]{1,0:T(8,128)(2,1)} %param.24) | copy-start | bytes 6291460
  1509.9 45.7 %copy-start.29 = (f32[1024]{0:T(1024)S(1)}, f32[1024]{0:T(1024)}, u32[]{:S(2)}) copy-start(f32[1024]{0:T(1024)} %copy-done.28) | copy-start | bytes 12292
  1509.9 45.7 %copy-start.33 = (f32[1024]{0:T(1024)S(1)}, f32[1024]{0:T(1024)}, u32[]{:S(2)}) copy-start(f32[1024]{0:T(1024)} %copy-done.32) | copy-start | bytes 12292
  1509.9 45.7 %copy-start.35 = (f32[1024]{0:T(1024)S(1)}, f32[1024]{0:T(1024)}, u32[]{:S(2)}) copy-start(f32[1024]{0:T(1024)} %copy-done.34) | copy-start | bytes 12292
  1514.4 44.8 %copy-start.40 = (f32[1024]{0:T(1024)S(1)}, f32[1024]{0:T(1024)}, u32[]{:S(2)}) copy-start(f32[1024]{0:T(1024)} %get-tuple-element.252) | copy-start | bytes 12292
  1514.4 44.9 %copy-start.41 = (f32[1024]{0:T(1024)S(1)}, f32[1024]{0:T(1024)}, u32[]{:S(2)}) copy-start(f32[1024]{0:T(1024)} %get-tuple-element.258) | copy-start | bytes 12292
  1514.4 44.9 %copy-start.42 = (f32[1024]{0:T(1024)S(1)}, f32[1024]{0:T(1024)}, u32[]{:S(2)}) copy-start(f32[1024]{0:T(1024)} %get-tuple-element.299) | copy-start | bytes 12292
  1514.4 44.9 %copy-start.43 = (f32[1024]{0:T(1024)S(1)}, f32[1024]{0:T(1024)}, u32[]{:S(2)}) copy-start(f32[1024]{0:T(1024)} %get-tuple-element.309) | copy-start | bytes 12292
  1559.9 73.2 %copy-start.1 = (bf16[512,1024]{1,0:T(8,128)(2,1)S(1)}, bf16[512,1024]{1,0:T(8,128)(2,1)}, u32[]{:S(2)}) copy-start(bf16[512,1024]{1,0:T(8,128)(2,1)} %param.29) | copy-start | bytes 3145732
  1560.0 10.7 copy-start.47
  (15 other events, 27.7 us)
Sparse Core Ops, SparseCore 0:
  16.0 59.4 all-gather.4
  308.9 54.3 reduce-scatter.5
  370.0 56.7 all-gather.6
  428.3 56.7 all-gather.8
  519.8 54.3 reduce-scatter.9
  576.3 54.2 reduce-scatter.7
  638.6 56.7 all-gather.10
  1264.3 234.6 all-reduce.3
  1501.3 54.3 reduce-scatter.11
  1560.1 9.7 reduce-scatter.13
where the time goes:
time: 1650 us; the launch traced here: 1640 us
  matrix products  575 us (35%)
  waiting for transfers between devices  554 us (34%)
  other arithmetic  253 us (15%)
  local copies, waits for them, and re-layouts  181 us (11%)
  blocking collectives  60.7 us (4%)
    psum x1, waiting for transfers between devices, on_device(): lax.psum(qkv_weight_grad.astype(jnp.bfloat16), 'dp').astype(jnp.float32)  223 us
    dot_general x8, matrix products, one_block(): jnp.einsum('qhd,khd->hqk', query_blk, clip_k, preferred_element_type=jnp....  113 us
    convert_element_type x4, other arithmetic, one_block(): score_grad = (shares * (share_grad - centre)).astype(jnp.bfloat16)  111 us
    dot_general x4, matrix products, one_block(): jnp.einsum('qhd,khd->hqk', dout_blk, clip_v, preferred_element_type=jnp.f...  94.5 us
    dynamic_update_slice x8, local copies, waits for them, and re-layouts, one_clip(): outputs, log_totals = lax.map(one_block, blocks_q)  87 us
    dot_general x4, matrix products, one_block(): jnp.einsum('hqk,qhd->khd', shares.astype(jnp.bfloat16), dout_blk, preferr...  67.9 us
    dot_general x4, matrix products, one_block(): jnp.einsum('hqk,khd->qhd', shares_low, clip_v, preferred_element_type=jnp...  62.2 us
    psum x1, blocking collectives, on_device(): lax.psum(vector_parts.astype(jnp.bfloat16), 'dp').astype(jnp.float32)  60.7 us
  transfers between devices with their start and end apart: 10, of which 10 were waited for; matrix products, arithmetic and copies ran while one was open for 9% of the time, Pallas kernels for 0%

commit v1 on v0

v1 whole, which is shorter than its diff:
```python
import functools
import math

import jax
import jax.numpy as jnp
import numpy as np
from jax import lax
from jax.experimental import pallas as pl
from jax.experimental.pallas import tpu as pltpu
from jax.sharding import PartitionSpec as P

HD = 64
GH = 16
GW = 16
SEQ = 2048
EPS = 1e-06
LANES = 128
ROT = 2 * (HD // 3 // 2)
HALF_ROT = ROT // 2
LOG2E = math.log2(math.e)
SCALE = 1.0 / math.sqrt(HD)
BF = jnp.bfloat16
F32 = jnp.float32
VMEM_BYTES = 56 << 20


def dot_nt(left, right):
    return lax.dot_general(left, right, (((1,), (1,)), ((), ())), preferred_element_type=F32)


def dot_nn(left, right):
    return lax.dot_general(left, right, (((1,), (0,)), ((), ())), preferred_element_type=F32)


def dot_tn(left, right):
    return lax.dot_general(left, right, (((0,), (0,)), ((), ())), preferred_element_type=F32)


def call(kernel, flops, moved, exps=0, **kw):
    return pl.pallas_call(
        kernel,
        compiler_params=pltpu.CompilerParams(vmem_limit_bytes=VMEM_BYTES),
        cost_estimate=pl.CostEstimate(flops=flops, bytes_accessed=moved, transcendentals=exps),
        **kw,
    )


def rotary_tables(first, count):
    lane = np.arange(LANES) % HD
    axis = lane // ROT
    inside = lane % ROT
    freq = np.float32(10000.0) ** (
        -(inside % HALF_ROT).astype(np.float32) / np.float32(HALF_ROT)
    )
    turned = axis < 3
    early = turned & (inside < HALF_ROT)
    late = turned & (inside >= HALF_ROT)
    index = first + jnp.arange(count, dtype=jnp.int32)[:, None]
    places = (index // (GH * GW), index // GW % GH, index % GW)
    place = jnp.where(axis == 0, places[0], jnp.where(axis == 1, places[1], places[2]))
    angle = place.astype(F32) * freq.astype(np.float32)[None, :]
    cos = jnp.where(turned, jnp.cos(angle), 1.0)
    sin = jnp.sin(angle)
    return cos, jnp.where(early, -sin, 0.0), jnp.where(late, sin, 0.0)


def turn(x, cos, sin_a, sin_b):
    return (
        x * cos
        + pltpu.roll(x, LANES - HALF_ROT, 1) * sin_a
        + pltpu.roll(x, HALF_ROT, 1) * sin_b
    )


def turn_back(g, cos, sin_a, sin_b):
    return (
        g * cos
        + pltpu.roll(g * sin_b, LANES - HALF_ROT, 1)
        + pltpu.roll(g * sin_a, HALF_ROT, 1)
    )


def qkv_kernel(n_ref, w_ref, b_ref, c_ref, sa_ref, sb_ref, q_ref, kv_ref, *, q_steps):
    step = pl.program_id(0)
    rows = dot_nn(n_ref[...], w_ref[...]) + b_ref[...]
    wide = rows.shape[1]

    def turned():
        tables = (c_ref[...], sa_ref[...], sb_ref[...])
        parts = [
            turn(rows[:, at : at + LANES], *tables).astype(BF) for at in range(0, wide, LANES)
        ]
        return jnp.concatenate(parts, axis=1)

    @pl.when(step < q_steps)
    def _():
        q_ref[...] = turned()

    @pl.when((step >= q_steps) & (step < 2 * q_steps))
    def _():
        kv_ref[...] = turned()

    @pl.when(step >= 2 * q_steps)
    def _():
        kv_ref[...] = rows.astype(BF)


def qkv_rows(normed, weight, bias, tables):
    tokens, width = normed.shape
    cols = weight.shape[1] // 3
    tile = 256 if cols % 256 == 0 else LANES
    q_steps = cols // tile
    whole = lambda n: (0, 0)
    return call(
        functools.partial(qkv_kernel, q_steps=q_steps),
        2 * tokens * width * 3 * cols,
        2 * (tokens * width + width * 3 * cols + tokens * 3 * cols),
        grid=(3 * q_steps,),
        in_specs=[
            pl.BlockSpec((tokens, width), whole),
            pl.BlockSpec((width, tile), lambda n: (0, n)),
            pl.BlockSpec((1, tile), lambda n: (0, n)),
        ]
        + [pl.BlockSpec((tokens, LANES), whole)] * 3,
        out_specs=[
            pl.BlockSpec((tokens, tile), lambda n: (0, jnp.minimum(n, q_steps - 1))),
            pl.BlockSpec((tokens, tile), lambda n: (0, jnp.maximum(n - q_steps, 0))),
        ],
        out_shape=[
            jax.ShapeDtypeStruct((tokens, cols), BF),
            jax.ShapeDtypeStruct((tokens, 2 * cols), BF),
        ],
    )(normed, weight, bias, *tables)


def attend_kernel(*refs, sources, rows_at):
    q_ref = refs[0]
    k_refs = refs[1 : 1 + sources]
    v_refs = refs[1 + sources : 1 + 2 * sources]
    o_ref, lse_ref = refs[1 + 2 * sources :]
    lane = lax.broadcasted_iota(jnp.int32, (1, LANES), 1)

    def body(i, carry):
        rows = pl.ds(pl.multiple_of(i * rows_at, rows_at), rows_at)
        q = q_ref[rows, :]
        outs, logs = [], []
        for head in range(2):
            mine = (lane // HD) == head
            q_head = jnp.where(mine, q, jnp.zeros_like(q))
            scores = [dot_nt(q_head, k[...]) for k in k_refs]
            peak = functools.reduce(
                jnp.maximum, [jnp.max(s, axis=1, keepdims=True) for s in scores]
            )
            weights = [jnp.exp2((s - peak) * (SCALE * LOG2E)) for s in scores]
            total = sum(jnp.sum(w, axis=1, keepdims=True) for w in weights)
            out = sum(dot_nn(w.astype(BF), v[...]) for w, v in zip(weights, v_refs))
            outs.append(out / total)
            logs.append(peak * (SCALE * LOG2E) + jnp.log2(total))
        first = lane < HD
        o_ref[rows, :] = jnp.where(first, outs[0], outs[1]).astype(BF)
        logs_t = jnp.where(first, logs[0], logs[1]).T
        lse_ref[0, 0:1, rows] = logs_t[0:1]
        lse_ref[0, 1:2, rows] = logs_t[HD : HD + 1]
        return carry

    steps = q_ref.shape[0] // rows_at
    lax.fori_loop(0, steps, body, 0, unroll=2 if steps % 2 == 0 else 1)


def attend(q, kvs):
    tokens, cols = q.shape
    pairs = cols // LANES
    keys = sum(kv.shape[0] for kv in kvs)
    q_spec = pl.BlockSpec((tokens, LANES), lambda i: (0, i))
    k_specs = [pl.BlockSpec((kv.shape[0], LANES), lambda i: (0, i)) for kv in kvs]
    v_specs = [pl.BlockSpec((kv.shape[0], LANES), lambda i: (0, pairs + i)) for kv in kvs]
    return call(
        functools.partial(attend_kernel, sources=len(kvs), rows_at=256),
        4 * 4 * tokens * keys * cols,
        2 * (2 * tokens * cols + 2 * keys * cols),
        tokens * keys * 2 * pairs,
        grid=(pairs,),
        in_specs=[q_spec] + k_specs + v_specs,
        out_specs=[q_spec, pl.BlockSpec((1, 2, tokens), lambda i: (i, 0, 0))],
        out_shape=[
            jax.ShapeDtypeStruct((tokens, cols), BF),
            jax.ShapeDtypeStruct((pairs, 2, tokens), F32),
        ],
    )(q, *kvs, *kvs)


def attend_back_kernel(*refs, sources, keys_at, queries_at):
    q_ref, do_ref, o_ref, lse_ref, c_ref, sa_ref, sb_ref = refs[:7]
    at = 7
    k_refs = refs[at : at + sources]
    v_refs = refs[at + sources : at + 2 * sources]
    at += 2 * sources
    dq_ref = refs[at]
    dk_refs = refs[at + 1 : at + 1 + sources]
    dv_refs = refs[at + 1 + sources : at + 1 + 2 * sources]
    dq_acc, centre = refs[at + 1 + 2 * sources :]
    lane = lax.broadcasted_iota(jnp.int32, (1, LANES), 1)
    tokens = q_ref.shape[0]
    product = (do_ref[...].astype(F32) * o_ref[...].astype(F32)).T
    for head in range(2):
        centre[head : head + 1, :] = jnp.sum(
            product[head * HD : head * HD + HD], axis=0, keepdims=True
        )
    dq_acc[...] = jnp.zeros_like(dq_acc)
    for k_ref, v_ref, dk_ref, dv_ref in zip(k_refs, v_refs, dk_refs, dv_refs):

        def body(j, carry):
            rows = pl.ds(pl.multiple_of(j * keys_at, keys_at), keys_at)
            k, v = k_ref[rows, :], v_ref[rows, :]
            k_t = k.astype(F32).T.astype(BF)
            dv = jnp.zeros((keys_at, LANES), F32)
            dk = jnp.zeros((keys_at, LANES), F32)
            for head in range(2):
                mine = (lane // HD) == head
                for first in range(0, tokens, queries_at):
                    cut = slice(first, first + queries_at)
                    q, do = q_ref[cut, :], do_ref[cut, :]
                    q_head = jnp.where(mine, q, jnp.zeros_like(q))
                    do_head = jnp.where(mine, do, jnp.zeros_like(do))
                    scores = dot_nt(k, q_head)
                    share_grad = dot_nt(v, do_head)
                    shares = jnp.exp2(
                        scores * (SCALE * LOG2E) - lse_ref[0, head : head + 1, cut]
                    )
                    score_grad = (
                        shares * (share_grad - centre[head : head + 1, cut])
                    ).astype(BF)
                    dv += dot_nn(shares.astype(BF), do_head)
                    dk += dot_nn(score_grad, q_head)
                    part = slice(head * HD, head * HD + HD)
                    dq_acc[part, cut] += dot_nn(k_t[part], score_grad)
            dv_ref[rows, :] = dv.astype(BF)
            dk_ref[rows, :] = (dk * SCALE).astype(BF)
            return carry

        lax.fori_loop(0, k_ref.shape[0] // keys_at, body, 0)
    dq = (dq_acc[...] * SCALE).T
    dq_ref[...] = turn_back(dq, c_ref[...], sa_ref[...], sb_ref[...]).astype(BF)


def attend_back(q, out_grad, out, lse, kvs, tables):
    tokens, cols = q.shape
    pairs = cols // LANES
    keys = sum(kv.shape[0] for kv in kvs)
    q_spec = pl.BlockSpec((tokens, LANES), lambda i: (0, i))
    k_specs = [pl.BlockSpec((kv.shape[0], LANES), lambda i: (0, i)) for kv in kvs]
    v_specs = [pl.BlockSpec((kv.shape[0], LANES), lambda i: (0, pairs + i)) for kv in kvs]
    table = pl.BlockSpec((tokens, LANES), lambda i: (0, 0))
    piece = min(512, tokens)
    outs = call(
        functools.partial(
            attend_back_kernel, sources=len(kvs), keys_at=512, queries_at=piece
        ),
        10 * 4 * tokens * keys * cols,
        2 * (4 * tokens * cols + 4 * keys * cols),
        tokens * keys * 2 * pairs,
        grid=(pairs,),
        in_specs=[q_spec, q_spec, q_spec]
        + [pl.BlockSpec((1, 2, tokens), lambda i: (i, 0, 0))]
        + [table] * 3
        + k_specs
        + v_specs,
        out_specs=[q_spec] + k_specs + k_specs,
        out_shape=[jax.ShapeDtypeStruct((tokens, cols), BF)]
        + [jax.ShapeDtypeStruct((kv.shape[0], cols), BF) for kv in kvs] * 2,
        scratch_shapes=[pltpu.VMEM((LANES, tokens), F32), pltpu.VMEM((2, tokens), F32)],
    )(q, out_grad, out, lse, *tables, *kvs, *kvs)
    n = len(kvs)
    return outs[0], outs[1 : 1 + n], outs[1 + n :]


def key_sum_kernel(own_ref, got_ref, c_ref, sa_ref, sb_ref, dk_ref):
    total = own_ref[...].astype(F32) + got_ref[...].astype(F32)
    dk_ref[...] = turn_back(total, c_ref[...], sa_ref[...], sb_ref[...]).astype(BF)


def key_sum(own, got, tables):
    tokens, cols = own.shape
    spec = pl.BlockSpec((tokens, LANES), lambda i: (0, i))
    table = pl.BlockSpec((tokens, LANES), lambda i: (0, 0))
    return call(
        key_sum_kernel,
        12 * tokens * cols,
        6 * tokens * cols,
        grid=(cols // LANES,),
        in_specs=[spec, spec] + [table] * 3,
        out_specs=spec,
        out_shape=jax.ShapeDtypeStruct((tokens, cols), BF),
    )(own, got, *tables)


def gelu_parts(hidden):
    size = jnp.abs(hidden)
    bell = jnp.exp2(hidden * hidden * (-0.5 * LOG2E))
    t = 1.0 / (1.0 + (0.3275911 / math.sqrt(2.0)) * size)
    poly = 0.5 * 1.061405429
    for factor in (-1.453152027, 1.421413741, -0.284496736, 0.254829592):
        poly = poly * t + 0.5 * factor
    tail = poly * t * bell
    cdf = jnp.where(hidden >= 0.0, 1.0 - tail, tail)
    return hidden * cdf, cdf + hidden * bell * (1.0 / math.sqrt(2.0 * math.pi))


def up_kernel(n_ref, w_ref, b_ref, acted_ref, slope_ref):
    hidden = dot_nn(n_ref[...], w_ref[...]) + b_ref[...]
    acted, slope = gelu_parts(hidden)
    acted_ref[...] = acted.astype(BF)
    slope_ref[...] = slope.astype(BF)


def up_rows(normed, weight, bias):
    tokens, width = normed.shape
    cols = weight.shape[1]
    tile = 256
    out = pl.BlockSpec((tokens, tile), lambda n: (0, n))
    return call(
        up_kernel,
        2 * tokens * width * cols,
        2 * (tokens * width + width * cols + 2 * tokens * cols),
        tokens * cols,
        grid=(cols // tile,),
        in_specs=[
            pl.BlockSpec((tokens, width), lambda n: (0, 0)),
            pl.BlockSpec((width, tile), lambda n: (0, n)),
            pl.BlockSpec((1, tile), lambda n: (0, n)),
        ],
        out_specs=[out, out],
        out_shape=[jax.ShapeDtypeStruct((tokens, cols), BF)] * 2,
    )(normed, weight, bias)


def hidden_grad_kernel(g_ref, w_ref, slope_ref, hg_ref, sum_ref):
    grad = dot_nt(g_ref[...], w_ref[...]) * slope_ref[...].astype(F32)
    low = grad.astype(BF)
    hg_ref[...] = low
    sum_ref[...] = jnp.sum(low.astype(F32), axis=0, keepdims=True)


def hidden_grads(grad, down, slope):
    tokens, width = grad.shape
    cols = down.shape[0]
    tile = 256
    out = pl.BlockSpec((tokens, tile), lambda n: (0, n))
    return call(
        hidden_grad_kernel,
        2 * tokens * width * cols,
        2 * (tokens * width + width * cols + 2 * tokens * cols),
        grid=(cols // tile,),
        in_specs=[
            pl.BlockSpec((tokens, width), lambda n: (0, 0)),
            pl.BlockSpec((tile, width), lambda n: (n, 0)),
            out,
        ],
        out_specs=[out, pl.BlockSpec((1, tile), lambda n: (0, n))],
        out_shape=[
            jax.ShapeDtypeStruct((tokens, cols), BF),
            jax.ShapeDtypeStruct((1, cols), F32),
        ],
    )(grad, down, slope)


def norm_parts(values, gain, shift):
    centred = values - jnp.mean(values, axis=-1, keepdims=True)
    inv_dev = lax.rsqrt(jnp.mean(centred * centred, axis=-1, keepdims=True) + EPS)
    normal = centred * inv_dev
    return (normal * gain + shift).astype(BF), normal, inv_dev


def norm_back(upstream, normal, inv_dev, gain):
    scaled = upstream * gain
    mean_first = jnp.mean(scaled, axis=-1, keepdims=True)
    mean_second = jnp.mean(scaled * normal, axis=-1, keepdims=True)
    back = inv_dev * (scaled - mean_first - normal * mean_second)
    return back, jnp.sum(upstream * normal, 0), jnp.sum(upstream, 0)


class Paired:
    def __init__(self, n_dp):
        self.n_dp = n_dp
        self.me_dp = lax.axis_index("dp")
        self.me_y = lax.axis_index("tensor")
        self.core = self.me_dp % 2
        self.first = self.core * (SEQ // 2)

    def move(self, x, to):
        pairs = []
        for dp in range(self.n_dp):
            for y in range(2):
                a, b = to(dp, y)
                if (a, b) != (dp, y):
                    pairs.append((dp * 2 + y, a * 2 + b))
        return lax.ppermute(x, ("dp", "tensor"), pairs)

    def swap_rows(self, rows):
        got = self.move(rows, lambda dp, y: (dp - dp % 2 + y, dp % 2))
        return jnp.where(self.core == self.me_y, rows, got)

    def over_y(self, x):
        return self.move(x, lambda dp, y: (dp, 1 - y))

    def over_core(self, x):
        return self.move(x, lambda dp, y: (dp ^ 1, y))

    def over_chip(self, x, bit):
        return self.move(x, lambda dp, y: (dp ^ (2 << bit), y))

    def other_half(self, own):
        rows = own.shape[0] // self.n_dp
        piece = lax.dynamic_slice_in_dim(own, self.me_dp * rows, rows, 0)
        return lax.all_gather(self.over_y(piece), "dp", axis=0, tiled=True)

    def weights(self, own):
        return [own, self.other_half(own)]

    def biases(self, own):
        return [own, self.over_y(own)]

    def keys(self, kv):
        return [kv, self.over_core(kv)]

    def keys_back(self, grads):
        return grads[0], self.over_core(grads[1])

    def reduce(self, own, other):
        rows, cols = own.shape
        chips = self.n_dp // 2
        piece = rows // self.n_dp

        def split(x, axis, bit):
            take = lambda b: lax.dynamic_index_in_dim(x, b, axis, keepdims=False)
            return take(bit), take(1 - bit)

        kept = []
        for half in (own, other):
            keep, send = split(half.reshape(chips, 2, piece, cols), 1, self.core)
            kept.append(keep + self.over_core(send))
        total = kept[0] + self.over_y(kept[1])
        chip = self.me_dp // 2
        for level in range(chips.bit_length() - 1):
            left = total.shape[0] // 2
            keep, send = split(total.reshape(left, 2, piece, cols), 1, (chip >> level) & 1)
            total = keep + self.over_chip(send, level)
        total = total.reshape(piece, cols)
        return lax.all_gather(total, "dp", axis=0, tiled=True).astype(F32)

    def reduce_vectors(self, both, own, other):
        k, width = both.shape
        both = both.reshape(k, 2, width // 2)
        take = lambda b: lax.dynamic_index_in_dim(both, b, 1, keepdims=False).reshape(-1)
        mine = jnp.concatenate([take(self.me_y), own]).reshape(-1, LANES)
        theirs = jnp.concatenate([take(1 - self.me_y), other]).reshape(-1, LANES)
        total = mine + self.over_y(theirs)
        total = total + self.over_core(total)
        for level in range((self.n_dp // 2).bit_length() - 1):
            total = total + self.over_chip(total, level)
        total = total.reshape(-1)
        return total[: k * width // 2].reshape(k, width // 2), total[k * width // 2 :]


class Spread:
    def __init__(self, tokens):
        self.first = lax.axis_index("tensor") * tokens

    def swap_rows(self, rows):
        return rows

    def keys(self, kv):
        return [lax.all_gather(kv, "tensor", axis=0, tiled=True)]

    def keys_back(self, grads):
        return lax.psum_scatter(grads[0], "tensor", scatter_dimension=0, tiled=True), None


def block_step(
    move,
    block_in,
    ln1_scale,
    ln1_shift,
    qkv_ws,
    qkv_bs,
    out_ws,
    out_bias,
    ln2_scale,
    ln2_shift,
    up_ws,
    up_bs,
    down_ws,
    down_bias,
    out_grad,
):
    f32 = lambda v: v.astype(F32)
    tokens = block_in.shape[0]
    tables = rotary_tables(move.first, tokens)
    ln1_gain, ln2_gain = f32(ln1_scale), f32(ln2_scale)
    block_in = move.swap_rows(block_in)
    x_rows = f32(block_in)
    normed1, normal1, inv_one = norm_parts(x_rows, ln1_gain, f32(ln1_shift))
    queries, keys, outs, logs = [], [], [], []
    for weight, bias in zip(qkv_ws, qkv_bs):
        q, kv = qkv_rows(normed1, weight, f32(bias)[None, :], tables)
        queries.append(q)
        keys.append(move.keys(kv))
    for q, kvs in zip(queries, keys):
        out, log = attend(q, kvs)
        outs.append(out)
        logs.append(log)
    grad_low = move.swap_rows(out_grad)
    grad_rows = f32(grad_low)
    branch_one = sum(dot_nn(o, w) for o, w in zip(outs, out_ws)) + f32(out_bias)
    resid = x_rows + branch_one
    normed2, normal2, inv_two = norm_parts(resid, ln2_gain, f32(ln2_shift))
    acts, slopes = [], []
    for weight, bias in zip(up_ws, up_bs):
        acted, slope = up_rows(normed2, weight, f32(bias)[None, :])
        acts.append(acted)
        slopes.append(slope)
    branch_two = sum(dot_nn(a, w) for a, w in zip(acts, down_ws)) + f32(down_bias)
    block_out = move.swap_rows((resid + branch_two).astype(BF))
    down_bias_grad = jnp.sum(grad_rows, 0)
    down_grads = [dot_tn(a, grad_low).astype(BF) for a in acts]
    hidden_gs, up_b_grads = [], []
    for down, slope in zip(down_ws, slopes):
        hg, total = hidden_grads(grad_low, down, slope)
        hidden_gs.append(hg)
        up_b_grads.append(total[0])
    up_grads = [dot_tn(normed2, hg).astype(BF) for hg in hidden_gs]
    normed2_grad = sum(dot_nt(hg, w) for hg, w in zip(hidden_gs, up_ws))
    resid_part, ln2_scale_grad, ln2_shift_grad = norm_back(normed2_grad, normal2, inv_two, ln2_gain)
    resid_grad = grad_rows + resid_part
    branch_grad = resid_grad.astype(BF)
    out_bias_grad = jnp.sum(branch_grad, 0, dtype=F32)
    out_w_grads = [dot_tn(o, branch_grad).astype(BF) for o in outs]
    qkv_w_grads, qkv_b_grads = [], []
    normed1_grad = 0.0
    for q, kvs, out, log, out_w, qkv_w in zip(queries, keys, outs, logs, out_ws, qkv_ws):
        out_g = dot_nt(branch_grad, out_w).astype(BF)
        dq, dks, dvs = attend_back(q, out_g, out, log, kvs, tables)
        dk_own, dk_got = move.keys_back(dks)
        dv_own, dv_got = move.keys_back(dvs)
        if dk_got is None:
            dk_got, dv_got = jnp.zeros_like(dk_own), jnp.zeros_like(dv_own)
        dk = key_sum(dk_own, dk_got, tables)
        dv = dv_own + dv_got
        qkv_g = jnp.concatenate([dq, dk, dv], axis=1)
        qkv_w_grads.append(dot_tn(normed1, qkv_g).astype(BF))
        qkv_b_grads.append(jnp.sum(qkv_g, 0, dtype=F32))
        normed1_grad = normed1_grad + dot_nt(qkv_g, qkv_w)
    input_part, ln1_scale_grad, ln1_shift_grad = norm_back(normed1_grad, normal1, inv_one, ln1_gain)
    in_grad = move.swap_rows((resid_grad + input_part).astype(BF))
    vectors = [
        ln1_scale_grad,
        ln1_shift_grad,
        out_bias_grad,
        ln2_scale_grad,
        ln2_shift_grad,
        down_bias_grad,
    ]
    return (
        block_out,
        in_grad,
        vectors,
        (qkv_w_grads, out_w_grads, up_grads, down_grads),
        (qkv_b_grads, up_b_grads),
    )


def paired_device(n_dp, *args):
    (block_in, ln1_scale, ln1_shift, qkv_weight, qkv_bias, out_weight, out_bias) = args[:7]
    (ln2_scale, ln2_shift, up_weight, up_bias, down_weight, down_bias, out_grad) = args[7:]
    move = Paired(n_dp)
    width, _, part = qkv_weight.shape
    qkv_flat = qkv_weight.reshape(width, 3 * part)
    out = block_step(
        move,
        block_in,
        ln1_scale,
        ln1_shift,
        move.weights(qkv_flat),
        move.biases(qkv_bias.reshape(3 * part)),
        move.weights(out_weight),
        out_bias,
        ln2_scale,
        ln2_shift,
        move.weights(up_weight),
        move.biases(up_bias),
        move.weights(down_weight),
        down_bias,
        out_grad,
    )
    block_out, in_grad, vectors, weight_grads, (qkv_b, up_b) = out
    qkv_g, out_g, up_g, down_g = (move.reduce(*pair) for pair in weight_grads)
    vec, flat = move.reduce_vectors(
        jnp.stack(vectors),
        jnp.concatenate([qkv_b[0], up_b[0]]),
        jnp.concatenate([qkv_b[1], up_b[1]]),
    )
    return (
        block_out,
        in_grad,
        vec[0],
        vec[1],
        qkv_g.reshape(width, 3, part),
        flat[: 3 * part].reshape(3, part),
        out_g,
        vec[2],
        vec[3],
        vec[4],
        up_g,
        flat[3 * part :],
        down_g,
        vec[5],
    )


def spread_device(*args):
    (block_in, ln1_scale, ln1_shift, qkv_weight, qkv_bias, out_weight, out_bias) = args[:7]
    (ln2_scale, ln2_shift, up_weight, up_bias, down_weight, down_bias, out_grad) = args[7:]
    gather = lambda w, axis: lax.all_gather(w, "tensor", axis=axis, tiled=True)
    scatter = lambda g, axis: lax.psum(
        lax.psum_scatter(g, "tensor", scatter_dimension=axis, tiled=True), "dp"
    ).astype(F32)
    width = qkv_weight.shape[0]
    qkv_all = gather(qkv_weight, 2)
    full = qkv_all.shape[2]
    out = block_step(
        Spread(block_in.shape[0]),
        block_in,
        ln1_scale,
        ln1_shift,
        [qkv_all.reshape(width, 3 * full)],
        [gather(qkv_bias, 1).reshape(3 * full)],
        [gather(out_weight, 0)],
        out_bias,
        ln2_scale,
        ln2_shift,
        [gather(up_weight, 1)],
        [gather(up_bias, 0)],
        [gather(down_weight, 0)],
        down_bias,
        out_grad,
    )
    block_out, in_grad, vectors, weight_grads, (qkv_b, up_b) = out
    ((qkv_g,), (out_g,), (up_g,), (down_g,)) = weight_grads
    vec = scatter(jnp.stack(vectors), 1)
    return (
        block_out,
        in_grad,
        vec[0],
        vec[1],
        scatter(qkv_g.reshape(width, 3, full), 2),
        scatter(qkv_b[0].reshape(3, full), 1),
        scatter(out_g, 0),
        vec[2],
        vec[3],
        vec[4],
        scatter(up_g, 1),
        scatter(up_b[0], 0),
        scatter(down_g, 0),
        vec[5],
    )


def solution(mesh):
    n_dp, n_tensor = mesh.shape["dp"], mesh.shape["tensor"]
    rows = P(("dp", "tensor"), None)
    vector = P("tensor")
    placed = (
        rows,
        P(),
        P(),
        P(None, None, "tensor"),
        P(None, "tensor"),
        P("tensor", None),
        P(),
        P(),
        P(),
        P(None, "tensor"),
        vector,
        P("tensor", None),
        P(),
        rows,
    )
    paired = n_tensor == 2 and n_dp & (n_dp - 1) == 0
    return jax.shard_map(
        functools.partial(paired_device, n_dp) if paired else spread_device,
        mesh=mesh,
        in_specs=placed,
        out_specs=(
            rows,
            rows,
            vector,
            vector,
            P(None, None, "tensor"),
            P(None, "tensor"),
            P("tensor", None),
            vector,
            vector,
            vector,
            P(None, "tensor"),
            vector,
            P("tensor", None),
            vector,
        ),
        check_vma=False,
    )
```

time: 1650 us -> 839 us (0.51)
  matrix products: 575 us -> 97.2 us
  waiting for transfers between devices: 554 us -> 278 us
  Pallas kernels: 0 us -> 246 us
  other arithmetic: 253 us -> 76 us
  local copies, waits for them, and re-layouts: 181 us -> 46.3 us
  starting transfers between devices: 0.58 us -> 72.3 us
  blocking collectives: 60.7 us -> 0 us
    dot_general x40 -> x18, matrix products: 575 us -> 97.2 us  [the longest x6 36 us: dot_nt(): lax.dot_general(left, right, (((1,), (1,)), ((), ())), preferred_element_...]
    ppermute x0 -> x45, waiting for transfers between devices: none -> 278 us  [move(): return lax.ppermute(x, ('dp', 'tensor'), pairs)]
    pallas_call x0 -> x12, Pallas kernels: none -> 246 us  [the longest x2 103 us: attend_back(): call(functools.partial(attend_back_kernel, sources=len(kvs), keys_at=512,...]
    psum x1 -> x0, waiting for transfers between devices: 223 us -> none  [on_device(): lax.psum(qkv_weight_grad.astype(jnp.bfloat16), 'dp').astype(jnp.float32)]
    reduce_scatter x5 -> x0, waiting for transfers between devices: 192 us -> none  [the longest x1 53.8 us: on_device(): lax.psum_scatter(jnp.dot(attended, out_weight, preferred_element_type=jnp...]
    all_gather x4 -> x8, waiting for transfers between devices: 139 us -> 0.05 us  [the longest x4 0.05 us: other_half(): return lax.all_gather(self.over_y(piece), 'dp', axis=0, tiled=True)]
    convert_element_type x23 -> x12, other arithmetic: 140 us -> 25.8 us  [the longest x3 16.2 us: reduce(): return lax.all_gather(total, 'dp', axis=0, tiled=True).astype(F32)]
    dynamic_update_slice x8 -> x0, local copies, waits for them, and re-layouts: 87 us -> none  [one_clip(): outputs, log_totals = lax.map(one_block, blocks_q)]
  transfers between devices with their start and end apart: 10 -> 53, of which waited for: 10 -> 24; matrix products, arithmetic and copies ran while one was open for 9% -> 20% of each run, Pallas kernels for 0% -> 22%
where the time goes in v1:
time: 839 us; the launch traced here: 832 us
  waiting for transfers between devices  278 us (33%)
  Pallas kernels  246 us (29%)
  matrix products  97.2 us (12%)
  other arithmetic  76 us (9%)
  starting transfers between devices  72.3 us (9%)
  local copies, waits for them, and re-layouts  46.3 us (6%)
  between operations  15.7 us (2%)
    ppermute x45, waiting for transfers between devices, move(): return lax.ppermute(x, ('dp', 'tensor'), pairs)  278 us
    pallas_call x2, Pallas kernels, attend_back(): call(functools.partial(attend_back_kernel, sources=len(kvs), keys_at=512,...  103 us
    ppermute x45, starting transfers between devices, move(): return lax.ppermute(x, ('dp', 'tensor'), pairs)  71.4 us
    pallas_call x2, Pallas kernels, attend(): call(functools.partial(attend_kernel, sources=len(kvs), rows_at=256), 4 *...  59.9 us
    dot_general x6, matrix products, dot_nt(): lax.dot_general(left, right, (((1,), (1,)), ((), ())), preferred_element_...  36 us
    dot_general x8, matrix products, dot_tn(): lax.dot_general(left, right, (((0,), (0,)), ((), ())), preferred_element_...  35 us
    pallas_call x2, Pallas kernels, up_rows(): call(up_kernel, 2 * tokens * width * cols, 2 * (tokens * width + width *...  28.2 us
    dot_general x4, matrix products, dot_nn(): lax.dot_general(left, right, (((1,), (0,)), ((), ())), preferred_element_...  26.2 us
  transfers between devices with their start and end apart: 53, of which 24 were waited for; matrix products, arithmetic and copies ran while one was open for 20% of the time, Pallas kernels for 22%

profile of v1, /device:TPU:0, one launch (start us, length us, event | category | flops | bytes accessed | tf_op | source)
XLA Modules:
  0.0 831.6 jit_solution(12139670768119491107)
XLA Ops:
  7.2 4.8 copy.49
  12.1 4.8 copy.50.w_ref
  17.8 3.0 collective-permute-start.2
  20.9 4.9 collective-permute-done.2
  34.4 4.6 collective-permute-done.6
  44.5 3.6 fusion.20
  53.7 11.1 %shard_map.299 = (bf16[1024,512]{1,0:T(8,128)(2,1)}, bf16[1024,1024]{1,0:T(8,128)(2,1)}) custom-call(bf16[1024,1024]{1,0:T(8,128)(2,1)} %fusion.7.n_ref, bf16[1024,1536]{1,0:T(8,128)(2,1)} %copy.50.w_ref, f32[1,1536]{1,0:T(1,128)} %bitcast.206, f32[1024,128]{1,0:T(8,128)} %get-tuple-element.133.c_ref.refs_4_, f32[1024,128]{1,0:T(8,128)} %get-tuple-element.132.sa_ref.refs_5_, ...), custom_call_target="tpu_custom_call" | custom-call | flops 3221225472 | bytes 8388608 | tf_op jit(solution)/shard_map/pallas_call | solution.py:114
  64.7 19.4 %collective-permute-start.1 = (bf16[1024,1024]{1,0:T(8,128)(2,1)}, bf16[1024,1024]{1,0:T(8,128)(2,1)}, u32[]{:S(2)}, u32[]{:S(2)}) collective-permute-start(bf16[1024,1024]{1,0:T(8,128)(2,1)} %get-tuple-element.41.refs_1_.refs_3_.refs_7_.refs_9_), channel_id=1, source_target_pairs={{0,2},{1,3},{2,0},{3,1},{4,6},{5,7},{6,4},{7,5},{8,10},{9,11},{10,... | collective-permute-start | bytes 6291464 | tf_op jit(solution)/shard_map/ppermute | solution.py:397
  86.5 9.0 %collective-permute-done.8 = bf16[128,1024]{1,0:T(8,128)(2,1)S(1)} collective-permute-done((bf16[128,1024]{1,0:T(8,128)(2,1)S(1)}, bf16[128,1024]{1,0:T(8,128)(2,1)S(1)}, u32[]{:S(2)}, u32[]{:S(2)}) %collective-permute-start.8) | collective-permute-done | bytes 262176 | tf_op jit(solution)/shard_map/ppermute | solution.py:397
  96.9 3.4 collective-permute-done.3
  100.9 11.0 %shard_map.301 = (bf16[1024,512]{1,0:T(8,128)(2,1)}, bf16[1024,1024]{1,0:T(8,128)(2,1)}) custom-call(bf16[1024,1024]{1,0:T(8,128)(2,1)} %fusion.7.n_ref, bf16[1024,1536]{1,0:T(8,128)(2,1)} %all-gather.13.cloned.1.call-done.w_ref, f32[1,1536]{1,0:T(1,128)} %reshape.359.b_ref, f32[1024,128]{1,0:T(8,128)} %get-tuple-element.133.c_ref.refs_4_, ...), custom_call_target="tpu_custom_call" | custom-call | flops 3221225472 | bytes 8388608 | tf_op jit(solution)/shard_map/pallas_call | solution.py:114
  113.0 2.7 collective-permute-done.7
  116.2 4.5 convert_reduce_fusion.3
  120.7 29.7 %shard_map.300 = (bf16[1024,512]{1,0:T(8,128)(2,1)}, f32[4,2,1024]{2,1,0:T(2,128)}) custom-call(bf16[1024,512]{1,0:T(8,128)(2,1)} %get-tuple-element.40.refs_0_, bf16[1024,1024]{1,0:T(8,128)(2,1)} %get-tuple-element.41.refs_1_.refs_3_.refs_7_.refs_9_, bf16[1024,1024]{1,0:T(8,128)(2,1)} %collective-permute-done.1.refs_2_.refs_4_.refs_8_.refs_10_, ...), custom_call_target="tpu_custom_call" | custom-call | flops 17179869184 | bytes 6291456 | tf_op jit(solution)/shard_map/pallas_call | solution.py:177
  150.4 30.2 %shard_map.302 = (bf16[1024,512]{1,0:T(8,128)(2,1)}, f32[4,2,1024]{2,1,0:T(2,128)}) custom-call(bf16[1024,512]{1,0:T(8,128)(2,1)} %get-tuple-element.43.refs_0_, bf16[1024,1024]{1,0:T(8,128)(2,1)} %get-tuple-element.44.refs_1_.refs_3_.refs_7_.refs_9_, bf16[1024,1024]{1,0:T(8,128)(2,1)} %collective-permute-done.4.refs_2_.refs_4_.refs_8_.refs_10_, ...), custom_call_target="tpu_custom_call" | custom-call | flops 17179869184 | bytes 6291456 | tf_op jit(solution)/shard_map/pallas_call | solution.py:177
  180.7 2.9 fusion.31
  188.0 14.1 %shard_map.303 = (bf16[1024,2048]{1,0:T(8,128)(2,1)}, bf16[1024,2048]{1,0:T(8,128)(2,1)}) custom-call(bf16[1024,1024]{1,0:T(8,128)(2,1)} %add_convert_fusion.1.n_ref, bf16[1024,2048]{1,0:T(8,128)(2,1)} %w_ref.2, f32[1,2048]{1,0:T(1,128)} %bitcast.204), custom_call_target="tpu_custom_call" | custom-call | flops 4294967296 | bytes 14680064 | tf_op jit(solution)/shard_map/pallas_call | solution.py:321
  202.0 11.3 %shard_map.305 = (bf16[1024,2048]{1,0:T(8,128)(2,1)}, f32[1,2048]{1,0:T(1,128)}) custom-call(bf16[1024,1024]{1,0:T(8,128)(2,1)} %get-tuple-element.117.g_ref, bf16[2048,1024]{1,0:T(8,128)(2,1)} %w_ref.3, bf16[1024,2048]{1,0:T(8,128)(2,1)} %get-tuple-element.48.slope_ref), custom_call_target="tpu_custom_call" | custom-call | flops 4294967296 | bytes 14680064 | tf_op jit(solution)/shard_map/pallas_call | solution.py:349
  213.3 14.1 %shard_map.304 = (bf16[1024,2048]{1,0:T(8,128)(2,1)}, bf16[1024,2048]{1,0:T(8,128)(2,1)}) custom-call(bf16[1024,1024]{1,0:T(8,128)(2,1)} %add_convert_fusion.1.n_ref, bf16[1024,2048]{1,0:T(8,128)(2,1)} %all-gather.17.cloned.1.call-done.w_ref, f32[1,2048]{1,0:T(1,128)} %bitcast.205), custom_call_target="tpu_custom_call" | custom-call | flops 4294967296 | bytes 14680064 | tf_op jit(solution)/shard_map/pallas_call | solution.py:321
  227.4 11.3 %shard_map.306 = (bf16[1024,2048]{1,0:T(8,128)(2,1)}, f32[1,2048]{1,0:T(1,128)}) custom-call(bf16[1024,1024]{1,0:T(8,128)(2,1)} %get-tuple-element.117.g_ref, bf16[2048,1024]{1,0:T(8,128)(2,1)} %all-gather.19.cloned.1.call-done.w_ref, bf16[1024,2048]{1,0:T(8,128)(2,1)} %get-tuple-element.50.slope_ref), custom_call_target="tpu_custom_call" | custom-call | flops 4294967296 | bytes 14680064 | tf_op jit(solution)/shard_map/pallas_call | solution.py:349
  238.7 8.6 %fusion.33 = f32[1024,1024]{1,0:T(8,128)} fusion(bf16[1024,2048]{1,0:T(8,128)(2,1)} %get-tuple-element.51, bf16[1024,2048]{1,0:T(8,128)(2,1)S(1)} %copy-done.70), kind=kOutput, calls=%fused_computation.156 | convolution fusion | flops 4294967296 | bytes 12582912 | tf_op jit(solution)/shard_map/dot_general | solution.py:28
  247.3 9.9 %multiply_reduce_fusion = (f32[1024]{0:T(1024)}, f32[1024]{0:T(1024)S(1)}, f32[1024]{0:T(1024)S(1)}, f32[1024]{0:T(1024)}, f32[1024,1024]{1,0:T(8,128)S(1)}) fusion(f32[1024,1024]{1,0:T(8,128)S(1)} %copy-done.3, f32[1024]{0:T(1024)S(1)} %add_rsqrt_fusion, f32[1024]{0:T(1024)S(1)} %broadcast_multiply_fusion.4, f32[1024]{0:T(1024)S(1)} %convert_element_type.115, ...), kind=kOutput, calls=%fused_computation.24 | convolution fusion | flops 4305448960 | bytes 21000192 | tf_op jit(solution)/shard_map/dot_general | solution.py:28
  257.2 3.7 convert_reduce_fusion.4
  265.5 51.5 %shard_map.309 = (bf16[1024,512]{1,0:T(8,128)(2,1)}, bf16[1024,512]{1,0:T(8,128)(2,1)}, bf16[1024,512]{1,0:T(8,128)(2,1)}, bf16[1024,512]{1,0:T(8,128)(2,1)}, bf16[1024,512]{1,0:T(8,128)(2,1)}) custom-call(bf16[1024,512]{1,0:T(8,128)(2,1)} %get-tuple-element.43.refs_0_, bf16[1024,512]{1,0:T(8,128)(2,1)} %convolution_convert_fusion.8.refs_1_, ...), custom_call_target="tpu_custom_call" | custom-call | flops 42949672960 | bytes 12582912 | tf_op jit(solution)/shard_map/pallas_call | solution.py:255
  317.5 51.7 %shard_map.307 = (bf16[1024,512]{1,0:T(8,128)(2,1)}, bf16[1024,512]{1,0:T(8,128)(2,1)}, bf16[1024,512]{1,0:T(8,128)(2,1)}, bf16[1024,512]{1,0:T(8,128)(2,1)}, bf16[1024,512]{1,0:T(8,128)(2,1)}) custom-call(bf16[1024,512]{1,0:T(8,128)(2,1)} %get-tuple-element.40.refs_0_, bf16[1024,512]{1,0:T(8,128)(2,1)} %convolution_convert_fusion.9.refs_1_, ...), custom_call_target="tpu_custom_call" | custom-call | flops 42949672960 | bytes 12582912 | tf_op jit(solution)/shard_map/pallas_call | solution.py:255
  371.1 4.8 shard_map.310
  378.7 5.3 convolution_convert_fusion
  390.6 5.1 shard_map.308
  395.7 5.3 convolution_convert_fusion.1
  404.7 2.8 bitcast_add_fusion.4
  410.3 45.3 %collective-permute-done.29 = bf16[8,32,1024]{2,1,0:T(8,128)(2,1)} collective-permute-done((bf16[8,32,1024]{2,1,0:T(8,128)(2,1)}, bf16[8,32,1024]{2,1,0:T(8,128)(2,1)}, u32[]{:S(2)}, u32[]{:S(2)}) %collective-permute-start.29) | collective-permute-done | bytes 524320 | tf_op jit(solution)/shard_map/ppermute | solution.py:397
  459.4 6.4 collective-permute-done.30
  474.7 5.0 convolution_convert_fusion.2
  486.4 4.9 collective-permute-done.24
  493.5 7.0 convolution_convert_fusion.3
  503.0 3.1 collective-permute-start.26
  506.2 3.1 bitcast_add_fusion
  509.8 7.1 collective-permute-done.26
  517.7 38.4 %collective-permute-done.41 = bf16[8,128,1024]{2,1,0:T(8,128)(2,1)} collective-permute-done((bf16[8,128,1024]{2,1,0:T(8,128)(2,1)}, bf16[8,128,1024]{2,1,0:T(8,128)(2,1)}, u32[]{:S(2)}, u32[]{:S(2)}) %collective-permute-start.41) | collective-permute-done | bytes 2097184 | tf_op jit(solution)/shard_map/ppermute | solution.py:397
  556.1 3.2 fusion.15
  561.0 4.9 convolution_convert_fusion.4
  567.5 17.7 %collective-permute-done.42 = bf16[4,128,1024]{2,1,0:T(8,128)(2,1)S(1)} collective-permute-done((bf16[4,128,1024]{2,1,0:T(8,128)(2,1)S(1)}, bf16[4,128,1024]{2,1,0:T(8,128)(2,1)S(1)}, u32[]{:S(2)}, u32[]{:S(2)}) %collective-permute-start.42) | collective-permute-done | bytes 1048608 | tf_op jit(solution)/shard_map/ppermute | solution.py:397
  586.9 4.9 convolution_convert_fusion.5
  591.8 6.7 collective-permute-done.43
  601.1 10.7 %collective-permute-done.44 = bf16[1,128,1024]{2,1,0:T(8,128)(2,1)S(1)} collective-permute-done((bf16[1,128,1024]{2,1,0:T(8,128)(2,1)S(1)}, bf16[1,128,1024]{2,1,0:T(8,128)(2,1)S(1)}, u32[]{:S(2)}, u32[]{:S(2)}) %collective-permute-start.44) | collective-permute-done | bytes 262176 | tf_op jit(solution)/shard_map/ppermute | solution.py:397
  616.9 44.7 %collective-permute-done.35 = bf16[8,64,2048]{2,1,0:T(8,128)(2,1)S(1)} collective-permute-done((bf16[8,64,2048]{2,1,0:T(8,128)(2,1)S(1)}, bf16[8,64,2048]{2,1,0:T(8,128)(2,1)S(1)}, u32[]{:S(2)}, u32[]{:S(2)}) %collective-permute-start.35) | collective-permute-done | bytes 2097184 | tf_op jit(solution)/shard_map/ppermute | solution.py:397
  663.9 22.5 %collective-permute-done.36 = bf16[4,64,2048]{2,1,0:T(8,128)(2,1)S(1)} collective-permute-done((bf16[4,64,2048]{2,1,0:T(8,128)(2,1)S(1)}, bf16[4,64,2048]{2,1,0:T(8,128)(2,1)S(1)}, u32[]{:S(2)}, u32[]{:S(2)}) %collective-permute-start.36) | collective-permute-done | bytes 1048608 | tf_op jit(solution)/shard_map/ppermute | solution.py:397
  686.6 2.7 collective-permute-start.37
  689.4 10.4 %collective-permute-done.37 = bf16[2,64,2048]{2,1,0:T(8,128)(2,1)S(1)} collective-permute-done((bf16[2,64,2048]{2,1,0:T(8,128)(2,1)S(1)}, bf16[2,64,2048]{2,1,0:T(8,128)(2,1)S(1)}, u32[]{:S(2)}, u32[]{:S(2)}) %collective-permute-start.37) | collective-permute-done | bytes 524320 | tf_op jit(solution)/shard_map/ppermute | solution.py:397
  699.8 3.2 collective-permute-start.38
  703.1 10.0 %fusion.32 = f32[1024,1024]{1,0:T(8,128)} fusion(bf16[1024,2048]{1,0:T(8,128)(2,1)} %get-tuple-element.46, bf16[2048,1024]{1,0:T(8,128)(2,1)} %w_ref.3), kind=kOutput, calls=%fused_computation.155 | convolution fusion | flops 4294967296 | bytes 12582912 | tf_op jit(solution)/shard_map/dot_general | solution.py:32
  713.8 11.7 %add_convert_fusion = bf16[1024,1024]{1,0:T(8,128)(2,1)} fusion(f32[1024,1024]{1,0:T(8,128)} %copy-done.2, f32[1024,1024]{1,0:T(8,128)} %fusion.32, f32[1024]{0:T(1024)S(1)} %convert_element_type.118, bf16[1024,2048]{1,0:T(8,128)(2,1)} %get-tuple-element.47, bf16[2048,1024]{1,0:T(8,128)(2,1)} %all-gather.19.cloned.1.call-done.w_ref), kind=kOutput, calls=%fused_computation.27 | convolution fusion | flops 4299161600 | bytes 18878464 | tf_op jit(solution)/shard_map/dot_general | solution.py:32
  727.7 6.8 fusion.29
  734.6 6.3 fusion.13
  741.0 5.4 fusion.12
  751.8 24.2 %collective-permute-done.16 = f32[52,128]{1,0:T(8,128)S(1)} collective-permute-done((f32[52,128]{1,0:T(8,128)S(1)}, f32[52,128]{1,0:T(8,128)S(1)}, u32[]{:S(2)}, u32[]{:S(2)}) %collective-permute-start.16) | collective-permute-done | bytes 26656 | tf_op jit(solution)/shard_map/ppermute | solution.py:397
  778.0 3.2 collective-permute-done.18
  787.0 2.8 collective-permute-done.20
  793.3 3.1 broadcast_select_fusion
  796.4 2.8 bitcast_convert_fusion.2
  799.2 5.4 copy.54
  804.6 6.6 copy.55
  811.1 6.7 bitcast_convert_fusion
  817.8 6.7 bitcast_convert_fusion.1
  (341 shorter events, 113.4 us)
Async XLA Ops:
  7.2 93.7 %all-gather.13.cloned.1.call-start = ((), (), s32[]{:S(2)}) async-start(), calls=%async_computation | async-start | bytes 3342336 | tf_op jit(solution)/shard_map/all_gather | solution.py:415
  12.0 32.5 %copy-start.64 = (f32[128]{0:T(128)S(1)}, f32[128]{0:T(128)}, u32[]{:S(2)}) copy-start(f32[128]{0:T(128)} %constant.251) | copy-start | bytes 1540
  12.0 32.5 %copy-start.65 = (pred[128]{0:T(512)(128)(4,1)S(1)}, pred[128]{0:T(512)(128)(4,1)}, u32[]{:S(2)}) copy-start(pred[128]{0:T(512)(128)(4,1)} %constant.250.clone) | copy-start | bytes 388
  12.1 32.5 %copy-start.66 = (pred[128]{0:T(512)(128)(4,1)S(1)}, pred[128]{0:T(512)(128)(4,1)}, u32[]{:S(2)}) copy-start(pred[128]{0:T(512)(128)(4,1)} %constant.249.clone) | copy-start | bytes 388
  12.1 32.5 %copy-start.67 = (pred[128]{0:T(512)(128)(4,1)S(1)}, pred[128]{0:T(512)(128)(4,1)}, u32[]{:S(2)}) copy-start(pred[128]{0:T(512)(128)(4,1)} %constant.248.clone) | copy-start | bytes 388
  12.1 32.4 %copy-start.68 = (pred[128]{0:T(512)(128)(4,1)S(1)}, pred[128]{0:T(512)(128)(4,1)}, u32[]{:S(2)}) copy-start(pred[128]{0:T(512)(128)(4,1)} %constant.246.clone) | copy-start | bytes 388
  17.8 7.9 collective-permute-start.2
  26.5 154.2 %all-gather.15.cloned.1.call-start = ((), (), s32[]{:S(2)}) async-start(), calls=%async_computation.1 | async-start | bytes 1114112 | tf_op jit(solution)/shard_map/all_gather | solution.py:415
  26.5 4.3 collective-permute-start.5
  31.5 181.8 %all-gather.17.cloned.1.call-start = ((), (), s32[]{:S(2)}) async-start(), calls=%async_computation.2 | async-start | bytes 4456448 | tf_op jit(solution)/shard_map/all_gather | solution.py:415
  32.6 6.4 collective-permute-start.6
  39.7 187.7 %all-gather.19.cloned.1.call-start = ((), (), s32[]{:S(2)}) async-start(), calls=%async_computation.3 | async-start | bytes 4456448 | tf_op jit(solution)/shard_map/all_gather | solution.py:415
  39.8 8.4 %collective-permute-start = (bf16[1024,1024]{1,0:T(8,128)(2,1)S(1)}, bf16[1024,1024]{1,0:T(8,128)(2,1)}, u32[]{:S(2)}, u32[]{:S(2)}) collective-permute-start(bf16[1024,1024]{1,0:T(8,128)(2,1)S(1)} %copy-done.30), channel_id=1, source_target_pairs={{1,2},{2,1},{5,6},{6,5},{9,10},{10,9},{13,14},{14,13},{17,18},{18,... | collective-permute-start | bytes 6291464 | tf_op jit(solution)/shard_map/ppermute | solution.py:397
  41.8 74.4 %collective-permute-start.10 = (bf16[1024,1024]{1,0:T(8,128)(2,1)}, bf16[1024,1024]{1,0:T(8,128)(2,1)}, u32[]{:S(2)}, u32[]{:S(2)}) collective-permute-start(bf16[1024,1024]{1,0:T(8,128)(2,1)} %param.33), channel_id=1, source_target_pairs={{1,2},{2,1},{5,6},{6,5},{9,10},{10,9},{13,14},{14,13},{17,18},{18,... | collective-permute-start | bytes 6291464 | tf_op jit(solution)/shard_map/ppermute | solution.py:397
  50.5 133.1 %copy-start.4 = (bf16[1024,1024]{1,0:T(8,128)(2,1)}, bf16[1024,1024]{1,0:T(8,128)(2,1)S(1)}, u32[]{:S(2)}) copy-start(bf16[1024,1024]{1,0:T(8,128)(2,1)S(1)} %get-tuple-element.122) | copy-start | bytes 6291460
  64.7 56.0 %collective-permute-start.1 = (bf16[1024,1024]{1,0:T(8,128)(2,1)}, bf16[1024,1024]{1,0:T(8,128)(2,1)}, u32[]{:S(2)}, u32[]{:S(2)}) collective-permute-start(bf16[1024,1024]{1,0:T(8,128)(2,1)} %get-tuple-element.41.refs_1_.refs_3_.refs_7_.refs_9_), channel_id=1, source_target_pairs={{0,2},{1,3},{2,0},{3,1},{4,6},{5,7},{6,4},{7,5},{8,10},{9,11},{10,... | collective-permute-start | bytes 6291464 | tf_op jit(solution)/shard_map/ppermute | solution.py:397
  85.1 10.4 %collective-permute-start.8 = (bf16[128,1024]{1,0:T(8,128)(2,1)S(1)}, bf16[128,1024]{1,0:T(8,128)(2,1)S(1)}, u32[]{:S(2)}, u32[]{:S(2)}) collective-permute-start(bf16[128,1024]{1,0:T(8,128)(2,1)S(1)} %constant_dynamic-slice_fusion.6), channel_id=1, source_target_pairs={{0,1},{1,0},{2,3},{3,2},{4,5},{5,4},{6,7},{7,6},{8,9},{9,8},{10,11... | collective-permute-start | bytes 786440 | tf_op jit(solution)/shard_map/ppermute | solution.py:397
  96.2 700.1 %all-gather.23.cloned.1.call-start = ((), (), s32[]{:S(2)}) async-start(), calls=%async_computation.5 | async-start | bytes 1114112 | tf_op jit(solution)/shard_map/all_gather | solution.py:449
  96.6 3.7 collective-permute-start.3
  111.9 38.5 %collective-permute-start.4 = (bf16[1024,1024]{1,0:T(8,128)(2,1)}, bf16[1024,1024]{1,0:T(8,128)(2,1)}, u32[]{:S(2)}, u32[]{:S(2)}) collective-permute-start(bf16[1024,1024]{1,0:T(8,128)(2,1)} %get-tuple-element.44.refs_1_.refs_3_.refs_7_.refs_9_), channel_id=1, source_target_pairs={{0,2},{1,3},{2,0},{3,1},{4,6},{5,7},{6,4},{7,5},{8,10},{9,11},{10,... | collective-permute-start | bytes 6291464 | tf_op jit(solution)/shard_map/ppermute | solution.py:397
  111.9 3.7 collective-permute-start.7
  317.0 54.1 %collective-permute-start.13 = (bf16[1024,512]{1,0:T(8,128)(2,1)}, bf16[1024,512]{1,0:T(8,128)(2,1)}, u32[]{:S(2)}, u32[]{:S(2)}) collective-permute-start(bf16[1024,512]{1,0:T(8,128)(2,1)} %get-tuple-element.61), channel_id=1, source_target_pairs={{0,2},{1,3},{2,0},{3,1},{4,6},{5,7},{6,4},{7,5},{8,10},{9,11},{10,... | collective-permute-start | bytes 3145736 | tf_op jit(solution)/shard_map/ppermute | solution.py:397
  317.0 58.9 %collective-permute-start.14 = (bf16[1024,512]{1,0:T(8,128)(2,1)}, bf16[1024,512]{1,0:T(8,128)(2,1)S(1)}, u32[]{:S(2)}, u32[]{:S(2)}) collective-permute-start(bf16[1024,512]{1,0:T(8,128)(2,1)} %get-tuple-element.63), channel_id=1, source_target_pairs={{0,2},{1,3},{2,0},{3,1},{4,6},{5,7},{6,4},{7,5},{8,10},{9,11},{10,... | collective-permute-start | bytes 3145736 | tf_op jit(solution)/shard_map/ppermute | solution.py:397
  317.5 52.3 %copy-start.38 = (bf16[1024,512]{1,0:T(8,128)(2,1)S(1)}, bf16[1024,512]{1,0:T(8,128)(2,1)}, u32[]{:S(2)}) copy-start(bf16[1024,512]{1,0:T(8,128)(2,1)} %get-tuple-element.45.refs_2_) | copy-start | bytes 3145732
  369.2 21.4 %collective-permute-start.11 = (bf16[1024,512]{1,0:T(8,128)(2,1)}, bf16[1024,512]{1,0:T(8,128)(2,1)}, u32[]{:S(2)}, u32[]{:S(2)}) collective-permute-start(bf16[1024,512]{1,0:T(8,128)(2,1)} %get-tuple-element.55), channel_id=1, source_target_pairs={{0,2},{1,3},{2,0},{3,1},{4,6},{5,7},{6,4},{7,5},{8,10},{9,11},{10,... | collective-permute-start | bytes 3145736 | tf_op jit(solution)/shard_map/ppermute | solution.py:397
  369.4 19.6 %collective-permute-start.12 = (bf16[1024,512]{1,0:T(8,128)(2,1)}, bf16[1024,512]{1,0:T(8,128)(2,1)}, u32[]{:S(2)}, u32[]{:S(2)}) collective-permute-start(bf16[1024,512]{1,0:T(8,128)(2,1)} %get-tuple-element.57), channel_id=1, source_target_pairs={{0,2},{1,3},{2,0},{3,1},{4,6},{5,7},{6,4},{7,5},{8,10},{9,11},{10,... | collective-permute-start | bytes 3145736 | tf_op jit(solution)/shard_map/ppermute | solution.py:397
  385.4 17.4 %collective-permute-start.22 = (bf16[8,64,1536]{2,1,0:T(8,128)(2,1)}, bf16[8,64,1536]{2,1,0:T(8,128)(2,1)}, u32[]{:S(2)}, u32[]{:S(2)}) collective-permute-start(bf16[8,64,1536]{2,1,0:T(8,128)(2,1)} %dynamic-slice_bitcast_fusion.4), channel_id=1, source_target_pairs={{0,2},{1,3},{2,0},{3,1},{4,6},{5,7},{6,4},{7,5},{8,10},{9,11},{10,... | collective-permute-start | bytes 4718600 | tf_op jit(solution)/shard_map/ppermute | solution.py:397
  386.3 21.4 %collective-permute-start.28 = (bf16[8,32,1024]{2,1,0:T(8,128)(2,1)}, bf16[8,32,1024]{2,1,0:T(8,128)(2,1)S(1)}, u32[]{:S(2)}, u32[]{:S(2)}) collective-permute-start(bf16[8,32,1024]{2,1,0:T(8,128)(2,1)} %dynamic-slice_bitcast_fusion.11), channel_id=1, source_target_pairs={{0,2},{1,3},{2,0},{3,1},{4,6},{5,7},{6,4},{7,5},{8,10},{9,11},{10,... | collective-permute-start | bytes 1572872 | tf_op jit(solution)/shard_map/ppermute | solution.py:397
  388.9 21.4 %collective-permute-start.27 = (bf16[8,32,1024]{2,1,0:T(8,128)(2,1)}, bf16[8,32,1024]{2,1,0:T(8,128)(2,1)}, u32[]{:S(2)}, u32[]{:S(2)}) collective-permute-start(bf16[8,32,1024]{2,1,0:T(8,128)(2,1)} %dynamic-slice_bitcast_fusion.12), channel_id=1, source_target_pairs={{0,2},{1,3},{2,0},{3,1},{4,6},{5,7},{6,4},{7,5},{8,10},{9,11},{10,... | collective-permute-start | bytes 1572872 | tf_op jit(solution)/shard_map/ppermute | solution.py:397
  402.4 66.2 %collective-permute-start.21 = (bf16[8,64,1536]{2,1,0:T(8,128)(2,1)}, bf16[8,64,1536]{2,1,0:T(8,128)(2,1)}, u32[]{:S(2)}, u32[]{:S(2)}) collective-permute-start(bf16[8,64,1536]{2,1,0:T(8,128)(2,1)} %dynamic-slice_bitcast_fusion.5), channel_id=1, source_target_pairs={{0,2},{1,3},{2,0},{3,1},{4,6},{5,7},{6,4},{7,5},{8,10},{9,11},{10,... | collective-permute-start | bytes 4718600 | tf_op jit(solution)/shard_map/ppermute | solution.py:397
  407.4 61.1 %collective-permute-start.23 = (bf16[8,64,1536]{2,1,0:T(8,128)(2,1)}, bf16[8,64,1536]{2,1,0:T(8,128)(2,1)}, u32[]{:S(2)}, u32[]{:S(2)}) collective-permute-start(bf16[8,64,1536]{2,1,0:T(8,128)(2,1)} %bitcast_add_fusion.4), channel_id=1, source_target_pairs={{0,1},{1,0},{2,3},{3,2},{4,5},{5,4},{6,7},{7,6},{8,9},{9,8},{10,11... | collective-permute-start | bytes 4718600 | tf_op jit(solution)/shard_map/ppermute | solution.py:397
  408.5 47.2 %collective-permute-start.29 = (bf16[8,32,1024]{2,1,0:T(8,128)(2,1)}, bf16[8,32,1024]{2,1,0:T(8,128)(2,1)}, u32[]{:S(2)}, u32[]{:S(2)}) collective-permute-start(bf16[8,32,1024]{2,1,0:T(8,128)(2,1)} %bitcast_add_fusion.11), channel_id=1, source_target_pairs={{0,1},{1,0},{2,3},{3,2},{4,5},{5,4},{6,7},{7,6},{8,9},{9,8},{10,11... | collective-permute-start | bytes 1572872 | tf_op jit(solution)/shard_map/ppermute | solution.py:397
  457.9 7.9 collective-permute-start.30
  466.9 12.8 %collective-permute-start.31 = (bf16[2,32,1024]{2,1,0:T(8,128)(2,1)S(1)}, bf16[2,32,1024]{2,1,0:T(8,128)(2,1)S(1)}, u32[]{:S(2)}, u32[]{:S(2)}) collective-permute-start(bf16[2,32,1024]{2,1,0:T(8,128)(2,1)S(1)} %dynamic-slice_bitcast_fusion.15), channel_id=1, source_target_pairs={{0,8},{1,9},{2,10},{3,11},{4,12},{5,13},{6,14},{7,15},{8,0},{9,1},... | collective-permute-start | bytes 393224 | tf_op jit(solution)/shard_map/ppermute | solution.py:397
  473.2 18.1 %collective-permute-start.24 = (bf16[4,64,1536]{2,1,0:T(8,128)(2,1)}, bf16[4,64,1536]{2,1,0:T(8,128)(2,1)}, u32[]{:S(2)}, u32[]{:S(2)}) collective-permute-start(bf16[4,64,1536]{2,1,0:T(8,128)(2,1)} %dynamic-slice_bitcast_fusion.8), channel_id=1, source_target_pairs={{0,4},{1,5},{2,6},{3,7},{4,0},{5,1},{6,2},{7,3},{8,12},{9,13},{10,... | collective-permute-start | bytes 2359304 | tf_op jit(solution)/shard_map/ppermute | solution.py:397
  479.8 5.9 collective-permute-start.32
  484.0 22.2 %collective-permute-start.40 = (bf16[8,128,1024]{2,1,0:T(8,128)(2,1)}, bf16[8,128,1024]{2,1,0:T(8,128)(2,1)}, u32[]{:S(2)}, u32[]{:S(2)}) collective-permute-start(bf16[8,128,1024]{2,1,0:T(8,128)(2,1)} %dynamic-slice_bitcast_fusion), channel_id=1, source_target_pairs={{0,2},{1,3},{2,0},{3,1},{4,6},{5,7},{6,4},{7,5},{8,10},{9,11},{10,... | collective-permute-start | bytes 6291464 | tf_op jit(solution)/shard_map/ppermute | solution.py:397
  486.4 312.8 %all-gather.21.cloned.1.call-start = ((), (), s32[]{:S(2)}) async-start(), calls=%async_computation.4 | async-start | bytes 3342336 | tf_op jit(solution)/shard_map/all_gather | solution.py:449
  492.9 10.1 %collective-permute-start.25 = (bf16[2,64,1536]{2,1,0:T(8,128)(2,1)S(1)}, bf16[2,64,1536]{2,1,0:T(8,128)(2,1)S(1)}, u32[]{:S(2)}, u32[]{:S(2)}) collective-permute-start(bf16[2,64,1536]{2,1,0:T(8,128)(2,1)S(1)} %dynamic-slice_bitcast_fusion.13), channel_id=1, source_target_pairs={{0,8},{1,9},{2,10},{3,11},{4,12},{5,13},{6,14},{7,15},{8,0},{9,1},... | collective-permute-start | bytes 1179656 | tf_op jit(solution)/shard_map/ppermute | solution.py:397
  502.1 15.6 %collective-permute-start.39 = (bf16[8,128,1024]{2,1,0:T(8,128)(2,1)}, bf16[8,128,1024]{2,1,0:T(8,128)(2,1)}, u32[]{:S(2)}, u32[]{:S(2)}) collective-permute-start(bf16[8,128,1024]{2,1,0:T(8,128)(2,1)} %dynamic-slice_bitcast_fusion.1), channel_id=1, source_target_pairs={{0,2},{1,3},{2,0},{3,1},{4,6},{5,7},{6,4},{7,5},{8,10},{9,11},{10,... | collective-permute-start | bytes 6291464 | tf_op jit(solution)/shard_map/ppermute | solution.py:397
  503.0 13.9 %collective-permute-start.26 = (bf16[1,64,1536]{2,1,0:T(8,128)(2,1)S(1)}, bf16[1,64,1536]{2,1,0:T(8,128)(2,1)S(1)}, u32[]{:S(2)}, u32[]{:S(2)}) collective-permute-start(bf16[1,64,1536]{2,1,0:T(8,128)(2,1)S(1)} %constant_dynamic-slice_fusion.3), channel_id=1, source_target_pairs={{0,16},{1,17},{2,18},{3,19},{4,20},{5,21},{6,22},{7,23},{8,24},{9,... | collective-permute-start | bytes 589832 | tf_op jit(solution)/shard_map/ppermute | solution.py:397
  509.3 46.8 %collective-permute-start.41 = (bf16[8,128,1024]{2,1,0:T(8,128)(2,1)}, bf16[8,128,1024]{2,1,0:T(8,128)(2,1)}, u32[]{:S(2)}, u32[]{:S(2)}) collective-permute-start(bf16[8,128,1024]{2,1,0:T(8,128)(2,1)} %bitcast_add_fusion), channel_id=1, source_target_pairs={{0,1},{1,0},{2,3},{3,2},{4,5},{5,4},{6,7},{7,6},{8,9},{9,8},{10,11... | collective-permute-start | bytes 6291464 | tf_op jit(solution)/shard_map/ppermute | solution.py:397
  517.6 43.3 %copy-start.27 = (bf16[1024,1024]{1,0:T(8,128)(2,1)S(1)}, bf16[1024,1024]{1,0:T(8,128)(2,1)}, u32[]{:S(2)}) copy-start(bf16[1024,1024]{1,0:T(8,128)(2,1)} %add_convert_fusion.1.n_ref) | copy-start | bytes 6291460
  517.7 293.5 %all-gather.27.cloned.1.call-start = ((), (), s32[]{:S(2)}) async-start(), calls=%async_computation.7 | async-start | bytes 4456448 | tf_op jit(solution)/shard_map/all_gather | solution.py:449
  517.7 43.3 %copy-start.73 = (bf16[1024,2048]{1,0:T(8,128)(2,1)S(1)}, bf16[1024,2048]{1,0:T(8,128)(2,1)}, u32[]{:S(2)}) copy-start(bf16[1024,2048]{1,0:T(8,128)(2,1)} %get-tuple-element.51) | copy-start | bytes 12582916
  559.4 25.8 %collective-permute-start.42 = (bf16[4,128,1024]{2,1,0:T(8,128)(2,1)S(1)}, bf16[4,128,1024]{2,1,0:T(8,128)(2,1)S(1)}, u32[]{:S(2)}, u32[]{:S(2)}) collective-permute-start(bf16[4,128,1024]{2,1,0:T(8,128)(2,1)S(1)} %dynamic-slice_bitcast_fusion.6), channel_id=1, source_target_pairs={{0,4},{1,5},{2,6},{3,7},{4,0},{5,1},{6,2},{7,3},{8,12},{9,13},{10,... | collective-permute-start | bytes 3145736 | tf_op jit(solution)/shard_map/ppermute | solution.py:397
  567.5 45.3 %collective-permute-start.34 = (bf16[8,64,2048]{2,1,0:T(8,128)(2,1)}, bf16[8,64,2048]{2,1,0:T(8,128)(2,1)}, u32[]{:S(2)}, u32[]{:S(2)}) collective-permute-start(bf16[8,64,2048]{2,1,0:T(8,128)(2,1)} %dynamic-slice_bitcast_fusion.2), channel_id=1, source_target_pairs={{0,2},{1,3},{2,0},{3,1},{4,6},{5,7},{6,4},{7,5},{8,10},{9,11},{10,... | collective-permute-start | bytes 6291464 | tf_op jit(solution)/shard_map/ppermute | solution.py:397
  585.3 13.2 %collective-permute-start.43 = (bf16[2,128,1024]{2,1,0:T(8,128)(2,1)S(1)}, bf16[2,128,1024]{2,1,0:T(8,128)(2,1)S(1)}, u32[]{:S(2)}, u32[]{:S(2)}) collective-permute-start(bf16[2,128,1024]{2,1,0:T(8,128)(2,1)S(1)} %dynamic-slice_bitcast_fusion.9), channel_id=1, source_target_pairs={{0,8},{1,9},{2,10},{3,11},{4,12},{5,13},{6,14},{7,15},{8,0},{9,1},... | collective-permute-start | bytes 1572872 | tf_op jit(solution)/shard_map/ppermute | solution.py:397
  598.6 13.2 %collective-permute-start.44 = (bf16[1,128,1024]{2,1,0:T(8,128)(2,1)S(1)}, bf16[1,128,1024]{2,1,0:T(8,128)(2,1)S(1)}, u32[]{:S(2)}, u32[]{:S(2)}) collective-permute-start(bf16[1,128,1024]{2,1,0:T(8,128)(2,1)S(1)} %constant_dynamic-slice_fusion), channel_id=1, source_target_pairs={{0,16},{1,17},{2,18},{3,19},{4,20},{5,21},{6,22},{7,23},{8,24},{9,... | collective-permute-start | bytes 786440 | tf_op jit(solution)/shard_map/ppermute | solution.py:397
  601.0 15.9 %collective-permute-start.33 = (bf16[8,64,2048]{2,1,0:T(8,128)(2,1)S(1)}, bf16[8,64,2048]{2,1,0:T(8,128)(2,1)}, u32[]{:S(2)}, u32[]{:S(2)}) collective-permute-start(bf16[8,64,2048]{2,1,0:T(8,128)(2,1)S(1)} %dynamic-slice_bitcast_fusion.3), channel_id=1, source_target_pairs={{0,2},{1,3},{2,0},{3,1},{4,6},{5,7},{6,4},{7,5},{8,10},{9,11},{10,... | collective-permute-start | bytes 6291464 | tf_op jit(solution)/shard_map/ppermute | solution.py:397
  612.5 205.3 %all-gather.25.cloned.1.call-start = ((), (), s32[]{:S(2)}) async-start(), calls=%async_computation.6 | async-start | bytes 4456448 | tf_op jit(solution)/shard_map/all_gather | solution.py:449
  612.8 48.7 %copy-start.19 = (bf16[1024,2048]{1,0:T(8,128)(2,1)S(1)}, bf16[1024,2048]{1,0:T(8,128)(2,1)}, u32[]{:S(2)}) copy-start(bf16[1024,2048]{1,0:T(8,128)(2,1)} %copy-done.18) | copy-start | bytes 12582916
  615.4 46.1 %collective-permute-start.35 = (bf16[8,64,2048]{2,1,0:T(8,128)(2,1)S(1)}, bf16[8,64,2048]{2,1,0:T(8,128)(2,1)S(1)}, u32[]{:S(2)}, u32[]{:S(2)}) collective-permute-start(bf16[8,64,2048]{2,1,0:T(8,128)(2,1)S(1)} %bitcast_add_fusion.2), channel_id=1, source_target_pairs={{0,1},{1,0},{2,3},{3,2},{4,5},{5,4},{6,7},{7,6},{8,9},{9,8},{10,11... | collective-permute-start | bytes 6291464 | tf_op jit(solution)/shard_map/ppermute | solution.py:397
  663.6 22.9 %collective-permute-start.36 = (bf16[4,64,2048]{2,1,0:T(8,128)(2,1)S(1)}, bf16[4,64,2048]{2,1,0:T(8,128)(2,1)S(1)}, u32[]{:S(2)}, u32[]{:S(2)}) collective-permute-start(bf16[4,64,2048]{2,1,0:T(8,128)(2,1)S(1)} %dynamic-slice_bitcast_fusion.7), channel_id=1, source_target_pairs={{0,4},{1,5},{2,6},{3,7},{4,0},{5,1},{6,2},{7,3},{8,12},{9,13},{10,... | collective-permute-start | bytes 3145736 | tf_op jit(solution)/shard_map/ppermute | solution.py:397
  686.6 13.1 %collective-permute-start.37 = (bf16[2,64,2048]{2,1,0:T(8,128)(2,1)S(1)}, bf16[2,64,2048]{2,1,0:T(8,128)(2,1)S(1)}, u32[]{:S(2)}, u32[]{:S(2)}) collective-permute-start(bf16[2,64,2048]{2,1,0:T(8,128)(2,1)S(1)} %dynamic-slice_bitcast_fusion.10), channel_id=1, source_target_pairs={{0,8},{1,9},{2,10},{3,11},{4,12},{5,13},{6,14},{7,15},{8,0},{9,1},... | collective-permute-start | bytes 1572872 | tf_op jit(solution)/shard_map/ppermute | solution.py:397
  699.8 13.2 %collective-permute-start.38 = (bf16[1,64,2048]{2,1,0:T(8,128)(2,1)S(1)}, bf16[1,64,2048]{2,1,0:T(8,128)(2,1)S(1)}, u32[]{:S(2)}, u32[]{:S(2)}) collective-permute-start(bf16[1,64,2048]{2,1,0:T(8,128)(2,1)S(1)} %constant_dynamic-slice_fusion.1), channel_id=1, source_target_pairs={{0,16},{1,17},{2,18},{3,19},{4,20},{5,21},{6,22},{7,23},{8,24},{9,... | collective-permute-start | bytes 786440 | tf_op jit(solution)/shard_map/ppermute | solution.py:397
  725.6 66.0 %collective-permute-start.9 = (bf16[1024,1024]{1,0:T(8,128)(2,1)}, bf16[1024,1024]{1,0:T(8,128)(2,1)}, u32[]{:S(2)}, u32[]{:S(2)}) collective-permute-start(bf16[1024,1024]{1,0:T(8,128)(2,1)} %add_convert_fusion), channel_id=1, source_target_pairs={{1,2},{2,1},{5,6},{6,5},{9,10},{10,9},{13,14},{14,13},{17,18},{18,... | collective-permute-start | bytes 6291464 | tf_op jit(solution)/shard_map/ppermute | solution.py:397
  746.3 45.4 %copy-start.28 = (bf16[1024,1024]{1,0:T(8,128)(2,1)S(1)}, bf16[1024,1024]{1,0:T(8,128)(2,1)}, u32[]{:S(2)}) copy-start(bf16[1024,1024]{1,0:T(8,128)(2,1)} %add_convert_fusion) | copy-start | bytes 6291460
  746.3 46.9 %collective-permute-start.15 = (bf16[1024,1024]{1,0:T(8,128)(2,1)}, bf16[1024,1024]{1,0:T(8,128)(2,1)}, u32[]{:S(2)}, u32[]{:S(2)}) collective-permute-start(bf16[1024,1024]{1,0:T(8,128)(2,1)} %fusion.12), channel_id=1, source_target_pairs={{1,2},{2,1},{5,6},{6,5},{9,10},{10,9},{13,14},{14,13},{17,18},{18,... | collective-permute-start | bytes 6291464 | tf_op jit(solution)/shard_map/ppermute | solution.py:397
  749.4 26.6 %collective-permute-start.16 = (f32[52,128]{1,0:T(8,128)S(1)}, f32[52,128]{1,0:T(8,128)S(1)}, u32[]{:S(2)}, u32[]{:S(2)}) collective-permute-start(f32[52,128]{1,0:T(8,128)S(1)} %maximum_bitcast_fusion.1), channel_id=1, source_target_pairs={{0,1},{1,0},{2,3},{3,2},{4,5},{5,4},{6,7},{7,6},{8,9},{9,8},{10,11... | collective-permute-start | bytes 79880 | tf_op jit(solution)/shard_map/ppermute | solution.py:397
  776.0 1.3 collective-permute-start.17
  777.3 3.9 collective-permute-start.18
  781.2 3.9 collective-permute-start.19
  785.1 4.8 collective-permute-start.20
  (64 other events, 670.6 us)
Sparse Core Ops, SparseCore 0:
  26.6 46.8 all-gather.12
  76.2 36.7 all-gather.14
  115.2 49.4 all-gather.16
  166.7 49.0 all-gather.18
  486.5 36.6 all-gather.22
  525.4 50.2 all-gather.20
  612.7 49.5 all-gather.26
  713.9 49.5 all-gather.24

commit v2 on v1

--- a/solution.py
+++ b/solution.py
@@ -243,13 +243,19 @@
     dq_ref[...] = turn_back(dq, c_ref[...], sa_ref[...], sb_ref[...]).astype(BF)
 
 
-def attend_back(q, out_grad, out, lse, kvs, tables):
+def attend_back(q, out_grad, out, lse, kvs, tables, skip=0, pairs=None):
     tokens, cols = q.shape
-    pairs = cols // LANES
+    all_pairs = cols // LANES
+    pairs = pairs or all_pairs
+    cols = pairs * LANES
     keys = sum(kv.shape[0] for kv in kvs)
-    q_spec = pl.BlockSpec((tokens, LANES), lambda i: (0, i))
-    k_specs = [pl.BlockSpec((kv.shape[0], LANES), lambda i: (0, i)) for kv in kvs]
-    v_specs = [pl.BlockSpec((kv.shape[0], LANES), lambda i: (0, pairs + i)) for kv in kvs]
+    q_spec = pl.BlockSpec((tokens, LANES), lambda i: (0, skip + i))
+    k_specs = [pl.BlockSpec((kv.shape[0], LANES), lambda i: (0, skip + i)) for kv in kvs]
+    v_specs = [
+        pl.BlockSpec((kv.shape[0], LANES), lambda i: (0, all_pairs + skip + i)) for kv in kvs
+    ]
+    dq_spec = pl.BlockSpec((tokens, LANES), lambda i: (0, i))
+    dk_specs = [pl.BlockSpec((kv.shape[0], LANES), lambda i: (0, i)) for kv in kvs]
     table = pl.BlockSpec((tokens, LANES), lambda i: (0, 0))
     piece = min(512, tokens)
     outs = call(
@@ -261,11 +267,11 @@
         tokens * keys * 2 * pairs,
         grid=(pairs,),
         in_specs=[q_spec, q_spec, q_spec]
-        + [pl.BlockSpec((1, 2, tokens), lambda i: (i, 0, 0))]
+        + [pl.BlockSpec((1, 2, tokens), lambda i: (skip + i, 0, 0))]
         + [table] * 3
         + k_specs
         + v_specs,
-        out_specs=[q_spec] + k_specs + k_specs,
+        out_specs=[dq_spec] + dk_specs + dk_specs,
         out_shape=[jax.ShapeDtypeStruct((tokens, cols), BF)]
         + [jax.ShapeDtypeStruct((kv.shape[0], cols), BF) for kv in kvs] * 2,
         scratch_shapes=[pltpu.VMEM((LANES, tokens), F32), pltpu.VMEM((2, tokens), F32)],
@@ -379,6 +385,15 @@
     return back, jnp.sum(upstream * normal, 0), jnp.sum(upstream, 0)
 
 
+def pick(x, index):
+    return lax.dynamic_index_in_dim(x, index, 1, keepdims=False)
+
+
+def tie(*trees):
+    leaves, form = jax.tree.flatten(trees)
+    return jax.tree.unflatten(form, lax.optimization_barrier(tuple(leaves)))
+
+
 class Paired:
     def __init__(self, n_dp):
         self.n_dp = n_dp
@@ -409,13 +424,12 @@
     def over_chip(self, x, bit):
         return self.move(x, lambda dp, y: (dp ^ (2 << bit), y))
 
-    def other_half(self, own):
+    def piece(self, own):
         rows = own.shape[0] // self.n_dp
-        piece = lax.dynamic_slice_in_dim(own, self.me_dp * rows, rows, 0)
-        return lax.all_gather(self.over_y(piece), "dp", axis=0, tiled=True)
-
-    def weights(self, own):
-        return [own, self.other_half(own)]
+        return lax.dynamic_slice_in_dim(own, self.me_dp * rows, rows, 0)
+
+    def spread(self, got):
+        return lax.all_gather(got, "dp", axis=0, tiled=True)
 
     def biases(self, own):
         return [own, self.over_y(own)]
@@ -426,27 +440,19 @@
     def keys_back(self, grads):
         return grads[0], self.over_core(grads[1])
 
-    def reduce(self, own, other):
-        rows, cols = own.shape
-        chips = self.n_dp // 2
-        piece = rows // self.n_dp
-
-        def split(x, axis, bit):
-            take = lambda b: lax.dynamic_index_in_dim(x, b, axis, keepdims=False)
-            return take(bit), take(1 - bit)
-
-        kept = []
-        for half in (own, other):
-            keep, send = split(half.reshape(chips, 2, piece, cols), 1, self.core)
-            kept.append(keep + self.over_core(send))
-        total = kept[0] + self.over_y(kept[1])
-        chip = self.me_dp // 2
-        for level in range(chips.bit_length() - 1):
-            left = total.shape[0] // 2
-            keep, send = split(total.reshape(left, 2, piece, cols), 1, (chip >> level) & 1)
-            total = keep + self.over_chip(send, level)
-        total = total.reshape(piece, cols)
-        return lax.all_gather(total, "dp", axis=0, tiled=True).astype(F32)
+    def core_split(self, half):
+        rows, cols = half.shape
+        blocks = half.reshape(self.n_dp // 2, 2, rows // self.n_dp, cols)
+        return pick(blocks, self.core), pick(blocks, 1 - self.core)
+
+    def chip_split(self, blocks, level):
+        bit = (self.me_dp >> (level + 1)) & 1
+        left = blocks.shape[0] // 2
+        blocks = blocks.reshape(left, 2, *blocks.shape[1:])
+        return pick(blocks, bit), pick(blocks, 1 - bit)
+
+    def gather(self, block):
+        return lax.all_gather(block[0], "dp", axis=0, tiled=True)
 
     def reduce_vectors(self, both, own, other):
         k, width = both.shape
@@ -573,46 +579,189 @@
     (block_in, ln1_scale, ln1_shift, qkv_weight, qkv_bias, out_weight, out_bias) = args[:7]
     (ln2_scale, ln2_shift, up_weight, up_bias, down_weight, down_bias, out_grad) = args[7:]
     move = Paired(n_dp)
+    f32 = lambda v: v.astype(F32)
     width, _, part = qkv_weight.shape
-    qkv_flat = qkv_weight.reshape(width, 3 * part)
-    out = block_step(
-        move,
-        block_in,
-        ln1_scale,
-        ln1_shift,
-        move.weights(qkv_flat),
-        move.biases(qkv_bias.reshape(3 * part)),
-        move.weights(out_weight),
-        out_bias,
-        ln2_scale,
-        ln2_shift,
-        move.weights(up_weight),
-        move.biases(up_bias),
-        move.weights(down_weight),
-        down_bias,
-        out_grad,
-    )
-    block_out, in_grad, vectors, weight_grads, (qkv_b, up_b) = out
-    qkv_g, out_g, up_g, down_g = (move.reduce(*pair) for pair in weight_grads)
+    tokens = block_in.shape[0]
+    pairs = part // LANES
+    levels = (n_dp // 2).bit_length() - 1
+    ln1_gain, ln2_gain = f32(ln1_scale), f32(ln2_scale)
+
+    block_in = move.swap_rows(block_in)
+    qkv_own = qkv_weight.reshape(width, 3 * part)
+    qkv_got = move.over_y(move.piece(qkv_own))
+    qkv_bs = move.biases(qkv_bias.reshape(3 * part))
+    tables = rotary_tables(move.first, tokens)
+    x_rows = f32(block_in)
+    normed1, normal1, inv_one = norm_parts(x_rows, ln1_gain, f32(ln1_shift))
+    qkv_got, normed1 = tie(qkv_got, normed1)
+    qkv_ws = [qkv_own, move.spread(qkv_got)]
+    q_own, kv_own = qkv_rows(normed1, qkv_own, f32(qkv_bs[0])[None, :], tables)
+    rest = [move.piece(w) for w in (out_weight, up_weight, down_weight)]
+    rest, up_bias, kv_own = tie(rest, up_bias, kv_own)
+    kvs_own = move.keys(kv_own)
+    rest = [move.over_y(w) for w in rest]
+    up_bs = move.biases(up_bias)
+    q_oth, kv_oth = qkv_rows(normed1, qkv_ws[1], f32(qkv_bs[1])[None, :], tables)
+    kvs_own, rest, kv_oth, q_own = tie(kvs_own, rest, kv_oth, q_own)
+    out_ws, up_ws, down_ws = (
+        [w, move.spread(got)] for w, got in zip((out_weight, up_weight, down_weight), rest)
+    )
+    kvs_oth = move.keys(kv_oth)
+    out_own, log_own = attend(q_own, kvs_own)
+    out_own, kvs_oth, q_oth, out_grad = tie(out_own, kvs_oth, q_oth, out_grad)
+    grad_low = move.swap_rows(out_grad)
+    out_oth, log_oth = attend(q_oth, kvs_oth)
+    out_oth, grad_low = tie(out_oth, grad_low)
+    grad_rows = f32(grad_low)
+    outs = [out_own, out_oth]
+
+    branch_one = sum(dot_nn(o, w) for o, w in zip(outs, out_ws)) + f32(out_bias)
+    resid = x_rows + branch_one
+    normed2, normal2, inv_two = norm_parts(resid, ln2_gain, f32(ln2_shift))
+    acts, slopes = [], []
+    for weight, bias in zip(up_ws, up_bs):
+        acted, slope = up_rows(normed2, weight, f32(bias)[None, :])
+        acts.append(acted)
+        slopes.append(slope)
+    branch_two = sum(dot_nn(a, w) for a, w in zip(acts, down_ws)) + f32(down_bias)
+    block_out = (resid + branch_two).astype(BF)
+    block_out, acts = tie(block_out, acts)
+    block_out = move.swap_rows(block_out)
+    down_bias_grad = jnp.sum(grad_rows, 0)
+    down_grads = [dot_tn(a, grad_low).astype(BF) for a in acts]
+    down_keep, down_send = zip(*[move.core_split(g) for g in down_grads])
+
+    down_keep, down_send, acts, grad_low = tie(down_keep, down_send, acts, grad_low)
+    down_got = [move.over_core(x) for x in down_send]
+    hidden_gs, up_b_grads = [], []
+    for down, slope in zip(down_ws, slopes):
+        hg, total = hidden_grads(grad_low, down, slope)
+        hidden_gs.append(hg)
+        up_b_grads.append(total[0])
+    down_got, hidden_gs, block_out = tie(down_got, hidden_gs, block_out)
+    down_send = down_keep[1] + down_got[1]
+    down_keep = down_keep[0] + down_got[0]
+
+    down_send, hidden_gs = tie(down_send, hidden_gs)
+    down_got = move.over_y(down_send)
+    up_grads = [dot_tn(normed2, hg).astype(BF) for hg in hidden_gs]
+    up_keep, up_send = zip(*[move.core_split(g) for g in up_grads])
+    up_keep, up_send, hidden_gs = tie(up_keep, up_send, hidden_gs)
+    up_got = [move.over_core(x) for x in up_send]
+    normed2_grad = sum(dot_nt(hg, w) for hg, w in zip(hidden_gs, up_ws))
+    resid_part, ln2_scale_grad, ln2_shift_grad = norm_back(normed2_grad, normal2, inv_two, ln2_gain)
+    resid_grad = grad_rows + resid_part
+    branch_grad = resid_grad.astype(BF)
+    out_bias_grad = jnp.sum(branch_grad, 0, dtype=F32)
+    out_w_grads = [dot_tn(o, branch_grad).astype(BF) for o in outs]
+    out_gs = [dot_nt(branch_grad, w).astype(BF) for w in out_ws]
+    up_got, down_got, out_gs, out_w_grads = tie(up_got, down_got, out_gs, out_w_grads)
+    up_send = up_keep[1] + up_got[1]
+    up_keep = up_keep[0] + up_got[0]
+    down = down_keep + down_got
+
+    def step(total, level):
+        keep, send = move.chip_split(total, level)
+        return keep, send
+
+    def back(which, skip):
+        q, kvs, log = ((q_own, kvs_own, log_own), (q_oth, kvs_oth, log_oth))[which]
+        return q, out_gs[which], outs[which], log, kvs
+
+    half = pairs // 2
+    down_keep, down_send = step(down, 0)
+    ins, up_send, down_send = tie(back(1, 0), up_send, down_send)
+    up_got = move.over_y(up_send)
+    down_got = move.over_chip(down_send, 0)
+    first = attend_back(*ins, tables, 0, half)
+    first, down_got = tie(first, down_got)
+    down_keep, down_send = step(down_keep + down_got, 1)
+    ins, down_send, first = tie(back(1, half), down_send, first)
+    down_got = move.over_chip(down_send, 1)
+    first_got = [move.over_core(x[1]) for x in first[1:]]
+    second = attend_back(*ins, tables, half, half)
+    second, down_got, up_got, first_got = tie(second, down_got, up_got, first_got)
+    down_keep, down_send = step(down_keep + down_got, 2)
+    up_keep, up_send = step(up_keep + up_got, 0)
+    second, down_send, up_send = tie(second, down_send, up_send)
+    second_got = [move.over_core(x[1]) for x in second[1:]]
+    down_got = move.over_chip(down_send, 2)
+    up_got = move.over_chip(up_send, 0)
+
+    def finish(parts, gots):
+        dk = [key_sum(p[1][0], g[0], tables) for p, g in zip(parts, gots)]
+        dv = [p[2][0] + g[1] for p, g in zip(parts, gots)]
+        return jnp.concatenate([p[0] for p in parts] + dk + dv, axis=1)
+
+    third = attend_back(*back(0, 0), tables, 0, half)
+    third, second_got, down_got, up_got = tie(third, second_got, down_got, up_got)
+    down_block = down_keep + down_got
+    up_keep, up_send = step(up_keep + up_got, 1)
+    qkv_g_oth = finish((first, second), (first_got, second_got))
+    qkv_w_oth = dot_tn(normed1, qkv_g_oth).astype(BF)
+    ins, down_block, up_send, third, qkv_w_oth = tie(
+        back(0, half), down_block, up_send, third, qkv_w_oth
+    )
+    third_got = [move.over_core(x[1]) for x in third[1:]]
+    down_all = move.gather(down_block)
+    up_got = move.over_chip(up_send, 1)
+    oth_keep, oth_send = zip(*[move.core_split(g) for g in (qkv_w_oth, out_w_grads[1])])
+    oth_got = [move.over_core(x) for x in oth_send]
+    fourth = attend_back(*ins, tables, half, half)
+    fourth, third_got, up_got, oth_got = tie(fourth, third_got, up_got, oth_got)
+    up_keep, up_send = step(up_keep + up_got, 2)
+    oth_send = [k + g for k, g in zip(oth_keep, oth_got)]
+    fourth, up_send, oth_send = tie(fourth, up_send, oth_send)
+    fourth_got = [move.over_core(x[1]) for x in fourth[1:]]
+    up_got = move.over_chip(up_send, 2)
+    oth_got = [move.over_y(x) for x in oth_send]
+    normed1_grad = dot_nt(qkv_g_oth, qkv_ws[1])
+    fourth_got, normed1_grad = tie(fourth_got, normed1_grad)
+    qkv_g_own = finish((third, fourth), (third_got, fourth_got))
+    qkv_w_own = dot_tn(normed1, qkv_g_own).astype(BF)
+    qkv_w_own, qkv_g_own, up_got, down_all = tie(qkv_w_own, qkv_g_own, up_got, down_all)
+    up_all = move.gather(up_keep + up_got)
+    own_keep, own_send = zip(*[move.core_split(g) for g in (qkv_w_own, out_w_grads[0])])
+    own_got = [move.over_core(x) for x in own_send]
+    normed1_grad = normed1_grad + dot_nt(qkv_g_own, qkv_ws[0])
+    input_part, ln1_scale_grad, ln1_shift_grad = norm_back(normed1_grad, normal1, inv_one, ln1_gain)
+    in_grad = (resid_grad + input_part).astype(BF)
+    own_got, in_grad, oth_got = tie(own_got, in_grad, oth_got)
+    in_grad = move.swap_rows(in_grad)
+    totals = [k + g + h for k, g, h in zip(own_keep, own_got, oth_got)]
+    for level in range(levels):
+        keeps, sends = zip(*[step(t, level) for t in totals])
+        totals = [k + move.over_chip(s, level) for k, s in zip(keeps, sends)]
+    qkv_g, out_g = (move.gather(t) for t in totals)
+    qkv_b = [jnp.sum(g, 0, dtype=F32) for g in (qkv_g_own, qkv_g_oth)]
     vec, flat = move.reduce_vectors(
-        jnp.stack(vectors),
-        jnp.concatenate([qkv_b[0], up_b[0]]),
-        jnp.concatenate([qkv_b[1], up_b[1]]),
+        jnp.stack(
+            [
+                ln1_scale_grad,
+                ln1_shift_grad,
+                out_bias_grad,
+                ln2_scale_grad,
+                ln2_shift_grad,
+                down_bias_grad,
+            ]
+        ),
+        jnp.concatenate([qkv_b[0], up_b_grads[0]]),
+        jnp.concatenate([qkv_b[1], up_b_grads[1]]),
     )
     return (
         block_out,
         in_grad,
         vec[0],
         vec[1],
-        qkv_g.reshape(width, 3, part),
+        f32(qkv_g).reshape(width, 3, part),
         flat[: 3 * part].reshape(3, part),
-        out_g,
+        f32(out_g),
         vec[2],
         vec[3],
         vec[4],
-        up_g,
+        f32(up_all),
         flat[3 * part :],
-        down_g,
+        f32(down_all),
         vec[5],
     )
 

time: 839 us -> 796 us (0.949)
  waiting for transfers between devices: 278 us -> 241 us
  starting transfers between devices: 72.3 us -> 43 us
  local copies, waits for them, and re-layouts: 46.3 us -> 58.1 us
    ppermute x45 -> x49, waiting for transfers between devices: 278 us -> 185 us  [move(): return lax.ppermute(x, ('dp', 'tensor'), pairs)]
    all_gather x8, waiting for transfers between devices: 0.05 us -> 54.9 us  [the longest x4 32.8 us: gather(): return lax.all_gather(block[0], 'dp', axis=0, tiled=True)]
    ppermute x45 -> x49, starting transfers between devices: 71.4 us -> 42.7 us  [move(): return lax.ppermute(x, ('dp', 'tensor'), pairs)]
    unnamed x158 -> x160, local copies, waits for them, and re-layouts: 20.2 us -> 29.4 us
    pallas_call x2 -> x4, Pallas kernels: 103 us -> 109 us  [attend_back(): call(functools.partial(attend_back_kernel, sources=len(kvs), keys_at=512,...]
    add x22 -> x20, other arithmetic: 27.7 us -> 25.3 us  [the longest x2 4.44 us: paired_device(): totals = [k + g + h for k, g, h in zip(own_keep, own_got, oth_got)]]
  transfers between devices with their start and end apart: 53 -> 57, of which waited for: 24 -> 20; matrix products, arithmetic and copies ran while one was open for 20% -> 18% of each run, Pallas kernels for 22% -> 32%
where the time goes in v2:
time: 796 us; the launch traced here: 786 us
  Pallas kernels  253 us (32%)
  waiting for transfers between devices  241 us (30%)
  matrix products  94.3 us (12%)
  other arithmetic  80.7 us (10%)
  local copies, waits for them, and re-layouts  58.1 us (7%)
  starting transfers between devices  43 us (5%)
  between operations  15.6 us (2%)
    ppermute x49, waiting for transfers between devices, move(): return lax.ppermute(x, ('dp', 'tensor'), pairs)  185 us
    pallas_call x4, Pallas kernels, attend_back(): call(functools.partial(attend_back_kernel, sources=len(kvs), keys_at=512,...  109 us
    pallas_call x2, Pallas kernels, attend(): call(functools.partial(attend_kernel, sources=len(kvs), rows_at=256), 4 *...  59.3 us
    ppermute x49, starting transfers between devices, move(): return lax.ppermute(x, ('dp', 'tensor'), pairs)  42.7 us
    dot_general x6, matrix products, dot_nt(): lax.dot_general(left, right, (((1,), (1,)), ((), ())), preferred_element_...  34.9 us
    dot_general x8, matrix products, dot_tn(): lax.dot_general(left, right, (((0,), (0,)), ((), ())), preferred_element_...  34.3 us
    all_gather x4, waiting for transfers between devices, gather(): return lax.all_gather(block[0], 'dp', axis=0, tiled=True)  32.8 us
    unnamed x160, local copies, waits for them, and re-layouts  29.4 us
  transfers between devices with their start and end apart: 57, of which 20 were waited for; matrix products, arithmetic and copies ran while one was open for 18% of the time, Pallas kernels for 32%

profile of v2, /device:TPU:0, one launch (start us, length us, event | category | flops | bytes accessed | tf_op | source)
XLA Modules:
  0.0 785.6 jit_solution(1496991464376377221)
XLA Ops:
  9.3 4.7 copy.49
  14.0 4.7 copy.50.w_ref
  19.6 3.0 collective-permute-start.1
  27.9 12.8 %collective-permute-done.1 = bf16[64,1536]{1,0:T(8,128)(2,1)S(1)} collective-permute-done((bf16[64,1536]{1,0:T(8,128)(2,1)S(1)}, bf16[64,1536]{1,0:T(8,128)(2,1)S(1)}, u32[]{:S(2)}, u32[]{:S(2)}) %collective-permute-start.1) | collective-permute-done | bytes 196640 | tf_op jit(solution)/shard_map/ppermute | solution.py:412
  44.8 4.4 fusion.18
  49.1 11.1 %shard_map.299 = (bf16[1024,512]{1,0:T(8,128)(2,1)}, bf16[1024,1024]{1,0:T(8,128)(2,1)}) custom-call(bf16[1024,1024]{1,0:T(8,128)(2,1)} %fusion.7.n_ref, bf16[1024,1536]{1,0:T(8,128)(2,1)} %copy.50.w_ref, f32[1,1536]{1,0:T(1,128)} %bitcast.201, f32[1024,128]{1,0:T(8,128)} %get-tuple-element.451.c_ref.refs_4_, f32[1024,128]{1,0:T(8,128)} %get-tuple-element.450.sa_ref.refs_5_, ...), custom_call_target="tpu_custom_call" | custom-call | flops 3221225472 | bytes 8388608 | tf_op jit(solution)/shard_map/pallas_call | solution.py:114
  60.2 3.2 collective-permute-start.2
  71.3 19.8 %all-gather.13.cloned.1.call-done.w_ref = bf16[1024,1536]{1,0:T(8,128)(2,1)} async-done(((bf16[64,1536]{1,0:T(8,128)(2,1)}), bf16[1024,1536]{1,0:T(8,128)(2,1)}) %all-gather.13.cloned.1.call-update) | async-done | bytes 3145744 | tf_op jit(solution)/shard_map/all_gather | solution.py:432
  91.1 11.0 %shard_map.300 = (bf16[1024,512]{1,0:T(8,128)(2,1)}, bf16[1024,1024]{1,0:T(8,128)(2,1)}) custom-call(bf16[1024,1024]{1,0:T(8,128)(2,1)} %fusion.7.n_ref, bf16[1024,1536]{1,0:T(8,128)(2,1)} %all-gather.13.cloned.1.call-done.w_ref, f32[1,1536]{1,0:T(1,128)} %reshape.343.b_ref, f32[1024,128]{1,0:T(8,128)} %get-tuple-element.451.c_ref.refs_4_, ...), custom_call_target="tpu_custom_call" | custom-call | flops 3221225472 | bytes 8388608 | tf_op jit(solution)/shard_map/pallas_call | solution.py:114
  104.2 29.7 %shard_map.301 = (bf16[1024,512]{1,0:T(8,128)(2,1)}, f32[4,2,1024]{2,1,0:T(2,128)}) custom-call(bf16[1024,512]{1,0:T(8,128)(2,1)} %get-tuple-element.324.refs_0_, bf16[1024,1024]{1,0:T(8,128)(2,1)} %get-tuple-element.328.refs_1_.refs_3_.refs_7_.refs_9_, bf16[1024,1024]{1,0:T(8,128)(2,1)} %collective-permute-done.2.refs_2_.refs_4_.refs_8_.refs_10_, ...), custom_call_target="tpu_custom_call" | custom-call | flops 17179869184 | bytes 6291456 | tf_op jit(solution)/shard_map/pallas_call | solution.py:177
  133.8 2.4 collective-permute-start.8
  138.8 23.5 %collective-permute-done.9 = bf16[2048]{0:T(1024)(128)(2,1)S(1)} collective-permute-done((bf16[2048]{0:T(1024)(128)(2,1)S(1)}, bf16[2048]{0:T(1024)(128)(2,1)S(1)}, u32[]{:S(2)}, u32[]{:S(2)}) %collective-permute-start.9) | collective-permute-done | bytes 4128 | tf_op jit(solution)/shard_map/ppermute | solution.py:412
  163.0 29.6 %shard_map.302 = (bf16[1024,512]{1,0:T(8,128)(2,1)}, f32[4,2,1024]{2,1,0:T(2,128)}) custom-call(bf16[1024,512]{1,0:T(8,128)(2,1)} %get-tuple-element.273.refs_0_, bf16[1024,1024]{1,0:T(8,128)(2,1)} %get-tuple-element.277.refs_1_.refs_3_.refs_7_.refs_9_, bf16[1024,1024]{1,0:T(8,128)(2,1)} %collective-permute-done.7.refs_2_.refs_4_.refs_8_.refs_10_, ...), custom_call_target="tpu_custom_call" | custom-call | flops 17179869184 | bytes 6291456 | tf_op jit(solution)/shard_map/pallas_call | solution.py:177
  192.6 3.1 broadcast_select_fusion.2.g_ref
  195.7 2.9 fusion.28
  203.0 14.2 %shard_map.303 = (bf16[1024,2048]{1,0:T(8,128)(2,1)}, bf16[1024,2048]{1,0:T(8,128)(2,1)}) custom-call(bf16[1024,1024]{1,0:T(8,128)(2,1)} %add_convert_fusion.1.n_ref, bf16[1024,2048]{1,0:T(8,128)(2,1)} %w_ref.2, f32[1,2048]{1,0:T(1,128)} %bitcast.200), custom_call_target="tpu_custom_call" | custom-call | flops 4294967296 | bytes 14680064 | tf_op jit(solution)/shard_map/pallas_call | solution.py:327
  217.1 8.7 %fusion.29 = f32[1024,1024]{1,0:T(8,128)} fusion(bf16[1024,2048]{1,0:T(8,128)(2,1)} %get-tuple-element.223, bf16[2048,1024]{1,0:T(8,128)(2,1)S(1)} %copy-done.52), kind=kOutput, calls=%fused_computation.162 | convolution fusion | flops 4294967296 | bytes 12582912 | tf_op jit(solution)/shard_map/dot_general | solution.py:32
  225.9 14.3 %shard_map.304 = (bf16[1024,2048]{1,0:T(8,128)(2,1)}, bf16[1024,2048]{1,0:T(8,128)(2,1)}) custom-call(bf16[1024,1024]{1,0:T(8,128)(2,1)} %add_convert_fusion.1.n_ref, bf16[1024,2048]{1,0:T(8,128)(2,1)} %all-gather.17.cloned.1.call-done.w_ref, f32[1,2048]{1,0:T(1,128)} %bitcast.199), custom_call_target="tpu_custom_call" | custom-call | flops 4294967296 | bytes 14680064 | tf_op jit(solution)/shard_map/pallas_call | solution.py:327
  242.4 11.8 %add_convert_fusion = bf16[1024,1024]{1,0:T(8,128)(2,1)} fusion(f32[1024,1024]{1,0:T(8,128)} %copy-done.4, f32[1024,1024]{1,0:T(8,128)} %fusion.29, f32[1024]{0:T(1024)S(1)} %convert_element_type.118, bf16[1024,2048]{1,0:T(8,128)(2,1)} %get-tuple-element.225, bf16[2048,1024]{1,0:T(8,128)(2,1)} %all-gather.19.cloned.1.call-done.w_ref), kind=kOutput, calls=%fused_computation.26 | convolution fusion | flops 4299161600 | bytes 18878464 | tf_op jit(solution)/shard_map/dot_general | solution.py:32
  256.4 4.9 convolution_convert_fusion.4
  261.3 5.0 convolution_convert_fusion.5
  272.1 11.1 %shard_map.305 = (bf16[1024,2048]{1,0:T(8,128)(2,1)}, f32[1,2048]{1,0:T(1,128)}) custom-call(bf16[1024,1024]{1,0:T(8,128)(2,1)} %broadcast_select_fusion.2.g_ref, bf16[2048,1024]{1,0:T(8,128)(2,1)} %w_ref.3, bf16[1024,2048]{1,0:T(8,128)(2,1)} %get-tuple-element.229.slope_ref), custom_call_target="tpu_custom_call" | custom-call | flops 4294967296 | bytes 14680064 | tf_op jit(solution)/shard_map/pallas_call | solution.py:355
  283.3 11.1 %shard_map.306 = (bf16[1024,2048]{1,0:T(8,128)(2,1)}, f32[1,2048]{1,0:T(1,128)}) custom-call(bf16[1024,1024]{1,0:T(8,128)(2,1)} %broadcast_select_fusion.2.g_ref, bf16[2048,1024]{1,0:T(8,128)(2,1)} %all-gather.19.cloned.1.call-done.w_ref, bf16[1024,2048]{1,0:T(8,128)(2,1)} %get-tuple-element.231.slope_ref), custom_call_target="tpu_custom_call" | custom-call | flops 4294967296 | bytes 14680064 | tf_op jit(solution)/shard_map/pallas_call | solution.py:355
  294.4 3.1 broadcast_select_fusion.1
  297.5 4.0 add.342
  301.6 4.9 convolution_convert_fusion.2
  309.4 5.1 convolution_convert_fusion.3
  317.5 6.1 fusion.30
  323.6 11.0 %multiply_reduce_fusion = (f32[1024]{0:T(1024)}, f32[1024]{0:T(1024)S(1)}, f32[1024]{0:T(1024)S(1)}, f32[1024]{0:T(1024)}, f32[1024,1024]{1,0:T(8,128)S(1)}) fusion(f32[1024,1024]{1,0:T(8,128)S(1)} %copy-done.5, f32[1024]{0:T(1024)S(1)} %add_rsqrt_fusion, f32[1024]{0:T(1024)S(1)} %broadcast_multiply_fusion.4, f32[1024]{0:T(1024)S(1)} %convert_element_type.115, ...), kind=kOutput, calls=%fused_computation.23 | convolution fusion | flops 4305448960 | bytes 21000192 | tf_op jit(solution)/shard_map/dot_general | solution.py:28
  335.9 4.4 convert_reduce_fusion.4
  348.8 34.6 %collective-permute-done.15 = bf16[8,128,1024]{2,1,0:T(8,128)(2,1)S(1)} collective-permute-done((bf16[8,128,1024]{2,1,0:T(8,128)(2,1)}, bf16[8,128,1024]{2,1,0:T(8,128)(2,1)S(1)}, u32[]{:S(2)}, u32[]{:S(2)}) %collective-permute-start.15) | collective-permute-done | bytes 2097184 | tf_op jit(solution)/shard_map/ppermute | solution.py:412
  388.6 27.1 %shard_map.307 = (bf16[1024,256]{1,0:T(8,128)(2,1)}, bf16[1024,256]{1,0:T(8,128)(2,1)}, bf16[1024,256]{1,0:T(8,128)(2,1)}, bf16[1024,256]{1,0:T(8,128)(2,1)}, bf16[1024,256]{1,0:T(8,128)(2,1)}) custom-call(bf16[1024,512]{1,0:T(8,128)(2,1)} %get-tuple-element.273.refs_0_, bf16[1024,512]{1,0:T(8,128)(2,1)} %convolution_convert_fusion.8.refs_1_, ...), custom_call_target="tpu_custom_call" | custom-call | flops 21474836480 | bytes 6291456 | tf_op jit(solution)/shard_map/pallas_call | solution.py:261
  419.3 27.4 %shard_map.308 = (bf16[1024,256]{1,0:T(8,128)(2,1)}, bf16[1024,256]{1,0:T(8,128)(2,1)}, bf16[1024,256]{1,0:T(8,128)(2,1)}, bf16[1024,256]{1,0:T(8,128)(2,1)}, bf16[1024,256]{1,0:T(8,128)(2,1)}) custom-call(bf16[1024,512]{1,0:T(8,128)(2,1)} %get-tuple-element.273.refs_0_, bf16[1024,512]{1,0:T(8,128)(2,1)} %convolution_convert_fusion.8.refs_1_, ...), custom_call_target="tpu_custom_call" | custom-call | flops 21474836480 | bytes 6291456 | tf_op jit(solution)/shard_map/pallas_call | solution.py:261
  447.7 2.6 add_add_fusion
  452.6 27.2 %shard_map.309 = (bf16[1024,256]{1,0:T(8,128)(2,1)}, bf16[1024,256]{1,0:T(8,128)(2,1)}, bf16[1024,256]{1,0:T(8,128)(2,1)}, bf16[1024,256]{1,0:T(8,128)(2,1)}, bf16[1024,256]{1,0:T(8,128)(2,1)}) custom-call(bf16[1024,512]{1,0:T(8,128)(2,1)} %get-tuple-element.324.refs_0_, bf16[1024,512]{1,0:T(8,128)(2,1)} %convolution_convert_fusion.9.refs_1_, ...), custom_call_target="tpu_custom_call" | custom-call | flops 21474836480 | bytes 6291456 | tf_op jit(solution)/shard_map/pallas_call | solution.py:261
  481.6 3.3 shard_map.310
  487.6 7.0 collective-permute-done.23
  495.5 3.1 shard_map.311
  504.7 6.7 convolution_convert_fusion.1
  519.7 27.3 %shard_map.312 = (bf16[1024,256]{1,0:T(8,128)(2,1)}, bf16[1024,256]{1,0:T(8,128)(2,1)}, bf16[1024,256]{1,0:T(8,128)(2,1)}, bf16[1024,256]{1,0:T(8,128)(2,1)}, bf16[1024,256]{1,0:T(8,128)(2,1)}) custom-call(bf16[1024,512]{1,0:T(8,128)(2,1)} %get-tuple-element.324.refs_0_, bf16[1024,512]{1,0:T(8,128)(2,1)} %convolution_convert_fusion.9.refs_1_, ...), custom_call_target="tpu_custom_call" | custom-call | flops 21474836480 | bytes 6291456 | tf_op jit(solution)/shard_map/pallas_call | solution.py:261
  551.2 6.9 fusion.31
  558.2 2.4 collective-permute-start.32
  562.3 3.0 shard_map.313
  567.3 3.0 shard_map.314
  571.6 5.1 convolution_convert_fusion
  579.1 6.4 fusion.32
  587.1 2.7 fusion.13
  591.5 16.7 %collective-permute-done.36 = bf16[8,32,1024]{2,1,0:T(8,128)(2,1)} collective-permute-done((bf16[8,32,1024]{2,1,0:T(8,128)(2,1)}, bf16[8,32,1024]{2,1,0:T(8,128)(2,1)}, u32[]{:S(2)}, u32[]{:S(2)}) %collective-permute-start.36) | collective-permute-done | bytes 524320 | tf_op jit(solution)/shard_map/ppermute | solution.py:412
  610.7 6.5 collective-permute-done.46
  617.6 4.7 collective-permute-done.47
  623.1 4.9 collective-permute-done.48
  630.5 2.6 fusion.15
  633.9 15.2 %collective-permute-done.43 = bf16[4,64,1536]{2,1,0:T(8,128)(2,1)S(1)} collective-permute-done((bf16[4,64,1536]{2,1,0:T(8,128)(2,1)S(1)}, bf16[4,64,1536]{2,1,0:T(8,128)(2,1)S(1)}, u32[]{:S(2)}, u32[]{:S(2)}) %collective-permute-start.43) | collective-permute-done | bytes 786464 | tf_op jit(solution)/shard_map/ppermute | solution.py:412
  649.4 13.4 %collective-permute-done.44 = bf16[2,64,1536]{2,1,0:T(8,128)(2,1)S(1)} collective-permute-done((bf16[2,64,1536]{2,1,0:T(8,128)(2,1)S(1)}, bf16[2,64,1536]{2,1,0:T(8,128)(2,1)S(1)}, u32[]{:S(2)}, u32[]{:S(2)}) %collective-permute-start.44) | collective-permute-done | bytes 393248 | tf_op jit(solution)/shard_map/ppermute | solution.py:412
  663.3 7.7 collective-permute-done.45
  680.9 22.0 %collective-permute-done.38 = f32[52,128]{1,0:T(8,128)S(1)} collective-permute-done((f32[52,128]{1,0:T(8,128)S(1)}, f32[52,128]{1,0:T(8,128)S(1)}, u32[]{:S(2)}, u32[]{:S(2)}) %collective-permute-start.38) | collective-permute-done | bytes 26656 | tf_op jit(solution)/shard_map/ppermute | solution.py:412
  704.2 4.4 collective-permute-done.40
  708.6 5.6 collective-permute-done.41
  714.2 6.6 convert_element_type.138
  724.2 2.8 bitcast_convert_fusion.1
  727.0 6.7 bitcast_convert_fusion
  733.8 32.8 %all-gather.23.cloned.1.call-done = bf16[1,1024,1536]{2,1,0:T(8,128)(2,1)} async-done(((bf16[1,64,1536]{2,1,0:T(8,128)(2,1)}), bf16[1,1024,1536]{2,1,0:T(8,128)(2,1)}) %all-gather.23.cloned.1.call-update) | async-done | bytes 3145744 | tf_op jit(solution)/shard_map/all_gather | solution.py:455
  766.5 5.4 copy.54
  771.9 6.6 copy.55
  (358 shorter events, 123.9 us)
Async XLA Ops:
  7.2 83.9 %all-gather.13.cloned.1.call-start = ((), (), s32[]{:S(2)}) async-start(), calls=%async_computation | async-start | bytes 3342336 | tf_op jit(solution)/shard_map/all_gather | solution.py:432
  7.2 15.4 %collective-permute-start = (bf16[1024,1024]{1,0:T(8,128)(2,1)}, bf16[1024,1024]{1,0:T(8,128)(2,1)}, u32[]{:S(2)}, u32[]{:S(2)}) collective-permute-start(bf16[1024,1024]{1,0:T(8,128)(2,1)} %param.20), channel_id=1, source_target_pairs={{1,2},{2,1},{5,6},{6,5},{9,10},{10,9},{13,14},{14,13},{17,18},{18,... | collective-permute-start | bytes 6291464 | tf_op jit(solution)/shard_map/ppermute | solution.py:412
  19.6 21.1 %collective-permute-start.1 = (bf16[64,1536]{1,0:T(8,128)(2,1)S(1)}, bf16[64,1536]{1,0:T(8,128)(2,1)S(1)}, u32[]{:S(2)}, u32[]{:S(2)}) collective-permute-start(bf16[64,1536]{1,0:T(8,128)(2,1)S(1)} %constant_dynamic-slice_fusion.6), channel_id=1, source_target_pairs={{0,1},{1,0},{2,3},{3,2},{4,5},{5,4},{6,7},{7,6},{8,9},{9,8},{10,11... | collective-permute-start | bytes 589832 | tf_op jit(solution)/shard_map/ppermute | solution.py:412
  25.0 173.7 %copy-start.2 = (bf16[1024,1024]{1,0:T(8,128)(2,1)}, bf16[1024,1024]{1,0:T(8,128)(2,1)S(1)}, u32[]{:S(2)}) copy-start(bf16[1024,1024]{1,0:T(8,128)(2,1)S(1)} %get-tuple-element.431) | copy-start | bytes 6291460
  41.4 154.3 %all-gather.15.cloned.1.call-start = ((), (), s32[]{:S(2)}) async-start(), calls=%async_computation.1 | async-start | bytes 1114112 | tf_op jit(solution)/shard_map/all_gather | solution.py:432
  60.2 41.9 %collective-permute-start.2 = (bf16[1024,1024]{1,0:T(8,128)(2,1)}, bf16[1024,1024]{1,0:T(8,128)(2,1)}, u32[]{:S(2)}, u32[]{:S(2)}) collective-permute-start(bf16[1024,1024]{1,0:T(8,128)(2,1)} %get-tuple-element.328.refs_1_.refs_3_.refs_7_.refs_9_), channel_id=1, source_target_pairs={{0,2},{1,3},{2,0},{3,1},{4,6},{5,7},{6,4},{7,5},{8,10},{9,11},{10,... | collective-permute-start | bytes 6291464 | tf_op jit(solution)/shard_map/ppermute | solution.py:412
  63.4 3.6 collective-permute-start.6
  67.6 34.5 %collective-permute-start.4 = (bf16[64,2048]{1,0:T(8,128)(2,1)}, bf16[64,2048]{1,0:T(8,128)(2,1)}, u32[]{:S(2)}, u32[]{:S(2)}) collective-permute-start(bf16[64,2048]{1,0:T(8,128)(2,1)} %constant_dynamic-slice_fusion.8), channel_id=1, source_target_pairs={{0,1},{1,0},{2,3},{3,2},{4,5},{5,4},{6,7},{7,6},{8,9},{9,8},{10,11... | collective-permute-start | bytes 786440 | tf_op jit(solution)/shard_map/ppermute | solution.py:412
  69.3 32.8 %collective-permute-start.5 = (bf16[128,1024]{1,0:T(8,128)(2,1)S(1)}, bf16[128,1024]{1,0:T(8,128)(2,1)}, u32[]{:S(2)}, u32[]{:S(2)}) collective-permute-start(bf16[128,1024]{1,0:T(8,128)(2,1)S(1)} %constant_dynamic-slice_fusion.7), channel_id=1, source_target_pairs={{0,1},{1,0},{2,3},{3,2},{4,5},{5,4},{6,7},{7,6},{8,9},{9,8},{10,11... | collective-permute-start | bytes 786440 | tf_op jit(solution)/shard_map/ppermute | solution.py:412
  69.6 32.4 %collective-permute-start.3 = (bf16[32,1024]{1,0:T(8,128)(2,1)S(1)}, bf16[32,1024]{1,0:T(8,128)(2,1)S(1)}, u32[]{:S(2)}, u32[]{:S(2)}) collective-permute-start(bf16[32,1024]{1,0:T(8,128)(2,1)S(1)} %constant_dynamic-slice_fusion.9), channel_id=1, source_target_pairs={{0,1},{1,0},{2,3},{3,2},{4,5},{5,4},{6,7},{7,6},{8,9},{9,8},{10,11... | collective-permute-start | bytes 196616 | tf_op jit(solution)/shard_map/ppermute | solution.py:412
  102.7 123.1 %all-gather.17.cloned.1.call-start = ((), (), s32[]{:S(2)}) async-start(), calls=%async_computation.2 | async-start | bytes 4456448 | tf_op jit(solution)/shard_map/all_gather | solution.py:432
  103.5 139.0 %all-gather.19.cloned.1.call-start = ((), (), s32[]{:S(2)}) async-start(), calls=%async_computation.3 | async-start | bytes 4456448 | tf_op jit(solution)/shard_map/all_gather | solution.py:432
  103.5 30.3 %collective-permute-start.7 = (bf16[1024,1024]{1,0:T(8,128)(2,1)}, bf16[1024,1024]{1,0:T(8,128)(2,1)}, u32[]{:S(2)}, u32[]{:S(2)}) collective-permute-start(bf16[1024,1024]{1,0:T(8,128)(2,1)} %get-tuple-element.277.refs_1_.refs_3_.refs_7_.refs_9_), channel_id=1, source_target_pairs={{0,2},{1,3},{2,0},{3,1},{4,6},{5,7},{6,4},{7,5},{8,10},{9,11},{10,... | collective-permute-start | bytes 6291464 | tf_op jit(solution)/shard_map/ppermute | solution.py:412
  104.1 475.0 %all-gather.21.cloned.1.call-start = ((), (), s32[]{:S(2)}) async-start(), calls=%async_computation.4 | async-start | bytes 4456448 | tf_op jit(solution)/shard_map/all_gather | solution.py:455
  133.8 58.8 %collective-permute-start.8 = (bf16[1024,1024]{1,0:T(8,128)(2,1)}, bf16[1024,1024]{1,0:T(8,128)(2,1)}, u32[]{:S(2)}, u32[]{:S(2)}) collective-permute-start(bf16[1024,1024]{1,0:T(8,128)(2,1)} %param.33), channel_id=1, source_target_pairs={{1,2},{2,1},{5,6},{6,5},{9,10},{10,9},{13,14},{14,13},{17,18},{18,... | collective-permute-start | bytes 6291464 | tf_op jit(solution)/shard_map/ppermute | solution.py:412
  136.2 26.1 %collective-permute-start.9 = (bf16[2048]{0:T(1024)(128)(2,1)S(1)}, bf16[2048]{0:T(1024)(128)(2,1)S(1)}, u32[]{:S(2)}, u32[]{:S(2)}) collective-permute-start(bf16[2048]{0:T(1024)(128)(2,1)S(1)} %copy-done.56), channel_id=1, source_target_pairs={{0,1},{1,0},{2,3},{3,2},{4,5},{5,4},{6,7},{7,6},{8,9},{9,8},{10,11... | collective-permute-start | bytes 12296 | tf_op jit(solution)/shard_map/ppermute | solution.py:412
  254.3 40.1 %collective-permute-start.12 = (bf16[1024,1024]{1,0:T(8,128)(2,1)}, bf16[1024,1024]{1,0:T(8,128)(2,1)}, u32[]{:S(2)}, u32[]{:S(2)}) collective-permute-start(bf16[1024,1024]{1,0:T(8,128)(2,1)} %add_convert_fusion), channel_id=1, source_target_pairs={{1,2},{2,1},{5,6},{6,5},{9,10},{10,9},{13,14},{14,13},{17,18},{18,... | collective-permute-start | bytes 6291464 | tf_op jit(solution)/shard_map/ppermute | solution.py:412
  270.4 27.1 %collective-permute-start.10 = (bf16[8,128,1024]{2,1,0:T(8,128)(2,1)}, bf16[8,128,1024]{2,1,0:T(8,128)(2,1)}, u32[]{:S(2)}, u32[]{:S(2)}) collective-permute-start(bf16[8,128,1024]{2,1,0:T(8,128)(2,1)} %get-tuple-element.226), channel_id=1, source_target_pairs={{0,2},{1,3},{2,0},{3,1},{4,6},{5,7},{6,4},{7,5},{8,10},{9,11},{10,... | collective-permute-start | bytes 6291464 | tf_op jit(solution)/shard_map/ppermute | solution.py:412
  272.1 25.4 %collective-permute-start.11 = (bf16[8,128,1024]{2,1,0:T(8,128)(2,1)}, bf16[8,128,1024]{2,1,0:T(8,128)(2,1)}, u32[]{:S(2)}, u32[]{:S(2)}) collective-permute-start(bf16[8,128,1024]{2,1,0:T(8,128)(2,1)} %get-tuple-element.227), channel_id=1, source_target_pairs={{0,2},{1,3},{2,0},{3,1},{4,6},{5,7},{6,4},{7,5},{8,10},{9,11},{10,... | collective-permute-start | bytes 6291464 | tf_op jit(solution)/shard_map/ppermute | solution.py:412
  334.6 12.8 %collective-permute-start.13 = (bf16[8,64,2048]{2,1,0:T(8,128)(2,1)}, bf16[8,64,2048]{2,1,0:T(8,128)(2,1)S(1)}, u32[]{:S(2)}, u32[]{:S(2)}) collective-permute-start(bf16[8,64,2048]{2,1,0:T(8,128)(2,1)} %get-tuple-element.241), channel_id=1, source_target_pairs={{0,2},{1,3},{2,0},{3,1},{4,6},{5,7},{6,4},{7,5},{8,10},{9,11},{10,... | collective-permute-start | bytes 6291464 | tf_op jit(solution)/shard_map/ppermute | solution.py:412
  335.1 12.4 %collective-permute-start.14 = (bf16[8,64,2048]{2,1,0:T(8,128)(2,1)}, bf16[8,64,2048]{2,1,0:T(8,128)(2,1)S(1)}, u32[]{:S(2)}, u32[]{:S(2)}) collective-permute-start(bf16[8,64,2048]{2,1,0:T(8,128)(2,1)} %get-tuple-element.242), channel_id=1, source_target_pairs={{0,2},{1,3},{2,0},{3,1},{4,6},{5,7},{6,4},{7,5},{8,10},{9,11},{10,... | collective-permute-start | bytes 6291464 | tf_op jit(solution)/shard_map/ppermute | solution.py:412
  335.2 48.2 %collective-permute-start.15 = (bf16[8,128,1024]{2,1,0:T(8,128)(2,1)}, bf16[8,128,1024]{2,1,0:T(8,128)(2,1)S(1)}, u32[]{:S(2)}, u32[]{:S(2)}) collective-permute-start(bf16[8,128,1024]{2,1,0:T(8,128)(2,1)} %add.342), channel_id=1, source_target_pairs={{0,1},{1,0},{2,3},{3,2},{4,5},{5,4},{6,7},{7,6},{8,9},{9,8},{10,11... | collective-permute-start | bytes 6291464 | tf_op jit(solution)/shard_map/ppermute | solution.py:412
  342.9 173.3 %copy-start.13 = (bf16[512,1024]{1,0:T(8,128)(2,1)}, bf16[512,1024]{1,0:T(8,128)(2,1)S(1)}, u32[]{:S(2)}) copy-start(bf16[512,1024]{1,0:T(8,128)(2,1)S(1)} %convolution_convert_fusion.7) | copy-start | bytes 3145732
  345.2 38.2 %copy-start.9 = (bf16[8,128,1024]{2,1,0:T(8,128)(2,1)S(1)}, bf16[8,128,1024]{2,1,0:T(8,128)(2,1)}, u32[]{:S(2)}) copy-start(bf16[8,128,1024]{2,1,0:T(8,128)(2,1)} %get-tuple-element.248) | copy-start | bytes 6291460
  387.6 28.1 %collective-permute-start.16 = (bf16[4,128,1024]{2,1,0:T(8,128)(2,1)S(1)}, bf16[4,128,1024]{2,1,0:T(8,128)(2,1)}, u32[]{:S(2)}, u32[]{:S(2)}) collective-permute-start(bf16[4,128,1024]{2,1,0:T(8,128)(2,1)S(1)} %dynamic-slice_bitcast_fusion.11), channel_id=1, source_target_pairs={{0,4},{1,5},{2,6},{3,7},{4,0},{5,1},{6,2},{7,3},{8,12},{9,13},{10,... | collective-permute-start | bytes 3145736 | tf_op jit(solution)/shard_map/ppermute | solution.py:412
  388.2 58.5 %collective-permute-start.18 = (bf16[8,64,2048]{2,1,0:T(8,128)(2,1)}, bf16[8,64,2048]{2,1,0:T(8,128)(2,1)}, u32[]{:S(2)}, u32[]{:S(2)}) collective-permute-start(bf16[8,64,2048]{2,1,0:T(8,128)(2,1)} %add.348), channel_id=1, source_target_pairs={{0,1},{1,0},{2,3},{3,2},{4,5},{5,4},{6,7},{7,6},{8,9},{9,8},{10,11... | collective-permute-start | bytes 6291464 | tf_op jit(solution)/shard_map/ppermute | solution.py:412
  417.2 29.4 %collective-permute-start.17 = (bf16[2,128,1024]{2,1,0:T(8,128)(2,1)S(1)}, bf16[2,128,1024]{2,1,0:T(8,128)(2,1)S(1)}, u32[]{:S(2)}, u32[]{:S(2)}) collective-permute-start(bf16[2,128,1024]{2,1,0:T(8,128)(2,1)S(1)} %dynamic-slice_bitcast_fusion.16), channel_id=1, source_target_pairs={{0,8},{1,9},{2,10},{3,11},{4,12},{5,13},{6,14},{7,15},{8,0},{9,1},... | collective-permute-start | bytes 1572872 | tf_op jit(solution)/shard_map/ppermute | solution.py:412
  418.7 27.9 %collective-permute-start.19 = (bf16[1024,256]{1,0:T(8,128)(2,1)}, bf16[1024,256]{1,0:T(8,128)(2,1)S(1)}, u32[]{:S(2)}, u32[]{:S(2)}) collective-permute-start(bf16[1024,256]{1,0:T(8,128)(2,1)} %get-tuple-element.286), channel_id=1, source_target_pairs={{0,2},{1,3},{2,0},{3,1},{4,6},{5,7},{6,4},{7,5},{8,10},{9,11},{10,... | collective-permute-start | bytes 1572872 | tf_op jit(solution)/shard_map/ppermute | solution.py:412
  418.7 27.9 %collective-permute-start.20 = (bf16[1024,256]{1,0:T(8,128)(2,1)S(1)}, bf16[1024,256]{1,0:T(8,128)(2,1)S(1)}, u32[]{:S(2)}, u32[]{:S(2)}) collective-permute-start(bf16[1024,256]{1,0:T(8,128)(2,1)S(1)} %copy-done.67), channel_id=1, source_target_pairs={{0,2},{1,3},{2,0},{3,1},{4,6},{5,7},{6,4},{7,5},{8,10},{9,11},{10,... | collective-permute-start | bytes 1572872 | tf_op jit(solution)/shard_map/ppermute | solution.py:412
  450.6 44.1 %collective-permute-start.24 = (bf16[4,64,2048]{2,1,0:T(8,128)(2,1)S(1)}, bf16[4,64,2048]{2,1,0:T(8,128)(2,1)S(1)}, u32[]{:S(2)}, u32[]{:S(2)}) collective-permute-start(bf16[4,64,2048]{2,1,0:T(8,128)(2,1)S(1)} %dynamic-slice_bitcast_fusion.10), channel_id=1, source_target_pairs={{0,4},{1,5},{2,6},{3,7},{4,0},{5,1},{6,2},{7,3},{8,12},{9,13},{10,... | collective-permute-start | bytes 3145736 | tf_op jit(solution)/shard_map/ppermute | solution.py:412
  452.1 42.6 %collective-permute-start.21 = (bf16[1024,256]{1,0:T(8,128)(2,1)}, bf16[1024,256]{1,0:T(8,128)(2,1)}, u32[]{:S(2)}, u32[]{:S(2)}) collective-permute-start(bf16[1024,256]{1,0:T(8,128)(2,1)} %get-tuple-element.302), channel_id=1, source_target_pairs={{0,2},{1,3},{2,0},{3,1},{4,6},{5,7},{6,4},{7,5},{8,10},{9,11},{10,... | collective-permute-start | bytes 1572872 | tf_op jit(solution)/shard_map/ppermute | solution.py:412
  452.1 42.6 %collective-permute-start.22 = (bf16[1024,256]{1,0:T(8,128)(2,1)}, bf16[1024,256]{1,0:T(8,128)(2,1)S(1)}, u32[]{:S(2)}, u32[]{:S(2)}) collective-permute-start(bf16[1024,256]{1,0:T(8,128)(2,1)} %get-tuple-element.303), channel_id=1, source_target_pairs={{0,2},{1,3},{2,0},{3,1},{4,6},{5,7},{6,4},{7,5},{8,10},{9,11},{10,... | collective-permute-start | bytes 1572872 | tf_op jit(solution)/shard_map/ppermute | solution.py:412
  479.8 14.9 %collective-permute-start.23 = (bf16[1,128,1024]{2,1,0:T(8,128)(2,1)S(1)}, bf16[1,128,1024]{2,1,0:T(8,128)(2,1)}, u32[]{:S(2)}, u32[]{:S(2)}) collective-permute-start(bf16[1,128,1024]{2,1,0:T(8,128)(2,1)S(1)} %constant_dynamic-slice_fusion.5), channel_id=1, source_target_pairs={{0,16},{1,17},{2,18},{3,19},{4,20},{5,21},{6,22},{7,23},{8,24},{9,... | collective-permute-start | bytes 786440 | tf_op jit(solution)/shard_map/ppermute | solution.py:412
  515.3 208.9 %all-gather.25.cloned.1.call-start = ((), (), s32[]{:S(2)}) async-start(), calls=%async_computation.6 | async-start | bytes 1114112 | tf_op jit(solution)/shard_map/all_gather | solution.py:455
  516.2 30.7 %collective-permute-start.29 = (bf16[8,32,1024]{2,1,0:T(8,128)(2,1)}, bf16[8,32,1024]{2,1,0:T(8,128)(2,1)S(1)}, u32[]{:S(2)}, u32[]{:S(2)}) collective-permute-start(bf16[8,32,1024]{2,1,0:T(8,128)(2,1)} %dynamic-slice_bitcast_fusion.14), channel_id=1, source_target_pairs={{0,2},{1,3},{2,0},{3,1},{4,6},{5,7},{6,4},{7,5},{8,10},{9,11},{10,... | collective-permute-start | bytes 1572872 | tf_op jit(solution)/shard_map/ppermute | solution.py:412
  518.6 28.5 %collective-permute-start.28 = (bf16[8,64,1536]{2,1,0:T(8,128)(2,1)S(1)}, bf16[8,64,1536]{2,1,0:T(8,128)(2,1)S(1)}, u32[]{:S(2)}, u32[]{:S(2)}) collective-permute-start(bf16[8,64,1536]{2,1,0:T(8,128)(2,1)S(1)} %dynamic-slice_bitcast_fusion.9), channel_id=1, source_target_pairs={{0,2},{1,3},{2,0},{3,1},{4,6},{5,7},{6,4},{7,5},{8,10},{9,11},{10,... | collective-permute-start | bytes 4718600 | tf_op jit(solution)/shard_map/ppermute | solution.py:412
  519.1 27.9 %collective-permute-start.25 = (bf16[1024,256]{1,0:T(8,128)(2,1)}, bf16[1024,256]{1,0:T(8,128)(2,1)S(1)}, u32[]{:S(2)}, u32[]{:S(2)}) collective-permute-start(bf16[1024,256]{1,0:T(8,128)(2,1)} %get-tuple-element.335), channel_id=1, source_target_pairs={{0,2},{1,3},{2,0},{3,1},{4,6},{5,7},{6,4},{7,5},{8,10},{9,11},{10,... | collective-permute-start | bytes 1572872 | tf_op jit(solution)/shard_map/ppermute | solution.py:412
  519.2 27.8 %collective-permute-start.26 = (bf16[1024,256]{1,0:T(8,128)(2,1)}, bf16[1024,256]{1,0:T(8,128)(2,1)S(1)}, u32[]{:S(2)}, u32[]{:S(2)}) collective-permute-start(bf16[1024,256]{1,0:T(8,128)(2,1)} %get-tuple-element.336), channel_id=1, source_target_pairs={{0,2},{1,3},{2,0},{3,1},{4,6},{5,7},{6,4},{7,5},{8,10},{9,11},{10,... | collective-permute-start | bytes 1572872 | tf_op jit(solution)/shard_map/ppermute | solution.py:412
  519.7 27.4 %collective-permute-start.27 = (bf16[2,64,2048]{2,1,0:T(8,128)(2,1)S(1)}, bf16[2,64,2048]{2,1,0:T(8,128)(2,1)S(1)}, u32[]{:S(2)}, u32[]{:S(2)}) collective-permute-start(bf16[2,64,2048]{2,1,0:T(8,128)(2,1)S(1)} %copy-done.37), channel_id=1, source_target_pairs={{0,8},{1,9},{2,10},{3,11},{4,12},{5,13},{6,14},{7,15},{8,0},{9,1},... | collective-permute-start | bytes 1572872 | tf_op jit(solution)/shard_map/ppermute | solution.py:412
  546.9 44.5 %collective-permute-start.34 = (bf16[8,32,1024]{2,1,0:T(8,128)(2,1)}, bf16[8,32,1024]{2,1,0:T(8,128)(2,1)}, u32[]{:S(2)}, u32[]{:S(2)}) collective-permute-start(bf16[8,32,1024]{2,1,0:T(8,128)(2,1)} %dynamic-slice_bitcast_fusion.13), channel_id=1, source_target_pairs={{0,2},{1,3},{2,0},{3,1},{4,6},{5,7},{6,4},{7,5},{8,10},{9,11},{10,... | collective-permute-start | bytes 1572872 | tf_op jit(solution)/shard_map/ppermute | solution.py:412
  550.7 15.7 %collective-permute-start.30 = (bf16[1024,256]{1,0:T(8,128)(2,1)}, bf16[1024,256]{1,0:T(8,128)(2,1)S(1)}, u32[]{:S(2)}, u32[]{:S(2)}) collective-permute-start(bf16[1024,256]{1,0:T(8,128)(2,1)} %get-tuple-element.352), channel_id=1, source_target_pairs={{0,2},{1,3},{2,0},{3,1},{4,6},{5,7},{6,4},{7,5},{8,10},{9,11},{10,... | collective-permute-start | bytes 1572872 | tf_op jit(solution)/shard_map/ppermute | solution.py:412
  550.7 16.2 %collective-permute-start.31 = (bf16[1024,256]{1,0:T(8,128)(2,1)}, bf16[1024,256]{1,0:T(8,128)(2,1)S(1)}, u32[]{:S(2)}, u32[]{:S(2)}) collective-permute-start(bf16[1024,256]{1,0:T(8,128)(2,1)} %get-tuple-element.353), channel_id=1, source_target_pairs={{0,2},{1,3},{2,0},{3,1},{4,6},{5,7},{6,4},{7,5},{8,10},{9,11},{10,... | collective-permute-start | bytes 1572872 | tf_op jit(solution)/shard_map/ppermute | solution.py:412
  558.2 20.9 %collective-permute-start.32 = (bf16[1,64,2048]{2,1,0:T(8,128)(2,1)S(1)}, bf16[1,64,2048]{2,1,0:T(8,128)(2,1)}, u32[]{:S(2)}, u32[]{:S(2)}) collective-permute-start(bf16[1,64,2048]{2,1,0:T(8,128)(2,1)S(1)} %constant_dynamic-slice_fusion.4), channel_id=1, source_target_pairs={{0,16},{1,17},{2,18},{3,19},{4,20},{5,21},{6,22},{7,23},{8,24},{9,... | collective-permute-start | bytes 786440 | tf_op jit(solution)/shard_map/ppermute | solution.py:412
  560.6 47.6 %collective-permute-start.35 = (bf16[8,64,1536]{2,1,0:T(8,128)(2,1)}, bf16[8,64,1536]{2,1,0:T(8,128)(2,1)}, u32[]{:S(2)}, u32[]{:S(2)}) collective-permute-start(bf16[8,64,1536]{2,1,0:T(8,128)(2,1)} %bitcast_add_fusion.1), channel_id=1, source_target_pairs={{0,1},{1,0},{2,3},{3,2},{4,5},{5,4},{6,7},{7,6},{8,9},{9,8},{10,11... | collective-permute-start | bytes 4718600 | tf_op jit(solution)/shard_map/ppermute | solution.py:412
  566.5 41.7 %collective-permute-start.36 = (bf16[8,32,1024]{2,1,0:T(8,128)(2,1)}, bf16[8,32,1024]{2,1,0:T(8,128)(2,1)}, u32[]{:S(2)}, u32[]{:S(2)}) collective-permute-start(bf16[8,32,1024]{2,1,0:T(8,128)(2,1)} %bitcast_add_fusion.6), channel_id=1, source_target_pairs={{0,1},{1,0},{2,3},{3,2},{4,5},{5,4},{6,7},{7,6},{8,9},{9,8},{10,11... | collective-permute-start | bytes 1572872 | tf_op jit(solution)/shard_map/ppermute | solution.py:412
  585.7 22.5 %collective-permute-start.33 = (bf16[8,64,1536]{2,1,0:T(8,128)(2,1)S(1)}, bf16[8,64,1536]{2,1,0:T(8,128)(2,1)S(1)}, u32[]{:S(2)}, u32[]{:S(2)}) collective-permute-start(bf16[8,64,1536]{2,1,0:T(8,128)(2,1)S(1)} %dynamic-slice_bitcast_fusion.8), channel_id=1, source_target_pairs={{0,2},{1,3},{2,0},{3,1},{4,6},{5,7},{6,4},{7,5},{8,10},{9,11},{10,... | collective-permute-start | bytes 4718600 | tf_op jit(solution)/shard_map/ppermute | solution.py:412
  610.1 7.1 collective-permute-start.46
  617.3 5.0 collective-permute-start.47
  622.4 5.6 collective-permute-start.48
  628.6 98.4 %all-gather.27.cloned.1.call-start = ((), (), s32[]{:S(2)}) async-start(), calls=%async_computation.7 | async-start | bytes 4456448 | tf_op jit(solution)/shard_map/all_gather | solution.py:455
  630.5 136.0 %all-gather.23.cloned.1.call-start = ((), (), s32[]{:S(2)}) async-start(), calls=%async_computation.5 | async-start | bytes 3342336 | tf_op jit(solution)/shard_map/all_gather | solution.py:455
  633.2 38.6 %copy-start.51 = (f32[1024]{0:T(1024)S(1)}, f32[1024]{0:T(1024)}, u32[]{:S(2)}) copy-start(f32[1024]{0:T(1024)} %get-tuple-element.426) | copy-start | bytes 12292
  633.2 38.6 %copy-start.58 = (f32[1024]{0:T(1024)S(1)}, f32[1024]{0:T(1024)}, u32[]{:S(2)}) copy-start(f32[1024]{0:T(1024)} %get-tuple-element.418) | copy-start | bytes 12292
  633.2 38.6 %copy-start.57 = (f32[1024]{0:T(1024)S(1)}, f32[1024]{0:T(1024)}, u32[]{:S(2)}) copy-start(f32[1024]{0:T(1024)} %get-tuple-element.424) | copy-start | bytes 12292
  633.2 38.6 %copy-start.50 = (f32[1024]{0:T(1024)S(1)}, f32[1024]{0:T(1024)}, u32[]{:S(2)}) copy-start(f32[1024]{0:T(1024)} %get-tuple-element.440) | copy-start | bytes 12292
  633.2 15.9 %collective-permute-start.43 = (bf16[4,64,1536]{2,1,0:T(8,128)(2,1)S(1)}, bf16[4,64,1536]{2,1,0:T(8,128)(2,1)S(1)}, u32[]{:S(2)}, u32[]{:S(2)}) collective-permute-start(bf16[4,64,1536]{2,1,0:T(8,128)(2,1)S(1)} %dynamic-slice_bitcast_fusion.12), channel_id=1, source_target_pairs={{0,4},{1,5},{2,6},{3,7},{4,0},{5,1},{6,2},{7,3},{8,12},{9,13},{10,... | collective-permute-start | bytes 2359304 | tf_op jit(solution)/shard_map/ppermute | solution.py:412
  649.3 13.5 %collective-permute-start.44 = (bf16[2,64,1536]{2,1,0:T(8,128)(2,1)S(1)}, bf16[2,64,1536]{2,1,0:T(8,128)(2,1)S(1)}, u32[]{:S(2)}, u32[]{:S(2)}) collective-permute-start(bf16[2,64,1536]{2,1,0:T(8,128)(2,1)S(1)} %dynamic-slice_bitcast_fusion.17), channel_id=1, source_target_pairs={{0,8},{1,9},{2,10},{3,11},{4,12},{5,13},{6,14},{7,15},{8,0},{9,1},... | collective-permute-start | bytes 1179656 | tf_op jit(solution)/shard_map/ppermute | solution.py:412
  662.9 8.2 %collective-permute-start.45 = (bf16[1,64,1536]{2,1,0:T(8,128)(2,1)S(1)}, bf16[1,64,1536]{2,1,0:T(8,128)(2,1)S(1)}, u32[]{:S(2)}, u32[]{:S(2)}) collective-permute-start(bf16[1,64,1536]{2,1,0:T(8,128)(2,1)S(1)} %constant_dynamic-slice_fusion.1), channel_id=1, source_target_pairs={{0,16},{1,17},{2,18},{3,19},{4,20},{5,21},{6,22},{7,23},{8,24},{9,... | collective-permute-start | bytes 589832 | tf_op jit(solution)/shard_map/ppermute | solution.py:412
  674.3 48.4 %collective-permute-start.37 = (bf16[1024,1024]{1,0:T(8,128)(2,1)S(1)}, bf16[1024,1024]{1,0:T(8,128)(2,1)}, u32[]{:S(2)}, u32[]{:S(2)}) collective-permute-start(bf16[1024,1024]{1,0:T(8,128)(2,1)S(1)} %fusion.12), channel_id=1, source_target_pairs={{1,2},{2,1},{5,6},{6,5},{9,10},{10,9},{13,14},{14,13},{17,18},{18,... | collective-permute-start | bytes 6291464 | tf_op jit(solution)/shard_map/ppermute | solution.py:412
  676.4 26.4 %collective-permute-start.38 = (f32[52,128]{1,0:T(8,128)S(1)}, f32[52,128]{1,0:T(8,128)S(1)}, u32[]{:S(2)}, u32[]{:S(2)}) collective-permute-start(f32[52,128]{1,0:T(8,128)S(1)} %maximum_bitcast_fusion.1), channel_id=1, source_target_pairs={{0,1},{1,0},{2,3},{3,2},{4,5},{5,4},{6,7},{7,6},{8,9},{9,8},{10,11... | collective-permute-start | bytes 79880 | tf_op jit(solution)/shard_map/ppermute | solution.py:412
  702.9 1.3 collective-permute-start.39
  704.1 4.5 collective-permute-start.40
  708.6 5.6 collective-permute-start.41
  714.2 6.7 collective-permute-start.42
  (65 other events, 590.4 us)
Sparse Core Ops, SparseCore 0:
  41.5 49.5 all-gather.12
  102.9 36.7 all-gather.14
  141.8 49.4 all-gather.16
  193.3 49.0 all-gather.18
  515.4 63.1 all-gather.20
  628.8 37.2 all-gather.24
  668.8 51.4 all-gather.26
  722.5 43.9 all-gather.22

commit v3 on v2

--- a/solution.py
+++ b/solution.py
@@ -385,13 +385,44 @@
     return back, jnp.sum(upstream * normal, 0), jnp.sum(upstream, 0)
 
 
-def pick(x, index):
-    return lax.dynamic_index_in_dim(x, index, 1, keepdims=False)
-
-
 def tie(*trees):
     leaves, form = jax.tree.flatten(trees)
     return jax.tree.unflatten(form, lax.optimization_barrier(tuple(leaves)))
+
+
+def split_kernel(t_ref, own_m, own_f, oth_m, oth_f, got_om, got_of, got_tm, got_tf, ka, kb, sa, sb, *, last):
+    total = lambda a, b: (a[...].astype(F32) + b[...].astype(F32)).astype(BF)
+    by_y = t_ref[last] == 0
+    own_far, oth_me = total(own_f, got_of), total(oth_m, got_tm)
+    ka[...] = total(own_m, got_om)
+    kb[...] = jnp.where(by_y, own_far, oth_me)
+    sa[...] = jnp.where(by_y, oth_me, own_far)
+    sb[...] = total(oth_f, got_tf)
+
+
+def first_split(table, own, oth, got_own, got_oth):
+    chips, piece, cols = got_own.shape
+    count = chips // 2
+    own, oth = (g.reshape(chips, 2, piece, cols) for g in (own, oth))
+    whole = lambda far: pl.BlockSpec(
+        (None, None, piece, cols), lambda i, t: (t[far * count + i], t[2 * count], 0, 0)
+    )
+    part = lambda far: pl.BlockSpec((None, piece, cols), lambda i, t: (t[far * count + i], 0, 0))
+    out = pl.BlockSpec((None, piece, cols), lambda i, t: (i, 0, 0))
+    return pl.pallas_call(
+        functools.partial(split_kernel, last=2 * count),
+        grid_spec=pltpu.PrefetchScalarGridSpec(
+            num_scalar_prefetch=1,
+            grid=(count,),
+            in_specs=[whole(0), whole(1)] * 2 + [part(0), part(1)] * 2,
+            out_specs=[out] * 4,
+        ),
+        out_shape=[jax.ShapeDtypeStruct((count, piece, cols), BF)] * 4,
+        compiler_params=pltpu.CompilerParams(vmem_limit_bytes=VMEM_BYTES),
+        cost_estimate=pl.CostEstimate(
+            flops=4 * count * piece * cols, bytes_accessed=24 * count * piece * cols, transcendentals=0
+        ),
+    )(table, own, own, oth, oth, got_own, got_own, got_oth, got_oth)
 
 
 class Paired:
@@ -421,9 +452,6 @@
     def over_core(self, x):
         return self.move(x, lambda dp, y: (dp ^ 1, y))
 
-    def over_chip(self, x, bit):
-        return self.move(x, lambda dp, y: (dp ^ (2 << bit), y))
-
     def piece(self, own):
         rows = own.shape[0] // self.n_dp
         return lax.dynamic_slice_in_dim(own, self.me_dp * rows, rows, 0)
@@ -431,25 +459,32 @@
     def spread(self, got):
         return lax.all_gather(got, "dp", axis=0, tiled=True)
 
-    def biases(self, own):
-        return [own, self.over_y(own)]
-
-    def keys(self, kv):
-        return [kv, self.over_core(kv)]
-
-    def keys_back(self, grads):
-        return grads[0], self.over_core(grads[1])
-
-    def core_split(self, half):
+    def core_send(self, half):
         rows, cols = half.shape
         blocks = half.reshape(self.n_dp // 2, 2, rows // self.n_dp, cols)
-        return pick(blocks, self.core), pick(blocks, 1 - self.core)
-
-    def chip_split(self, blocks, level):
-        bit = (self.me_dp >> (level + 1)) & 1
-        left = blocks.shape[0] // 2
-        blocks = blocks.reshape(left, 2, *blocks.shape[1:])
-        return pick(blocks, bit), pick(blocks, 1 - bit)
+        return lax.dynamic_index_in_dim(blocks, 1 - self.core, 1, keepdims=False)
+
+    def over_first(self, x):
+        return self.move(x, lambda dp, y: (dp ^ 2, y) if dp % 2 else (dp, 1 - y))
+
+    def over_second(self, x):
+        return self.move(x, lambda dp, y: (dp, 1 - y) if dp % 2 else (dp ^ 2, y))
+
+    def over_z(self, x, level):
+        return self.move(x, lambda dp, y: (dp ^ (4 << level), y))
+
+    def blocks_of(self, x_bit):
+        count = self.n_dp // 4
+        levels = count.bit_length() - 1
+        z = self.me_dp // 4
+        places = np.arange(count)
+        far = sum(((places >> (levels - 1 - k)) & 1) << k for k in range(levels))
+        return (jnp.asarray(far, jnp.int32) ^ z) * 2 + x_bit
+
+    def table(self):
+        x = (self.me_dp // 2) % 2
+        me, far = self.blocks_of(x), self.blocks_of(1 - x)
+        return jnp.concatenate([me, far, jnp.stack([self.core])]).astype(jnp.int32)
 
     def gather(self, block):
         return lax.all_gather(block[0], "dp", axis=0, tiled=True)
@@ -463,7 +498,7 @@
         total = mine + self.over_y(theirs)
         total = total + self.over_core(total)
         for level in range((self.n_dp // 2).bit_length() - 1):
-            total = total + self.over_chip(total, level)
+            total = total + self.move(total, lambda dp, y: (dp ^ (2 << level), y))
         total = total.reshape(-1)
         return total[: k * width // 2].reshape(k, width // 2), total[k * width // 2 :]
 
@@ -575,6 +610,67 @@
     )
 
 
+class Reduction:
+    def __init__(self, move, table, own, oth):
+        self.move, self.table = move, table
+        self.grads = own, oth
+        self.sends = [move.core_send(g) for g in (own, oth)]
+        self.at = 0
+
+    def start(self):
+        at = self.at
+        if at == 0:
+            go = self.move.over_core
+        elif at == 1:
+            go = self.move.over_first
+        elif at == 2:
+            go = self.move.over_second
+        else:
+            go = functools.partial(self.move.over_z, level=at - 3)
+        return [go(x) for x in self.sends]
+
+    def take(self, got):
+        at, self.at = self.at, self.at + 1
+        if at == 0:
+            ka, kb, sa, sb = first_split(self.table, *self.grads, *got)
+            self.keep, self.sends = (ka, kb), [sa, sb]
+        elif at == 1:
+            self.sends = [self.keep[1] + got[1]]
+            self.keep = self.keep[0] + got[0]
+        else:
+            total = self.keep + got[0]
+            half = total.shape[0] // 2
+            if half:
+                self.keep, self.sends = total[:half], [total[half:]]
+            else:
+                self.done = total
+
+    @property
+    def last(self):
+        return 2 + (self.move.n_dp // 4).bit_length() - 1
+
+
+def beside(compute, inputs, *steps):
+    sends = [s.sends if isinstance(s, Reduction) else s[1] for s in steps]
+    inputs, sends = tie(inputs, sends)
+    got = []
+    for s, x in zip(steps, sends):
+        if isinstance(s, Reduction):
+            s.sends = x
+            got.append(s.start())
+        else:
+            got.append(s[0](x))
+    out = compute(*inputs)
+    out, got = tie(out, got)
+    moved = []
+    for s, x in zip(steps, got):
+        if isinstance(s, Reduction):
+            s.take(x)
+        else:
+            moved.append(x)
+    return out, moved
+
+
 def paired_device(n_dp, *args):
     (block_in, ln1_scale, ln1_shift, qkv_weight, qkv_bias, out_weight, out_bias) = args[:7]
     (ln2_scale, ln2_shift, up_weight, up_bias, down_weight, down_bias, out_grad) = args[7:]
@@ -583,35 +679,40 @@
     width, _, part = qkv_weight.shape
     tokens = block_in.shape[0]
     pairs = part // LANES
-    levels = (n_dp // 2).bit_length() - 1
     ln1_gain, ln2_gain = f32(ln1_scale), f32(ln2_scale)
-
+    table = move.table()
+
+    small = jnp.concatenate([qkv_bias.reshape(3 * part), up_bias])
+    qkv_piece = move.piece(qkv_weight).reshape(width // n_dp, 3 * part)
+    qkv_piece, small, block_in = tie(qkv_piece, small, block_in)
+    qkv_got = move.over_y(qkv_piece)
+    small_got = move.over_y(small)
     block_in = move.swap_rows(block_in)
+    qkv_bs = [v[: 3 * part] for v in (small, small_got)]
+    up_bs = [v[3 * part :] for v in (small, small_got)]
+    tables = rotary_tables(move.first, tokens)
     qkv_own = qkv_weight.reshape(width, 3 * part)
-    qkv_got = move.over_y(move.piece(qkv_own))
-    qkv_bs = move.biases(qkv_bias.reshape(3 * part))
-    tables = rotary_tables(move.first, tokens)
+    qkv_oth = move.spread(qkv_got)
     x_rows = f32(block_in)
     normed1, normal1, inv_one = norm_parts(x_rows, ln1_gain, f32(ln1_shift))
-    qkv_got, normed1 = tie(qkv_got, normed1)
-    qkv_ws = [qkv_own, move.spread(qkv_got)]
     q_own, kv_own = qkv_rows(normed1, qkv_own, f32(qkv_bs[0])[None, :], tables)
     rest = [move.piece(w) for w in (out_weight, up_weight, down_weight)]
-    rest, up_bias, kv_own = tie(rest, up_bias, kv_own)
-    kvs_own = move.keys(kv_own)
-    rest = [move.over_y(w) for w in rest]
-    up_bs = move.biases(up_bias)
-    q_oth, kv_oth = qkv_rows(normed1, qkv_ws[1], f32(qkv_bs[1])[None, :], tables)
-    kvs_own, rest, kv_oth, q_own = tie(kvs_own, rest, kv_oth, q_own)
+    (q_oth, kv_oth), (rest, kv_got) = beside(
+        lambda n, w: qkv_rows(n, w, f32(qkv_bs[1])[None, :], tables),
+        (normed1, qkv_oth),
+        (lambda ws: [move.over_y(w) for w in ws], rest),
+        (move.over_core, kv_own),
+    )
+    kvs_own = [kv_own, kv_got]
+    spread = [move.spread(got) for got in rest]
+    (out_own, log_own), (kv_got, grad_low) = beside(
+        attend, (q_own, kvs_own), (move.over_core, kv_oth), (move.swap_rows, out_grad)
+    )
+    kvs_oth = [kv_oth, kv_got]
     out_ws, up_ws, down_ws = (
-        [w, move.spread(got)] for w, got in zip((out_weight, up_weight, down_weight), rest)
-    )
-    kvs_oth = move.keys(kv_oth)
-    out_own, log_own = attend(q_own, kvs_own)
-    out_own, kvs_oth, q_oth, out_grad = tie(out_own, kvs_oth, q_oth, out_grad)
-    grad_low = move.swap_rows(out_grad)
+        [w, got] for w, got in zip((out_weight, up_weight, down_weight), spread)
+    )
     out_oth, log_oth = attend(q_oth, kvs_oth)
-    out_oth, grad_low = tie(out_oth, grad_low)
     grad_rows = f32(grad_low)
     outs = [out_own, out_oth]
 
@@ -625,115 +726,131 @@
         slopes.append(slope)
     branch_two = sum(dot_nn(a, w) for a, w in zip(acts, down_ws)) + f32(down_bias)
     block_out = (resid + branch_two).astype(BF)
-    block_out, acts = tie(block_out, acts)
-    block_out = move.swap_rows(block_out)
     down_bias_grad = jnp.sum(grad_rows, 0)
-    down_grads = [dot_tn(a, grad_low).astype(BF) for a in acts]
-    down_keep, down_send = zip(*[move.core_split(g) for g in down_grads])
-
-    down_keep, down_send, acts, grad_low = tie(down_keep, down_send, acts, grad_low)
-    down_got = [move.over_core(x) for x in down_send]
-    hidden_gs, up_b_grads = [], []
-    for down, slope in zip(down_ws, slopes):
-        hg, total = hidden_grads(grad_low, down, slope)
-        hidden_gs.append(hg)
-        up_b_grads.append(total[0])
-    down_got, hidden_gs, block_out = tie(down_got, hidden_gs, block_out)
-    down_send = down_keep[1] + down_got[1]
-    down_keep = down_keep[0] + down_got[0]
-
-    down_send, hidden_gs = tie(down_send, hidden_gs)
-    down_got = move.over_y(down_send)
-    up_grads = [dot_tn(normed2, hg).astype(BF) for hg in hidden_gs]
-    up_keep, up_send = zip(*[move.core_split(g) for g in up_grads])
-    up_keep, up_send, hidden_gs = tie(up_keep, up_send, hidden_gs)
-    up_got = [move.over_core(x) for x in up_send]
-    normed2_grad = sum(dot_nt(hg, w) for hg, w in zip(hidden_gs, up_ws))
-    resid_part, ln2_scale_grad, ln2_shift_grad = norm_back(normed2_grad, normal2, inv_two, ln2_gain)
-    resid_grad = grad_rows + resid_part
-    branch_grad = resid_grad.astype(BF)
-    out_bias_grad = jnp.sum(branch_grad, 0, dtype=F32)
-    out_w_grads = [dot_tn(o, branch_grad).astype(BF) for o in outs]
-    out_gs = [dot_nt(branch_grad, w).astype(BF) for w in out_ws]
-    up_got, down_got, out_gs, out_w_grads = tie(up_got, down_got, out_gs, out_w_grads)
-    up_send = up_keep[1] + up_got[1]
-    up_keep = up_keep[0] + up_got[0]
-    down = down_keep + down_got
-
-    def step(total, level):
-        keep, send = move.chip_split(total, level)
-        return keep, send
-
-    def back(which, skip):
+    low_product = lambda a, b: dot_tn(a, b).astype(BF)
+    down_grads, (block_out,) = beside(
+        lambda xs, g: [low_product(a, g) for a in xs],
+        (acts, grad_low),
+        (move.swap_rows, block_out),
+    )
+    down = Reduction(move, table, *down_grads)
+    (hg_own, up_b_own), _ = beside(hidden_grads, (grad_low, down_ws[0], slopes[0]), down)
+
+    def others(g, hg_own):
+        hg_oth, up_b_oth = hidden_grads(g, down_ws[1], slopes[1])
+        return hg_oth, up_b_oth, [low_product(normed2, h) for h in (hg_own, hg_oth)]
+
+    (hg_oth, up_b_oth, up_grads), _ = beside(others, (grad_low, hg_own), down)
+    hidden_gs = [hg_own, hg_oth]
+    up = Reduction(move, table, *up_grads)
+
+    def middle(hidden_gs, grad_rows, normal2):
+        normed2_grad = sum(dot_nt(hg, w) for hg, w in zip(hidden_gs, up_ws))
+        resid_part, scale_grad, shift_grad = norm_back(normed2_grad, normal2, inv_two, ln2_gain)
+        resid_grad = grad_rows + resid_part
+        branch_grad = resid_grad.astype(BF)
+        bias_grad = jnp.sum(branch_grad, 0, dtype=F32)
+        return resid_grad, branch_grad, scale_grad, shift_grad, bias_grad
+
+    (resid_grad, branch_grad, ln2_scale_grad, ln2_shift_grad, out_bias_grad), _ = beside(
+        middle, (hidden_gs, grad_rows, normal2), up, down
+    )
+    (out_w_grads, out_gs), _ = beside(
+        lambda xs, g: ([low_product(o, g) for o in xs], [dot_nt(g, w).astype(BF) for w in out_ws]),
+        (outs, branch_grad),
+        down,
+    )
+    proj = Reduction(move, table, *out_w_grads)
+
+    def back(which, skip, count):
         q, kvs, log = ((q_own, kvs_own, log_own), (q_oth, kvs_oth, log_oth))[which]
-        return q, out_gs[which], outs[which], log, kvs
-
-    half = pairs // 2
-    down_keep, down_send = step(down, 0)
-    ins, up_send, down_send = tie(back(1, 0), up_send, down_send)
-    up_got = move.over_y(up_send)
-    down_got = move.over_chip(down_send, 0)
-    first = attend_back(*ins, tables, 0, half)
-    first, down_got = tie(first, down_got)
-    down_keep, down_send = step(down_keep + down_got, 1)
-    ins, down_send, first = tie(back(1, half), down_send, first)
-    down_got = move.over_chip(down_send, 1)
-    first_got = [move.over_core(x[1]) for x in first[1:]]
-    second = attend_back(*ins, tables, half, half)
-    second, down_got, up_got, first_got = tie(second, down_got, up_got, first_got)
-    down_keep, down_send = step(down_keep + down_got, 2)
-    up_keep, up_send = step(up_keep + up_got, 0)
-    second, down_send, up_send = tie(second, down_send, up_send)
-    second_got = [move.over_core(x[1]) for x in second[1:]]
-    down_got = move.over_chip(down_send, 2)
-    up_got = move.over_chip(up_send, 0)
+        inputs = q, out_gs[which], outs[which], log, kvs
+        return lambda *xs: attend_back(*xs, tables, skip, count), inputs
+
+    def keys_of(x):
+        return lambda xs: [move.over_core(g) for g in xs], [x[1][1], x[2][1]]
 
     def finish(parts, gots):
         dk = [key_sum(p[1][0], g[0], tables) for p, g in zip(parts, gots)]
         dv = [p[2][0] + g[1] for p, g in zip(parts, gots)]
-        return jnp.concatenate([p[0] for p in parts] + dk + dv, axis=1)
-
-    third = attend_back(*back(0, 0), tables, 0, half)
-    third, second_got, down_got, up_got = tie(third, second_got, down_got, up_got)
-    down_block = down_keep + down_got
-    up_keep, up_send = step(up_keep + up_got, 1)
-    qkv_g_oth = finish((first, second), (first_got, second_got))
-    qkv_w_oth = dot_tn(normed1, qkv_g_oth).astype(BF)
-    ins, down_block, up_send, third, qkv_w_oth = tie(
-        back(0, half), down_block, up_send, third, qkv_w_oth
-    )
-    third_got = [move.over_core(x[1]) for x in third[1:]]
+        rows = jnp.concatenate([p[0] for p in parts] + dk + dv, axis=1)
+        return rows, low_product(normed1, rows)
+
+    half = pairs // 2
+    first, _ = beside(*back(1, 0, half), up, down, proj)
+    (down_block, first) = tie(down.done, first)
     down_all = move.gather(down_block)
-    up_got = move.over_chip(up_send, 1)
-    oth_keep, oth_send = zip(*[move.core_split(g) for g in (qkv_w_oth, out_w_grads[1])])
-    oth_got = [move.over_core(x) for x in oth_send]
-    fourth = attend_back(*ins, tables, half, half)
-    fourth, third_got, up_got, oth_got = tie(fourth, third_got, up_got, oth_got)
-    up_keep, up_send = step(up_keep + up_got, 2)
-    oth_send = [k + g for k, g in zip(oth_keep, oth_got)]
-    fourth, up_send, oth_send = tie(fourth, up_send, oth_send)
-    fourth_got = [move.over_core(x[1]) for x in fourth[1:]]
-    up_got = move.over_chip(up_send, 2)
-    oth_got = [move.over_y(x) for x in oth_send]
-    normed1_grad = dot_nt(qkv_g_oth, qkv_ws[1])
-    fourth_got, normed1_grad = tie(fourth_got, normed1_grad)
-    qkv_g_own = finish((third, fourth), (third_got, fourth_got))
-    qkv_w_own = dot_tn(normed1, qkv_g_own).astype(BF)
-    qkv_w_own, qkv_g_own, up_got, down_all = tie(qkv_w_own, qkv_g_own, up_got, down_all)
-    up_all = move.gather(up_keep + up_got)
-    own_keep, own_send = zip(*[move.core_split(g) for g in (qkv_w_own, out_w_grads[0])])
-    own_got = [move.over_core(x) for x in own_send]
-    normed1_grad = normed1_grad + dot_nt(qkv_g_own, qkv_ws[0])
-    input_part, ln1_scale_grad, ln1_shift_grad = norm_back(normed1_grad, normal1, inv_one, ln1_gain)
-    in_grad = (resid_grad + input_part).astype(BF)
-    own_got, in_grad, oth_got = tie(own_got, in_grad, oth_got)
+    second, (first_got,) = beside(*back(1, half, half), keys_of(first), up, proj)
+    third, (second_got,) = beside(*back(0, 0, half), keys_of(second), up, proj)
+    (rows_oth, w_oth), (third_got,) = beside(
+        lambda *x: finish(*x), ((first, second), (first_got, second_got)), keys_of(third), up, proj
+    )
+    up_block, third, down_all = tie(up.done, third, down_all)
+    up_all = move.gather(up_block)
+    (rows_a, w_a), (oth_got,) = beside(
+        lambda *x: finish(*x), ((third,), (third_got,)), (move.over_core, move.core_send(w_oth)), proj
+    )
+    out_block, w_a = tie(proj.done, w_a)
+    out_all = move.gather(out_block)
+    chips = n_dp // 2
+
+    def keep_of(half):
+        blocks = half.reshape(chips, 2, half.shape[0] // n_dp, half.shape[1])
+        return lax.dynamic_index_in_dim(blocks, move.core, 1, keepdims=False)
+
+    fourth, (oth_got, a_got) = beside(
+        *back(0, half, half),
+        (move.over_y, keep_of(w_oth) + oth_got),
+        (move.over_core, move.core_send(w_a)),
+    )
+
+    def columns(x, lo, hi):
+        x = x.reshape(*x.shape[:-1], 3, part)
+        return x[..., lo * LANES : hi * LANES].reshape(*x.shape[:-2], -1)
+
+    def chip_split(total, level):
+        bit = (move.me_dp >> (level + 1)) & 1
+        blocks = total.reshape(total.shape[0] // 2, 2, *total.shape[1:])
+        take = lambda b: lax.dynamic_index_in_dim(blocks, b, 1, keepdims=False)
+        return take(bit), take(1 - bit)
+
+    over_chip = lambda x, level: move.move(x, lambda dp, y: (dp ^ (2 << level), y))
+    total_a = keep_of(w_a) + a_got + columns(oth_got, 0, half)
+    keep_a, send_a = chip_split(total_a, 0)
+    normed1_part, (fourth_got, a_got) = beside(
+        lambda a, b: dot_nt(a, qkv_oth), (rows_oth, rows_a), keys_of(fourth), (lambda x: over_chip(x, 0), send_a)
+    )
+    keep_a, send_a = chip_split(keep_a + a_got, 1)
+    (rows_b, w_b), (a_got,) = beside(
+        lambda *x: finish(*x), ((fourth,), (fourth_got,)), (lambda x: over_chip(x, 1), send_a)
+    )
+    keep_a, send_a = chip_split(keep_a + a_got, 2)
+    own_cols = lambda lo, hi: columns(qkv_own, lo, hi)
+
+    def last(rows_a, rows_b, part_sum):
+        normed1_grad = part_sum + dot_nt(rows_a, own_cols(0, half)) + dot_nt(rows_b, own_cols(half, pairs))
+        input_part, scale_grad, shift_grad = norm_back(normed1_grad, normal1, inv_one, ln1_gain)
+        return (resid_grad + input_part).astype(BF), scale_grad, shift_grad
+
+    (in_grad, ln1_scale_grad, ln1_shift_grad), (b_got, a_got) = beside(
+        last,
+        (rows_a, rows_b, normed1_part),
+        (move.over_core, move.core_send(w_b)),
+        (lambda x: over_chip(x, 2), send_a),
+    )
+    total_a = keep_a + a_got
+    total_b = keep_of(w_b) + b_got + columns(oth_got, half, pairs)
     in_grad = move.swap_rows(in_grad)
-    totals = [k + g + h for k, g, h in zip(own_keep, own_got, oth_got)]
-    for level in range(levels):
-        keeps, sends = zip(*[step(t, level) for t in totals])
-        totals = [k + move.over_chip(s, level) for k, s in zip(keeps, sends)]
-    qkv_g, out_g = (move.gather(t) for t in totals)
-    qkv_b = [jnp.sum(g, 0, dtype=F32) for g in (qkv_g_own, qkv_g_oth)]
+    for level in range(chips.bit_length() - 1):
+        keep_b, send_b = chip_split(total_b, level)
+        total_b = keep_b + over_chip(send_b, level)
+    three = lambda x: x.reshape(x.shape[1], 3, -1)
+    merged = jnp.concatenate([three(total_a), three(total_b)], axis=2).reshape(1, -1, 3 * part)
+    qkv_g = move.gather(merged)
+    colsum = lambda g: jnp.sum(g, 0, dtype=F32)
+    b_own = jnp.concatenate(
+        [colsum(g).reshape(3, -1) for g in (rows_a, rows_b)], axis=1
+    ).reshape(-1)
     vec, flat = move.reduce_vectors(
         jnp.stack(
             [
@@ -745,8 +862,8 @@
                 down_bias_grad,
             ]
         ),
-        jnp.concatenate([qkv_b[0], up_b_grads[0]]),
-        jnp.concatenate([qkv_b[1], up_b_grads[1]]),
+        jnp.concatenate([b_own, up_b_own[0]]),
+        jnp.concatenate([colsum(rows_oth), up_b_oth[0]]),
     )
     return (
         block_out,
@@ -755,7 +872,7 @@
         vec[1],
         f32(qkv_g).reshape(width, 3, part),
         flat[: 3 * part].reshape(3, part),
-        f32(out_g),
+        f32(out_all),
         vec[2],
         vec[3],
         vec[4],
@@ -834,7 +951,7 @@
         P(),
         rows,
     )
-    paired = n_tensor == 2 and n_dp & (n_dp - 1) == 0
+    paired = n_tensor == 2 and n_dp >= 8 and n_dp & (n_dp - 1) == 0
     return jax.shard_map(
         functools.partial(paired_device, n_dp) if paired else spread_device,
         mesh=mesh,

time: 796 us -> 719 us (0.903)
  waiting for transfers between devices: 241 us -> 107 us
  starting transfers between devices: 43 us -> 64.1 us
  Pallas kernels: 253 us -> 271 us
  matrix products: 94.3 us -> 110 us
    ppermute x49 -> x55, waiting for transfers between devices: 185 us -> 81.6 us  [move(): return lax.ppermute(x, ('dp', 'tensor'), pairs)]
    all_gather x4, waiting for transfers between devices: 32.8 us -> 0.01 us  [gather(): return lax.all_gather(block[0], 'dp', axis=0, tiled=True)]
    ppermute x49 -> x55, starting transfers between devices: 42.7 us -> 63.5 us  [move(): return lax.ppermute(x, ('dp', 'tensor'), pairs)]
    pallas_call x0 -> x3, Pallas kernels: none -> 17.9 us  [first_split(): pl.pallas_call(functools.partial(split_kernel, last=2 * count), grid_spec...]
    dot_general x4, matrix products: 25.1 us -> 37.1 us  [dot_nn(): lax.dot_general(left, right, (((1,), (0,)), ((), ())), preferred_element_...]
    reshape x1 -> x10, local copies, waits for them, and re-layouts: 0.02 us -> 8.96 us  [the longest x1 4.6 us: columns(): x = x.reshape(*x.shape[:-1], 3, part)]
    unnamed x160 -> x197, local copies, waits for them, and re-layouts: 29.4 us -> 21.6 us
    dot_general x8 -> x9, matrix products: 34.3 us -> 40.1 us  [dot_tn(): lax.dot_general(left, right, (((0,), (0,)), ((), ())), preferred_element_...]
  transfers between devices with their start and end apart: 57 -> 63, of which waited for: 20 -> 18; matrix products, arithmetic and copies ran while one was open for 18% -> 25% of each run, Pallas kernels for 32% -> 37%
where the time goes in v3:
time: 719 us; the launch traced here: 709 us
  Pallas kernels  271 us (38%)
  matrix products  110 us (15%)
  waiting for transfers between devices  107 us (15%)
  other arithmetic  80.2 us (11%)
  starting transfers between devices  64.1 us (9%)
  local copies, waits for them, and re-layouts  60.2 us (8%)
  between operations  16.1 us (2%)
    pallas_call x4, Pallas kernels, attend_back(): call(functools.partial(attend_back_kernel, sources=len(kvs), keys_at=512,...  109 us
    ppermute x55, waiting for transfers between devices, move(): return lax.ppermute(x, ('dp', 'tensor'), pairs)  81.6 us
    ppermute x55, starting transfers between devices, move(): return lax.ppermute(x, ('dp', 'tensor'), pairs)  63.5 us
    pallas_call x2, Pallas kernels, attend(): call(functools.partial(attend_kernel, sources=len(kvs), rows_at=256), 4 *...  59.4 us
    dot_general x9, matrix products, dot_tn(): lax.dot_general(left, right, (((0,), (0,)), ((), ())), preferred_element_...  40.1 us
    dot_general x4, matrix products, dot_nn(): lax.dot_general(left, right, (((1,), (0,)), ((), ())), preferred_element_...  37.1 us
    dot_general x7, matrix products, dot_nt(): lax.dot_general(left, right, (((1,), (1,)), ((), ())), preferred_element_...  33.2 us
    pallas_call x2, Pallas kernels, up_rows(): call(up_kernel, 2 * tokens * width * cols, 2 * (tokens * width + width *...  28.5 us
  transfers between devices with their start and end apart: 63, of which 18 were waited for; matrix products, arithmetic and copies ran while one was open for 25% of the time, Pallas kernels for 37%

profile of v3, /device:TPU:0, one launch (start us, length us, event | category | flops | bytes accessed | tf_op | source)
XLA Modules:
  0.0 709.4 jit_solution(16367275939743450876)
XLA Ops:
  9.7 3.0 collective-permute-start.1
  12.7 4.9 collective-permute-done.1
  20.3 4.7 copy.50
  25.1 4.7 copy.51.w_ref
  33.1 3.7 fusion.18
  42.0 11.1 %shard_map.317 = (bf16[1024,512]{1,0:T(8,128)(2,1)}, bf16[1024,1024]{1,0:T(8,128)(2,1)}) custom-call(bf16[1024,1024]{1,0:T(8,128)(2,1)} %fusion.7.n_ref, bf16[1024,1536]{1,0:T(8,128)(2,1)} %copy.51.w_ref, f32[1,1536]{1,0:T(1,128)} %reshape.362.b_ref, f32[1024,128]{1,0:T(8,128)} %get-tuple-element.609.c_ref.refs_4_, ...), custom_call_target="tpu_custom_call" | custom-call | flops 3221225472 | bytes 8388608 | tf_op jit(solution)/shard_map/pallas_call | solution.py:114
  53.0 12.3 %all-gather.12.cloned.1.call-done.w_ref = bf16[1024,1536]{1,0:T(8,128)(2,1)} async-done(((bf16[64,1536]{1,0:T(8,128)(2,1)}), bf16[1024,1536]{1,0:T(8,128)(2,1)}) %all-gather.12.cloned.1.call-update) | async-done | bytes 3145744 | tf_op jit(solution)/shard_map/all_gather | solution.py:460
  73.3 11.0 %shard_map.318 = (bf16[1024,512]{1,0:T(8,128)(2,1)}, bf16[1024,1024]{1,0:T(8,128)(2,1)}) custom-call(bf16[1024,1024]{1,0:T(8,128)(2,1)} %fusion.7.n_ref, bf16[1024,1536]{1,0:T(8,128)(2,1)} %all-gather.12.cloned.1.call-done.w_ref, f32[1,1536]{1,0:T(1,128)} %reshape.363.b_ref, f32[1024,128]{1,0:T(8,128)} %get-tuple-element.609.c_ref.refs_4_, ...), custom_call_target="tpu_custom_call" | custom-call | flops 3221225472 | bytes 8388608 | tf_op jit(solution)/shard_map/pallas_call | solution.py:114
  92.9 29.8 %shard_map.319 = (bf16[1024,512]{1,0:T(8,128)(2,1)}, f32[4,2,1024]{2,1,0:T(2,128)}) custom-call(bf16[1024,512]{1,0:T(8,128)(2,1)} %get-tuple-element.496.refs_0_, bf16[1024,1024]{1,0:T(8,128)(2,1)} %get-tuple-element.500.refs_1_.refs_3_.refs_7_.refs_9_, bf16[1024,1024]{1,0:T(8,128)(2,1)} %collective-permute-done.6.refs_2_.refs_4_.refs_8_.refs_10_, ...), custom_call_target="tpu_custom_call" | custom-call | flops 17179869184 | bytes 6291456 | tf_op jit(solution)/shard_map/pallas_call | solution.py:177
  124.3 29.6 %shard_map.320 = (bf16[1024,512]{1,0:T(8,128)(2,1)}, f32[4,2,1024]{2,1,0:T(2,128)}) custom-call(bf16[1024,512]{1,0:T(8,128)(2,1)} %get-tuple-element.404.refs_0_, bf16[1024,1024]{1,0:T(8,128)(2,1)} %get-tuple-element.408.refs_1_.refs_3_.refs_7_.refs_9_, bf16[1024,1024]{1,0:T(8,128)(2,1)} %collective-permute-done.7.refs_2_.refs_4_.refs_8_.refs_10_, ...), custom_call_target="tpu_custom_call" | custom-call | flops 17179869184 | bytes 6291456 | tf_op jit(solution)/shard_map/pallas_call | solution.py:177
  153.9 2.9 fusion.32
  159.1 3.5 add_convert_fusion.1
  162.6 14.3 %shard_map.321 = (bf16[1024,2048]{1,0:T(8,128)(2,1)}, bf16[1024,2048]{1,0:T(8,128)(2,1)}) custom-call(bf16[1024,1024]{1,0:T(8,128)(2,1)} %get-tuple-element.591.n_ref, bf16[1024,2048]{1,0:T(8,128)(2,1)} %w_ref.1, f32[1,2048]{1,0:T(1,128)} %bitcast.186), custom_call_target="tpu_custom_call" | custom-call | flops 4294967296 | bytes 14680064 | tf_op jit(solution)/shard_map/pallas_call | solution.py:327
  176.9 20.7 %fusion.33 = f32[1024,1024]{1,0:T(8,128)} fusion(bf16[1024,2048]{1,0:T(8,128)(2,1)} %get-tuple-element.315, bf16[2048,1024]{1,0:T(8,128)(2,1)S(1)} %copy-done.70), kind=kOutput, calls=%fused_computation.164 | convolution fusion | flops 4294967296 | bytes 12582912 | tf_op jit(solution)/shard_map/dot_general | solution.py:32
  197.6 14.1 %shard_map.322 = (bf16[1024,2048]{1,0:T(8,128)(2,1)}, bf16[1024,2048]{1,0:T(8,128)(2,1)}) custom-call(bf16[1024,1024]{1,0:T(8,128)(2,1)} %get-tuple-element.591.n_ref, bf16[1024,2048]{1,0:T(8,128)(2,1)} %all-gather.16.cloned.1.call-done.w_ref, f32[1,2048]{1,0:T(1,128)} %bitcast.187), custom_call_target="tpu_custom_call" | custom-call | flops 4294967296 | bytes 14680064 | tf_op jit(solution)/shard_map/pallas_call | solution.py:327
  211.7 12.3 %all-gather.18.cloned.1.call-done.w_ref = bf16[2048,1024]{1,0:T(8,128)(2,1)} async-done(((bf16[128,1024]{1,0:T(8,128)(2,1)}), bf16[2048,1024]{1,0:T(8,128)(2,1)}) %all-gather.18.cloned.1.call-update) | async-done | bytes 4194320 | tf_op jit(solution)/shard_map/all_gather | solution.py:460
  224.0 11.8 %add_convert_fusion = bf16[1024,1024]{1,0:T(8,128)(2,1)} fusion(f32[1024,1024]{1,0:T(8,128)} %copy-done.4, f32[1024,1024]{1,0:T(8,128)} %fusion.33, f32[1024]{0:T(1024)S(1)} %convert_element_type.110, bf16[1024,2048]{1,0:T(8,128)(2,1)} %get-tuple-element.317, bf16[2048,1024]{1,0:T(8,128)(2,1)} %all-gather.18.cloned.1.call-done.w_ref), kind=kOutput, calls=%fused_computation.25 | convolution fusion | flops 4299161600 | bytes 18878464 | tf_op jit(solution)/shard_map/dot_general | solution.py:32
  237.8 7.1 %convolution_convert_fusion.4 = bf16[2048,1024]{1,0:T(8,128)(2,1)S(1)} fusion(bf16[1024,2048]{1,0:T(8,128)(2,1)} %get-tuple-element.315, bf16[1024,1024]{1,0:T(8,128)(2,1)S(1)} %copy-done.9), kind=kOutput, calls=%fused_computation.33 | convolution fusion | flops 4297064448 | bytes 10485760 | tf_op jit(solution)/shard_map/dot_general | solution.py:36
  245.0 4.9 convolution_convert_fusion.3
  249.9 4.6 broadcast_select_fusion.1
  257.7 12.3 %collective-permute-start.10 = (bf16[8,128,1024]{2,1,0:T(8,128)(2,1)}, bf16[8,128,1024]{2,1,0:T(8,128)(2,1)}, u32[]{:S(2)}, u32[]{:S(2)}) collective-permute-start(bf16[8,128,1024]{2,1,0:T(8,128)(2,1)} %dynamic-slice_bitcast_fusion.3), channel_id=1, source_target_pairs={{0,2},{1,3},{2,0},{3,1},{4,6},{5,7},{6,4},{7,5},{8,10},{9,11},{10,... | collective-permute-start | bytes 6291464 | tf_op jit(solution)/shard_map/ppermute | solution.py:443
  273.1 11.1 %shard_map.323 = (bf16[1024,2048]{1,0:T(8,128)(2,1)}, f32[1,2048]{1,0:T(1,128)}) custom-call(bf16[1024,1024]{1,0:T(8,128)(2,1)} %broadcast_select_fusion.2.g_ref, bf16[2048,1024]{1,0:T(8,128)(2,1)} %w_ref.2, bf16[1024,2048]{1,0:T(8,128)(2,1)} %get-tuple-element.325.slope_ref), custom_call_target="tpu_custom_call" | custom-call | flops 4294967296 | bytes 14680064 | tf_op jit(solution)/shard_map/pallas_call | solution.py:355
  284.3 6.7 shard_map.324
  291.0 7.0 convolution_convert_fusion.2
  300.1 11.1 %shard_map.325 = (bf16[1024,2048]{1,0:T(8,128)(2,1)}, f32[1,2048]{1,0:T(1,128)}) custom-call(bf16[1024,1024]{1,0:T(8,128)(2,1)} %broadcast_select_fusion.2.g_ref, bf16[2048,1024]{1,0:T(8,128)(2,1)} %all-gather.18.cloned.1.call-done.w_ref, bf16[1024,2048]{1,0:T(8,128)(2,1)} %get-tuple-element.336.slope_ref), custom_call_target="tpu_custom_call" | custom-call | flops 4294967296 | bytes 14680064 | tf_op jit(solution)/shard_map/pallas_call | solution.py:355
  311.2 7.4 %convolution_convert_fusion.1 = bf16[1024,2048]{1,0:T(8,128)(2,1)S(1)} fusion(bf16[1024,1024]{1,0:T(8,128)(2,1)S(1)} %copy-done.26, bf16[1024,2048]{1,0:T(8,128)(2,1)} %get-tuple-element.349), kind=kOutput, calls=%fused_computation.30 | convolution fusion | flops 4297064448 | bytes 10485760 | tf_op jit(solution)/shard_map/dot_general | solution.py:36
  318.7 5.8 collective-permute-done.13
  326.1 3.4 add.348
  329.4 6.1 fusion.34
  336.6 10.7 %multiply_reduce_fusion = (f32[1024]{0:T(1024)}, f32[1024]{0:T(1024)S(1)}, f32[1024]{0:T(1024)S(1)}, f32[1024]{0:T(1024)}, f32[1024,1024]{1,0:T(8,128)S(1)}) fusion(f32[1024,1024]{1,0:T(8,128)S(1)} %copy-done.12, f32[1024]{0:T(1024)S(1)} %convert_element_type.107, f32[1024,1024]{1,0:T(8,128)} %fusion.34, bf16[1024,2048]{1,0:T(8,128)(2,1)} %get-tuple-element.349, ...), kind=kOutput, calls=%fused_computation.22 | convolution fusion | flops 4303351808 | bytes 20992000 | tf_op jit(solution)/shard_map/dot_general | solution.py:28
  347.3 3.3 convert_reduce_fusion.2
  351.2 3.2 add_add_fusion.2
  361.7 6.8 shard_map.326
  377.9 27.1 %shard_map.327 = (bf16[1024,256]{1,0:T(8,128)(2,1)}, bf16[1024,256]{1,0:T(8,128)(2,1)}, bf16[1024,256]{1,0:T(8,128)(2,1)}, bf16[1024,256]{1,0:T(8,128)(2,1)}, bf16[1024,256]{1,0:T(8,128)(2,1)}) custom-call(bf16[1024,512]{1,0:T(8,128)(2,1)} %get-tuple-element.404.refs_0_, bf16[1024,512]{1,0:T(8,128)(2,1)} %convolution_convert_fusion.7.refs_1_, ...), custom_call_target="tpu_custom_call" | custom-call | flops 21474836480 | bytes 6291456 | tf_op jit(solution)/shard_map/pallas_call | solution.py:261
  407.5 4.3 shard_map.328
  415.1 27.4 %shard_map.329 = (bf16[1024,256]{1,0:T(8,128)(2,1)}, bf16[1024,256]{1,0:T(8,128)(2,1)}, bf16[1024,256]{1,0:T(8,128)(2,1)}, bf16[1024,256]{1,0:T(8,128)(2,1)}, bf16[1024,256]{1,0:T(8,128)(2,1)}) custom-call(bf16[1024,512]{1,0:T(8,128)(2,1)} %get-tuple-element.404.refs_0_, bf16[1024,512]{1,0:T(8,128)(2,1)} %convolution_convert_fusion.7.refs_1_, ...), custom_call_target="tpu_custom_call" | custom-call | flops 21474836480 | bytes 6291456 | tf_op jit(solution)/shard_map/pallas_call | solution.py:261
  448.1 27.5 %shard_map.330 = (bf16[1024,256]{1,0:T(8,128)(2,1)}, bf16[1024,256]{1,0:T(8,128)(2,1)}, bf16[1024,256]{1,0:T(8,128)(2,1)}, bf16[1024,256]{1,0:T(8,128)(2,1)}, bf16[1024,256]{1,0:T(8,128)(2,1)}) custom-call(bf16[1024,512]{1,0:T(8,128)(2,1)} %get-tuple-element.496.refs_0_, bf16[1024,512]{1,0:T(8,128)(2,1)} %convolution_convert_fusion.8.refs_1_, ...), custom_call_target="tpu_custom_call" | custom-call | flops 21474836480 | bytes 6291456 | tf_op jit(solution)/shard_map/pallas_call | solution.py:261
  480.8 2.9 shard_map.331
  483.7 3.1 shard_map.332
  489.2 3.8 convolution_convert_fusion
  499.6 3.0 shard_map.333
  502.6 4.4 convolution_convert_fusion.6
  509.0 4.2 fusion.29
  516.0 27.3 %shard_map.334 = (bf16[1024,256]{1,0:T(8,128)(2,1)}, bf16[1024,256]{1,0:T(8,128)(2,1)}, bf16[1024,256]{1,0:T(8,128)(2,1)}, bf16[1024,256]{1,0:T(8,128)(2,1)}, bf16[1024,256]{1,0:T(8,128)(2,1)}) custom-call(bf16[1024,512]{1,0:T(8,128)(2,1)} %get-tuple-element.496.refs_0_, bf16[1024,512]{1,0:T(8,128)(2,1)} %convolution_convert_fusion.8.refs_1_, ...), custom_call_target="tpu_custom_call" | custom-call | flops 21474836480 | bytes 6291456 | tf_op jit(solution)/shard_map/pallas_call | solution.py:261
  543.4 8.7 %collective-permute-done.38 = bf16[8,64,1536]{2,1,0:T(8,128)(2,1)S(1)} collective-permute-done((bf16[8,64,1536]{2,1,0:T(8,128)(2,1)S(1)}, bf16[8,64,1536]{2,1,0:T(8,128)(2,1)S(1)}, u32[]{:S(2)}, u32[]{:S(2)}) %collective-permute-start.38) | collective-permute-done | bytes 1572896 | tf_op jit(solution)/shard_map/ppermute | solution.py:443
  553.2 4.6 reshape.340
  559.8 2.6 reshape.341
  565.9 6.9 fusion.35
  573.7 5.3 collective-permute-done.42
  580.3 3.2 shard_map.335
  583.5 3.0 convolution_convert_fusion.5
  586.6 6.1 collective-permute-done.43
  596.6 3.2 fusion.13
  599.9 2.6 fusion.12
  605.0 9.7 %collective-permute-done.52 = bf16[4,64,768]{2,1,0:T(8,128)(2,1)S(1)} collective-permute-done((bf16[4,64,768]{2,1,0:T(8,128)(2,1)S(1)}, bf16[4,64,768]{2,1,0:T(8,128)(2,1)S(1)}, u32[]{:S(2)}, u32[]{:S(2)}) %collective-permute-start.52) | collective-permute-done | bytes 393248 | tf_op jit(solution)/shard_map/ppermute | solution.py:443
  614.8 2.6 collective-permute-start.53
  617.4 4.4 collective-permute-done.53
  637.3 24.4 %collective-permute-done.47 = f32[52,128]{1,0:T(8,128)S(1)} collective-permute-done((f32[52,128]{1,0:T(8,128)S(1)}, f32[52,128]{1,0:T(8,128)S(1)}, u32[]{:S(2)}, u32[]{:S(2)}) %collective-permute-start.47) | collective-permute-done | bytes 26656 | tf_op jit(solution)/shard_map/ppermute | solution.py:443
  664.2 2.8 collective-permute-done.49
  668.7 6.7 convert_element_type.132
  677.2 2.8 bitcast_convert_fusion.1
  683.6 6.7 bitcast_convert_fusion
  690.2 5.4 copy.56
  695.7 6.6 copy.57
  (435 shorter events, 134.5 us)
Async XLA Ops:
  7.2 58.1 %all-gather.12.cloned.1.call-start = ((), (), s32[]{:S(2)}) async-start(), calls=%async_computation | async-start | bytes 3342336 | tf_op jit(solution)/shard_map/all_gather | solution.py:460
  9.7 7.9 %collective-permute-start.1 = (bf16[64,1536]{1,0:T(8,128)(2,1)S(1)}, bf16[64,1536]{1,0:T(8,128)(2,1)S(1)}, u32[]{:S(2)}, u32[]{:S(2)}) collective-permute-start(bf16[64,1536]{1,0:T(8,128)(2,1)S(1)} %bitcast.179), channel_id=1, source_target_pairs={{0,1},{1,0},{2,3},{3,2},{4,5},{5,4},{6,7},{7,6},{8,9},{9,8},{10,11... | collective-permute-start | bytes 589832 | tf_op jit(solution)/shard_map/ppermute | solution.py:443
  18.3 135.6 %all-gather.14.cloned.1.call-start = ((), (), s32[]{:S(2)}) async-start(), calls=%async_computation.1 | async-start | bytes 1114112 | tf_op jit(solution)/shard_map/all_gather | solution.py:460
  18.3 18.5 %collective-permute-start = (bf16[1024,1024]{1,0:T(8,128)(2,1)}, bf16[1024,1024]{1,0:T(8,128)(2,1)}, u32[]{:S(2)}, u32[]{:S(2)}) collective-permute-start(bf16[1024,1024]{1,0:T(8,128)(2,1)} %param.22), channel_id=1, source_target_pairs={{1,2},{2,1},{5,6},{6,5},{9,10},{10,9},{13,14},{14,13},{17,18},{18,... | collective-permute-start | bytes 6291464 | tf_op jit(solution)/shard_map/ppermute | solution.py:443
  39.1 117.7 %copy-start.2 = (bf16[1024,1024]{1,0:T(8,128)(2,1)}, bf16[1024,1024]{1,0:T(8,128)(2,1)S(1)}, u32[]{:S(2)}) copy-start(bf16[1024,1024]{1,0:T(8,128)(2,1)S(1)} %get-tuple-element.594) | copy-start | bytes 6291460
  65.3 19.7 %collective-permute-start.6 = (bf16[1024,1024]{1,0:T(8,128)(2,1)}, bf16[1024,1024]{1,0:T(8,128)(2,1)}, u32[]{:S(2)}, u32[]{:S(2)}) collective-permute-start(bf16[1024,1024]{1,0:T(8,128)(2,1)} %get-tuple-element.500.refs_1_.refs_3_.refs_7_.refs_9_), channel_id=1, source_target_pairs={{0,2},{1,3},{2,0},{3,1},{4,6},{5,7},{6,4},{7,5},{8,10},{9,11},{10,... | collective-permute-start | bytes 6291464 | tf_op jit(solution)/shard_map/ppermute | solution.py:443
  65.6 3.7 collective-permute-start.2
  69.8 14.5 %collective-permute-start.3 = (bf16[32,1024]{1,0:T(8,128)(2,1)S(1)}, bf16[32,1024]{1,0:T(8,128)(2,1)S(1)}, u32[]{:S(2)}, u32[]{:S(2)}) collective-permute-start(bf16[32,1024]{1,0:T(8,128)(2,1)S(1)} %constant_dynamic-slice_fusion.6), channel_id=1, source_target_pairs={{0,1},{1,0},{2,3},{3,2},{4,5},{5,4},{6,7},{7,6},{8,9},{9,8},{10,11... | collective-permute-start | bytes 196616 | tf_op jit(solution)/shard_map/ppermute | solution.py:443
  71.3 13.0 %collective-permute-start.4 = (bf16[64,2048]{1,0:T(8,128)(2,1)}, bf16[64,2048]{1,0:T(8,128)(2,1)}, u32[]{:S(2)}, u32[]{:S(2)}) collective-permute-start(bf16[64,2048]{1,0:T(8,128)(2,1)} %constant_dynamic-slice_fusion.5), channel_id=1, source_target_pairs={{0,1},{1,0},{2,3},{3,2},{4,5},{5,4},{6,7},{7,6},{8,9},{9,8},{10,11... | collective-permute-start | bytes 786440 | tf_op jit(solution)/shard_map/ppermute | solution.py:443
  71.8 13.1 %collective-permute-start.5 = (bf16[128,1024]{1,0:T(8,128)(2,1)S(1)}, bf16[128,1024]{1,0:T(8,128)(2,1)}, u32[]{:S(2)}, u32[]{:S(2)}) collective-permute-start(bf16[128,1024]{1,0:T(8,128)(2,1)S(1)} %constant_dynamic-slice_fusion.4), channel_id=1, source_target_pairs={{0,1},{1,0},{2,3},{3,2},{4,5},{5,4},{6,7},{7,6},{8,9},{9,8},{10,11... | collective-permute-start | bytes 786440 | tf_op jit(solution)/shard_map/ppermute | solution.py:443
  85.0 112.6 %all-gather.16.cloned.1.call-start = ((), (), s32[]{:S(2)}) async-start(), calls=%async_computation.2 | async-start | bytes 4456448 | tf_op jit(solution)/shard_map/all_gather | solution.py:460
  85.7 138.2 %all-gather.18.cloned.1.call-start = ((), (), s32[]{:S(2)}) async-start(), calls=%async_computation.3 | async-start | bytes 4456448 | tf_op jit(solution)/shard_map/all_gather | solution.py:460
  85.8 36.8 %collective-permute-start.8 = (bf16[1024,1024]{1,0:T(8,128)(2,1)}, bf16[1024,1024]{1,0:T(8,128)(2,1)}, u32[]{:S(2)}, u32[]{:S(2)}) collective-permute-start(bf16[1024,1024]{1,0:T(8,128)(2,1)} %param.35), channel_id=1, source_target_pairs={{1,2},{2,1},{5,6},{6,5},{9,10},{10,9},{13,14},{14,13},{17,18},{18,... | collective-permute-start | bytes 6291464 | tf_op jit(solution)/shard_map/ppermute | solution.py:443
  91.1 33.1 %collective-permute-start.7 = (bf16[1024,1024]{1,0:T(8,128)(2,1)}, bf16[1024,1024]{1,0:T(8,128)(2,1)}, u32[]{:S(2)}, u32[]{:S(2)}) collective-permute-start(bf16[1024,1024]{1,0:T(8,128)(2,1)} %get-tuple-element.408.refs_1_.refs_3_.refs_7_.refs_9_), channel_id=1, source_target_pairs={{0,2},{1,3},{2,0},{3,1},{4,6},{5,7},{6,4},{7,5},{8,10},{9,11},{10,... | collective-permute-start | bytes 6291464 | tf_op jit(solution)/shard_map/ppermute | solution.py:443
  92.0 404.8 %all-gather.22.cloned.1.call-start = ((), (), s32[]{:S(2)}) async-start(), calls=%async_computation.5 | async-start | bytes 4456448 | tf_op jit(solution)/shard_map/all_gather | solution.py:490
  235.8 14.1 %collective-permute-start.9 = (bf16[1024,1024]{1,0:T(8,128)(2,1)}, bf16[1024,1024]{1,0:T(8,128)(2,1)}, u32[]{:S(2)}, u32[]{:S(2)}) collective-permute-start(bf16[1024,1024]{1,0:T(8,128)(2,1)} %add_convert_fusion), channel_id=1, source_target_pairs={{1,2},{2,1},{5,6},{6,5},{9,10},{10,9},{13,14},{14,13},{17,18},{18,... | collective-permute-start | bytes 6291464 | tf_op jit(solution)/shard_map/ppermute | solution.py:443
  257.7 26.5 %collective-permute-start.10 = (bf16[8,128,1024]{2,1,0:T(8,128)(2,1)}, bf16[8,128,1024]{2,1,0:T(8,128)(2,1)}, u32[]{:S(2)}, u32[]{:S(2)}) collective-permute-start(bf16[8,128,1024]{2,1,0:T(8,128)(2,1)} %dynamic-slice_bitcast_fusion.3), channel_id=1, source_target_pairs={{0,2},{1,3},{2,0},{3,1},{4,6},{5,7},{6,4},{7,5},{8,10},{9,11},{10,... | collective-permute-start | bytes 6291464 | tf_op jit(solution)/shard_map/ppermute | solution.py:443
  270.0 14.2 %collective-permute-start.11 = (bf16[8,128,1024]{2,1,0:T(8,128)(2,1)}, bf16[8,128,1024]{2,1,0:T(8,128)(2,1)}, u32[]{:S(2)}, u32[]{:S(2)}) collective-permute-start(bf16[8,128,1024]{2,1,0:T(8,128)(2,1)} %dynamic-slice_bitcast_fusion.2), channel_id=1, source_target_pairs={{0,2},{1,3},{2,0},{3,1},{4,6},{5,7},{6,4},{7,5},{8,10},{9,11},{10,... | collective-permute-start | bytes 6291464 | tf_op jit(solution)/shard_map/ppermute | solution.py:443
  298.0 20.6 %collective-permute-start.12 = (bf16[4,128,1024]{2,1,0:T(8,128)(2,1)}, bf16[4,128,1024]{2,1,0:T(8,128)(2,1)}, u32[]{:S(2)}, u32[]{:S(2)}) collective-permute-start(bf16[4,128,1024]{2,1,0:T(8,128)(2,1)} %get-tuple-element.340), channel_id=1, source_target_pairs={{0,1},{1,0},{2,6},{3,7},{4,5},{5,4},{6,2},{7,3},{8,9},{9,8},{10,14... | collective-permute-start | bytes 3145736 | tf_op jit(solution)/shard_map/ppermute | solution.py:443
  299.8 24.6 %collective-permute-start.13 = (bf16[4,128,1024]{2,1,0:T(8,128)(2,1)}, bf16[4,128,1024]{2,1,0:T(8,128)(2,1)}, u32[]{:S(2)}, u32[]{:S(2)}) collective-permute-start(bf16[4,128,1024]{2,1,0:T(8,128)(2,1)} %get-tuple-element.341), channel_id=1, source_target_pairs={{0,1},{1,0},{2,6},{3,7},{4,5},{5,4},{6,2},{7,3},{8,9},{9,8},{10,14... | collective-permute-start | bytes 3145736 | tf_op jit(solution)/shard_map/ppermute | solution.py:443
  335.5 15.6 %collective-permute-start.14 = (bf16[8,64,2048]{2,1,0:T(8,128)(2,1)S(1)}, bf16[8,64,2048]{2,1,0:T(8,128)(2,1)S(1)}, u32[]{:S(2)}, u32[]{:S(2)}) collective-permute-start(bf16[8,64,2048]{2,1,0:T(8,128)(2,1)S(1)} %dynamic-slice_bitcast_fusion.1), channel_id=1, source_target_pairs={{0,2},{1,3},{2,0},{3,1},{4,6},{5,7},{6,4},{7,5},{8,10},{9,11},{10,... | collective-permute-start | bytes 6291464 | tf_op jit(solution)/shard_map/ppermute | solution.py:443
  335.5 15.6 %collective-permute-start.15 = (bf16[8,64,2048]{2,1,0:T(8,128)(2,1)S(1)}, bf16[8,64,2048]{2,1,0:T(8,128)(2,1)S(1)}, u32[]{:S(2)}, u32[]{:S(2)}) collective-permute-start(bf16[8,64,2048]{2,1,0:T(8,128)(2,1)S(1)} %dynamic-slice_bitcast_fusion), channel_id=1, source_target_pairs={{0,2},{1,3},{2,0},{3,1},{4,6},{5,7},{6,4},{7,5},{8,10},{9,11},{10,... | collective-permute-start | bytes 6291464 | tf_op jit(solution)/shard_map/ppermute | solution.py:443
  336.0 15.1 %collective-permute-start.16 = (bf16[4,128,1024]{2,1,0:T(8,128)(2,1)}, bf16[4,128,1024]{2,1,0:T(8,128)(2,1)}, u32[]{:S(2)}, u32[]{:S(2)}) collective-permute-start(bf16[4,128,1024]{2,1,0:T(8,128)(2,1)} %add.348), channel_id=1, source_target_pairs={{0,4},{1,5},{2,3},{3,2},{4,0},{5,1},{6,7},{7,6},{8,12},{9,13},{10,... | collective-permute-start | bytes 3145736 | tf_op jit(solution)/shard_map/ppermute | solution.py:443
  358.8 14.4 %collective-permute-start.17 = (bf16[2,128,1024]{2,1,0:T(8,128)(2,1)}, bf16[2,128,1024]{2,1,0:T(8,128)(2,1)S(1)}, u32[]{:S(2)}, u32[]{:S(2)}) collective-permute-start(bf16[2,128,1024]{2,1,0:T(8,128)(2,1)} %slice.137), channel_id=1, source_target_pairs={{0,8},{1,9},{2,10},{3,11},{4,12},{5,13},{6,14},{7,15},{8,0},{9,1},... | collective-permute-start | bytes 1572872 | tf_op jit(solution)/shard_map/ppermute | solution.py:443
  373.5 31.5 %collective-permute-start.18 = (bf16[4,64,2048]{2,1,0:T(8,128)(2,1)}, bf16[4,64,2048]{2,1,0:T(8,128)(2,1)}, u32[]{:S(2)}, u32[]{:S(2)}) collective-permute-start(bf16[4,64,2048]{2,1,0:T(8,128)(2,1)} %get-tuple-element.384), channel_id=1, source_target_pairs={{0,1},{1,0},{2,6},{3,7},{4,5},{5,4},{6,2},{7,3},{8,9},{9,8},{10,14... | collective-permute-start | bytes 3145736 | tf_op jit(solution)/shard_map/ppermute | solution.py:443
  374.1 30.9 %collective-permute-start.19 = (bf16[4,64,2048]{2,1,0:T(8,128)(2,1)S(1)}, bf16[4,64,2048]{2,1,0:T(8,128)(2,1)}, u32[]{:S(2)}, u32[]{:S(2)}) collective-permute-start(bf16[4,64,2048]{2,1,0:T(8,128)(2,1)S(1)} %copy-done.86), channel_id=1, source_target_pairs={{0,1},{1,0},{2,6},{3,7},{4,5},{5,4},{6,2},{7,3},{8,9},{9,8},{10,14... | collective-permute-start | bytes 3145736 | tf_op jit(solution)/shard_map/ppermute | solution.py:443
  375.6 29.4 %collective-permute-start.20 = (bf16[1,128,1024]{2,1,0:T(8,128)(2,1)S(1)}, bf16[1,128,1024]{2,1,0:T(8,128)(2,1)S(1)}, u32[]{:S(2)}, u32[]{:S(2)}) collective-permute-start(bf16[1,128,1024]{2,1,0:T(8,128)(2,1)S(1)} %slice.139), channel_id=1, source_target_pairs={{0,16},{1,17},{2,18},{3,19},{4,20},{5,21},{6,22},{7,23},{8,24},{9,... | collective-permute-start | bytes 786440 | tf_op jit(solution)/shard_map/ppermute | solution.py:443
  377.4 27.6 %collective-permute-start.21 = (bf16[8,32,1024]{2,1,0:T(8,128)(2,1)S(1)}, bf16[8,32,1024]{2,1,0:T(8,128)(2,1)S(1)}, u32[]{:S(2)}, u32[]{:S(2)}) collective-permute-start(bf16[8,32,1024]{2,1,0:T(8,128)(2,1)S(1)} %dynamic-slice_bitcast_fusion.8), channel_id=1, source_target_pairs={{0,2},{1,3},{2,0},{3,1},{4,6},{5,7},{6,4},{7,5},{8,10},{9,11},{10,... | collective-permute-start | bytes 1572872 | tf_op jit(solution)/shard_map/ppermute | solution.py:443
  377.4 27.6 %collective-permute-start.22 = (bf16[8,32,1024]{2,1,0:T(8,128)(2,1)S(1)}, bf16[8,32,1024]{2,1,0:T(8,128)(2,1)S(1)}, u32[]{:S(2)}, u32[]{:S(2)}) collective-permute-start(bf16[8,32,1024]{2,1,0:T(8,128)(2,1)S(1)} %dynamic-slice_bitcast_fusion.7), channel_id=1, source_target_pairs={{0,2},{1,3},{2,0},{3,1},{4,6},{5,7},{6,4},{7,5},{8,10},{9,11},{10,... | collective-permute-start | bytes 1572872 | tf_op jit(solution)/shard_map/ppermute | solution.py:443
  411.9 30.7 %collective-permute-start.23 = (bf16[1024,256]{1,0:T(8,128)(2,1)}, bf16[1024,256]{1,0:T(8,128)(2,1)}, u32[]{:S(2)}, u32[]{:S(2)}) collective-permute-start(bf16[1024,256]{1,0:T(8,128)(2,1)} %get-tuple-element.415), channel_id=1, source_target_pairs={{0,2},{1,3},{2,0},{3,1},{4,6},{5,7},{6,4},{7,5},{8,10},{9,11},{10,... | collective-permute-start | bytes 1572872 | tf_op jit(solution)/shard_map/ppermute | solution.py:443
  411.9 30.7 %collective-permute-start.24 = (bf16[1024,256]{1,0:T(8,128)(2,1)}, bf16[1024,256]{1,0:T(8,128)(2,1)}, u32[]{:S(2)}, u32[]{:S(2)}) collective-permute-start(bf16[1024,256]{1,0:T(8,128)(2,1)} %get-tuple-element.416), channel_id=1, source_target_pairs={{0,2},{1,3},{2,0},{3,1},{4,6},{5,7},{6,4},{7,5},{8,10},{9,11},{10,... | collective-permute-start | bytes 1572872 | tf_op jit(solution)/shard_map/ppermute | solution.py:443
  412.4 30.2 %collective-permute-start.25 = (bf16[4,64,2048]{2,1,0:T(8,128)(2,1)S(1)}, bf16[4,64,2048]{2,1,0:T(8,128)(2,1)S(1)}, u32[]{:S(2)}, u32[]{:S(2)}) collective-permute-start(bf16[4,64,2048]{2,1,0:T(8,128)(2,1)S(1)} %add.356), channel_id=1, source_target_pairs={{0,4},{1,5},{2,3},{3,2},{4,0},{5,1},{6,7},{7,6},{8,12},{9,13},{10,... | collective-permute-start | bytes 3145736 | tf_op jit(solution)/shard_map/ppermute | solution.py:443
  413.0 29.6 %collective-permute-start.26 = (bf16[4,32,1024]{2,1,0:T(8,128)(2,1)}, bf16[4,32,1024]{2,1,0:T(8,128)(2,1)}, u32[]{:S(2)}, u32[]{:S(2)}) collective-permute-start(bf16[4,32,1024]{2,1,0:T(8,128)(2,1)} %get-tuple-element.418), channel_id=1, source_target_pairs={{0,1},{1,0},{2,6},{3,7},{4,5},{5,4},{6,2},{7,3},{8,9},{9,8},{10,14... | collective-permute-start | bytes 786440 | tf_op jit(solution)/shard_map/ppermute | solution.py:443
  413.5 29.0 %collective-permute-start.27 = (bf16[4,32,1024]{2,1,0:T(8,128)(2,1)}, bf16[4,32,1024]{2,1,0:T(8,128)(2,1)S(1)}, u32[]{:S(2)}, u32[]{:S(2)}) collective-permute-start(bf16[4,32,1024]{2,1,0:T(8,128)(2,1)} %get-tuple-element.419), channel_id=1, source_target_pairs={{0,1},{1,0},{2,6},{3,7},{4,5},{5,4},{6,2},{7,3},{8,9},{9,8},{10,14... | collective-permute-start | bytes 786440 | tf_op jit(solution)/shard_map/ppermute | solution.py:443
  415.1 262.1 %all-gather.24.cloned.1.call-start = ((), (), s32[]{:S(2)}) async-start(), calls=%async_computation.6 | async-start | bytes 1114112 | tf_op jit(solution)/shard_map/all_gather | solution.py:490
  445.4 30.2 %collective-permute-start.28 = (bf16[1024,256]{1,0:T(8,128)(2,1)S(1)}, bf16[1024,256]{1,0:T(8,128)(2,1)S(1)}, u32[]{:S(2)}, u32[]{:S(2)}) collective-permute-start(bf16[1024,256]{1,0:T(8,128)(2,1)S(1)} %copy-done.88), channel_id=1, source_target_pairs={{0,2},{1,3},{2,0},{3,1},{4,6},{5,7},{6,4},{7,5},{8,10},{9,11},{10,... | collective-permute-start | bytes 1572872 | tf_op jit(solution)/shard_map/ppermute | solution.py:443
  445.5 30.1 %collective-permute-start.29 = (bf16[1024,256]{1,0:T(8,128)(2,1)S(1)}, bf16[1024,256]{1,0:T(8,128)(2,1)S(1)}, u32[]{:S(2)}, u32[]{:S(2)}) collective-permute-start(bf16[1024,256]{1,0:T(8,128)(2,1)S(1)} %copy-done.87), channel_id=1, source_target_pairs={{0,2},{1,3},{2,0},{3,1},{4,6},{5,7},{6,4},{7,5},{8,10},{9,11},{10,... | collective-permute-start | bytes 1572872 | tf_op jit(solution)/shard_map/ppermute | solution.py:443
  446.0 29.7 %collective-permute-start.30 = (bf16[2,64,2048]{2,1,0:T(8,128)(2,1)S(1)}, bf16[2,64,2048]{2,1,0:T(8,128)(2,1)S(1)}, u32[]{:S(2)}, u32[]{:S(2)}) collective-permute-start(bf16[2,64,2048]{2,1,0:T(8,128)(2,1)S(1)} %slice.142), channel_id=1, source_target_pairs={{0,8},{1,9},{2,10},{3,11},{4,12},{5,13},{6,14},{7,15},{8,0},{9,1},... | collective-permute-start | bytes 1572872 | tf_op jit(solution)/shard_map/ppermute | solution.py:443
  446.6 29.0 %collective-permute-start.31 = (bf16[4,32,1024]{2,1,0:T(8,128)(2,1)S(1)}, bf16[4,32,1024]{2,1,0:T(8,128)(2,1)S(1)}, u32[]{:S(2)}, u32[]{:S(2)}) collective-permute-start(bf16[4,32,1024]{2,1,0:T(8,128)(2,1)S(1)} %add.358), channel_id=1, source_target_pairs={{0,4},{1,5},{2,3},{3,2},{4,0},{5,1},{6,7},{7,6},{8,12},{9,13},{10,... | collective-permute-start | bytes 786440 | tf_op jit(solution)/shard_map/ppermute | solution.py:443
  477.5 15.6 %collective-permute-start.32 = (bf16[1024,256]{1,0:T(8,128)(2,1)}, bf16[1024,256]{1,0:T(8,128)(2,1)S(1)}, u32[]{:S(2)}, u32[]{:S(2)}) collective-permute-start(bf16[1024,256]{1,0:T(8,128)(2,1)} %get-tuple-element.468), channel_id=1, source_target_pairs={{0,2},{1,3},{2,0},{3,1},{4,6},{5,7},{6,4},{7,5},{8,10},{9,11},{10,... | collective-permute-start | bytes 1572872 | tf_op jit(solution)/shard_map/ppermute | solution.py:443
  477.5 15.6 %collective-permute-start.33 = (bf16[1024,256]{1,0:T(8,128)(2,1)}, bf16[1024,256]{1,0:T(8,128)(2,1)S(1)}, u32[]{:S(2)}, u32[]{:S(2)}) collective-permute-start(bf16[1024,256]{1,0:T(8,128)(2,1)} %get-tuple-element.469), channel_id=1, source_target_pairs={{0,2},{1,3},{2,0},{3,1},{4,6},{5,7},{6,4},{7,5},{8,10},{9,11},{10,... | collective-permute-start | bytes 1572872 | tf_op jit(solution)/shard_map/ppermute | solution.py:443
  478.0 15.0 %collective-permute-start.34 = (bf16[1,64,2048]{2,1,0:T(8,128)(2,1)S(1)}, bf16[1,64,2048]{2,1,0:T(8,128)(2,1)S(1)}, u32[]{:S(2)}, u32[]{:S(2)}) collective-permute-start(bf16[1,64,2048]{2,1,0:T(8,128)(2,1)S(1)} %slice.144), channel_id=1, source_target_pairs={{0,16},{1,17},{2,18},{3,19},{4,20},{5,21},{6,22},{7,23},{8,24},{9,... | collective-permute-start | bytes 786440 | tf_op jit(solution)/shard_map/ppermute | solution.py:443
  480.2 12.9 %collective-permute-start.35 = (bf16[2,32,1024]{2,1,0:T(8,128)(2,1)}, bf16[2,32,1024]{2,1,0:T(8,128)(2,1)S(1)}, u32[]{:S(2)}, u32[]{:S(2)}) collective-permute-start(bf16[2,32,1024]{2,1,0:T(8,128)(2,1)} %slice.145), channel_id=1, source_target_pairs={{0,8},{1,9},{2,10},{3,11},{4,12},{5,13},{6,14},{7,15},{8,0},{9,1},... | collective-permute-start | bytes 393224 | tf_op jit(solution)/shard_map/ppermute | solution.py:443
  496.8 11.5 %collective-permute-start.36 = (bf16[8,64,1536]{2,1,0:T(8,128)(2,1)}, bf16[8,64,1536]{2,1,0:T(8,128)(2,1)}, u32[]{:S(2)}, u32[]{:S(2)}) collective-permute-start(bf16[8,64,1536]{2,1,0:T(8,128)(2,1)} %dynamic-slice_bitcast_fusion.4), channel_id=1, source_target_pairs={{0,2},{1,3},{2,0},{3,1},{4,6},{5,7},{6,4},{7,5},{8,10},{9,11},{10,... | collective-permute-start | bytes 4718600 | tf_op jit(solution)/shard_map/ppermute | solution.py:443
  496.8 11.5 %collective-permute-start.37 = (bf16[1,32,1024]{2,1,0:T(8,128)(2,1)S(1)}, bf16[1,32,1024]{2,1,0:T(8,128)(2,1)S(1)}, u32[]{:S(2)}, u32[]{:S(2)}) collective-permute-start(bf16[1,32,1024]{2,1,0:T(8,128)(2,1)S(1)} %slice.147), channel_id=1, source_target_pairs={{0,16},{1,17},{2,18},{3,19},{4,20},{5,21},{6,22},{7,23},{8,24},{9,... | collective-permute-start | bytes 196616 | tf_op jit(solution)/shard_map/ppermute | solution.py:443
  508.9 174.7 %all-gather.26.cloned.1.call-start = ((), (), s32[]{:S(2)}) async-start(), calls=%async_computation.7 | async-start | bytes 4456448 | tf_op jit(solution)/shard_map/all_gather | solution.py:490
  513.2 177.0 %all-gather.20.cloned.1.call-start = ((), (), s32[]{:S(2)}) async-start(), calls=%async_computation.4 | async-start | bytes 3342336 | tf_op jit(solution)/shard_map/all_gather | solution.py:490
  515.4 36.6 %collective-permute-start.38 = (bf16[8,64,1536]{2,1,0:T(8,128)(2,1)S(1)}, bf16[8,64,1536]{2,1,0:T(8,128)(2,1)S(1)}, u32[]{:S(2)}, u32[]{:S(2)}) collective-permute-start(bf16[8,64,1536]{2,1,0:T(8,128)(2,1)S(1)} %bitcast_add_fusion), channel_id=1, source_target_pairs={{0,1},{1,0},{2,3},{3,2},{4,5},{5,4},{6,7},{7,6},{8,9},{9,8},{10,11... | collective-permute-start | bytes 4718600 | tf_op jit(solution)/shard_map/ppermute | solution.py:443
  516.0 27.3 %collective-permute-start.39 = (bf16[8,64,768]{2,1,0:T(8,128)(2,1)S(1)}, bf16[8,64,768]{2,1,0:T(8,128)(2,1)S(1)}, u32[]{:S(2)}, u32[]{:S(2)}) collective-permute-start(bf16[8,64,768]{2,1,0:T(8,128)(2,1)S(1)} %dynamic-slice_bitcast_fusion.6), channel_id=1, source_target_pairs={{0,2},{1,3},{2,0},{3,1},{4,6},{5,7},{6,4},{7,5},{8,10},{9,11},{10,... | collective-permute-start | bytes 2359304 | tf_op jit(solution)/shard_map/ppermute | solution.py:443
  564.8 14.1 %collective-permute-start.40 = (bf16[1024,256]{1,0:T(8,128)(2,1)}, bf16[1024,256]{1,0:T(8,128)(2,1)}, u32[]{:S(2)}, u32[]{:S(2)}) collective-permute-start(bf16[1024,256]{1,0:T(8,128)(2,1)} %get-tuple-element.518), channel_id=1, source_target_pairs={{0,2},{1,3},{2,0},{3,1},{4,6},{5,7},{6,4},{7,5},{8,10},{9,11},{10,... | collective-permute-start | bytes 1572872 | tf_op jit(solution)/shard_map/ppermute | solution.py:443
  564.8 14.1 %collective-permute-start.41 = (bf16[1024,256]{1,0:T(8,128)(2,1)}, bf16[1024,256]{1,0:T(8,128)(2,1)}, u32[]{:S(2)}, u32[]{:S(2)}) collective-permute-start(bf16[1024,256]{1,0:T(8,128)(2,1)} %get-tuple-element.519), channel_id=1, source_target_pairs={{0,2},{1,3},{2,0},{3,1},{4,6},{5,7},{6,4},{7,5},{8,10},{9,11},{10,... | collective-permute-start | bytes 1572872 | tf_op jit(solution)/shard_map/ppermute | solution.py:443
  565.3 13.6 %collective-permute-start.42 = (bf16[4,64,768]{2,1,0:T(8,128)(2,1)}, bf16[4,64,768]{2,1,0:T(8,128)(2,1)S(1)}, u32[]{:S(2)}, u32[]{:S(2)}) collective-permute-start(bf16[4,64,768]{2,1,0:T(8,128)(2,1)} %dynamic-slice_bitcast_fusion.10), channel_id=1, source_target_pairs={{0,4},{1,5},{2,6},{3,7},{4,0},{5,1},{6,2},{7,3},{8,12},{9,13},{10,... | collective-permute-start | bytes 1179656 | tf_op jit(solution)/shard_map/ppermute | solution.py:443
  579.0 13.7 %collective-permute-start.43 = (bf16[2,64,768]{2,1,0:T(8,128)(2,1)S(1)}, bf16[2,64,768]{2,1,0:T(8,128)(2,1)S(1)}, u32[]{:S(2)}, u32[]{:S(2)}) collective-permute-start(bf16[2,64,768]{2,1,0:T(8,128)(2,1)S(1)} %dynamic-slice_bitcast_fusion.12), channel_id=1, source_target_pairs={{0,8},{1,9},{2,10},{3,11},{4,12},{5,13},{6,14},{7,15},{8,0},{9,1},... | collective-permute-start | bytes 589832 | tf_op jit(solution)/shard_map/ppermute | solution.py:443
  592.8 9.6 %collective-permute-start.44 = (bf16[8,64,768]{2,1,0:T(8,128)(2,1)S(1)}, bf16[8,64,768]{2,1,0:T(8,128)(2,1)S(1)}, u32[]{:S(2)}, u32[]{:S(2)}) collective-permute-start(bf16[8,64,768]{2,1,0:T(8,128)(2,1)S(1)} %dynamic-slice_bitcast_fusion.5), channel_id=1, source_target_pairs={{0,2},{1,3},{2,0},{3,1},{4,6},{5,7},{6,4},{7,5},{8,10},{9,11},{10,... | collective-permute-start | bytes 2359304 | tf_op jit(solution)/shard_map/ppermute | solution.py:443
  592.9 9.5 %collective-permute-start.45 = (bf16[1,64,768]{2,1,0:T(8,128)(2,1)S(1)}, bf16[1,64,768]{2,1,0:T(8,128)(2,1)S(1)}, u32[]{:S(2)}, u32[]{:S(2)}) collective-permute-start(bf16[1,64,768]{2,1,0:T(8,128)(2,1)S(1)} %constant_dynamic-slice_fusion.3), channel_id=1, source_target_pairs={{0,16},{1,17},{2,18},{3,19},{4,20},{5,21},{6,22},{7,23},{8,24},{9,... | collective-permute-start | bytes 294920 | tf_op jit(solution)/shard_map/ppermute | solution.py:443
  602.7 12.1 %collective-permute-start.52 = (bf16[4,64,768]{2,1,0:T(8,128)(2,1)S(1)}, bf16[4,64,768]{2,1,0:T(8,128)(2,1)S(1)}, u32[]{:S(2)}, u32[]{:S(2)}) collective-permute-start(bf16[4,64,768]{2,1,0:T(8,128)(2,1)S(1)} %dynamic-slice_bitcast_fusion.9), channel_id=1, source_target_pairs={{0,4},{1,5},{2,6},{3,7},{4,0},{5,1},{6,2},{7,3},{8,12},{9,13},{10,... | collective-permute-start | bytes 1179656 | tf_op jit(solution)/shard_map/ppermute | solution.py:443
  614.8 6.9 collective-permute-start.53
  621.8 5.6 collective-permute-start.54
  634.8 47.3 %collective-permute-start.46 = (bf16[1024,1024]{1,0:T(8,128)(2,1)S(1)}, bf16[1024,1024]{1,0:T(8,128)(2,1)}, u32[]{:S(2)}, u32[]{:S(2)}) collective-permute-start(bf16[1024,1024]{1,0:T(8,128)(2,1)S(1)} %copy-done.16), channel_id=1, source_target_pairs={{1,2},{2,1},{5,6},{6,5},{9,10},{10,9},{13,14},{14,13},{17,18},{18,... | collective-permute-start | bytes 6291464 | tf_op jit(solution)/shard_map/ppermute | solution.py:443
  636.9 24.8 %collective-permute-start.47 = (f32[52,128]{1,0:T(8,128)S(1)}, f32[52,128]{1,0:T(8,128)S(1)}, u32[]{:S(2)}, u32[]{:S(2)}) collective-permute-start(f32[52,128]{1,0:T(8,128)S(1)} %maximum_bitcast_fusion.1), channel_id=1, source_target_pairs={{0,1},{1,0},{2,3},{3,2},{4,5},{5,4},{6,7},{7,6},{8,9},{9,8},{10,11... | collective-permute-start | bytes 79880 | tf_op jit(solution)/shard_map/ppermute | solution.py:443
  661.7 1.3 collective-permute-start.48
  663.0 3.9 collective-permute-start.49
  666.9 8.4 %collective-permute-start.50 = (f32[52,128]{1,0:T(8,128)S(1)}, f32[52,128]{1,0:T(8,128)S(1)}, u32[]{:S(2)}, u32[]{:S(2)}) collective-permute-start(f32[52,128]{1,0:T(8,128)S(1)} %add.387), channel_id=1, source_target_pairs={{0,8},{1,9},{2,10},{3,11},{4,12},{5,13},{6,14},{7,15},{8,0},{9,1},... | collective-permute-start | bytes 79880 | tf_op jit(solution)/shard_map/ppermute | solution.py:443
  675.4 4.8 collective-permute-start.51
  (91 other events, 769.1 us)
Sparse Core Ops, SparseCore 0:
  18.4 46.8 all-gather.11
  85.1 36.0 all-gather.13
  123.4 49.4 all-gather.15
  174.9 49.0 all-gather.17
  415.2 56.0 all-gather.21
  509.0 36.1 all-gather.23
  547.4 50.4 all-gather.25
  628.4 44.7 all-gather.19

commit v4 on v3

--- a/solution.py
+++ b/solution.py
@@ -80,9 +80,35 @@
     )
 
 
+def norm_kernel(x_ref, scale_ref, shift_ref, n_ref, nt_ref):
+    normed, _, _ = norm_parts(x_ref[...].astype(F32), scale_ref[...], shift_ref[...])
+    n_ref[...] = normed.astype(BF)
+    nt_ref[...] = normed.T.astype(BF)
+
+
+def norm_rows(x, scale, shift):
+    tokens, width = x.shape
+    rows = min(256, tokens)
+    vector = pl.BlockSpec((1, width), lambda i: (0, 0))
+    tile = pl.BlockSpec((rows, width), lambda i: (i, 0))
+    return call(
+        norm_kernel,
+        10 * tokens * width,
+        6 * tokens * width,
+        grid=(tokens // rows,),
+        in_specs=[tile, vector, vector],
+        out_specs=[tile, pl.BlockSpec((width, rows), lambda i: (0, i))],
+        out_shape=[
+            jax.ShapeDtypeStruct((tokens, width), BF),
+            jax.ShapeDtypeStruct((width, tokens), BF),
+        ],
+    )(x, scale, shift)
+
+
 def qkv_kernel(n_ref, w_ref, b_ref, c_ref, sa_ref, sb_ref, q_ref, kv_ref, *, q_steps):
     step = pl.program_id(0)
-    rows = dot_nn(n_ref[...], w_ref[...]) + b_ref[...]
+    weight = w_ref[...].reshape(n_ref.shape[1], w_ref.shape[-1])
+    rows = dot_nn(n_ref[...], weight) + b_ref[...]
     wide = rows.shape[1]
 
     def turned():
@@ -107,8 +133,8 @@
 
 def qkv_rows(normed, weight, bias, tables):
     tokens, width = normed.shape
-    cols = weight.shape[1] // 3
-    tile = 256 if cols % 256 == 0 else LANES
+    groups, _, deep, cols = weight.shape
+    tile = next(t for t in (512, 256, LANES) if cols % t == 0)
     q_steps = cols // tile
     whole = lambda n: (0, 0)
     return call(
@@ -118,7 +144,7 @@
         grid=(3 * q_steps,),
         in_specs=[
             pl.BlockSpec((tokens, width), whole),
-            pl.BlockSpec((width, tile), lambda n: (0, n)),
+            pl.BlockSpec((groups, None, deep, tile), lambda n: (0, n // q_steps, 0, n % q_steps)),
             pl.BlockSpec((1, tile), lambda n: (0, n)),
         ]
         + [pl.BlockSpec((tokens, LANES), whole)] * 3,
@@ -137,55 +163,64 @@
     q_ref = refs[0]
     k_refs = refs[1 : 1 + sources]
     v_refs = refs[1 + sources : 1 + 2 * sources]
-    o_ref, lse_ref = refs[1 + 2 * sources :]
+    o_ref, lse_ref = refs[1 + 2 * sources : 3 + 2 * sources]
+    wide_refs = refs[3 + 2 * sources :]
     lane = lax.broadcasted_iota(jnp.int32, (1, LANES), 1)
-
-    def body(i, carry):
-        rows = pl.ds(pl.multiple_of(i * rows_at, rows_at), rows_at)
+    for v, wide in zip(v_refs, wide_refs):
+        wide[:, :LANES] = v[...]
+        wide[:, LANES:] = jnp.ones_like(v)
+
+    def scores_of(q, head):
+        q_head = jnp.where((lane // HD) == head, q, jnp.zeros_like(q))
+        return [dot_nt(q_head, k[...]) for k in k_refs]
+
+    def result(scores):
+        peak = functools.reduce(
+            jnp.maximum, [jnp.max(s, axis=1, keepdims=True) for s in scores]
+        )
+        weights = [jnp.exp2((s - peak) * (SCALE * LOG2E)).astype(BF) for s in scores]
+        both = sum(dot_nn(w, v[...]) for w, v in zip(weights, wide_refs))
+        total = both[:, LANES : LANES + 1]
+        return both[:, :LANES] / both[:, LANES:], peak * (SCALE * LOG2E) + jnp.log2(total)
+
+    for first in range(0, q_ref.shape[0], rows_at):
+        rows = slice(first, first + rows_at)
         q = q_ref[rows, :]
-        outs, logs = [], []
-        for head in range(2):
-            mine = (lane // HD) == head
-            q_head = jnp.where(mine, q, jnp.zeros_like(q))
-            scores = [dot_nt(q_head, k[...]) for k in k_refs]
-            peak = functools.reduce(
-                jnp.maximum, [jnp.max(s, axis=1, keepdims=True) for s in scores]
-            )
-            weights = [jnp.exp2((s - peak) * (SCALE * LOG2E)) for s in scores]
-            total = sum(jnp.sum(w, axis=1, keepdims=True) for w in weights)
-            out = sum(dot_nn(w.astype(BF), v[...]) for w, v in zip(weights, v_refs))
-            outs.append(out / total)
-            logs.append(peak * (SCALE * LOG2E) + jnp.log2(total))
-        first = lane < HD
-        o_ref[rows, :] = jnp.where(first, outs[0], outs[1]).astype(BF)
-        logs_t = jnp.where(first, logs[0], logs[1]).T
-        lse_ref[0, 0:1, rows] = logs_t[0:1]
-        lse_ref[0, 1:2, rows] = logs_t[HD : HD + 1]
-        return carry
-
-    steps = q_ref.shape[0] // rows_at
-    lax.fori_loop(0, steps, body, 0, unroll=2 if steps % 2 == 0 else 1)
-
-
-def attend(q, kvs):
+        (out_0, log_0), (out_1, log_1) = [result(s) for s in [scores_of(q, h) for h in range(2)]]
+        early = lane < HD
+        o_ref[rows, :] = jnp.where(early, out_0, out_1).astype(BF)
+        logs = jnp.where(early, log_0, log_1).T
+        lse_ref[0, 0:1, rows] = logs[0:1]
+        lse_ref[0, 1:2, rows] = logs[HD : HD + 1]
+
+
+def attend(q, kvs, skip=0, pairs=None):
     tokens, cols = q.shape
-    pairs = cols // LANES
+    all_pairs = cols // LANES
+    pairs = pairs or all_pairs
+    cols = pairs * LANES
     keys = sum(kv.shape[0] for kv in kvs)
-    q_spec = pl.BlockSpec((tokens, LANES), lambda i: (0, i))
-    k_specs = [pl.BlockSpec((kv.shape[0], LANES), lambda i: (0, i)) for kv in kvs]
-    v_specs = [pl.BlockSpec((kv.shape[0], LANES), lambda i: (0, pairs + i)) for kv in kvs]
+    q_spec = pl.BlockSpec((tokens, LANES), lambda i: (0, skip + i))
+    k_specs = [pl.BlockSpec((kv.shape[0], LANES), lambda i: (0, skip + i)) for kv in kvs]
+    v_specs = [
+        pl.BlockSpec((kv.shape[0], LANES), lambda i: (0, all_pairs + skip + i)) for kv in kvs
+    ]
     return call(
-        functools.partial(attend_kernel, sources=len(kvs), rows_at=256),
+        functools.partial(attend_kernel, sources=len(kvs), rows_at=min(512, tokens)),
         4 * 4 * tokens * keys * cols,
         2 * (2 * tokens * cols + 2 * keys * cols),
         tokens * keys * 2 * pairs,
         grid=(pairs,),
         in_specs=[q_spec] + k_specs + v_specs,
-        out_specs=[q_spec, pl.BlockSpec((1, 2, tokens), lambda i: (i, 0, 0))],
+        out_specs=[
+            pl.BlockSpec((tokens, LANES), lambda i: (0, i)),
+            pl.BlockSpec((1, 2, tokens), lambda i: (i, 0, 0)),
+        ],
         out_shape=[
             jax.ShapeDtypeStruct((tokens, cols), BF),
             jax.ShapeDtypeStruct((pairs, 2, tokens), F32),
         ],
+        scratch_shapes=[pltpu.VMEM((kv.shape[0], 2 * LANES), BF) for kv in kvs],
     )(q, *kvs, *kvs)
 
 
@@ -215,25 +250,30 @@
             k_t = k.astype(F32).T.astype(BF)
             dv = jnp.zeros((keys_at, LANES), F32)
             dk = jnp.zeros((keys_at, LANES), F32)
-            for head in range(2):
+
+            def products(cut, head):
                 mine = (lane // HD) == head
-                for first in range(0, tokens, queries_at):
-                    cut = slice(first, first + queries_at)
-                    q, do = q_ref[cut, :], do_ref[cut, :]
-                    q_head = jnp.where(mine, q, jnp.zeros_like(q))
-                    do_head = jnp.where(mine, do, jnp.zeros_like(do))
-                    scores = dot_nt(k, q_head)
-                    share_grad = dot_nt(v, do_head)
-                    shares = jnp.exp2(
-                        scores * (SCALE * LOG2E) - lse_ref[0, head : head + 1, cut]
-                    )
-                    score_grad = (
-                        shares * (share_grad - centre[head : head + 1, cut])
-                    ).astype(BF)
-                    dv += dot_nn(shares.astype(BF), do_head)
-                    dk += dot_nn(score_grad, q_head)
-                    part = slice(head * HD, head * HD + HD)
-                    dq_acc[part, cut] += dot_nn(k_t[part], score_grad)
+                q, do = q_ref[cut, :], do_ref[cut, :]
+                q_head = jnp.where(mine, q, jnp.zeros_like(q))
+                do_head = jnp.where(mine, do, jnp.zeros_like(do))
+                return q_head, do_head, dot_nt(k, q_head), dot_nt(v, do_head)
+
+            steps = [
+                (slice(first, first + queries_at), head)
+                for first in range(0, tokens, queries_at)
+                for head in range(2)
+            ]
+            later = products(*steps[0])
+            for at, (cut, head) in enumerate(steps):
+                q_head, do_head, scores, share_grad = later
+                if at + 1 < len(steps):
+                    later = products(*steps[at + 1])
+                shares = jnp.exp2(scores * (SCALE * LOG2E) - lse_ref[0, head : head + 1, cut])
+                score_grad = (shares * (share_grad - centre[head : head + 1, cut])).astype(BF)
+                dv += dot_nn(shares.astype(BF), do_head)
+                dk += dot_nn(score_grad, q_head)
+                part = slice(head * HD, head * HD + HD)
+                dq_acc[part, cut] += dot_nn(k_t[part], score_grad)
             dv_ref[rows, :] = dv.astype(BF)
             dk_ref[rows, :] = (dk * SCALE).astype(BF)
             return carry
@@ -243,13 +283,14 @@
     dq_ref[...] = turn_back(dq, c_ref[...], sa_ref[...], sb_ref[...]).astype(BF)
 
 
-def attend_back(q, out_grad, out, lse, kvs, tables, skip=0, pairs=None):
+def attend_back(q, out_grad, out, lse, kvs, tables, skip=0, pairs=None, at=0):
     tokens, cols = q.shape
     all_pairs = cols // LANES
     pairs = pairs or all_pairs
     cols = pairs * LANES
     keys = sum(kv.shape[0] for kv in kvs)
     q_spec = pl.BlockSpec((tokens, LANES), lambda i: (0, skip + i))
+    o_spec = pl.BlockSpec((tokens, LANES), lambda i: (0, at + i))
     k_specs = [pl.BlockSpec((kv.shape[0], LANES), lambda i: (0, skip + i)) for kv in kvs]
     v_specs = [
         pl.BlockSpec((kv.shape[0], LANES), lambda i: (0, all_pairs + skip + i)) for kv in kvs
@@ -257,17 +298,16 @@
     dq_spec = pl.BlockSpec((tokens, LANES), lambda i: (0, i))
     dk_specs = [pl.BlockSpec((kv.shape[0], LANES), lambda i: (0, i)) for kv in kvs]
     table = pl.BlockSpec((tokens, LANES), lambda i: (0, 0))
-    piece = min(512, tokens)
     outs = call(
         functools.partial(
-            attend_back_kernel, sources=len(kvs), keys_at=512, queries_at=piece
+            attend_back_kernel, sources=len(kvs), keys_at=1024, queries_at=min(256, tokens)
         ),
         10 * 4 * tokens * keys * cols,
         2 * (4 * tokens * cols + 4 * keys * cols),
         tokens * keys * 2 * pairs,
         grid=(pairs,),
-        in_specs=[q_spec, q_spec, q_spec]
-        + [pl.BlockSpec((1, 2, tokens), lambda i: (skip + i, 0, 0))]
+        in_specs=[q_spec, o_spec, o_spec]
+        + [pl.BlockSpec((1, 2, tokens), lambda i: (at + i, 0, 0))]
         + [table] * 3
         + k_specs
         + v_specs,
@@ -301,15 +341,9 @@
 
 
 def gelu_parts(hidden):
-    size = jnp.abs(hidden)
+    cdf = 0.5 + 0.5 * lax.erf(hidden * (1.0 / math.sqrt(2.0)))
     bell = jnp.exp2(hidden * hidden * (-0.5 * LOG2E))
-    t = 1.0 / (1.0 + (0.3275911 / math.sqrt(2.0)) * size)
-    poly = 0.5 * 1.061405429
-    for factor in (-1.453152027, 1.421413741, -0.284496736, 0.254829592):
-        poly = poly * t + 0.5 * factor
-    tail = poly * t * bell
-    cdf = jnp.where(hidden >= 0.0, 1.0 - tail, tail)
-    return hidden * cdf, cdf + hidden * bell * (1.0 / math.sqrt(2.0 * math.pi))
+    return hidden * cdf, cdf + hidden * (1.0 / math.sqrt(2.0 * math.pi)) * bell
 
 
 def up_kernel(n_ref, w_ref, b_ref, acted_ref, slope_ref):
@@ -322,7 +356,7 @@
 def up_rows(normed, weight, bias):
     tokens, width = normed.shape
     cols = weight.shape[1]
-    tile = 256
+    tile = 512
     out = pl.BlockSpec((tokens, tile), lambda n: (0, n))
     return call(
         up_kernel,
@@ -340,8 +374,9 @@
     )(normed, weight, bias)
 
 
-def hidden_grad_kernel(g_ref, w_ref, slope_ref, hg_ref, sum_ref):
-    grad = dot_nt(g_ref[...], w_ref[...]) * slope_ref[...].astype(F32)
+def hidden_grad_kernel(g_ref, w_ref, slope_ref, hg_ref, sum_ref, *, skip):
+    weight = w_ref[:, skip:].reshape(hg_ref.shape[1], g_ref.shape[1])
+    grad = dot_nt(g_ref[...], weight) * slope_ref[...].astype(F32)
     low = grad.astype(BF)
     hg_ref[...] = low
     sum_ref[...] = jnp.sum(low.astype(F32), axis=0, keepdims=True)
@@ -349,19 +384,21 @@
 
 def hidden_grads(grad, down, slope):
     tokens, width = grad.shape
-    cols = down.shape[0]
-    tile = 256
+    down, skip = down
+    groups, deep, _ = down.shape
+    cols = slope.shape[1]
+    tile = 512
     out = pl.BlockSpec((tokens, tile), lambda n: (0, n))
+    if groups == 1:
+        weight = pl.BlockSpec((1, tile, width), lambda n: (0, n, 0))
+    else:
+        weight = pl.BlockSpec((tile // (deep - skip), deep, width), lambda n: (n, 0, 0))
     return call(
-        hidden_grad_kernel,
+        functools.partial(hidden_grad_kernel, skip=skip),
         2 * tokens * width * cols,
         2 * (tokens * width + width * cols + 2 * tokens * cols),
         grid=(cols // tile,),
-        in_specs=[
-            pl.BlockSpec((tokens, width), lambda n: (0, 0)),
-            pl.BlockSpec((tile, width), lambda n: (n, 0)),
-            out,
-        ],
+        in_specs=[pl.BlockSpec((tokens, width), lambda n: (0, 0)), weight, out],
         out_specs=[out, pl.BlockSpec((1, tile), lambda n: (0, n))],
         out_shape=[
             jax.ShapeDtypeStruct((tokens, cols), BF),
@@ -374,7 +411,7 @@
     centred = values - jnp.mean(values, axis=-1, keepdims=True)
     inv_dev = lax.rsqrt(jnp.mean(centred * centred, axis=-1, keepdims=True) + EPS)
     normal = centred * inv_dev
-    return (normal * gain + shift).astype(BF), normal, inv_dev
+    return normal * gain + shift, normal, inv_dev
 
 
 def norm_back(upstream, normal, inv_dev, gain):
@@ -388,6 +425,272 @@
 def tie(*trees):
     leaves, form = jax.tree.flatten(trees)
     return jax.tree.unflatten(form, lax.optimization_barrier(tuple(leaves)))
+
+
+def project_kernel(*refs, parts):
+    x_ref, b_ref, scale_ref, shift_ref = refs[:4]
+    o_refs, w_refs = refs[4 : 4 + parts], refs[4 + parts : 4 + 2 * parts]
+    resid_ref, n_ref, nt_ref = refs[4 + 2 * parts :]
+    resid = x_ref[...].astype(F32) + b_ref[...]
+    for o, w in zip(o_refs, w_refs):
+        resid += dot_nn(o[...], w[...])
+    normed, _, _ = norm_parts(resid, scale_ref[...], shift_ref[...])
+    resid_ref[...] = resid
+    n_ref[...] = normed.astype(BF)
+    nt_ref[...] = normed.T.astype(BF)
+
+
+def project_rows(x, bias, scale, shift, outs, weights):
+    tokens, width = x.shape
+    rows = min(256, tokens)
+    vector = pl.BlockSpec((1, width), lambda i: (0, 0))
+    tile = pl.BlockSpec((rows, width), lambda i: (i, 0))
+    deep = sum(o.shape[1] for o in outs)
+    return call(
+        functools.partial(project_kernel, parts=len(outs)),
+        2 * tokens * width * deep,
+        2 * (tokens * deep + width * deep + 5 * tokens * width),
+        grid=(tokens // rows,),
+        in_specs=[tile, vector, vector, vector]
+        + [pl.BlockSpec((rows, o.shape[1]), lambda i: (i, 0)) for o in outs]
+        + [pl.BlockSpec(w.shape, lambda i: (0, 0)) for w in weights],
+        out_specs=[tile, tile, pl.BlockSpec((width, rows), lambda i: (0, i))],
+        out_shape=[
+            jax.ShapeDtypeStruct((tokens, width), F32),
+            jax.ShapeDtypeStruct((tokens, width), BF),
+            jax.ShapeDtypeStruct((width, tokens), BF),
+        ],
+    )(x, bias, scale, shift, *outs, *weights)
+
+
+def down_kernel(r_ref, b_ref, *refs, parts, skips):
+    total = r_ref[...] + b_ref[...]
+    for a, w, skip in zip(refs[:parts], refs[parts : 2 * parts], skips):
+        total += dot_nn(a[...], w[:, skip:].reshape(a.shape[1], w.shape[2]))
+    refs[-1][...] = total.astype(BF)
+
+
+def down_rows(resid, bias, acts, weights):
+    tokens, width = resid.shape
+    weights, skips = zip(*weights)
+    cols = min(512, width)
+    tile = pl.BlockSpec((tokens, cols), lambda i: (0, i))
+    deep = sum(a.shape[1] for a in acts)
+    return call(
+        functools.partial(down_kernel, parts=len(acts), skips=skips),
+        2 * tokens * width * deep,
+        2 * (tokens * deep + width * deep + 3 * tokens * width),
+        grid=(width // cols,),
+        in_specs=[tile, pl.BlockSpec((1, cols), lambda i: (0, i))]
+        + [pl.BlockSpec(a.shape, lambda i: (0, 0)) for a in acts]
+        + [pl.BlockSpec((*w.shape[:2], cols), lambda i: (0, 0, i)) for w in weights],
+        out_specs=tile,
+        out_shape=jax.ShapeDtypeStruct((tokens, width), BF),
+    )(resid, bias, *acts, *weights)
+
+
+def middle_kernel(r_ref, g_ref, scale_ref, *refs, parts):
+    branch_ref, sums_ref = refs[-2:]
+    upstream = sum(dot_nt(h[...], w[...]) for h, w in zip(refs[:parts], refs[parts : 2 * parts]))
+    grad = g_ref[...].astype(F32)
+    _, normal, inv_dev = norm_parts(r_ref[...], 1.0, 0.0)
+    back, scale_sum, shift_sum = norm_back(upstream, normal, inv_dev, scale_ref[...])
+    branch = (grad + back).astype(BF)
+    branch_ref[...] = branch
+    total = lambda v: jnp.sum(v, axis=0, keepdims=True)
+    sums = [scale_sum[None, :], shift_sum[None, :], total(branch.astype(F32)), total(grad)]
+    sums = jnp.concatenate(sums + [jnp.zeros((4, grad.shape[1]), F32)], axis=0)
+
+    @pl.when(pl.program_id(0) == 0)
+    def _():
+        sums_ref[...] = sums
+
+    @pl.when(pl.program_id(0) > 0)
+    def _():
+        sums_ref[...] += sums
+
+
+def middle_rows(resid, grad, scale, hidden_gs, weights):
+    tokens, width = resid.shape
+    rows = min(256, tokens)
+    tile = pl.BlockSpec((rows, width), lambda i: (i, 0))
+    deep = sum(h.shape[1] for h in hidden_gs)
+    return call(
+        functools.partial(middle_kernel, parts=len(hidden_gs)),
+        2 * tokens * width * deep,
+        2 * (tokens * deep + width * deep + 4 * tokens * width),
+        grid=(tokens // rows,),
+        in_specs=[tile, tile, pl.BlockSpec((1, width), lambda i: (0, 0))]
+        + [pl.BlockSpec((rows, h.shape[1]), lambda i: (i, 0)) for h in hidden_gs]
+        + [pl.BlockSpec(w.shape, lambda i: (0, 0)) for w in weights],
+        out_specs=[tile, pl.BlockSpec((8, width), lambda i: (0, 0))],
+        out_shape=[
+            jax.ShapeDtypeStruct((tokens, width), BF),
+            jax.ShapeDtypeStruct((8, width), F32),
+        ],
+    )(resid, grad, scale, *hidden_gs, *weights)
+
+
+def add_parts(total, refs, weights, units):
+    for (w_ref, lo, count), start in zip(weights, units):
+        for kind in range(3):
+            parts = [refs[start + 3 * u + kind][...] for u in range(count)]
+            cols = sum(p.shape[1] for p in parts)
+            weight = w_ref[:, kind, :, lo : lo + cols].reshape(total.shape[1], cols)
+            total += dot_nt(jnp.concatenate(parts, axis=1), weight)
+    return total
+
+
+def early_kernel(own_ref, oth_ref, *refs, units, cols):
+    out_ref = refs[-1]
+    weights = [(own_ref, 0, 1), (oth_ref, 0, units)]
+    out_ref[...] = add_parts(jnp.zeros(out_ref.shape, F32), refs, weights, (0, 3))
+
+
+def last_kernel(x_ref, g_ref, scale_ref, part_ref, own_ref, *refs, cols):
+    in_grad_ref, sums_ref = refs[-2:]
+    upstream = add_parts(part_ref[...], refs, [(own_ref, cols, 1)], (0,))
+    _, normal, inv_dev = norm_parts(x_ref[...].astype(F32), 1.0, 0.0)
+    back, scale_sum, shift_sum = norm_back(upstream, normal, inv_dev, scale_ref[...])
+    in_grad_ref[...] = (g_ref[...].astype(F32) + back).astype(BF)
+    sums = [scale_sum[None, :], shift_sum[None, :], jnp.zeros((6, x_ref.shape[1]), F32)]
+    sums = jnp.concatenate(sums, axis=0)
+
+    @pl.when(pl.program_id(0) == 0)
+    def _():
+        sums_ref[...] = sums
+
+    @pl.when(pl.program_id(0) > 0)
+    def _():
+        sums_ref[...] += sums
+
+
+def early_rows(own, oth, own_unit, oth_units):
+    flat = list(own_unit) + [p for unit in oth_units for p in unit]
+    tokens, cols = flat[0].shape
+    width = own.shape[0] * own.shape[2]
+    rows = min(512, tokens)
+    return call(
+        functools.partial(early_kernel, units=len(oth_units), cols=cols),
+        2 * tokens * width * cols * len(flat),
+        2 * (tokens * cols * len(flat) + width * cols * len(flat) + 2 * tokens * width),
+        grid=(tokens // rows,),
+        in_specs=[pl.BlockSpec(w.shape, lambda i: (0, 0, 0, 0)) for w in (own, oth)]
+        + [pl.BlockSpec((rows, cols), lambda i: (i, 0)) for p in flat],
+        out_specs=pl.BlockSpec((rows, width), lambda i: (i, 0)),
+        out_shape=jax.ShapeDtypeStruct((tokens, width), F32),
+    )(own, oth, *flat)
+
+
+def last_rows(x, branch_grad, scale, partial, own, unit):
+    tokens, width = x.shape
+    cols = unit[0].shape[1]
+    rows = min(256, tokens)
+    tile = pl.BlockSpec((rows, width), lambda i: (i, 0))
+    return call(
+        functools.partial(last_kernel, cols=cols),
+        6 * tokens * width * cols,
+        2 * (3 * tokens * cols + 3 * width * cols + 5 * tokens * width),
+        grid=(tokens // rows,),
+        in_specs=[tile, tile, pl.BlockSpec((1, width), lambda i: (0, 0)), tile]
+        + [pl.BlockSpec(own.shape, lambda i: (0, 0, 0, 0))]
+        + [pl.BlockSpec((rows, cols), lambda i: (i, 0))] * 3,
+        out_specs=[tile, pl.BlockSpec((8, width), lambda i: (0, 0))],
+        out_shape=[
+            jax.ShapeDtypeStruct((tokens, width), BF),
+            jax.ShapeDtypeStruct((8, width), F32),
+        ],
+    )(x, branch_grad, scale, partial, own, *unit)
+
+
+def unit_kernel(t_ref, nt_ref, dq_ref, dk_ref, gk_ref, dv_ref, gv_ref, c_ref, sa_ref, sb_ref, *refs, chips):
+    keep_ref, send_ref, dk_out, dv_out, sum_ref, rows_ref, acc_ref = refs
+    kind = pl.program_id(0)
+    added = lambda a, b: a[...].astype(F32) + b[...].astype(F32)
+
+    @pl.when(kind == 0)
+    def _():
+        rows_ref[...] = dq_ref[...]
+
+    @pl.when(kind == 1)
+    def _():
+        total = added(dk_ref, gk_ref)
+        tables = (c_ref[...], sa_ref[...], sb_ref[...])
+        for at in range(0, total.shape[1], LANES):
+            cut = slice(at, at + LANES)
+            rows_ref[:, cut] = turn_back(total[:, cut], *tables).astype(BF)
+        dk_out[...] = rows_ref[...]
+
+    @pl.when(kind == 2)
+    def _():
+        rows_ref[...] = added(dv_ref, gv_ref).astype(BF)
+        dv_out[...] = rows_ref[...]
+
+    rows = rows_ref[...]
+    acc_ref[...] = dot_nn(nt_ref[...], rows)
+    piece = keep_ref.shape[1]
+    for place in range(chips):
+        for ref, which in ((keep_ref, place), (send_ref, chips + place)):
+            at = pl.multiple_of(t_ref[which] * piece, piece)
+            ref[place] = acc_ref[pl.ds(at, piece), :].astype(BF)
+    sums = jnp.sum(rows.astype(F32), axis=0, keepdims=True)
+    sum_ref[...] = jnp.broadcast_to(sums, sum_ref.shape)
+
+
+def unit_grads(table, normed_t, dq, dk, got_k, dv, got_v, tables):
+    width, tokens = normed_t.shape
+    cols = dq.shape[1]
+    chips = table.shape[0] // 2
+    piece = width // (2 * chips)
+    part = pl.BlockSpec((tokens, cols), lambda i, t: (0, 0))
+    rotary = pl.BlockSpec((tokens, LANES), lambda i, t: (0, 0))
+    blocks = pl.BlockSpec((chips, None, piece, cols), lambda i, t: (0, i, 0, 0))
+    return pl.pallas_call(
+        functools.partial(unit_kernel, chips=chips),
+        grid_spec=pltpu.PrefetchScalarGridSpec(
+            num_scalar_prefetch=1,
+            grid=(3,),
+            in_specs=[pl.BlockSpec((width, tokens), lambda i, t: (0, 0))] + [part] * 5 + [rotary] * 3,
+            out_specs=[blocks, blocks, part, part, pl.BlockSpec((8, cols), lambda i, t: (0, i))],
+            scratch_shapes=[pltpu.VMEM((tokens, cols), BF), pltpu.VMEM((width, cols), F32)],
+        ),
+        out_shape=[jax.ShapeDtypeStruct((chips, 3, piece, cols), BF)] * 2
+        + [jax.ShapeDtypeStruct((tokens, cols), BF)] * 2
+        + [jax.ShapeDtypeStruct((8, 3 * cols), F32)],
+        compiler_params=pltpu.CompilerParams(vmem_limit_bytes=VMEM_BYTES),
+        cost_estimate=pl.CostEstimate(
+            flops=6 * tokens * width * cols,
+            bytes_accessed=2 * (tokens * width + 7 * tokens * cols + 3 * width * cols),
+            transcendentals=0,
+        ),
+    )(table, normed_t, dq, dk, got_k, dv, got_v, *tables)
+
+
+def widen_kernel(t_ref, a_ref, b_ref, out_ref):
+    count, piece, cols = a_ref.shape
+    out_ref[:, :cols] = a_ref[...].reshape(out_ref.shape[0], cols).astype(F32)
+    for place in range(count):
+        rows = pl.ds(pl.multiple_of(t_ref[place] * piece, piece), piece)
+        out_ref[rows, cols:] = b_ref[place].astype(F32)
+
+
+def widen(table, unit_a, unit_b):
+    n, _, piece, cols = unit_a.shape
+    spec = pl.BlockSpec((n, None, piece, cols), lambda i, t: (0, i, 0, 0))
+    return pl.pallas_call(
+        widen_kernel,
+        grid_spec=pltpu.PrefetchScalarGridSpec(
+            num_scalar_prefetch=1,
+            grid=(3,),
+            in_specs=[spec, spec],
+            out_specs=pl.BlockSpec((None, n * piece, 2 * cols), lambda i, t: (i, 0, 0)),
+        ),
+        out_shape=jax.ShapeDtypeStruct((3, n * piece, 2 * cols), F32),
+        compiler_params=pltpu.CompilerParams(vmem_limit_bytes=VMEM_BYTES),
+        cost_estimate=pl.CostEstimate(
+            flops=0, bytes_accessed=36 * n * piece * cols, transcendentals=0
+        ),
+    )(table, unit_a, unit_b)
 
 
 def split_kernel(t_ref, own_m, own_f, oth_m, oth_f, got_om, got_of, got_tm, got_tf, ka, kb, sa, sb, *, last):
@@ -432,19 +735,25 @@
         self.me_y = lax.axis_index("tensor")
         self.core = self.me_dp % 2
         self.first = self.core * (SEQ // 2)
+        chips = n_dp // 2
+        levels = chips.bit_length() - 1
+        places = np.arange(chips)
+        far = sum(((places >> (levels - 1 - k)) & 1) << k for k in range(levels))
+        chip = jnp.asarray(far, jnp.int32) ^ (self.me_dp // 2)
+        self.blocks = jnp.concatenate([chip * 2 + self.core, chip * 2 + 1 - self.core]).astype(
+            jnp.int32
+        )
 
     def move(self, x, to):
         pairs = []
         for dp in range(self.n_dp):
             for y in range(2):
                 a, b = to(dp, y)
-                if (a, b) != (dp, y):
-                    pairs.append((dp * 2 + y, a * 2 + b))
+                pairs.append((dp * 2 + y, a * 2 + b))
         return lax.ppermute(x, ("dp", "tensor"), pairs)
 
     def swap_rows(self, rows):
-        got = self.move(rows, lambda dp, y: (dp - dp % 2 + y, dp % 2))
-        return jnp.where(self.core == self.me_y, rows, got)
+        return self.move(rows, lambda dp, y: (dp - dp % 2 + y, dp % 2))
 
     def over_y(self, x):
         return self.move(x, lambda dp, y: (dp, 1 - y))
@@ -452,9 +761,9 @@
     def over_core(self, x):
         return self.move(x, lambda dp, y: (dp ^ 1, y))
 
-    def piece(self, own):
-        rows = own.shape[0] // self.n_dp
-        return lax.dynamic_slice_in_dim(own, self.me_dp * rows, rows, 0)
+    def piece(self, own, axis=0):
+        rows = own.shape[axis] // self.n_dp
+        return lax.dynamic_slice_in_dim(own, self.me_dp * rows, rows, axis)
 
     def spread(self, got):
         return lax.all_gather(got, "dp", axis=0, tiled=True)
@@ -463,6 +772,9 @@
         rows, cols = half.shape
         blocks = half.reshape(self.n_dp // 2, 2, rows // self.n_dp, cols)
         return lax.dynamic_index_in_dim(blocks, 1 - self.core, 1, keepdims=False)
+
+    def over_chip(self, x, level):
+        return self.move(x, lambda dp, y: (dp ^ (2 << level), y))
 
     def over_first(self, x):
         return self.move(x, lambda dp, y: (dp ^ 2, y) if dp % 2 else (dp, 1 - y))
@@ -495,11 +807,11 @@
         take = lambda b: lax.dynamic_index_in_dim(both, b, 1, keepdims=False).reshape(-1)
         mine = jnp.concatenate([take(self.me_y), own]).reshape(-1, LANES)
         theirs = jnp.concatenate([take(1 - self.me_y), other]).reshape(-1, LANES)
-        total = mine + self.over_y(theirs)
+        total = jnp.stack([mine, theirs])
         total = total + self.over_core(total)
         for level in range((self.n_dp // 2).bit_length() - 1):
-            total = total + self.move(total, lambda dp, y: (dp ^ (2 << level), y))
-        total = total.reshape(-1)
+            total = total + self.over_chip(total, level)
+        total = (total[0] + self.over_y(total[1])).reshape(-1)
         return total[: k * width // 2].reshape(k, width // 2), total[k * width // 2 :]
 
 
@@ -541,9 +853,11 @@
     block_in = move.swap_rows(block_in)
     x_rows = f32(block_in)
     normed1, normal1, inv_one = norm_parts(x_rows, ln1_gain, f32(ln1_shift))
+    normed1 = normed1.astype(BF)
     queries, keys, outs, logs = [], [], [], []
     for weight, bias in zip(qkv_ws, qkv_bs):
-        q, kv = qkv_rows(normed1, weight, f32(bias)[None, :], tables)
+        split = weight.reshape(1, weight.shape[0], 3, -1).transpose(0, 2, 1, 3)
+        q, kv = qkv_rows(normed1, split, f32(bias)[None, :], tables)
         queries.append(q)
         keys.append(move.keys(kv))
     for q, kvs in zip(queries, keys):
@@ -555,6 +869,7 @@
     branch_one = sum(dot_nn(o, w) for o, w in zip(outs, out_ws)) + f32(out_bias)
     resid = x_rows + branch_one
     normed2, normal2, inv_two = norm_parts(resid, ln2_gain, f32(ln2_shift))
+    normed2 = normed2.astype(BF)
     acts, slopes = [], []
     for weight, bias in zip(up_ws, up_bs):
         acted, slope = up_rows(normed2, weight, f32(bias)[None, :])
@@ -566,7 +881,7 @@
     down_grads = [dot_tn(a, grad_low).astype(BF) for a in acts]
     hidden_gs, up_b_grads = [], []
     for down, slope in zip(down_ws, slopes):
-        hg, total = hidden_grads(grad_low, down, slope)
+        hg, total = hidden_grads(grad_low, (down[None], 0), slope)
         hidden_gs.append(hg)
         up_b_grads.append(total[0])
     up_grads = [dot_tn(normed2, hg).astype(BF) for hg in hidden_gs]
@@ -650,9 +965,9 @@
         return 2 + (self.move.n_dp // 4).bit_length() - 1
 
 
-def beside(compute, inputs, *steps):
+def beside(compute, inputs, *steps, late=()):
     sends = [s.sends if isinstance(s, Reduction) else s[1] for s in steps]
-    inputs, sends = tie(inputs, sends)
+    inputs, sends, late_sends = tie(inputs, sends, [s[1] for s in late])
     got = []
     for s, x in zip(steps, sends):
         if isinstance(s, Reduction):
@@ -660,6 +975,7 @@
             got.append(s.start())
         else:
             got.append(s[0](x))
+    later = [s[0](x) for s, x in zip(late, late_sends)]
     out = compute(*inputs)
     out, got = tie(out, got)
     moved = []
@@ -668,214 +984,196 @@
             s.take(x)
         else:
             moved.append(x)
-    return out, moved
+    return out, moved + later
 
 
 def paired_device(n_dp, *args):
     (block_in, ln1_scale, ln1_shift, qkv_weight, qkv_bias, out_weight, out_bias) = args[:7]
     (ln2_scale, ln2_shift, up_weight, up_bias, down_weight, down_bias, out_grad) = args[7:]
     move = Paired(n_dp)
-    f32 = lambda v: v.astype(F32)
+    row = lambda v: v.astype(F32)[None, :]
     width, _, part = qkv_weight.shape
     tokens = block_in.shape[0]
     pairs = part // LANES
-    ln1_gain, ln2_gain = f32(ln1_scale), f32(ln2_scale)
+    half = pairs // 2
+    cols = half * LANES
     table = move.table()
-
+    low_product = lambda a, b: dot_tn(a, b).astype(BF)
+
+    qkv_own = jnp.transpose(qkv_weight, (1, 0, 2))
     small = jnp.concatenate([qkv_bias.reshape(3 * part), up_bias])
-    qkv_piece = move.piece(qkv_weight).reshape(width // n_dp, 3 * part)
-    qkv_piece, small, block_in = tie(qkv_piece, small, block_in)
+    qkv_piece = move.piece(qkv_own, 1)
+    block_in = move.swap_rows(block_in)
+    tables = rotary_tables(move.first, tokens)
+    qkv_piece, tables = tie(qkv_piece, tables)
     qkv_got = move.over_y(qkv_piece)
     small_got = move.over_y(small)
-    block_in = move.swap_rows(block_in)
-    qkv_bs = [v[: 3 * part] for v in (small, small_got)]
-    up_bs = [v[3 * part :] for v in (small, small_got)]
-    tables = rotary_tables(move.first, tokens)
-    qkv_own = qkv_weight.reshape(width, 3 * part)
-    qkv_oth = move.spread(qkv_got)
-    x_rows = f32(block_in)
-    normed1, normal1, inv_one = norm_parts(x_rows, ln1_gain, f32(ln1_shift))
-    q_own, kv_own = qkv_rows(normed1, qkv_own, f32(qkv_bs[0])[None, :], tables)
-    rest = [move.piece(w) for w in (out_weight, up_weight, down_weight)]
-    (q_oth, kv_oth), (rest, kv_got) = beside(
-        lambda n, w: qkv_rows(n, w, f32(qkv_bs[1])[None, :], tables),
-        (normed1, qkv_oth),
+    qkv_bs = [row(v[: 3 * part]) for v in (small, small_got)]
+    up_bs = [row(v[3 * part :]) for v in (small, small_got)]
+    qkv_own = qkv_own[None]
+    qkv_oth = lax.all_gather(qkv_got, "dp")
+    rest = [move.piece(up_weight), jnp.concatenate([move.piece(w) for w in (out_weight, down_weight)])]
+    normed1, normed1_t = norm_rows(block_in, row(ln1_scale), row(ln1_shift))
+    (q_own, kv_own), (rest,) = beside(
+        lambda n: qkv_rows(n, qkv_own, qkv_bs[0], tables),
+        (normed1,),
         (lambda ws: [move.over_y(w) for w in ws], rest),
-        (move.over_core, kv_own),
-    )
-    kvs_own = [kv_own, kv_got]
-    spread = [move.spread(got) for got in rest]
-    (out_own, log_own), (kv_got, grad_low) = beside(
-        attend, (q_own, kvs_own), (move.over_core, kv_oth), (move.swap_rows, out_grad)
+    )
+    kvs_own = [kv_own, move.over_core(kv_own)]
+    up_got, mixed_got = (lax.all_gather(got, "dp") for got in rest)
+    (out_a, log_a), _ = beside(lambda q, kvs: attend(q, kvs, 0, half), (q_own, kvs_own))
+    qkv_oth, out_a, out_grad = tie(qkv_oth, out_a, out_grad)
+    q_oth, kv_oth = qkv_rows(normed1, qkv_oth, qkv_bs[1], tables)
+    (out_b, log_b), (kv_got, grad_low) = beside(
+        lambda q, kvs: attend(q, kvs, half, half),
+        (q_own, kvs_own),
+        (move.over_core, kv_oth),
+        late=[(move.swap_rows, out_grad)],
     )
     kvs_oth = [kv_oth, kv_got]
-    out_ws, up_ws, down_ws = (
-        [w, got] for w, got in zip((out_weight, up_weight, down_weight), spread)
-    )
-    out_oth, log_oth = attend(q_oth, kvs_oth)
-    grad_rows = f32(grad_low)
-    outs = [out_own, out_oth]
-
-    branch_one = sum(dot_nn(o, w) for o, w in zip(outs, out_ws)) + f32(out_bias)
-    resid = x_rows + branch_one
-    normed2, normal2, inv_two = norm_parts(resid, ln2_gain, f32(ln2_shift))
-    acts, slopes = [], []
-    for weight, bias in zip(up_ws, up_bs):
-        acted, slope = up_rows(normed2, weight, f32(bias)[None, :])
-        acts.append(acted)
-        slopes.append(slope)
-    branch_two = sum(dot_nn(a, w) for a, w in zip(acts, down_ws)) + f32(down_bias)
-    block_out = (resid + branch_two).astype(BF)
-    down_bias_grad = jnp.sum(grad_rows, 0)
-    low_product = lambda a, b: dot_tn(a, b).astype(BF)
+    (out_oth, log_oth), _ = beside(attend, (q_oth, kvs_oth))
+    out_rows = part // n_dp
+    out_got = mixed_got[:, :out_rows].reshape(part, width)
+    up_ws = [up_weight, up_got.reshape(up_weight.shape)]
+    down_ws = [(down_weight[None], 0), (mixed_got, out_rows)]
+    outs = [out_a, out_b, out_oth]
+    out_ws = [out_weight[:cols], out_weight[cols:], out_got]
+
+    resid, normed2, normed2_t = project_rows(
+        block_in, row(out_bias), row(ln2_scale), row(ln2_shift), outs, out_ws
+    )
+    acts, slopes = zip(*[up_rows(normed2, w, b) for w, b in zip(up_ws, up_bs)])
+    block_out = down_rows(resid, row(down_bias), acts, down_ws)
     down_grads, (block_out,) = beside(
         lambda xs, g: [low_product(a, g) for a in xs],
         (acts, grad_low),
-        (move.swap_rows, block_out),
+        late=[(move.swap_rows, block_out)],
     )
     down = Reduction(move, table, *down_grads)
-    (hg_own, up_b_own), _ = beside(hidden_grads, (grad_low, down_ws[0], slopes[0]), down)
+    (hg_own, up_b_own), _ = beside(
+        lambda g, slope: hidden_grads(g, down_ws[0], slope), (grad_low, slopes[0]), down
+    )
 
     def others(g, hg_own):
         hg_oth, up_b_oth = hidden_grads(g, down_ws[1], slopes[1])
-        return hg_oth, up_b_oth, [low_product(normed2, h) for h in (hg_own, hg_oth)]
+        return hg_oth, up_b_oth, [dot_nn(normed2_t, h).astype(BF) for h in (hg_own, hg_oth)]
 
     (hg_oth, up_b_oth, up_grads), _ = beside(others, (grad_low, hg_own), down)
-    hidden_gs = [hg_own, hg_oth]
     up = Reduction(move, table, *up_grads)
-
-    def middle(hidden_gs, grad_rows, normal2):
-        normed2_grad = sum(dot_nt(hg, w) for hg, w in zip(hidden_gs, up_ws))
-        resid_part, scale_grad, shift_grad = norm_back(normed2_grad, normal2, inv_two, ln2_gain)
-        resid_grad = grad_rows + resid_part
-        branch_grad = resid_grad.astype(BF)
-        bias_grad = jnp.sum(branch_grad, 0, dtype=F32)
-        return resid_grad, branch_grad, scale_grad, shift_grad, bias_grad
-
-    (resid_grad, branch_grad, ln2_scale_grad, ln2_shift_grad, out_bias_grad), _ = beside(
-        middle, (hidden_gs, grad_rows, normal2), up, down
-    )
-    (out_w_grads, out_gs), _ = beside(
-        lambda xs, g: ([low_product(o, g) for o in xs], [dot_nt(g, w).astype(BF) for w in out_ws]),
-        (outs, branch_grad),
-        down,
-    )
+    (branch_grad, sums_two), _ = beside(
+        lambda *hs: middle_rows(resid, grad_low, row(ln2_scale), hs, up_ws), (hg_own, hg_oth), up, down
+    )
+
+    def projected(outs, g):
+        own = jnp.concatenate([low_product(o, g) for o in outs[:2]])
+        out_w_grads = own, low_product(outs[2], g)
+        return out_w_grads, [dot_nt(g, w).astype(BF) for w in out_ws]
+
+    (out_w_grads, out_gs), _ = beside(projected, (outs, branch_grad), down)
     proj = Reduction(move, table, *out_w_grads)
 
-    def back(which, skip, count):
-        q, kvs, log = ((q_own, kvs_own, log_own), (q_oth, kvs_oth, log_oth))[which]
-        inputs = q, out_gs[which], outs[which], log, kvs
-        return lambda *xs: attend_back(*xs, tables, skip, count), inputs
+    def back(which):
+        own = which >= 2
+        lo = (which % 2) * half
+        q, kvs = (q_own, kvs_own) if own else (q_oth, kvs_oth)
+        out, log, grad = (
+            (outs[which - 2], (log_a, log_b)[which - 2], out_gs[which - 2])
+            if own
+            else (out_oth, log_oth, out_gs[2])
+        )
+        inputs = q, grad, out, log, kvs
+        at = 0 if own else lo
+        return lambda *xs: attend_back(*xs, tables, lo, half, at), inputs
 
     def keys_of(x):
         return lambda xs: [move.over_core(g) for g in xs], [x[1][1], x[2][1]]
 
-    def finish(parts, gots):
-        dk = [key_sum(p[1][0], g[0], tables) for p, g in zip(parts, gots)]
-        dv = [p[2][0] + g[1] for p, g in zip(parts, gots)]
-        rows = jnp.concatenate([p[0] for p in parts] + dk + dv, axis=1)
-        return rows, low_product(normed1, rows)
-
-    half = pairs // 2
-    first, _ = beside(*back(1, 0, half), up, down, proj)
-    (down_block, first) = tie(down.done, first)
+    def unit(x, got):
+        keep, send, dk, dv, sums = unit_grads(
+            move.blocks, normed1_t, x[0], x[1][0], got[0], x[2][0], got[1], tables
+        )
+        return keep, send, (x[0], dk, dv), sums[0]
+
+    level = lambda n: functools.partial(move.over_chip, level=n)
+
+    def halves(total):
+        return total[: total.shape[0] // 2], total[total.shape[0] // 2 :]
+
+    oth_a, _ = beside(*back(0), up, down, proj)
+    down_block, oth_a, block_out = tie(down.done, oth_a, block_out)
     down_all = move.gather(down_block)
-    second, (first_got,) = beside(*back(1, half, half), keys_of(first), up, proj)
-    third, (second_got,) = beside(*back(0, 0, half), keys_of(second), up, proj)
-    (rows_oth, w_oth), (third_got,) = beside(
-        lambda *x: finish(*x), ((first, second), (first_got, second_got)), keys_of(third), up, proj
-    )
-    up_block, third, down_all = tie(up.done, third, down_all)
-    up_all = move.gather(up_block)
-    (rows_a, w_a), (oth_got,) = beside(
-        lambda *x: finish(*x), ((third,), (third_got,)), (move.over_core, move.core_send(w_oth)), proj
-    )
-    out_block, w_a = tie(proj.done, w_a)
-    out_all = move.gather(out_block)
-    chips = n_dp // 2
-
-    def keep_of(half):
-        blocks = half.reshape(chips, 2, half.shape[0] // n_dp, half.shape[1])
-        return lax.dynamic_index_in_dim(blocks, move.core, 1, keepdims=False)
-
-    fourth, (oth_got, a_got) = beside(
-        *back(0, half, half),
-        (move.over_y, keep_of(w_oth) + oth_got),
-        (move.over_core, move.core_send(w_a)),
-    )
-
-    def columns(x, lo, hi):
-        x = x.reshape(*x.shape[:-1], 3, part)
-        return x[..., lo * LANES : hi * LANES].reshape(*x.shape[:-2], -1)
-
-    def chip_split(total, level):
-        bit = (move.me_dp >> (level + 1)) & 1
-        blocks = total.reshape(total.shape[0] // 2, 2, *total.shape[1:])
-        take = lambda b: lax.dynamic_index_in_dim(blocks, b, 1, keepdims=False)
-        return take(bit), take(1 - bit)
-
-    over_chip = lambda x, level: move.move(x, lambda dp, y: (dp ^ (2 << level), y))
-    total_a = keep_of(w_a) + a_got + columns(oth_got, 0, half)
-    keep_a, send_a = chip_split(total_a, 0)
-    normed1_part, (fourth_got, a_got) = beside(
-        lambda a, b: dot_nt(a, qkv_oth), (rows_oth, rows_a), keys_of(fourth), (lambda x: over_chip(x, 0), send_a)
-    )
-    keep_a, send_a = chip_split(keep_a + a_got, 1)
-    (rows_b, w_b), (a_got,) = beside(
-        lambda *x: finish(*x), ((fourth,), (fourth_got,)), (lambda x: over_chip(x, 1), send_a)
-    )
-    keep_a, send_a = chip_split(keep_a + a_got, 2)
-    own_cols = lambda lo, hi: columns(qkv_own, lo, hi)
-
-    def last(rows_a, rows_b, part_sum):
-        normed1_grad = part_sum + dot_nt(rows_a, own_cols(0, half)) + dot_nt(rows_b, own_cols(half, pairs))
-        input_part, scale_grad, shift_grad = norm_back(normed1_grad, normal1, inv_one, ln1_gain)
-        return (resid_grad + input_part).astype(BF), scale_grad, shift_grad
-
-    (in_grad, ln1_scale_grad, ln1_shift_grad), (b_got, a_got) = beside(
-        last,
-        (rows_a, rows_b, normed1_part),
-        (move.over_core, move.core_send(w_b)),
-        (lambda x: over_chip(x, 2), send_a),
-    )
-    total_a = keep_a + a_got
-    total_b = keep_of(w_b) + b_got + columns(oth_got, half, pairs)
+    oth_b, (got,) = beside(*back(1), keys_of(oth_a), up, proj)
+    keep_oth_a, send, parts_oth_a, bias_oth_a = unit(oth_a, got)
+    own_a, (got, core_got) = beside(*back(2), keys_of(oth_b), (move.over_core, send), up, proj)
+    y_send = keep_oth_a + core_got
+    (keep_oth_b, send, parts_oth_b, bias_oth_b), (key_got, y_got_a) = beside(
+        unit, (oth_b, got), keys_of(own_a), proj, late=[(move.over_y, y_send)]
+    )
+    (keep_a, send_a, parts_a, bias_a), (core_got,) = beside(
+        unit, (own_a, key_got), (move.over_core, send), up, proj
+    )
+    mixed = jnp.concatenate([up.done[0], proj.done[0].reshape(-1, up.done.shape[2])])
+    mixed, keep_a, down_all = tie(mixed, keep_a, down_all)
+    mixed_all = lax.all_gather(mixed, "dp")
+    own_b, (core_got_a, y_got_a, y_got_b) = beside(
+        *back(3),
+        (move.over_core, send_a),
+        (lambda x: x, y_got_a),
+        late=[(move.over_y, keep_oth_b + core_got)],
+    )
+    keep_a, send_a = halves(keep_a + core_got_a + y_got_a)
+    partial, (key_got, a_got) = beside(
+        lambda *ps: early_rows(qkv_own, qkv_oth, *ps),
+        (parts_a, (parts_oth_a, parts_oth_b)),
+        keys_of(own_b),
+        late=[(level(0), send_a)],
+    )
+    (keep_b, send_b, parts_b, bias_b), (a_got, y_got_b) = beside(
+        unit, (own_b, key_got), (lambda x: x, a_got), (lambda x: x, y_got_b)
+    )
+    keep_a, send_a = halves(keep_a + a_got)
+    (in_grad, sums_one), (core_got, a_got) = beside(
+        lambda *xs: last_rows(block_in, branch_grad, row(ln1_scale), *xs),
+        (partial, qkv_own, parts_b),
+        (move.over_core, send_b),
+        (level(1), send_a),
+    )
+    keep_a, send_a = halves(keep_a + a_got)
+    keep_b, send_b = halves(keep_b + core_got + y_got_b)
+    in_grad, send_a, send_b, mixed_all = tie(in_grad, send_a, send_b, mixed_all)
     in_grad = move.swap_rows(in_grad)
-    for level in range(chips.bit_length() - 1):
-        keep_b, send_b = chip_split(total_b, level)
-        total_b = keep_b + over_chip(send_b, level)
-    three = lambda x: x.reshape(x.shape[1], 3, -1)
-    merged = jnp.concatenate([three(total_a), three(total_b)], axis=2).reshape(1, -1, 3 * part)
-    qkv_g = move.gather(merged)
-    colsum = lambda g: jnp.sum(g, 0, dtype=F32)
-    b_own = jnp.concatenate(
-        [colsum(g).reshape(3, -1) for g in (rows_a, rows_b)], axis=1
-    ).reshape(-1)
+    total_a = keep_a + move.over_chip(send_a, 2)
+    unit_a = lax.all_gather(total_a[0], "dp")
+    total_b = keep_b + move.over_chip(send_b, 0)
+    levels = (n_dp // 2).bit_length() - 1
+    for n in range(1, levels):
+        keep_b, send_b = halves(total_b)
+        total_b = keep_b + move.over_chip(send_b, n)
+    for n in reversed(range(levels)):
+        total_b = jnp.concatenate([total_b, move.over_chip(total_b, n)])
+    total_b = jnp.concatenate([total_b, move.over_core(total_b)])
+    qkv_g = jnp.transpose(widen(move.blocks, unit_a, total_b), (1, 0, 2))
+    up_rows_each = width // n_dp
+    up_all = mixed_all[:, :up_rows_each].reshape(width, -1)
+    out_all = mixed_all[:, up_rows_each:].reshape(part, width)
+    side = lambda a, b: jnp.concatenate([a.reshape(3, cols), b.reshape(3, cols)], axis=1).reshape(-1)
     vec, flat = move.reduce_vectors(
-        jnp.stack(
-            [
-                ln1_scale_grad,
-                ln1_shift_grad,
-                out_bias_grad,
-                ln2_scale_grad,
-                ln2_shift_grad,
-                down_bias_grad,
-            ]
-        ),
-        jnp.concatenate([b_own, up_b_own[0]]),
-        jnp.concatenate([colsum(rows_oth), up_b_oth[0]]),
-    )
+        jnp.concatenate([sums_one[:2], sums_two[:4]]),
+        jnp.concatenate([side(bias_a, bias_b), up_b_own[0]]),
+        jnp.concatenate([side(bias_oth_a, bias_oth_b), up_b_oth[0]]),
+    )
+    f32 = lambda v: v.astype(F32)
     return (
         block_out,
         in_grad,
         vec[0],
         vec[1],
-        f32(qkv_g).reshape(width, 3, part),
+        qkv_g,
         flat[: 3 * part].reshape(3, part),
         f32(out_all),
+        vec[4],
         vec[2],
         vec[3],
-        vec[4],
         f32(up_all),
         flat[3 * part :],
         f32(down_all),

time: 719 us -> 656 us (0.912)
  matrix products: 110 us -> 29.6 us
  Pallas kernels: 271 us -> 333 us
  other arithmetic: 80.2 us -> 38.4 us
  starting transfers between devices: 64.1 us -> 92.7 us
  local copies, waits for them, and re-layouts: 60.2 us -> 43.3 us
  waiting for transfers between devices: 107 us -> 95.1 us
    pallas_call x12 -> x20, Pallas kernels: 203 us -> 271 us  [the longest x4 97.3 us: attend_back(): call(functools.partial(attend_back_kernel, sources=len(kvs), keys_at=1024...]
    ppermute x55 -> x60, starting transfers between devices: 63.5 us -> 92.3 us  [move(): return lax.ppermute(x, ('dp', 'tensor'), pairs)]
    dot_general x7 -> x3, matrix products: 33.2 us -> 5.35 us  [dot_nt(): lax.dot_general(left, right, (((1,), (1,)), ((), ())), preferred_element_...]
    dot_general x9 -> x5, matrix products: 40.1 us -> 12.5 us  [dot_tn(): lax.dot_general(left, right, (((0,), (0,)), ((), ())), preferred_element_...]
    dot_general x4 -> x2, matrix products: 37.1 us -> 11.8 us  [dot_nn(): lax.dot_general(left, right, (((1,), (0,)), ((), ())), preferred_element_...]
    reshape x11 -> x6, local copies, waits for them, and re-layouts: 18.3 us -> 0.07 us  [the longest x1 0.03 us: reduce_vectors(): both = both.reshape(k, 2, width // 2)]
    reduce_sum x8 -> x0, other arithmetic: 13.2 us -> none  [the longest x3 5.93 us: paired_device(): colsum = lambda g: jnp.sum(g, 0, dtype=F32)]
    all_gather x4 -> x5, waiting for transfers between devices: 24.5 us -> 13.5 us  [the longest x2 13.5 us: paired_device(): up_got, mixed_got = (lax.all_gather(got, 'dp') for got in rest)]
  transfers between devices with their start and end apart: 63 -> 66, of which waited for: 18 -> 20; matrix products, arithmetic and copies ran while one was open for 25% -> 10% of each run, Pallas kernels for 37% -> 49%
where the time goes in v4:
time: 656 us; the launch traced here: 648 us
  Pallas kernels  333 us (51%)
  waiting for transfers between devices  95.1 us (14%)
  starting transfers between devices  92.7 us (14%)
  local copies, waits for them, and re-layouts  43.3 us (7%)
  other arithmetic  38.4 us (6%)
  matrix products  29.6 us (5%)
  between operations  15.9 us (2%)
    pallas_call x4, Pallas kernels, attend_back(): call(functools.partial(attend_back_kernel, sources=len(kvs), keys_at=1024...  97.3 us
    ppermute x60, starting transfers between devices, move(): return lax.ppermute(x, ('dp', 'tensor'), pairs)  92.3 us
    ppermute x60, waiting for transfers between devices, move(): return lax.ppermute(x, ('dp', 'tensor'), pairs)  80.9 us
    pallas_call x3, Pallas kernels, attend(): call(functools.partial(attend_kernel, sources=len(kvs), rows_at=min(512,...  48.8 us
    pallas_call x4, Pallas kernels, unit_grads(): pl.pallas_call(functools.partial(unit_kernel, chips=chips), grid_spec=plt...  33.1 us
    pallas_call x2, Pallas kernels, up_rows(): call(up_kernel, 2 * tokens * width * cols, 2 * (tokens * width + width *...  22.9 us
    pallas_call x2, Pallas kernels, qkv_rows(): call(functools.partial(qkv_kernel, q_steps=q_steps), 2 * tokens * width *...  21.3 us
    pallas_call x2, Pallas kernels, hidden_grads(): call(functools.partial(hidden_grad_kernel, skip=skip), 2 * tokens * width...  20 us
  transfers between devices with their start and end apart: 66, of which 20 were waited for; matrix products, arithmetic and copies ran while one was open for 10% of the time, Pallas kernels for 49%

profile of v4, /device:TPU:0, one launch (start us, length us, event | category | flops | bytes accessed | tf_op | source)
XLA Modules:
  0.0 647.6 jit_solution(5384888500245814801)
XLA Ops:
  8.3 4.4 fusion.1
  12.7 3.0 collective-permute-start.1
  15.7 4.9 collective-permute-done.1
  21.4 2.3 collective-permute-start
  28.1 4.9 shard_map.326
  33.0 23.9 %collective-permute-start.3 = (bf16[160,1024]{1,0:T(8,128)(2,1)S(1)}, bf16[160,1024]{1,0:T(8,128)(2,1)S(1)}, u32[]{:S(2)}, u32[]{:S(2)}) collective-permute-start(bf16[160,1024]{1,0:T(8,128)(2,1)S(1)} %pad_maximum_fusion.3), channel_id=1, source_target_pairs={{0,1},{1,0},{2,3},{3,2},{4,5},{5,4},{6,7},{7,6},{8,9},{9,8},{10,11... | collective-permute-start | bytes 983048 | tf_op jit(solution)/shard_map/ppermute | solution.py:753
  57.5 10.6 %shard_map.327 = (bf16[1024,512]{1,0:T(8,128)(2,1)}, bf16[1024,1024]{1,0:T(8,128)(2,1)}) custom-call(bf16[1024,1024]{1,0:T(8,128)(2,1)} %get-tuple-element.337.n_ref, bf16[1,3,1024,512]{3,2,1,0:T(8,128)(2,1)} %bitcast.116, f32[1,1536]{1,0:T(1,128)} %bitcast.135, f32[1024,128]{1,0:T(8,128)} %get-tuple-element.338.c_ref.refs_4_, ...), custom_call_target="tpu_custom_call" | custom-call | flops 3221225472 | bytes 8388608 | tf_op jit(solution)/shard_map/pallas_call | solution.py:140
  68.1 2.4 collective-permute-done.2
  72.7 3.4 collective-permute-done.5
  76.8 12.7 %shard_map.328 = (bf16[1024,256]{1,0:T(8,128)(2,1)}, f32[2,2,1024]{2,1,0:T(2,128)}) custom-call(bf16[1024,512]{1,0:T(8,128)(2,1)} %get-tuple-element.570.refs_0_, bf16[1024,1024]{1,0:T(8,128)(2,1)} %get-tuple-element.574.refs_1_.refs_3_.refs_7_.refs_9_, bf16[1024,1024]{1,0:T(8,128)(2,1)} %collective-permute-done.4.refs_2_.refs_4_.refs_8_.refs_10_, ...), custom_call_target="tpu_custom_call" | custom-call | flops 8589934592 | bytes 3145728 | tf_op jit(solution)/shard_map/pallas_call | solution.py:208
  89.5 10.7 %shard_map.329 = (bf16[1024,512]{1,0:T(8,128)(2,1)}, bf16[1024,1024]{1,0:T(8,128)(2,1)}) custom-call(bf16[1024,1024]{1,0:T(8,128)(2,1)} %get-tuple-element.337.n_ref, bf16[16,3,64,512]{3,2,1,0:T(8,128)(2,1)} %bitcast.141, f32[1,1536]{1,0:T(1,128)} %reshape.253.b_ref, f32[1024,128]{1,0:T(8,128)} %get-tuple-element.338.c_ref.refs_4_, ...), custom_call_target="tpu_custom_call" | custom-call | flops 3221225472 | bytes 8388608 | tf_op jit(solution)/shard_map/pallas_call | solution.py:140
  105.0 2.5 collective-permute-start.7
  107.4 12.7 %shard_map.330 = (bf16[1024,256]{1,0:T(8,128)(2,1)}, f32[2,2,1024]{2,1,0:T(2,128)}) custom-call(bf16[1024,512]{1,0:T(8,128)(2,1)} %get-tuple-element.570.refs_0_, bf16[1024,1024]{1,0:T(8,128)(2,1)} %get-tuple-element.574.refs_1_.refs_3_.refs_7_.refs_9_, bf16[1024,1024]{1,0:T(8,128)(2,1)} %collective-permute-done.4.refs_2_.refs_4_.refs_8_.refs_10_, ...), custom_call_target="tpu_custom_call" | custom-call | flops 8589934592 | bytes 3145728 | tf_op jit(solution)/shard_map/pallas_call | solution.py:208
  120.1 23.5 %shard_map.331 = (bf16[1024,512]{1,0:T(8,128)(2,1)}, f32[4,2,1024]{2,1,0:T(2,128)}) custom-call(bf16[1024,512]{1,0:T(8,128)(2,1)} %get-tuple-element.465.refs_0_, bf16[1024,1024]{1,0:T(8,128)(2,1)} %get-tuple-element.469.refs_1_.refs_3_.refs_7_.refs_9_, bf16[1024,1024]{1,0:T(8,128)(2,1)} %collective-permute-done.6.refs_2_.refs_4_.refs_8_.refs_10_, ...), custom_call_target="tpu_custom_call" | custom-call | flops 17179869184 | bytes 6291456 | tf_op jit(solution)/shard_map/pallas_call | solution.py:208
  143.6 2.3 slice.212
  145.9 7.9 %shard_map.332 = (f32[1024,1024]{1,0:T(8,128)}, bf16[1024,1024]{1,0:T(8,128)(2,1)}, bf16[1024,1024]{1,0:T(8,128)(2,1)}) custom-call(bf16[1024,1024]{1,0:T(8,128)(2,1)} %copy-done.7, f32[1,1024]{1,0:T(1,128)} %bitcast.139, f32[1,1024]{1,0:T(1,128)} %bitcast.136, f32[1,1024]{1,0:T(1,128)} %bitcast.140, bf16[1024,256]{1,0:T(8,128)(2,1)} %get-tuple-element.496.refs_4_.refs_2_, ...), custom_call_target="tpu_custom_call" | custom-call | flops 2147483648 | bytes 14680064 | tf_op jit(solution)/shard_map/pallas_call | solution.py:449
  153.8 11.9 %shard_map.333 = (bf16[1024,2048]{1,0:T(8,128)(2,1)}, bf16[1024,2048]{1,0:T(8,128)(2,1)}) custom-call(bf16[1024,1024]{1,0:T(8,128)(2,1)} %get-tuple-element.369.n_ref, bf16[1024,2048]{1,0:T(8,128)(2,1)} %refs_2_.1, f32[1,2048]{1,0:T(1,128)} %bitcast.133), custom_call_target="tpu_custom_call" | custom-call | flops 4294967296 | bytes 14680064 | tf_op jit(solution)/shard_map/pallas_call | solution.py:361
  165.8 13.5 %all-gather.18.cloned.1.call-done.w_ref.refs_3_ = bf16[1024,2048]{1,0:T(8,128)(2,1)} async-done(((bf16[64,2048]{1,0:T(8,128)(2,1)}), bf16[1024,2048]{1,0:T(8,128)(2,1)}) %all-gather.18.cloned.1.call-update) | async-done | bytes 4194320 | tf_op jit(solution)/shard_map/all_gather | solution.py:1023
  179.2 11.0 %shard_map.334 = (bf16[1024,2048]{1,0:T(8,128)(2,1)}, bf16[1024,2048]{1,0:T(8,128)(2,1)}) custom-call(bf16[1024,1024]{1,0:T(8,128)(2,1)} %get-tuple-element.369.n_ref, bf16[1024,2048]{1,0:T(8,128)(2,1)} %all-gather.18.cloned.1.call-done.w_ref.refs_3_, f32[1,2048]{1,0:T(1,128)} %bitcast.134), custom_call_target="tpu_custom_call" | custom-call | flops 4294967296 | bytes 14680064 | tf_op jit(solution)/shard_map/pallas_call | solution.py:361
  190.2 15.5 %shard_map.335 = bf16[1024,1024]{1,0:T(8,128)(2,1)} custom-call(f32[1024,1024]{1,0:T(8,128)} %get-tuple-element.374.r_ref, f32[1,1024]{1,0:T(1,128)} %bitcast.138, bf16[1024,2048]{1,0:T(8,128)(2,1)} %get-tuple-element.375.refs_0_, bf16[1024,2048]{1,0:T(8,128)(2,1)} %get-tuple-element.377.refs_1_, bf16[1,2048,1024]{2,1,0:T(8,128)(2,1)} %bitcast.129, ...), custom_call_target="tpu_custom_call" | custom-call | flops 8589934592 | bytes 23068672 | tf_op jit(solution)/shard_map/pallas_call | solution.py:479
  205.8 4.8 convolution_convert_fusion.3
  210.6 4.9 convolution_convert_fusion.2
  220.9 9.7 %shard_map.336 = (bf16[1024,2048]{1,0:T(8,128)(2,1)}, f32[1,2048]{1,0:T(1,128)}) custom-call(bf16[1024,1024]{1,0:T(8,128)(2,1)} %copy-done.60, bf16[1,2048,1024]{2,1,0:T(8,128)(2,1)} %bitcast.130, bf16[1024,2048]{1,0:T(8,128)(2,1)} %get-tuple-element.382.slope_ref), custom_call_target="tpu_custom_call" | custom-call | flops 4294967296 | bytes 14680064 | tf_op jit(solution)/shard_map/pallas_call | solution.py:396
  231.9 6.5 %shard_map.337 = (bf16[4,128,1024]{2,1,0:T(8,128)(2,1)}, bf16[4,128,1024]{2,1,0:T(8,128)(2,1)}, bf16[4,128,1024]{2,1,0:T(8,128)(2,1)}, bf16[4,128,1024]{2,1,0:T(8,128)(2,1)}) custom-call(s32[9]{0:T(128)} %pad_add_fusion.t_ref, bf16[8,2,128,1024]{3,2,1,0:T(8,128)(2,1)} %bitcast.95, bf16[8,2,128,1024]{3,2,1,0:T(8,128)(2,1)} %bitcast.96, ...), custom_call_target="tpu_custom_call" | custom-call | flops 2097152 | bytes 12582912 | tf_op jit(solution)/shard_map/pallas_call | solution.py:715
  240.6 10.3 %shard_map.338 = (bf16[1024,2048]{1,0:T(8,128)(2,1)}, f32[1,2048]{1,0:T(1,128)}) custom-call(bf16[1024,1024]{1,0:T(8,128)(2,1)} %copy-done.60, bf16[16,160,1024]{2,1,0:T(8,128)(2,1)} %bitcast.123, bf16[1024,2048]{1,0:T(8,128)(2,1)} %get-tuple-element.394.slope_ref), custom_call_target="tpu_custom_call" | custom-call | flops 4294967296 | bytes 14680064 | tf_op jit(solution)/shard_map/pallas_call | solution.py:396
  250.8 7.1 %convolution_convert_fusion = bf16[1024,2048]{1,0:T(8,128)(2,1)S(1)} fusion(bf16[1024,1024]{1,0:T(8,128)(2,1)S(1)} %copy-done.69, bf16[1024,2048]{1,0:T(8,128)(2,1)} %get-tuple-element.408.refs_1_), kind=kOutput, calls=%fused_computation.1 | convolution fusion | flops 4297064448 | bytes 10485760 | tf_op jit(solution)/shard_map/dot_general | solution.py:32
  257.9 4.8 convolution_convert_fusion.1
  262.8 2.0 collective-permute-done.11
  270.0 17.6 %shard_map.339 = (bf16[1024,1024]{1,0:T(8,128)(2,1)}, f32[8,1024]{1,0:T(8,128)}) custom-call(f32[1024,1024]{1,0:T(8,128)} %get-tuple-element.374.r_ref, bf16[1024,1024]{1,0:T(8,128)(2,1)} %copy-done.60, f32[1,1024]{1,0:T(1,128)} %bitcast.137, bf16[1024,2048]{1,0:T(8,128)(2,1)} %get-tuple-element.407.refs_0_, bf16[1024,2048]{1,0:T(8,128)(2,1)} %get-tuple-element.408.refs_1_, ...), custom_call_target="tpu_custom_call" | custom-call | flops 8589934592 | bytes 25165824 | tf_op jit(solution)/shard_map/pallas_call | solution.py:518
  288.5 2.9 add_add_fusion.1
  292.3 2.3 convolution_convert_fusion.4.refs_1_
  300.7 6.6 %shard_map.340 = (bf16[4,64,2048]{2,1,0:T(8,128)(2,1)}, bf16[4,64,2048]{2,1,0:T(8,128)(2,1)}, bf16[4,64,2048]{2,1,0:T(8,128)(2,1)}, bf16[4,64,2048]{2,1,0:T(8,128)(2,1)}) custom-call(s32[9]{0:T(128)} %pad_add_fusion.t_ref, bf16[8,2,64,2048]{3,2,1,0:T(8,128)(2,1)} %bitcast.104, bf16[8,2,64,2048]{3,2,1,0:T(8,128)(2,1)} %bitcast.105, ...), custom_call_target="tpu_custom_call" | custom-call | flops 2097152 | bytes 12582912 | tf_op jit(solution)/shard_map/pallas_call | solution.py:715
  309.8 3.3 collective-permute-done.15
  315.2 2.2 collective-permute-start.21
  318.8 9.1 %collective-permute-done.18 = bf16[1,128,1024]{2,1,0:T(8,128)(2,1)S(1)} collective-permute-done((bf16[1,128,1024]{2,1,0:T(8,128)(2,1)S(1)}, bf16[1,128,1024]{2,1,0:T(8,128)(2,1)S(1)}, u32[]{:S(2)}, u32[]{:S(2)}) %collective-permute-start.18) | collective-permute-done | bytes 262176 | tf_op jit(solution)/shard_map/ppermute | solution.py:753
  328.0 24.5 %shard_map.341 = (bf16[1024,256]{1,0:T(8,128)(2,1)}, bf16[1024,256]{1,0:T(8,128)(2,1)}, bf16[1024,256]{1,0:T(8,128)(2,1)}, bf16[1024,256]{1,0:T(8,128)(2,1)}, bf16[1024,256]{1,0:T(8,128)(2,1)}) custom-call(bf16[1024,512]{1,0:T(8,128)(2,1)} %get-tuple-element.465.refs_0_, bf16[1024,512]{1,0:T(8,128)(2,1)} %convolution_convert_fusion.4.refs_1_, ...), custom_call_target="tpu_custom_call" | custom-call | flops 21474836480 | bytes 6291456 | tf_op jit(solution)/shard_map/pallas_call | solution.py:301
  353.8 11.2 %collective-permute-done.17 = bf16[4,64,2048]{2,1,0:T(8,128)(2,1)} collective-permute-done((bf16[4,64,2048]{2,1,0:T(8,128)(2,1)}, bf16[4,64,2048]{2,1,0:T(8,128)(2,1)}, u32[]{:S(2)}, u32[]{:S(2)}) %collective-permute-start.17) | collective-permute-done | bytes 1048608 | tf_op jit(solution)/shard_map/ppermute | solution.py:753
  368.5 4.6 shard_map.342
  375.8 24.3 %shard_map.343 = (bf16[1024,256]{1,0:T(8,128)(2,1)}, bf16[1024,256]{1,0:T(8,128)(2,1)}, bf16[1024,256]{1,0:T(8,128)(2,1)}, bf16[1024,256]{1,0:T(8,128)(2,1)}, bf16[1024,256]{1,0:T(8,128)(2,1)}) custom-call(bf16[1024,512]{1,0:T(8,128)(2,1)} %get-tuple-element.465.refs_0_, bf16[1024,512]{1,0:T(8,128)(2,1)} %convolution_convert_fusion.4.refs_1_, ...), custom_call_target="tpu_custom_call" | custom-call | flops 21474836480 | bytes 6291456 | tf_op jit(solution)/shard_map/pallas_call | solution.py:301
  402.1 8.6 %shard_map.344 = (bf16[8,3,64,256]{3,2,1,0:T(8,128)(2,1)}, bf16[8,3,64,256]{3,2,1,0:T(8,128)(2,1)}, bf16[1024,256]{1,0:T(8,128)(2,1)}, bf16[1024,256]{1,0:T(8,128)(2,1)}, f32[8,768]{1,0:T(8,128)}) custom-call(s32[16]{0:T(128)} %pad_add_fusion.1.t_ref, bf16[1024,1024]{1,0:T(8,128)(2,1)} %get-tuple-element.454.nt_ref, ...), custom_call_target="tpu_custom_call" | custom-call | flops 1610612736 | bytes 7340032 | tf_op jit(solution)/shard_map/pallas_call | solution.py:648
  410.8 2.3 collective-permute-start.31
  414.1 24.1 %shard_map.345 = (bf16[1024,256]{1,0:T(8,128)(2,1)}, bf16[1024,256]{1,0:T(8,128)(2,1)}, bf16[1024,256]{1,0:T(8,128)(2,1)}, bf16[1024,256]{1,0:T(8,128)(2,1)}, bf16[1024,256]{1,0:T(8,128)(2,1)}) custom-call(bf16[1024,512]{1,0:T(8,128)(2,1)} %get-tuple-element.570.refs_0_, bf16[1024,256]{1,0:T(8,128)(2,1)} %convolution_convert_fusion.7.refs_1_, ...), custom_call_target="tpu_custom_call" | custom-call | flops 21474836480 | bytes 6291456 | tf_op jit(solution)/shard_map/pallas_call | solution.py:301
  440.9 8.3 %shard_map.346 = (bf16[8,3,64,256]{3,2,1,0:T(8,128)(2,1)}, bf16[8,3,64,256]{3,2,1,0:T(8,128)(2,1)}, bf16[1024,256]{1,0:T(8,128)(2,1)}, bf16[1024,256]{1,0:T(8,128)(2,1)}, f32[8,768]{1,0:T(8,128)}) custom-call(s32[16]{0:T(128)} %pad_add_fusion.1.t_ref, bf16[1024,1024]{1,0:T(8,128)(2,1)} %get-tuple-element.454.nt_ref, ...), custom_call_target="tpu_custom_call" | custom-call | flops 1610612736 | bytes 7340032 | tf_op jit(solution)/shard_map/pallas_call | solution.py:648
  453.2 8.1 %shard_map.347 = (bf16[8,3,64,256]{3,2,1,0:T(8,128)(2,1)}, bf16[8,3,64,256]{3,2,1,0:T(8,128)(2,1)}, bf16[1024,256]{1,0:T(8,128)(2,1)}, bf16[1024,256]{1,0:T(8,128)(2,1)}, f32[8,768]{1,0:T(8,128)}) custom-call(s32[16]{0:T(128)} %pad_add_fusion.1.t_ref, bf16[1024,1024]{1,0:T(8,128)(2,1)} %get-tuple-element.454.nt_ref, ...), custom_call_target="tpu_custom_call" | custom-call | flops 1610612736 | bytes 7340032 | tf_op jit(solution)/shard_map/pallas_call | solution.py:648
  463.0 5.1 collective-permute-done.36
  470.3 17.9 %collective-permute-done.38 = bf16[8,3,64,256]{3,2,1,0:T(8,128)(2,1)S(1)} collective-permute-done((bf16[8,3,64,256]{3,2,1,0:T(8,128)(2,1)S(1)}, bf16[8,3,64,256]{3,2,1,0:T(8,128)(2,1)S(1)}, u32[]{:S(2)}, u32[]{:S(2)}) %collective-permute-start.38) | collective-permute-done | bytes 786464 | tf_op jit(solution)/shard_map/ppermute | solution.py:753
  489.1 24.3 %shard_map.348 = (bf16[1024,256]{1,0:T(8,128)(2,1)}, bf16[1024,256]{1,0:T(8,128)(2,1)}, bf16[1024,256]{1,0:T(8,128)(2,1)}, bf16[1024,256]{1,0:T(8,128)(2,1)}, bf16[1024,256]{1,0:T(8,128)(2,1)}) custom-call(bf16[1024,512]{1,0:T(8,128)(2,1)} %get-tuple-element.570.refs_0_, bf16[1024,256]{1,0:T(8,128)(2,1)} %convolution_convert_fusion.6.refs_1_, ...), custom_call_target="tpu_custom_call" | custom-call | flops 21474836480 | bytes 6291456 | tf_op jit(solution)/shard_map/pallas_call | solution.py:301
  515.3 10.8 %shard_map.349.part_ref = f32[1024,1024]{1,0:T(8,128)} custom-call(bf16[1,3,1024,512]{3,2,1,0:T(8,128)(2,1)} %bitcast.117, bf16[16,3,64,512]{3,2,1,0:T(8,128)(2,1)} %bitcast.142, bf16[1024,256]{1,0:T(8,128)(2,1)} %get-tuple-element.592.dq_ref.refs_0_, bf16[1024,256]{1,0:T(8,128)(2,1)} %get-tuple-element.593.refs_1_, ...), custom_call_target="tpu_custom_call" | custom-call | flops 4831838208 | bytes 13631488 | tf_op jit(solution)/shard_map/pallas_call | solution.py:573
  527.1 8.1 %shard_map.350 = (bf16[8,3,64,256]{3,2,1,0:T(8,128)(2,1)}, bf16[8,3,64,256]{3,2,1,0:T(8,128)(2,1)}, bf16[1024,256]{1,0:T(8,128)(2,1)}, bf16[1024,256]{1,0:T(8,128)(2,1)}, f32[8,768]{1,0:T(8,128)}) custom-call(s32[16]{0:T(128)} %pad_add_fusion.1.t_ref, bf16[1024,1024]{1,0:T(8,128)(2,1)} %get-tuple-element.454.nt_ref, ...), custom_call_target="tpu_custom_call" | custom-call | flops 1610612736 | bytes 7340032 | tf_op jit(solution)/shard_map/pallas_call | solution.py:648
  537.1 9.0 %shard_map.351 = (bf16[1024,1024]{1,0:T(8,128)(2,1)}, f32[8,1024]{1,0:T(8,128)}) custom-call(bf16[1024,1024]{1,0:T(8,128)(2,1)} %copy-done.7, bf16[1024,1024]{1,0:T(8,128)(2,1)} %get-tuple-element.417.g_ref, f32[1,1024]{1,0:T(1,128)} %bitcast.127, f32[1024,1024]{1,0:T(8,128)} %shard_map.349.part_ref, bf16[1,3,1024,512]{3,2,1,0:T(8,128)(2,1)} %bitcast.118, ...), custom_call_target="tpu_custom_call" | custom-call | flops 1610612736 | bytes 13631488 | tf_op jit(solution)/shard_map/pallas_call | solution.py:590
  555.7 2.3 collective-permute-done.49
  558.0 2.6 collective-permute-start.50
  560.6 6.6 %convert_element_type.89 = f32[2048,1024]{1,0:T(8,128)} convert(bf16[2048,1024]{1,0:T(8,128)(2,1)} %bitcast.115) | non-fusion elementwise | flops 2097152 | bytes 12582912 | tf_op jit(solution)/shard_map/convert_element_type | solution.py:1165
  568.8 2.0 collective-permute-start.54
  570.7 3.9 collective-permute-done.52
  577.0 7.3 %collective-permute-done.55 = bf16[1,3,64,256]{3,2,1,0:T(8,128)(2,1)S(1)} collective-permute-done((bf16[1,3,64,256]{3,2,1,0:T(8,128)(2,1)S(1)}, bf16[1,3,64,256]{3,2,1,0:T(8,128)(2,1)S(1)}, u32[]{:S(2)}, u32[]{:S(2)}) %collective-permute-start.55) | collective-permute-done | bytes 98336 | tf_op jit(solution)/shard_map/ppermute | solution.py:753
  586.1 17.1 %collective-permute-start.46 = (bf16[1024,1024]{1,0:T(8,128)(2,1)}, bf16[1024,1024]{1,0:T(8,128)(2,1)}, u32[]{:S(2)}, u32[]{:S(2)}) collective-permute-start(bf16[1024,1024]{1,0:T(8,128)(2,1)} %get-tuple-element.643), channel_id=1, source_target_pairs={{0,0},{1,2},{2,1},{3,3},{4,4},{5,6},{6,5},{7,7},{8,8},{9,10},{10,9... | collective-permute-start | bytes 6291464 | tf_op jit(solution)/shard_map/ppermute | solution.py:753
  603.2 2.3 collective-permute-start.57
  606.2 4.8 slice.207
  611.0 3.8 collective-permute-start.58
  617.8 2.8 collective-permute-done.58
  620.8 6.7 %bitcast_convert_fusion = f32[1024,2048]{1,0:T(8,128)} fusion(bf16[16,64,2048]{2,1,0:T(8,128)(2,1)} %slice.207), kind=kLoop, calls=%fused_computation | loop fusion | flops 2097152 | bytes 12582912 | tf_op jit(solution)/shard_map/convert_element_type | solution.py:1165
  630.5 5.7 shard_map.352
  637.5 3.1 copy.45
  (372 shorter events, 91.8 us)
Async XLA Ops:
  7.2 82.3 %all-gather.14.cloned.1.call-start = ((), (), s32[]{:S(2)}) async-start(), calls=%async_computation.1 | async-start | bytes 3342336 | tf_op jit(solution)/shard_map/all_gather | solution.py:1014
  12.7 7.9 %collective-permute-start.1 = (bf16[3,64,512]{2,1,0:T(8,128)(2,1)S(1)}, bf16[3,64,512]{2,1,0:T(8,128)(2,1)S(1)}, u32[]{:S(2)}, u32[]{:S(2)}) collective-permute-start(bf16[3,64,512]{2,1,0:T(8,128)(2,1)S(1)} %dynamic-slice_bitcast_fusion.6), channel_id=1, source_target_pairs={{0,1},{1,0},{2,3},{3,2},{4,5},{5,4},{6,7},{7,6},{8,9},{9,8},{10,11... | collective-permute-start | bytes 589832 | tf_op jit(solution)/shard_map/ppermute | solution.py:753
  21.3 122.3 %all-gather.16.cloned.1.call-start = ((), (), s32[]{:S(2)}) async-start(), calls=%async_computation.2 | async-start | bytes 5570560 | tf_op jit(solution)/shard_map/all_gather | solution.py:1023
  21.4 5.4 collective-permute-start
  33.0 37.5 %collective-permute-start.3 = (bf16[160,1024]{1,0:T(8,128)(2,1)S(1)}, bf16[160,1024]{1,0:T(8,128)(2,1)S(1)}, u32[]{:S(2)}, u32[]{:S(2)}) collective-permute-start(bf16[160,1024]{1,0:T(8,128)(2,1)S(1)} %pad_maximum_fusion.3), channel_id=1, source_target_pairs={{0,1},{1,0},{2,3},{3,2},{4,5},{5,4},{6,7},{7,6},{8,9},{9,8},{10,11... | collective-permute-start | bytes 983048 | tf_op jit(solution)/shard_map/ppermute | solution.py:753
  57.5 13.0 %collective-permute-start.2 = (bf16[64,2048]{1,0:T(8,128)(2,1)S(1)}, bf16[64,2048]{1,0:T(8,128)(2,1)S(1)}, u32[]{:S(2)}, u32[]{:S(2)}) collective-permute-start(bf16[64,2048]{1,0:T(8,128)(2,1)S(1)} %constant_dynamic-slice_fusion.4), channel_id=1, source_target_pairs={{0,1},{1,0},{2,3},{3,2},{4,5},{5,4},{6,7},{7,6},{8,9},{9,8},{10,11... | collective-permute-start | bytes 786440 | tf_op jit(solution)/shard_map/ppermute | solution.py:753
  71.3 107.9 %all-gather.18.cloned.1.call-start = ((), (), s32[]{:S(2)}) async-start(), calls=%async_computation.3 | async-start | bytes 4456448 | tf_op jit(solution)/shard_map/all_gather | solution.py:1023
  72.0 396.9 %all-gather.20.cloned.1.call-start = ((), (), s32[]{:S(2)}) async-start(), calls=%async_computation.4 | async-start | bytes 4456448 | tf_op jit(solution)/shard_map/all_gather | solution.py:802
  72.2 4.6 collective-permute-start.4
  100.2 19.9 %collective-permute-start.6 = (bf16[1024,1024]{1,0:T(8,128)(2,1)}, bf16[1024,1024]{1,0:T(8,128)(2,1)}, u32[]{:S(2)}, u32[]{:S(2)}) collective-permute-start(bf16[1024,1024]{1,0:T(8,128)(2,1)} %get-tuple-element.469.refs_1_.refs_3_.refs_7_.refs_9_), channel_id=1, source_target_pairs={{0,2},{1,3},{2,0},{3,1},{4,6},{5,7},{6,4},{7,5},{8,10},{9,11},{10,... | collective-permute-start | bytes 6291464 | tf_op jit(solution)/shard_map/ppermute | solution.py:753
  105.0 100.8 %collective-permute-start.7 = (bf16[1024,1024]{1,0:T(8,128)(2,1)}, bf16[1024,1024]{1,0:T(8,128)(2,1)S(1)}, u32[]{:S(2)}, u32[]{:S(2)}) collective-permute-start(bf16[1024,1024]{1,0:T(8,128)(2,1)} %param.36), channel_id=1, source_target_pairs={{0,0},{1,2},{2,1},{3,3},{4,4},{5,6},{6,5},{7,7},{8,8},{9,10},{10,9... | collective-permute-start | bytes 6291464 | tf_op jit(solution)/shard_map/ppermute | solution.py:753
  219.8 10.8 %collective-permute-start.8 = (bf16[8,128,1024]{2,1,0:T(8,128)(2,1)}, bf16[8,128,1024]{2,1,0:T(8,128)(2,1)S(1)}, u32[]{:S(2)}, u32[]{:S(2)}) collective-permute-start(bf16[8,128,1024]{2,1,0:T(8,128)(2,1)} %dynamic-slice_bitcast_fusion.3), channel_id=1, source_target_pairs={{0,2},{1,3},{2,0},{3,1},{4,6},{5,7},{6,4},{7,5},{8,10},{9,11},{10,... | collective-permute-start | bytes 6291464 | tf_op jit(solution)/shard_map/ppermute | solution.py:753
  220.0 10.6 %collective-permute-start.9 = (bf16[8,128,1024]{2,1,0:T(8,128)(2,1)}, bf16[8,128,1024]{2,1,0:T(8,128)(2,1)}, u32[]{:S(2)}, u32[]{:S(2)}) collective-permute-start(bf16[8,128,1024]{2,1,0:T(8,128)(2,1)} %dynamic-slice_bitcast_fusion.2), channel_id=1, source_target_pairs={{0,2},{1,3},{2,0},{3,1},{4,6},{5,7},{6,4},{7,5},{8,10},{9,11},{10,... | collective-permute-start | bytes 6291464 | tf_op jit(solution)/shard_map/ppermute | solution.py:753
  238.5 24.3 %collective-permute-start.10 = (bf16[4,128,1024]{2,1,0:T(8,128)(2,1)}, bf16[4,128,1024]{2,1,0:T(8,128)(2,1)S(1)}, u32[]{:S(2)}, u32[]{:S(2)}) collective-permute-start(bf16[4,128,1024]{2,1,0:T(8,128)(2,1)} %get-tuple-element.399), channel_id=1, source_target_pairs={{0,1},{1,0},{2,6},{3,7},{4,5},{5,4},{6,2},{7,3},{8,9},{9,8},{10,14... | collective-permute-start | bytes 3145736 | tf_op jit(solution)/shard_map/ppermute | solution.py:753
  240.0 24.8 %collective-permute-start.11 = (bf16[4,128,1024]{2,1,0:T(8,128)(2,1)}, bf16[4,128,1024]{2,1,0:T(8,128)(2,1)S(1)}, u32[]{:S(2)}, u32[]{:S(2)}) collective-permute-start(bf16[4,128,1024]{2,1,0:T(8,128)(2,1)} %get-tuple-element.400), channel_id=1, source_target_pairs={{0,1},{1,0},{2,6},{3,7},{4,5},{5,4},{6,2},{7,3},{8,9},{9,8},{10,14... | collective-permute-start | bytes 3145736 | tf_op jit(solution)/shard_map/ppermute | solution.py:753
  268.9 18.7 %collective-permute-start.12 = (bf16[8,64,2048]{2,1,0:T(8,128)(2,1)}, bf16[8,64,2048]{2,1,0:T(8,128)(2,1)S(1)}, u32[]{:S(2)}, u32[]{:S(2)}) collective-permute-start(bf16[8,64,2048]{2,1,0:T(8,128)(2,1)} %dynamic-slice_bitcast_fusion.1), channel_id=1, source_target_pairs={{0,2},{1,3},{2,0},{3,1},{4,6},{5,7},{6,4},{7,5},{8,10},{9,11},{10,... | collective-permute-start | bytes 6291464 | tf_op jit(solution)/shard_map/ppermute | solution.py:753
  268.9 18.7 %collective-permute-start.13 = (bf16[8,64,2048]{2,1,0:T(8,128)(2,1)S(1)}, bf16[8,64,2048]{2,1,0:T(8,128)(2,1)S(1)}, u32[]{:S(2)}, u32[]{:S(2)}) collective-permute-start(bf16[8,64,2048]{2,1,0:T(8,128)(2,1)S(1)} %dynamic-slice_bitcast_fusion), channel_id=1, source_target_pairs={{0,2},{1,3},{2,0},{3,1},{4,6},{5,7},{6,4},{7,5},{8,10},{9,11},{10,... | collective-permute-start | bytes 6291464 | tf_op jit(solution)/shard_map/ppermute | solution.py:753
  269.4 18.2 %collective-permute-start.14 = (bf16[4,128,1024]{2,1,0:T(8,128)(2,1)}, bf16[4,128,1024]{2,1,0:T(8,128)(2,1)S(1)}, u32[]{:S(2)}, u32[]{:S(2)}) collective-permute-start(bf16[4,128,1024]{2,1,0:T(8,128)(2,1)} %add.220), channel_id=1, source_target_pairs={{0,4},{1,5},{2,3},{3,2},{4,0},{5,1},{6,7},{7,6},{8,12},{9,13},{10,... | collective-permute-start | bytes 3145736 | tf_op jit(solution)/shard_map/ppermute | solution.py:753
  298.4 14.7 %collective-permute-start.15 = (bf16[2,128,1024]{2,1,0:T(8,128)(2,1)}, bf16[2,128,1024]{2,1,0:T(8,128)(2,1)S(1)}, u32[]{:S(2)}, u32[]{:S(2)}) collective-permute-start(bf16[2,128,1024]{2,1,0:T(8,128)(2,1)} %slice.215), channel_id=1, source_target_pairs={{0,8},{1,9},{2,10},{3,11},{4,12},{5,13},{6,14},{7,15},{8,0},{9,1},... | collective-permute-start | bytes 1572872 | tf_op jit(solution)/shard_map/ppermute | solution.py:753
  313.3 14.7 %collective-permute-start.18 = (bf16[1,128,1024]{2,1,0:T(8,128)(2,1)S(1)}, bf16[1,128,1024]{2,1,0:T(8,128)(2,1)S(1)}, u32[]{:S(2)}, u32[]{:S(2)}) collective-permute-start(bf16[1,128,1024]{2,1,0:T(8,128)(2,1)S(1)} %slice.217), channel_id=1, source_target_pairs={{0,16},{1,17},{2,18},{3,19},{4,20},{5,21},{6,22},{7,23},{8,24},{9,... | collective-permute-start | bytes 786440 | tf_op jit(solution)/shard_map/ppermute | solution.py:753
  315.2 50.5 %collective-permute-start.21 = (bf16[1024,1024]{1,0:T(8,128)(2,1)}, bf16[1024,1024]{1,0:T(8,128)(2,1)S(1)}, u32[]{:S(2)}, u32[]{:S(2)}) collective-permute-start(bf16[1024,1024]{1,0:T(8,128)(2,1)} %shard_map.335), channel_id=1, source_target_pairs={{0,0},{1,2},{2,1},{3,3},{4,4},{5,6},{6,5},{7,7},{8,8},{9,10},{10,9... | collective-permute-start | bytes 6291464 | tf_op jit(solution)/shard_map/ppermute | solution.py:753
  317.5 35.1 %collective-permute-start.19 = (bf16[8,32,1024]{2,1,0:T(8,128)(2,1)S(1)}, bf16[8,32,1024]{2,1,0:T(8,128)(2,1)S(1)}, u32[]{:S(2)}, u32[]{:S(2)}) collective-permute-start(bf16[8,32,1024]{2,1,0:T(8,128)(2,1)S(1)} %dynamic-slice_bitcast_fusion.5), channel_id=1, source_target_pairs={{0,2},{1,3},{2,0},{3,1},{4,6},{5,7},{6,4},{7,5},{8,10},{9,11},{10,... | collective-permute-start | bytes 1572872 | tf_op jit(solution)/shard_map/ppermute | solution.py:753
  317.8 34.7 %collective-permute-start.20 = (bf16[8,32,1024]{2,1,0:T(8,128)(2,1)S(1)}, bf16[8,32,1024]{2,1,0:T(8,128)(2,1)S(1)}, u32[]{:S(2)}, u32[]{:S(2)}) collective-permute-start(bf16[8,32,1024]{2,1,0:T(8,128)(2,1)S(1)} %dynamic-slice_bitcast_fusion.4), channel_id=1, source_target_pairs={{0,2},{1,3},{2,0},{3,1},{4,6},{5,7},{6,4},{7,5},{8,10},{9,11},{10,... | collective-permute-start | bytes 1572872 | tf_op jit(solution)/shard_map/ppermute | solution.py:753
  318.0 35.8 %collective-permute-start.16 = (bf16[4,64,2048]{2,1,0:T(8,128)(2,1)}, bf16[4,64,2048]{2,1,0:T(8,128)(2,1)}, u32[]{:S(2)}, u32[]{:S(2)}) collective-permute-start(bf16[4,64,2048]{2,1,0:T(8,128)(2,1)} %get-tuple-element.441), channel_id=1, source_target_pairs={{0,1},{1,0},{2,6},{3,7},{4,5},{5,4},{6,2},{7,3},{8,9},{9,8},{10,14... | collective-permute-start | bytes 3145736 | tf_op jit(solution)/shard_map/ppermute | solution.py:753
  328.0 37.1 %collective-permute-start.17 = (bf16[4,64,2048]{2,1,0:T(8,128)(2,1)}, bf16[4,64,2048]{2,1,0:T(8,128)(2,1)}, u32[]{:S(2)}, u32[]{:S(2)}) collective-permute-start(bf16[4,64,2048]{2,1,0:T(8,128)(2,1)} %get-tuple-element.442), channel_id=1, source_target_pairs={{0,1},{1,0},{2,6},{3,7},{4,5},{5,4},{6,2},{7,3},{8,9},{9,8},{10,14... | collective-permute-start | bytes 3145736 | tf_op jit(solution)/shard_map/ppermute | solution.py:753
  365.8 184.7 %all-gather.22.cloned.1.call-start = ((), (), s32[]{:S(2)}) async-start(), calls=%async_computation.5 | async-start | bytes 5570560 | tf_op jit(solution)/shard_map/all_gather | solution.py:1117
  373.2 27.0 %collective-permute-start.25 = (bf16[4,32,1024]{2,1,0:T(8,128)(2,1)}, bf16[4,32,1024]{2,1,0:T(8,128)(2,1)S(1)}, u32[]{:S(2)}, u32[]{:S(2)}) collective-permute-start(bf16[4,32,1024]{2,1,0:T(8,128)(2,1)} %get-tuple-element.479), channel_id=1, source_target_pairs={{0,1},{1,0},{2,6},{3,7},{4,5},{5,4},{6,2},{7,3},{8,9},{9,8},{10,14... | collective-permute-start | bytes 786440 | tf_op jit(solution)/shard_map/ppermute | solution.py:753
  374.1 26.0 %collective-permute-start.26 = (bf16[4,32,1024]{2,1,0:T(8,128)(2,1)}, bf16[4,32,1024]{2,1,0:T(8,128)(2,1)S(1)}, u32[]{:S(2)}, u32[]{:S(2)}) collective-permute-start(bf16[4,32,1024]{2,1,0:T(8,128)(2,1)} %get-tuple-element.480), channel_id=1, source_target_pairs={{0,1},{1,0},{2,6},{3,7},{4,5},{5,4},{6,2},{7,3},{8,9},{9,8},{10,14... | collective-permute-start | bytes 786440 | tf_op jit(solution)/shard_map/ppermute | solution.py:753
  375.3 24.9 %collective-permute-start.22 = (bf16[1024,256]{1,0:T(8,128)(2,1)}, bf16[1024,256]{1,0:T(8,128)(2,1)S(1)}, u32[]{:S(2)}, u32[]{:S(2)}) collective-permute-start(bf16[1024,256]{1,0:T(8,128)(2,1)} %get-tuple-element.476), channel_id=1, source_target_pairs={{0,2},{1,3},{2,0},{3,1},{4,6},{5,7},{6,4},{7,5},{8,10},{9,11},{10,... | collective-permute-start | bytes 1572872 | tf_op jit(solution)/shard_map/ppermute | solution.py:753
  375.3 24.9 %collective-permute-start.23 = (bf16[1024,256]{1,0:T(8,128)(2,1)S(1)}, bf16[1024,256]{1,0:T(8,128)(2,1)S(1)}, u32[]{:S(2)}, u32[]{:S(2)}) collective-permute-start(bf16[1024,256]{1,0:T(8,128)(2,1)S(1)} %copy-done.62), channel_id=1, source_target_pairs={{0,2},{1,3},{2,0},{3,1},{4,6},{5,7},{6,4},{7,5},{8,10},{9,11},{10,... | collective-permute-start | bytes 1572872 | tf_op jit(solution)/shard_map/ppermute | solution.py:753
  375.8 24.4 %collective-permute-start.24 = (bf16[4,64,2048]{2,1,0:T(8,128)(2,1)S(1)}, bf16[4,64,2048]{2,1,0:T(8,128)(2,1)S(1)}, u32[]{:S(2)}, u32[]{:S(2)}) collective-permute-start(bf16[4,64,2048]{2,1,0:T(8,128)(2,1)S(1)} %add.227), channel_id=1, source_target_pairs={{0,4},{1,5},{2,3},{3,2},{4,0},{5,1},{6,7},{7,6},{8,12},{9,13},{10,... | collective-permute-start | bytes 3145736 | tf_op jit(solution)/shard_map/ppermute | solution.py:753
  410.8 27.5 %collective-permute-start.31 = (bf16[4,32,1024]{2,1,0:T(8,128)(2,1)S(1)}, bf16[4,32,1024]{2,1,0:T(8,128)(2,1)S(1)}, u32[]{:S(2)}, u32[]{:S(2)}) collective-permute-start(bf16[4,32,1024]{2,1,0:T(8,128)(2,1)S(1)} %add.230), channel_id=1, source_target_pairs={{0,4},{1,5},{2,3},{3,2},{4,0},{5,1},{6,7},{7,6},{8,12},{9,13},{10,... | collective-permute-start | bytes 786440 | tf_op jit(solution)/shard_map/ppermute | solution.py:753
  413.1 25.2 %collective-permute-start.27 = (bf16[1024,256]{1,0:T(8,128)(2,1)S(1)}, bf16[1024,256]{1,0:T(8,128)(2,1)S(1)}, u32[]{:S(2)}, u32[]{:S(2)}) collective-permute-start(bf16[1024,256]{1,0:T(8,128)(2,1)S(1)} %copy-done.64), channel_id=1, source_target_pairs={{0,2},{1,3},{2,0},{3,1},{4,6},{5,7},{6,4},{7,5},{8,10},{9,11},{10,... | collective-permute-start | bytes 1572872 | tf_op jit(solution)/shard_map/ppermute | solution.py:753
  413.1 25.3 %collective-permute-start.28 = (bf16[1024,256]{1,0:T(8,128)(2,1)S(1)}, bf16[1024,256]{1,0:T(8,128)(2,1)S(1)}, u32[]{:S(2)}, u32[]{:S(2)}) collective-permute-start(bf16[1024,256]{1,0:T(8,128)(2,1)S(1)} %copy-done.63), channel_id=1, source_target_pairs={{0,2},{1,3},{2,0},{3,1},{4,6},{5,7},{6,4},{7,5},{8,10},{9,11},{10,... | collective-permute-start | bytes 1572872 | tf_op jit(solution)/shard_map/ppermute | solution.py:753
  413.6 24.8 %collective-permute-start.30 = (bf16[2,64,2048]{2,1,0:T(8,128)(2,1)S(1)}, bf16[2,64,2048]{2,1,0:T(8,128)(2,1)S(1)}, u32[]{:S(2)}, u32[]{:S(2)}) collective-permute-start(bf16[2,64,2048]{2,1,0:T(8,128)(2,1)S(1)} %slice.218), channel_id=1, source_target_pairs={{0,8},{1,9},{2,10},{3,11},{4,12},{5,13},{6,14},{7,15},{8,0},{9,1},... | collective-permute-start | bytes 1572872 | tf_op jit(solution)/shard_map/ppermute | solution.py:753
  414.1 24.2 %collective-permute-start.29 = (bf16[8,3,64,256]{3,2,1,0:T(8,128)(2,1)}, bf16[8,3,64,256]{3,2,1,0:T(8,128)(2,1)S(1)}, u32[]{:S(2)}, u32[]{:S(2)}) collective-permute-start(bf16[8,3,64,256]{3,2,1,0:T(8,128)(2,1)} %get-tuple-element.507), channel_id=1, source_target_pairs={{0,2},{1,3},{2,0},{3,1},{4,6},{5,7},{6,4},{7,5},{8,10},{9,11},{10,... | collective-permute-start | bytes 2359304 | tf_op jit(solution)/shard_map/ppermute | solution.py:753
  438.7 11.2 %collective-permute-start.34 = (bf16[2,32,1024]{2,1,0:T(8,128)(2,1)S(1)}, bf16[2,32,1024]{2,1,0:T(8,128)(2,1)S(1)}, u32[]{:S(2)}, u32[]{:S(2)}) collective-permute-start(bf16[2,32,1024]{2,1,0:T(8,128)(2,1)S(1)} %slice.219), channel_id=1, source_target_pairs={{0,8},{1,9},{2,10},{3,11},{4,12},{5,13},{6,14},{7,15},{8,0},{9,1},... | collective-permute-start | bytes 393224 | tf_op jit(solution)/shard_map/ppermute | solution.py:753
  440.3 9.6 %collective-permute-start.32 = (bf16[1024,256]{1,0:T(8,128)(2,1)S(1)}, bf16[1024,256]{1,0:T(8,128)(2,1)S(1)}, u32[]{:S(2)}, u32[]{:S(2)}) collective-permute-start(bf16[1024,256]{1,0:T(8,128)(2,1)S(1)} %copy-done.66), channel_id=1, source_target_pairs={{0,2},{1,3},{2,0},{3,1},{4,6},{5,7},{6,4},{7,5},{8,10},{9,11},{10,... | collective-permute-start | bytes 1572872 | tf_op jit(solution)/shard_map/ppermute | solution.py:753
  440.5 9.4 %collective-permute-start.33 = (bf16[1024,256]{1,0:T(8,128)(2,1)S(1)}, bf16[1024,256]{1,0:T(8,128)(2,1)S(1)}, u32[]{:S(2)}, u32[]{:S(2)}) collective-permute-start(bf16[1024,256]{1,0:T(8,128)(2,1)S(1)} %copy-done.65), channel_id=1, source_target_pairs={{0,2},{1,3},{2,0},{3,1},{4,6},{5,7},{6,4},{7,5},{8,10},{9,11},{10,... | collective-permute-start | bytes 1572872 | tf_op jit(solution)/shard_map/ppermute | solution.py:753
  450.0 18.1 %collective-permute-start.35 = (bf16[8,3,64,256]{3,2,1,0:T(8,128)(2,1)}, bf16[8,3,64,256]{3,2,1,0:T(8,128)(2,1)S(1)}, u32[]{:S(2)}, u32[]{:S(2)}) collective-permute-start(bf16[8,3,64,256]{3,2,1,0:T(8,128)(2,1)} %get-tuple-element.553), channel_id=1, source_target_pairs={{0,2},{1,3},{2,0},{3,1},{4,6},{5,7},{6,4},{7,5},{8,10},{9,11},{10,... | collective-permute-start | bytes 2359304 | tf_op jit(solution)/shard_map/ppermute | solution.py:753
  450.3 12.7 %collective-permute-start.37 = (bf16[1,32,1024]{2,1,0:T(8,128)(2,1)S(1)}, bf16[1,32,1024]{2,1,0:T(8,128)(2,1)S(1)}, u32[]{:S(2)}, u32[]{:S(2)}) collective-permute-start(bf16[1,32,1024]{2,1,0:T(8,128)(2,1)S(1)} %slice.223), channel_id=1, source_target_pairs={{0,16},{1,17},{2,18},{3,19},{4,20},{5,21},{6,22},{7,23},{8,24},{9,... | collective-permute-start | bytes 196616 | tf_op jit(solution)/shard_map/ppermute | solution.py:753
  451.8 16.3 %collective-permute-start.36 = (bf16[1,64,2048]{2,1,0:T(8,128)(2,1)S(1)}, bf16[1,64,2048]{2,1,0:T(8,128)(2,1)S(1)}, u32[]{:S(2)}, u32[]{:S(2)}) collective-permute-start(bf16[1,64,2048]{2,1,0:T(8,128)(2,1)S(1)} %slice.221), channel_id=1, source_target_pairs={{0,16},{1,17},{2,18},{3,19},{4,20},{5,21},{6,22},{7,23},{8,24},{9,... | collective-permute-start | bytes 786440 | tf_op jit(solution)/shard_map/ppermute | solution.py:753
  469.0 161.5 %all-gather.12.cloned.1.call-start = ((), (), s32[]{:S(2)}) async-start(), calls=%async_computation | async-start | bytes 1671168 | tf_op jit(solution)/shard_map/all_gather | solution.py:1146
  469.0 19.1 %collective-permute-start.38 = (bf16[8,3,64,256]{3,2,1,0:T(8,128)(2,1)S(1)}, bf16[8,3,64,256]{3,2,1,0:T(8,128)(2,1)S(1)}, u32[]{:S(2)}, u32[]{:S(2)}) collective-permute-start(bf16[8,3,64,256]{3,2,1,0:T(8,128)(2,1)S(1)} %add.233), channel_id=1, source_target_pairs={{0,1},{1,0},{2,3},{3,2},{4,5},{5,4},{6,7},{7,6},{8,9},{9,8},{10,11... | collective-permute-start | bytes 2359304 | tf_op jit(solution)/shard_map/ppermute | solution.py:753
  488.1 25.3 %collective-permute-start.39 = (bf16[8,3,64,256]{3,2,1,0:T(8,128)(2,1)S(1)}, bf16[8,3,64,256]{3,2,1,0:T(8,128)(2,1)S(1)}, u32[]{:S(2)}, u32[]{:S(2)}) collective-permute-start(bf16[8,3,64,256]{3,2,1,0:T(8,128)(2,1)S(1)} %copy-done.61), channel_id=1, source_target_pairs={{0,2},{1,3},{2,0},{3,1},{4,6},{5,7},{6,4},{7,5},{8,10},{9,11},{10,... | collective-permute-start | bytes 2359304 | tf_op jit(solution)/shard_map/ppermute | solution.py:753
  488.1 38.0 %collective-permute-start.43 = (bf16[8,3,64,256]{3,2,1,0:T(8,128)(2,1)S(1)}, bf16[8,3,64,256]{3,2,1,0:T(8,128)(2,1)S(1)}, u32[]{:S(2)}, u32[]{:S(2)}) collective-permute-start(bf16[8,3,64,256]{3,2,1,0:T(8,128)(2,1)S(1)} %add.236), channel_id=1, source_target_pairs={{0,1},{1,0},{2,3},{3,2},{4,5},{5,4},{6,7},{7,6},{8,9},{9,8},{10,11... | collective-permute-start | bytes 2359304 | tf_op jit(solution)/shard_map/ppermute | solution.py:753
  514.4 11.7 %collective-permute-start.40 = (bf16[1024,256]{1,0:T(8,128)(2,1)S(1)}, bf16[1024,256]{1,0:T(8,128)(2,1)S(1)}, u32[]{:S(2)}, u32[]{:S(2)}) collective-permute-start(bf16[1024,256]{1,0:T(8,128)(2,1)S(1)} %copy-done.68), channel_id=1, source_target_pairs={{0,2},{1,3},{2,0},{3,1},{4,6},{5,7},{6,4},{7,5},{8,10},{9,11},{10,... | collective-permute-start | bytes 1572872 | tf_op jit(solution)/shard_map/ppermute | solution.py:753
  514.6 11.5 %collective-permute-start.41 = (bf16[1024,256]{1,0:T(8,128)(2,1)S(1)}, bf16[1024,256]{1,0:T(8,128)(2,1)S(1)}, u32[]{:S(2)}, u32[]{:S(2)}) collective-permute-start(bf16[1024,256]{1,0:T(8,128)(2,1)S(1)} %copy-done.67), channel_id=1, source_target_pairs={{0,2},{1,3},{2,0},{3,1},{4,6},{5,7},{6,4},{7,5},{8,10},{9,11},{10,... | collective-permute-start | bytes 1572872 | tf_op jit(solution)/shard_map/ppermute | solution.py:753
  514.9 11.2 %collective-permute-start.42 = (bf16[4,3,64,256]{3,2,1,0:T(8,128)(2,1)S(1)}, bf16[4,3,64,256]{3,2,1,0:T(8,128)(2,1)S(1)}, u32[]{:S(2)}, u32[]{:S(2)}) collective-permute-start(bf16[4,3,64,256]{3,2,1,0:T(8,128)(2,1)S(1)} %slice.226), channel_id=1, source_target_pairs={{0,4},{1,5},{2,6},{3,7},{4,0},{5,1},{6,2},{7,3},{8,12},{9,13},{10,... | collective-permute-start | bytes 1179656 | tf_op jit(solution)/shard_map/ppermute | solution.py:753
  536.0 10.1 %collective-permute-start.44 = (bf16[8,3,64,256]{3,2,1,0:T(8,128)(2,1)}, bf16[8,3,64,256]{3,2,1,0:T(8,128)(2,1)S(1)}, u32[]{:S(2)}, u32[]{:S(2)}) collective-permute-start(bf16[8,3,64,256]{3,2,1,0:T(8,128)(2,1)} %get-tuple-element.635), channel_id=1, source_target_pairs={{0,2},{1,3},{2,0},{3,1},{4,6},{5,7},{6,4},{7,5},{8,10},{9,11},{10,... | collective-permute-start | bytes 2359304 | tf_op jit(solution)/shard_map/ppermute | solution.py:753
  537.0 9.2 %collective-permute-start.45 = (bf16[2,3,64,256]{3,2,1,0:T(8,128)(2,1)S(1)}, bf16[2,3,64,256]{3,2,1,0:T(8,128)(2,1)S(1)}, u32[]{:S(2)}, u32[]{:S(2)}) collective-permute-start(bf16[2,3,64,256]{3,2,1,0:T(8,128)(2,1)S(1)} %slice.228), channel_id=1, source_target_pairs={{0,8},{1,9},{2,10},{3,11},{4,12},{5,13},{6,14},{7,15},{8,0},{9,1},... | collective-permute-start | bytes 589832 | tf_op jit(solution)/shard_map/ppermute | solution.py:753
  548.6 4.2 collective-permute-start.48
  550.5 18.2 %collective-permute-start.53 = (bf16[4,3,64,256]{3,2,1,0:T(8,128)(2,1)S(1)}, bf16[4,3,64,256]{3,2,1,0:T(8,128)(2,1)S(1)}, u32[]{:S(2)}, u32[]{:S(2)}) collective-permute-start(bf16[4,3,64,256]{3,2,1,0:T(8,128)(2,1)S(1)} %slice.231), channel_id=1, source_target_pairs={{0,4},{1,5},{2,6},{3,7},{4,0},{5,1},{6,2},{7,3},{8,12},{9,13},{10,... | collective-permute-start | bytes 1179656 | tf_op jit(solution)/shard_map/ppermute | solution.py:753
  553.7 4.2 collective-permute-start.49
  558.0 9.2 %collective-permute-start.50 = (f32[2,52,128]{2,1,0:T(8,128)S(1)}, f32[2,52,128]{2,1,0:T(8,128)S(1)}, u32[]{:S(2)}, u32[]{:S(2)}) collective-permute-start(f32[2,52,128]{2,1,0:T(8,128)S(1)} %add.249), channel_id=1, source_target_pairs={{0,16},{1,17},{2,18},{3,19},{4,20},{5,21},{6,22},{7,23},{8,24},{9,... | collective-permute-start | bytes 159752 | tf_op jit(solution)/shard_map/ppermute | solution.py:753
  567.2 9.7 %collective-permute-start.51 = (f32[52,128]{1,0:T(8,128)S(1)}, f32[52,128]{1,0:T(8,128)S(1)}, u32[]{:S(2)}, u32[]{:S(2)}) collective-permute-start(f32[52,128]{1,0:T(8,128)S(1)} %slice_bitcast_fusion), channel_id=1, source_target_pairs={{0,1},{1,0},{2,3},{3,2},{4,5},{5,4},{6,7},{7,6},{8,9},{9,8},{10,11... | collective-permute-start | bytes 79880 | tf_op jit(solution)/shard_map/ppermute | solution.py:753
  568.1 6.5 %collective-permute-start.52 = (bf16[1,3,64,256]{3,2,1,0:T(8,128)(2,1)S(1)}, bf16[1,3,64,256]{3,2,1,0:T(8,128)(2,1)S(1)}, u32[]{:S(2)}, u32[]{:S(2)}) collective-permute-start(bf16[1,3,64,256]{3,2,1,0:T(8,128)(2,1)S(1)} %slice.230), channel_id=1, source_target_pairs={{0,16},{1,17},{2,18},{3,19},{4,20},{5,21},{6,22},{7,23},{8,24},{9,... | collective-permute-start | bytes 294920 | tf_op jit(solution)/shard_map/ppermute | solution.py:753
  568.8 6.9 %collective-permute-start.54 = (bf16[2,3,64,256]{3,2,1,0:T(8,128)(2,1)S(1)}, bf16[2,3,64,256]{3,2,1,0:T(8,128)(2,1)S(1)}, u32[]{:S(2)}, u32[]{:S(2)}) collective-permute-start(bf16[2,3,64,256]{3,2,1,0:T(8,128)(2,1)S(1)} %slice.239), channel_id=1, source_target_pairs={{0,8},{1,9},{2,10},{3,11},{4,12},{5,13},{6,14},{7,15},{8,0},{9,1},... | collective-permute-start | bytes 589832 | tf_op jit(solution)/shard_map/ppermute | solution.py:753
  575.7 8.5 %collective-permute-start.55 = (bf16[1,3,64,256]{3,2,1,0:T(8,128)(2,1)S(1)}, bf16[1,3,64,256]{3,2,1,0:T(8,128)(2,1)S(1)}, u32[]{:S(2)}, u32[]{:S(2)}) collective-permute-start(bf16[1,3,64,256]{3,2,1,0:T(8,128)(2,1)S(1)} %slice.241), channel_id=1, source_target_pairs={{0,16},{1,17},{2,18},{3,19},{4,20},{5,21},{6,22},{7,23},{8,24},{9,... | collective-permute-start | bytes 294920 | tf_op jit(solution)/shard_map/ppermute | solution.py:753
  584.9 18.3 %collective-permute-start.56 = (bf16[1,3,64,256]{3,2,1,0:T(8,128)(2,1)S(1)}, bf16[1,3,64,256]{3,2,1,0:T(8,128)(2,1)S(1)}, u32[]{:S(2)}, u32[]{:S(2)}) collective-permute-start(bf16[1,3,64,256]{3,2,1,0:T(8,128)(2,1)S(1)} %get-tuple-element.657), channel_id=1, source_target_pairs={{0,16},{1,17},{2,18},{3,19},{4,20},{5,21},{6,22},{7,23},{8,24},{9,... | collective-permute-start | bytes 294920 | tf_op jit(solution)/shard_map/ppermute | solution.py:753
  586.1 43.4 %collective-permute-start.46 = (bf16[1024,1024]{1,0:T(8,128)(2,1)}, bf16[1024,1024]{1,0:T(8,128)(2,1)}, u32[]{:S(2)}, u32[]{:S(2)}) collective-permute-start(bf16[1024,1024]{1,0:T(8,128)(2,1)} %get-tuple-element.643), channel_id=1, source_target_pairs={{0,0},{1,2},{2,1},{3,3},{4,4},{5,6},{6,5},{7,7},{8,8},{9,10},{10,9... | collective-permute-start | bytes 6291464 | tf_op jit(solution)/shard_map/ppermute | solution.py:753
  603.2 7.7 %collective-permute-start.57 = (bf16[2,3,64,256]{3,2,1,0:T(8,128)(2,1)S(1)}, bf16[2,3,64,256]{3,2,1,0:T(8,128)(2,1)S(1)}, u32[]{:S(2)}, u32[]{:S(2)}) collective-permute-start(bf16[2,3,64,256]{3,2,1,0:T(8,128)(2,1)S(1)} %pad_maximum_fusion.5), channel_id=1, source_target_pairs={{0,8},{1,9},{2,10},{3,11},{4,12},{5,13},{6,14},{7,15},{8,0},{9,1},... | collective-permute-start | bytes 589832 | tf_op jit(solution)/shard_map/ppermute | solution.py:753
  611.0 9.6 %collective-permute-start.58 = (bf16[4,3,64,256]{3,2,1,0:T(8,128)(2,1)S(1)}, bf16[4,3,64,256]{3,2,1,0:T(8,128)(2,1)S(1)}, u32[]{:S(2)}, u32[]{:S(2)}) collective-permute-start(bf16[4,3,64,256]{3,2,1,0:T(8,128)(2,1)S(1)} %pad_maximum_fusion.2), channel_id=1, source_target_pairs={{0,4},{1,5},{2,6},{3,7},{4,0},{5,1},{6,2},{7,3},{8,12},{9,13},{10,... | collective-permute-start | bytes 1179656 | tf_op jit(solution)/shard_map/ppermute | solution.py:753
  620.7 8.8 %collective-permute-start.59 = (bf16[8,3,64,256]{3,2,1,0:T(8,128)(2,1)S(1)}, bf16[8,3,64,256]{3,2,1,0:T(8,128)(2,1)S(1)}, u32[]{:S(2)}, u32[]{:S(2)}) collective-permute-start(bf16[8,3,64,256]{3,2,1,0:T(8,128)(2,1)S(1)} %pad_maximum_fusion.1), channel_id=1, source_target_pairs={{0,2},{1,3},{2,0},{3,1},{4,6},{5,7},{6,4},{7,5},{8,10},{9,11},{10,... | collective-permute-start | bytes 2359304 | tf_op jit(solution)/shard_map/ppermute | solution.py:753
  (75 other events, 630.0 us)
Sparse Core Ops, SparseCore 0:
  21.4 46.8 all-gather.13
  71.4 56.2 all-gather.15
  129.9 49.2 all-gather.17
  365.9 49.8 all-gather.19
  469.1 53.9 all-gather.21
  575.4 40.7 all-gather.11

commit v5 on v4

--- a/solution.py
+++ b/solution.py
@@ -231,9 +231,8 @@
     v_refs = refs[at + sources : at + 2 * sources]
     at += 2 * sources
     dq_ref = refs[at]
-    dk_refs = refs[at + 1 : at + 1 + sources]
-    dv_refs = refs[at + 1 + sources : at + 1 + 2 * sources]
-    dq_acc, centre = refs[at + 1 + 2 * sources :]
+    dkv_refs = refs[at + 1 : at + 1 + sources]
+    dq_acc, centre = refs[at + 1 + sources :]
     lane = lax.broadcasted_iota(jnp.int32, (1, LANES), 1)
     tokens = q_ref.shape[0]
     product = (do_ref[...].astype(F32) * o_ref[...].astype(F32)).T
@@ -242,7 +241,7 @@
             product[head * HD : head * HD + HD], axis=0, keepdims=True
         )
     dq_acc[...] = jnp.zeros_like(dq_acc)
-    for k_ref, v_ref, dk_ref, dv_ref in zip(k_refs, v_refs, dk_refs, dv_refs):
+    for k_ref, v_ref, dkv_ref in zip(k_refs, v_refs, dkv_refs):
 
         def body(j, carry):
             rows = pl.ds(pl.multiple_of(j * keys_at, keys_at), keys_at)
@@ -274,8 +273,8 @@
                 dk += dot_nn(score_grad, q_head)
                 part = slice(head * HD, head * HD + HD)
                 dq_acc[part, cut] += dot_nn(k_t[part], score_grad)
-            dv_ref[rows, :] = dv.astype(BF)
-            dk_ref[rows, :] = (dk * SCALE).astype(BF)
+            dkv_ref[0, rows, :] = (dk * SCALE).astype(BF)
+            dkv_ref[1, rows, :] = dv.astype(BF)
             return carry
 
         lax.fori_loop(0, k_ref.shape[0] // keys_at, body, 0)
@@ -296,7 +295,7 @@
         pl.BlockSpec((kv.shape[0], LANES), lambda i: (0, all_pairs + skip + i)) for kv in kvs
     ]
     dq_spec = pl.BlockSpec((tokens, LANES), lambda i: (0, i))
-    dk_specs = [pl.BlockSpec((kv.shape[0], LANES), lambda i: (0, i)) for kv in kvs]
+    dkv_specs = [pl.BlockSpec((2, kv.shape[0], LANES), lambda i: (0, 0, i)) for kv in kvs]
     table = pl.BlockSpec((tokens, LANES), lambda i: (0, 0))
     outs = call(
         functools.partial(
@@ -311,13 +310,12 @@
         + [table] * 3
         + k_specs
         + v_specs,
-        out_specs=[dq_spec] + dk_specs + dk_specs,
+        out_specs=[dq_spec] + dkv_specs,
         out_shape=[jax.ShapeDtypeStruct((tokens, cols), BF)]
-        + [jax.ShapeDtypeStruct((kv.shape[0], cols), BF) for kv in kvs] * 2,
+        + [jax.ShapeDtypeStruct((2, kv.shape[0], cols), BF) for kv in kvs],
         scratch_shapes=[pltpu.VMEM((LANES, tokens), F32), pltpu.VMEM((2, tokens), F32)],
     )(q, out_grad, out, lse, *tables, *kvs, *kvs)
-    n = len(kvs)
-    return outs[0], outs[1 : 1 + n], outs[1 + n :]
+    return outs[0], outs[1:]
 
 
 def key_sum_kernel(own_ref, got_ref, c_ref, sa_ref, sb_ref, dk_ref):
@@ -531,25 +529,21 @@
     )(resid, grad, scale, *hidden_gs, *weights)
 
 
-def add_parts(total, refs, weights, units):
-    for (w_ref, lo, count), start in zip(weights, units):
-        for kind in range(3):
-            parts = [refs[start + 3 * u + kind][...] for u in range(count)]
-            cols = sum(p.shape[1] for p in parts)
-            weight = w_ref[:, kind, :, lo : lo + cols].reshape(total.shape[1], cols)
-            total += dot_nt(jnp.concatenate(parts, axis=1), weight)
+def add_parts(total, w_ref, rows_ref, lo):
+    cols = rows_ref.shape[1] // 3
+    for kind in range(3):
+        weight = w_ref[:, kind, :, lo : lo + cols].reshape(total.shape[1], cols)
+        total += dot_nt(rows_ref[:, kind * cols : (kind + 1) * cols], weight)
     return total
 
 
-def early_kernel(own_ref, oth_ref, *refs, units, cols):
-    out_ref = refs[-1]
-    weights = [(own_ref, 0, 1), (oth_ref, 0, units)]
-    out_ref[...] = add_parts(jnp.zeros(out_ref.shape, F32), refs, weights, (0, 3))
-
-
-def last_kernel(x_ref, g_ref, scale_ref, part_ref, own_ref, *refs, cols):
-    in_grad_ref, sums_ref = refs[-2:]
-    upstream = add_parts(part_ref[...], refs, [(own_ref, cols, 1)], (0,))
+def early_kernel(own_ref, oth_ref, own_rows, oth_rows, out_ref):
+    total = add_parts(jnp.zeros(out_ref.shape, F32), oth_ref, oth_rows, 0)
+    out_ref[...] = add_parts(total, own_ref, own_rows, 0)
+
+
+def last_kernel(x_ref, g_ref, scale_ref, part_ref, own_ref, rows_ref, in_grad_ref, sums_ref):
+    upstream = add_parts(part_ref[...], own_ref, rows_ref, rows_ref.shape[1] // 3)
     _, normal, inv_dev = norm_parts(x_ref[...].astype(F32), 1.0, 0.0)
     back, scale_sum, shift_sum = norm_back(upstream, normal, inv_dev, scale_ref[...])
     in_grad_ref[...] = (g_ref[...].astype(F32) + back).astype(BF)
@@ -565,68 +559,69 @@
         sums_ref[...] += sums
 
 
-def early_rows(own, oth, own_unit, oth_units):
-    flat = list(own_unit) + [p for unit in oth_units for p in unit]
-    tokens, cols = flat[0].shape
+def early_rows(own, oth, own_rows, oth_rows):
+    tokens, deep = own_rows.shape[0], own_rows.shape[1] + oth_rows.shape[1]
     width = own.shape[0] * own.shape[2]
     rows = min(512, tokens)
     return call(
-        functools.partial(early_kernel, units=len(oth_units), cols=cols),
-        2 * tokens * width * cols * len(flat),
-        2 * (tokens * cols * len(flat) + width * cols * len(flat) + 2 * tokens * width),
+        early_kernel,
+        2 * tokens * width * deep,
+        2 * (tokens * deep + width * deep + 2 * tokens * width),
         grid=(tokens // rows,),
         in_specs=[pl.BlockSpec(w.shape, lambda i: (0, 0, 0, 0)) for w in (own, oth)]
-        + [pl.BlockSpec((rows, cols), lambda i: (i, 0)) for p in flat],
+        + [pl.BlockSpec((rows, p.shape[1]), lambda i: (i, 0)) for p in (own_rows, oth_rows)],
         out_specs=pl.BlockSpec((rows, width), lambda i: (i, 0)),
         out_shape=jax.ShapeDtypeStruct((tokens, width), F32),
-    )(own, oth, *flat)
-
-
-def last_rows(x, branch_grad, scale, partial, own, unit):
+    )(own, oth, own_rows, oth_rows)
+
+
+def last_rows(x, branch_grad, scale, partial, own, own_rows):
     tokens, width = x.shape
-    cols = unit[0].shape[1]
+    deep = own_rows.shape[1]
     rows = min(256, tokens)
     tile = pl.BlockSpec((rows, width), lambda i: (i, 0))
     return call(
-        functools.partial(last_kernel, cols=cols),
-        6 * tokens * width * cols,
-        2 * (3 * tokens * cols + 3 * width * cols + 5 * tokens * width),
+        last_kernel,
+        2 * tokens * width * deep,
+        2 * (tokens * deep + width * deep + 5 * tokens * width),
         grid=(tokens // rows,),
         in_specs=[tile, tile, pl.BlockSpec((1, width), lambda i: (0, 0)), tile]
-        + [pl.BlockSpec(own.shape, lambda i: (0, 0, 0, 0))]
-        + [pl.BlockSpec((rows, cols), lambda i: (i, 0))] * 3,
+        + [pl.BlockSpec(own.shape, lambda i: (0, 0, 0, 0)), pl.BlockSpec((rows, deep), lambda i: (i, 0))],
         out_specs=[tile, pl.BlockSpec((8, width), lambda i: (0, 0))],
         out_shape=[
             jax.ShapeDtypeStruct((tokens, width), BF),
             jax.ShapeDtypeStruct((8, width), F32),
         ],
-    )(x, branch_grad, scale, partial, own, *unit)
-
-
-def unit_kernel(t_ref, nt_ref, dq_ref, dk_ref, gk_ref, dv_ref, gv_ref, c_ref, sa_ref, sb_ref, *refs, chips):
-    keep_ref, send_ref, dk_out, dv_out, sum_ref, rows_ref, acc_ref = refs
+    )(x, branch_grad, scale, partial, own, own_rows)
+
+
+def unit_kernel(t_ref, nt_ref, c_ref, sa_ref, sb_ref, *refs, chips, parts):
+    dq_refs, own_refs, got_refs = refs[:parts], refs[parts : 2 * parts], refs[2 * parts : 3 * parts]
+    keep_ref, send_ref, rows_out, sum_ref, acc_ref = refs[3 * parts :]
     kind = pl.program_id(0)
+    cols = dq_refs[0].shape[1]
     added = lambda a, b: a[...].astype(F32) + b[...].astype(F32)
 
     @pl.when(kind == 0)
     def _():
-        rows_ref[...] = dq_ref[...]
+        for u, dq in enumerate(dq_refs):
+            rows_out[:, u * cols : (u + 1) * cols] = dq[...]
 
     @pl.when(kind == 1)
     def _():
-        total = added(dk_ref, gk_ref)
         tables = (c_ref[...], sa_ref[...], sb_ref[...])
-        for at in range(0, total.shape[1], LANES):
-            cut = slice(at, at + LANES)
-            rows_ref[:, cut] = turn_back(total[:, cut], *tables).astype(BF)
-        dk_out[...] = rows_ref[...]
+        for u, (own, got) in enumerate(zip(own_refs, got_refs)):
+            total = added(own, got)
+            for at in range(0, cols, LANES):
+                turned = turn_back(total[:, at : at + LANES], *tables).astype(BF)
+                rows_out[:, u * cols + at : u * cols + at + LANES] = turned
 
     @pl.when(kind == 2)
     def _():
-        rows_ref[...] = added(dv_ref, gv_ref).astype(BF)
-        dv_out[...] = rows_ref[...]
-
-    rows = rows_ref[...]
+        for u, (own, got) in enumerate(zip(own_refs, got_refs)):
+            rows_out[:, u * cols : (u + 1) * cols] = added(own, got).astype(BF)
+
+    rows = rows_out[...]
     acc_ref[...] = dot_nn(nt_ref[...], rows)
     piece = keep_ref.shape[1]
     for place in range(chips):
@@ -637,33 +632,43 @@
     sum_ref[...] = jnp.broadcast_to(sums, sum_ref.shape)
 
 
-def unit_grads(table, normed_t, dq, dk, got_k, dv, got_v, tables):
+def unit_grads(table, normed_t, tables, dqs, owns, gots):
     width, tokens = normed_t.shape
-    cols = dq.shape[1]
+    parts = len(dqs)
+    cols = dqs[0].shape[1]
+    wide = parts * cols
     chips = table.shape[0] // 2
     piece = width // (2 * chips)
+    rotary = pl.BlockSpec((tokens, LANES), lambda i, t: (0, 0))
     part = pl.BlockSpec((tokens, cols), lambda i, t: (0, 0))
-    rotary = pl.BlockSpec((tokens, LANES), lambda i, t: (0, 0))
-    blocks = pl.BlockSpec((chips, None, piece, cols), lambda i, t: (0, i, 0, 0))
+    pair = pl.BlockSpec((None, tokens, cols), lambda i, t: (jnp.maximum(i - 1, 0), 0, 0))
+    blocks = pl.BlockSpec((chips, None, piece, wide), lambda i, t: (0, i, 0, 0))
     return pl.pallas_call(
-        functools.partial(unit_kernel, chips=chips),
+        functools.partial(unit_kernel, chips=chips, parts=parts),
         grid_spec=pltpu.PrefetchScalarGridSpec(
             num_scalar_prefetch=1,
             grid=(3,),
-            in_specs=[pl.BlockSpec((width, tokens), lambda i, t: (0, 0))] + [part] * 5 + [rotary] * 3,
-            out_specs=[blocks, blocks, part, part, pl.BlockSpec((8, cols), lambda i, t: (0, i))],
-            scratch_shapes=[pltpu.VMEM((tokens, cols), BF), pltpu.VMEM((width, cols), F32)],
+            in_specs=[pl.BlockSpec((width, tokens), lambda i, t: (0, 0))]
+            + [rotary] * 3
+            + [part] * parts
+            + [pair] * (2 * parts),
+            out_specs=[
+                blocks,
+                blocks,
+                pl.BlockSpec((tokens, wide), lambda i, t: (0, i)),
+                pl.BlockSpec((8, wide), lambda i, t: (0, i)),
+            ],
+            scratch_shapes=[pltpu.VMEM((width, wide), F32)],
         ),
-        out_shape=[jax.ShapeDtypeStruct((chips, 3, piece, cols), BF)] * 2
-        + [jax.ShapeDtypeStruct((tokens, cols), BF)] * 2
-        + [jax.ShapeDtypeStruct((8, 3 * cols), F32)],
+        out_shape=[jax.ShapeDtypeStruct((chips, 3, piece, wide), BF)] * 2
+        + [jax.ShapeDtypeStruct((tokens, 3 * wide), BF), jax.ShapeDtypeStruct((8, 3 * wide), F32)],
         compiler_params=pltpu.CompilerParams(vmem_limit_bytes=VMEM_BYTES),
         cost_estimate=pl.CostEstimate(
-            flops=6 * tokens * width * cols,
-            bytes_accessed=2 * (tokens * width + 7 * tokens * cols + 3 * width * cols),
+            flops=6 * tokens * width * wide,
+            bytes_accessed=2 * (tokens * width + 8 * tokens * wide + 3 * width * wide),
             transcendentals=0,
         ),
-    )(table, normed_t, dq, dk, got_k, dv, got_v, *tables)
+    )(table, normed_t, *tables, *dqs, *owns, *gots)
 
 
 def widen_kernel(t_ref, a_ref, b_ref, out_ref):
@@ -693,14 +698,14 @@
     )(table, unit_a, unit_b)
 
 
-def split_kernel(t_ref, own_m, own_f, oth_m, oth_f, got_om, got_of, got_tm, got_tf, ka, kb, sa, sb, *, last):
+def split_kernel(t_ref, own_m, own_f, oth_m, oth_f, got_om, got_of, got_tm, got_tf, ka, kb, send, *, last):
     total = lambda a, b: (a[...].astype(F32) + b[...].astype(F32)).astype(BF)
     by_y = t_ref[last] == 0
     own_far, oth_me = total(own_f, got_of), total(oth_m, got_tm)
     ka[...] = total(own_m, got_om)
     kb[...] = jnp.where(by_y, own_far, oth_me)
-    sa[...] = jnp.where(by_y, oth_me, own_far)
-    sb[...] = total(oth_f, got_tf)
+    send[0] = jnp.where(by_y, oth_me, own_far)
+    send[1] = total(oth_f, got_tf)
 
 
 def first_split(table, own, oth, got_own, got_oth):
@@ -718,9 +723,10 @@
             num_scalar_prefetch=1,
             grid=(count,),
             in_specs=[whole(0), whole(1)] * 2 + [part(0), part(1)] * 2,
-            out_specs=[out] * 4,
+            out_specs=[out, out, pl.BlockSpec((2, None, piece, cols), lambda i, t: (0, i, 0, 0))],
         ),
-        out_shape=[jax.ShapeDtypeStruct((count, piece, cols), BF)] * 4,
+        out_shape=[jax.ShapeDtypeStruct((count, piece, cols), BF)] * 2
+        + [jax.ShapeDtypeStruct((2, count, piece, cols), BF)],
         compiler_params=pltpu.CompilerParams(vmem_limit_bytes=VMEM_BYTES),
         cost_estimate=pl.CostEstimate(
             flops=4 * count * piece * cols, bytes_accessed=24 * count * piece * cols, transcendentals=0
@@ -749,11 +755,13 @@
         for dp in range(self.n_dp):
             for y in range(2):
                 a, b = to(dp, y)
-                pairs.append((dp * 2 + y, a * 2 + b))
+                if (a, b) != (dp, y):
+                    pairs.append((dp * 2 + y, a * 2 + b))
         return lax.ppermute(x, ("dp", "tensor"), pairs)
 
     def swap_rows(self, rows):
-        return self.move(rows, lambda dp, y: (dp - dp % 2 + y, dp % 2))
+        got = self.move(rows, lambda dp, y: (dp - dp % 2 + y, dp % 2))
+        return jnp.where(self.core == self.me_y, rows, got)
 
     def over_y(self, x):
         return self.move(x, lambda dp, y: (dp, 1 - y))
@@ -826,7 +834,7 @@
         return [lax.all_gather(kv, "tensor", axis=0, tiled=True)]
 
     def keys_back(self, grads):
-        return lax.psum_scatter(grads[0], "tensor", scatter_dimension=0, tiled=True), None
+        return lax.psum_scatter(grads, "tensor", scatter_dimension=1, tiled=True)
 
 
 def block_step(
@@ -895,13 +903,9 @@
     normed1_grad = 0.0
     for q, kvs, out, log, out_w, qkv_w in zip(queries, keys, outs, logs, out_ws, qkv_ws):
         out_g = dot_nt(branch_grad, out_w).astype(BF)
-        dq, dks, dvs = attend_back(q, out_g, out, log, kvs, tables)
-        dk_own, dk_got = move.keys_back(dks)
-        dv_own, dv_got = move.keys_back(dvs)
-        if dk_got is None:
-            dk_got, dv_got = jnp.zeros_like(dk_own), jnp.zeros_like(dv_own)
-        dk = key_sum(dk_own, dk_got, tables)
-        dv = dv_own + dv_got
+        dq, (dkv,) = attend_back(q, out_g, out, log, kvs, tables)
+        dk, dv = move.keys_back(dkv)
+        dk = key_sum(dk, jnp.zeros_like(dk), tables)
         qkv_g = jnp.concatenate([dq, dk, dv], axis=1)
         qkv_w_grads.append(dot_tn(normed1, qkv_g).astype(BF))
         qkv_b_grads.append(jnp.sum(qkv_g, 0, dtype=F32))
@@ -947,11 +951,11 @@
     def take(self, got):
         at, self.at = self.at, self.at + 1
         if at == 0:
-            ka, kb, sa, sb = first_split(self.table, *self.grads, *got)
-            self.keep, self.sends = (ka, kb), [sa, sb]
+            ka, kb, send = first_split(self.table, *self.grads, *got)
+            self.keep, self.sends = (ka, kb), [send]
         elif at == 1:
-            self.sends = [self.keep[1] + got[1]]
-            self.keep = self.keep[0] + got[0]
+            self.sends = [self.keep[1] + got[0][1]]
+            self.keep = self.keep[0] + got[0][0]
         else:
             total = self.keep + got[0]
             half = total.shape[0] // 2
@@ -1005,7 +1009,6 @@
     qkv_piece = move.piece(qkv_own, 1)
     block_in = move.swap_rows(block_in)
     tables = rotary_tables(move.first, tokens)
-    qkv_piece, tables = tie(qkv_piece, tables)
     qkv_got = move.over_y(qkv_piece)
     small_got = move.over_y(small)
     qkv_bs = [row(v[: 3 * part]) for v in (small, small_got)]
@@ -1086,13 +1089,12 @@
         return lambda *xs: attend_back(*xs, tables, lo, half, at), inputs
 
     def keys_of(x):
-        return lambda xs: [move.over_core(g) for g in xs], [x[1][1], x[2][1]]
-
-    def unit(x, got):
-        keep, send, dk, dv, sums = unit_grads(
-            move.blocks, normed1_t, x[0], x[1][0], got[0], x[2][0], got[1], tables
+        return move.over_core, x[1][1]
+
+    def unit(xs, gots):
+        return unit_grads(
+            move.blocks, normed1_t, tables, [x[0] for x in xs], [x[1][0] for x in xs], gots
         )
-        return keep, send, (x[0], dk, dv), sums[0]
 
     level = lambda n: functools.partial(move.over_chip, level=n)
 
@@ -1102,39 +1104,35 @@
     oth_a, _ = beside(*back(0), up, down, proj)
     down_block, oth_a, block_out = tie(down.done, oth_a, block_out)
     down_all = move.gather(down_block)
-    oth_b, (got,) = beside(*back(1), keys_of(oth_a), up, proj)
-    keep_oth_a, send, parts_oth_a, bias_oth_a = unit(oth_a, got)
-    own_a, (got, core_got) = beside(*back(2), keys_of(oth_b), (move.over_core, send), up, proj)
-    y_send = keep_oth_a + core_got
-    (keep_oth_b, send, parts_oth_b, bias_oth_b), (key_got, y_got_a) = beside(
-        unit, (oth_b, got), keys_of(own_a), proj, late=[(move.over_y, y_send)]
-    )
-    (keep_a, send_a, parts_a, bias_a), (core_got,) = beside(
-        unit, (own_a, key_got), (move.over_core, send), up, proj
+    oth_b, (got_a,) = beside(*back(1), keys_of(oth_a), up, proj)
+    own_a, (got_b,) = beside(*back(2), keys_of(oth_b), up, proj)
+    (keep_oth, send, rows_oth, bias_oth), (key_got,) = beside(
+        unit, ((oth_a, oth_b), (got_a, got_b)), keys_of(own_a), up, proj
+    )
+    (keep_a, send_a, rows_a, bias_a), (core_got,) = beside(
+        unit, ((own_a,), (key_got,)), (move.over_core, send), proj
     )
     mixed = jnp.concatenate([up.done[0], proj.done[0].reshape(-1, up.done.shape[2])])
     mixed, keep_a, down_all = tie(mixed, keep_a, down_all)
     mixed_all = lax.all_gather(mixed, "dp")
+    y_sends = [keep_oth[..., at : at + cols] + core_got[..., at : at + cols] for at in (0, cols)]
     own_b, (core_got_a, y_got_a, y_got_b) = beside(
-        *back(3),
-        (move.over_core, send_a),
-        (lambda x: x, y_got_a),
-        late=[(move.over_y, keep_oth_b + core_got)],
-    )
+        *back(3), (move.over_core, send_a), late=[(move.over_y, y) for y in y_sends]
+    )
+    y_got_a, own_b = tie(y_got_a, own_b)
     keep_a, send_a = halves(keep_a + core_got_a + y_got_a)
     partial, (key_got, a_got) = beside(
-        lambda *ps: early_rows(qkv_own, qkv_oth, *ps),
-        (parts_a, (parts_oth_a, parts_oth_b)),
+        lambda *xs: early_rows(qkv_own, qkv_oth, *xs),
+        (rows_a, rows_oth),
         keys_of(own_b),
         late=[(level(0), send_a)],
     )
-    (keep_b, send_b, parts_b, bias_b), (a_got, y_got_b) = beside(
-        unit, (own_b, key_got), (lambda x: x, a_got), (lambda x: x, y_got_b)
-    )
+    (keep_b, send_b, rows_b, bias_b), _ = beside(unit, ((own_b,), (key_got,)))
+    keep_b, a_got, y_got_b = tie(keep_b, a_got, y_got_b)
     keep_a, send_a = halves(keep_a + a_got)
     (in_grad, sums_one), (core_got, a_got) = beside(
         lambda *xs: last_rows(block_in, branch_grad, row(ln1_scale), *xs),
-        (partial, qkv_own, parts_b),
+        (partial, qkv_own, rows_b),
         (move.over_core, send_b),
         (level(1), send_a),
     )
@@ -1159,8 +1157,8 @@
     side = lambda a, b: jnp.concatenate([a.reshape(3, cols), b.reshape(3, cols)], axis=1).reshape(-1)
     vec, flat = move.reduce_vectors(
         jnp.concatenate([sums_one[:2], sums_two[:4]]),
-        jnp.concatenate([side(bias_a, bias_b), up_b_own[0]]),
-        jnp.concatenate([side(bias_oth_a, bias_oth_b), up_b_oth[0]]),
+        jnp.concatenate([side(bias_a[0], bias_b[0]), up_b_own[0]]),
+        jnp.concatenate([bias_oth[0], up_b_oth[0]]),
     )
     f32 = lambda v: v.astype(F32)
     return (

time: 656 us -> 591 us (0.901)
  waiting for transfers between devices: 95.1 us -> 61.3 us
  starting transfers between devices: 92.7 us -> 65.7 us
  Pallas kernels: 333 us -> 324 us
    ppermute x60 -> x52, waiting for transfers between devices: 80.9 us -> 47.6 us  [move(): return lax.ppermute(x, ('dp', 'tensor'), pairs)]
    ppermute x60 -> x52, starting transfers between devices: 92.3 us -> 65.2 us  [move(): return lax.ppermute(x, ('dp', 'tensor'), pairs)]
    select_n x0 -> x4, other arithmetic: none -> 9.46 us  [swap_rows(): return jnp.where(self.core == self.me_y, rows, got)]
    pallas_call x6 -> x5, Pallas kernels: 52.9 us -> 45.3 us  [the longest x3 25.9 us: unit_grads(): pl.pallas_call(functools.partial(unit_kernel, chips=chips, parts=parts),...]
    unnamed x152 -> x140, local copies, waits for them, and re-layouts: 17.1 us -> 18.7 us
  transfers between devices with their start and end apart: 66 -> 58, of which waited for: 20 -> 16; matrix products, arithmetic and copies ran while one was open for 10% -> 14% of each run, Pallas kernels for 49% -> 49%
where the time goes in v5:
time: 591 us; the launch traced here: 583 us
  Pallas kernels  324 us (55%)
  starting transfers between devices  65.7 us (11%)
  waiting for transfers between devices  61.3 us (10%)
  other arithmetic  44.5 us (8%)
  local copies, waits for them, and re-layouts  42.1 us (7%)
  matrix products  29.7 us (5%)
  between operations  15.7 us (3%)
    pallas_call x4, Pallas kernels, attend_back(): call(functools.partial(attend_back_kernel, sources=len(kvs), keys_at=1024...  97.1 us
    ppermute x52, starting transfers between devices, move(): return lax.ppermute(x, ('dp', 'tensor'), pairs)  65.2 us
    pallas_call x3, Pallas kernels, attend(): call(functools.partial(attend_kernel, sources=len(kvs), rows_at=min(512,...  48.9 us
    ppermute x52, waiting for transfers between devices, move(): return lax.ppermute(x, ('dp', 'tensor'), pairs)  47.6 us
    pallas_call x3, Pallas kernels, unit_grads(): pl.pallas_call(functools.partial(unit_kernel, chips=chips, parts=parts),...  25.9 us
    pallas_call x2, Pallas kernels, up_rows(): call(up_kernel, 2 * tokens * width * cols, 2 * (tokens * width + width *...  22.1 us
    pallas_call x2, Pallas kernels, qkv_rows(): call(functools.partial(qkv_kernel, q_steps=q_steps), 2 * tokens * width *...  21.4 us
    pallas_call x2, Pallas kernels, hidden_grads(): call(functools.partial(hidden_grad_kernel, skip=skip), 2 * tokens * width...  20.3 us
  transfers between devices with their start and end apart: 58, of which 16 were waited for; matrix products, arithmetic and copies ran while one was open for 14% of the time, Pallas kernels for 49%

profile of v5, /device:TPU:0, one launch (start us, length us, event | category | flops | bytes accessed | tf_op | source)
XLA Modules:
  0.0 583.1 jit_solution(14025404371905691767)
XLA Ops:
  8.4 3.0 collective-permute-start.1
  11.4 4.9 collective-permute-done.1
  17.1 2.0 collective-permute-start
  24.6 3.6 fusion.3
  29.7 5.0 shard_map.326
  34.8 19.9 %collective-permute-start.3 = (bf16[160,1024]{1,0:T(8,128)(2,1)S(1)}, bf16[160,1024]{1,0:T(8,128)(2,1)S(1)}, u32[]{:S(2)}, u32[]{:S(2)}) collective-permute-start(bf16[160,1024]{1,0:T(8,128)(2,1)S(1)} %pad_maximum_fusion.3), channel_id=1, source_target_pairs={{0,1},{1,0},{2,3},{3,2},{4,5},{5,4},{6,7},{7,6},{8,9},{9,8},{10,11... | collective-permute-start | bytes 983048 | tf_op jit(solution)/shard_map/ppermute | solution.py:760
  55.3 10.7 %shard_map.327 = (bf16[1024,512]{1,0:T(8,128)(2,1)}, bf16[1024,1024]{1,0:T(8,128)(2,1)}) custom-call(bf16[1024,1024]{1,0:T(8,128)(2,1)} %get-tuple-element.266.n_ref, bf16[1,3,1024,512]{3,2,1,0:T(8,128)(2,1)} %bitcast.134, f32[1,1536]{1,0:T(1,128)} %bitcast.153, f32[1024,128]{1,0:T(8,128)} %get-tuple-element.532.c_ref.refs_4_, ...), custom_call_target="tpu_custom_call" | custom-call | flops 3221225472 | bytes 8388608 | tf_op jit(solution)/shard_map/pallas_call | solution.py:140
  66.0 2.3 collective-permute-done.2
  70.5 3.4 collective-permute-done.5
  75.8 12.7 %shard_map.328 = (bf16[1024,256]{1,0:T(8,128)(2,1)}, f32[2,2,1024]{2,1,0:T(2,128)}) custom-call(bf16[1024,512]{1,0:T(8,128)(2,1)} %get-tuple-element.454.refs_0_, bf16[1024,1024]{1,0:T(8,128)(2,1)} %get-tuple-element.458.refs_1_.refs_3_.refs_7_.refs_9_, bf16[1024,1024]{1,0:T(8,128)(2,1)} %copy-done.59, ...), custom_call_target="tpu_custom_call" | custom-call | flops 8589934592 | bytes 3145728 | tf_op jit(solution)/shard_map/pallas_call | solution.py:208
  88.5 10.7 %shard_map.329 = (bf16[1024,512]{1,0:T(8,128)(2,1)}, bf16[1024,1024]{1,0:T(8,128)(2,1)}) custom-call(bf16[1024,1024]{1,0:T(8,128)(2,1)} %get-tuple-element.266.n_ref, bf16[16,3,64,512]{3,2,1,0:T(8,128)(2,1)} %bitcast.159, f32[1,1536]{1,0:T(1,128)} %reshape.237.b_ref, f32[1024,128]{1,0:T(8,128)} %get-tuple-element.532.c_ref.refs_4_, ...), custom_call_target="tpu_custom_call" | custom-call | flops 3221225472 | bytes 8388608 | tf_op jit(solution)/shard_map/pallas_call | solution.py:140
  105.1 12.7 %shard_map.330 = (bf16[1024,256]{1,0:T(8,128)(2,1)}, f32[2,2,1024]{2,1,0:T(2,128)}) custom-call(bf16[1024,512]{1,0:T(8,128)(2,1)} %get-tuple-element.454.refs_0_, bf16[1024,1024]{1,0:T(8,128)(2,1)} %get-tuple-element.458.refs_1_.refs_3_.refs_7_.refs_9_, bf16[1024,1024]{1,0:T(8,128)(2,1)} %copy-done.59, ...), custom_call_target="tpu_custom_call" | custom-call | flops 8589934592 | bytes 3145728 | tf_op jit(solution)/shard_map/pallas_call | solution.py:208
  117.8 23.5 %shard_map.331 = (bf16[1024,512]{1,0:T(8,128)(2,1)}, f32[4,2,1024]{2,1,0:T(2,128)}) custom-call(bf16[1024,512]{1,0:T(8,128)(2,1)} %get-tuple-element.380.refs_0_, bf16[1024,1024]{1,0:T(8,128)(2,1)} %get-tuple-element.384.refs_1_.refs_3_.refs_7_.refs_9_, bf16[1024,1024]{1,0:T(8,128)(2,1)} %collective-permute-done.6.refs_2_.refs_4_.refs_8_.refs_10_, ...), custom_call_target="tpu_custom_call" | custom-call | flops 17179869184 | bytes 6291456 | tf_op jit(solution)/shard_map/pallas_call | solution.py:208
  142.8 2.3 slice.248
  145.1 7.9 %shard_map.332 = (f32[1024,1024]{1,0:T(8,128)}, bf16[1024,1024]{1,0:T(8,128)(2,1)}, bf16[1024,1024]{1,0:T(8,128)(2,1)}) custom-call(bf16[1024,1024]{1,0:T(8,128)(2,1)} %broadcast_select_fusion.3.x_ref.refs_0_, f32[1,1024]{1,0:T(1,128)} %bitcast.157, f32[1,1024]{1,0:T(1,128)} %bitcast.154, f32[1,1024]{1,0:T(1,128)} %bitcast.158, ...), custom_call_target="tpu_custom_call" | custom-call | flops 2147483648 | bytes 14680064 | tf_op jit(solution)/shard_map/pallas_call | solution.py:447
  153.0 11.1 %shard_map.333 = (bf16[1024,2048]{1,0:T(8,128)(2,1)}, bf16[1024,2048]{1,0:T(8,128)(2,1)}) custom-call(bf16[1024,1024]{1,0:T(8,128)(2,1)} %get-tuple-element.295.n_ref, bf16[1024,2048]{1,0:T(8,128)(2,1)} %refs_2_.1, f32[1,2048]{1,0:T(1,128)} %bitcast.151), custom_call_target="tpu_custom_call" | custom-call | flops 4294967296 | bytes 14680064 | tf_op jit(solution)/shard_map/pallas_call | solution.py:359
  164.1 13.0 %all-gather.18.cloned.1.call-done.w_ref.refs_3_ = bf16[1024,2048]{1,0:T(8,128)(2,1)} async-done(((bf16[64,2048]{1,0:T(8,128)(2,1)}), bf16[1024,2048]{1,0:T(8,128)(2,1)}) %all-gather.18.cloned.1.call-update) | async-done | bytes 4194320 | tf_op jit(solution)/shard_map/all_gather | solution.py:1026
  177.1 11.0 %shard_map.334 = (bf16[1024,2048]{1,0:T(8,128)(2,1)}, bf16[1024,2048]{1,0:T(8,128)(2,1)}) custom-call(bf16[1024,1024]{1,0:T(8,128)(2,1)} %get-tuple-element.295.n_ref, bf16[1024,2048]{1,0:T(8,128)(2,1)} %all-gather.18.cloned.1.call-done.w_ref.refs_3_, f32[1,2048]{1,0:T(1,128)} %bitcast.152), custom_call_target="tpu_custom_call" | custom-call | flops 4294967296 | bytes 14680064 | tf_op jit(solution)/shard_map/pallas_call | solution.py:359
  188.0 15.5 %shard_map.335 = bf16[1024,1024]{1,0:T(8,128)(2,1)} custom-call(f32[1024,1024]{1,0:T(8,128)} %get-tuple-element.300.r_ref, f32[1,1024]{1,0:T(1,128)} %bitcast.156, bf16[1024,2048]{1,0:T(8,128)(2,1)} %get-tuple-element.301.refs_0_, bf16[1024,2048]{1,0:T(8,128)(2,1)} %get-tuple-element.303.refs_1_, bf16[1,2048,1024]{2,1,0:T(8,128)(2,1)} %bitcast.147, ...), custom_call_target="tpu_custom_call" | custom-call | flops 8589934592 | bytes 23068672 | tf_op jit(solution)/shard_map/pallas_call | solution.py:477
  203.6 4.8 convolution_convert_fusion.3
  208.4 4.9 convolution_convert_fusion.2
  213.3 1.8 dynamic-slice_bitcast_fusion.2
  218.7 9.7 %shard_map.336 = (bf16[1024,2048]{1,0:T(8,128)(2,1)}, f32[1,2048]{1,0:T(1,128)}) custom-call(bf16[1024,1024]{1,0:T(8,128)(2,1)} %broadcast_select_fusion.2.g_ref, bf16[1,2048,1024]{2,1,0:T(8,128)(2,1)} %bitcast.148, bf16[1024,2048]{1,0:T(8,128)(2,1)} %get-tuple-element.308.slope_ref), custom_call_target="tpu_custom_call" | custom-call | flops 4294967296 | bytes 14680064 | tf_op jit(solution)/shard_map/pallas_call | solution.py:394
  229.7 6.5 %shard_map.337 = (bf16[4,128,1024]{2,1,0:T(8,128)(2,1)}, bf16[4,128,1024]{2,1,0:T(8,128)(2,1)}, bf16[2,4,128,1024]{3,2,1,0:T(8,128)(2,1)}) custom-call(s32[9]{0:T(128)} %pad_add_fusion.t_ref, bf16[8,2,128,1024]{3,2,1,0:T(8,128)(2,1)} %bitcast.113, bf16[8,2,128,1024]{3,2,1,0:T(8,128)(2,1)} %bitcast.114, bf16[8,2,128,1024]{3,2,1,0:T(8,128)(2,1)} %bitcast.116, ...), custom_call_target="tpu_custom_call" | custom-call | flops 2097152 | bytes 12582912 | tf_op jit(solution)/shard_map/pallas_call | solution.py:720
  237.7 10.6 %shard_map.338 = (bf16[1024,2048]{1,0:T(8,128)(2,1)}, f32[1,2048]{1,0:T(1,128)}) custom-call(bf16[1024,1024]{1,0:T(8,128)(2,1)} %broadcast_select_fusion.2.g_ref, bf16[16,160,1024]{2,1,0:T(8,128)(2,1)} %bitcast.141, bf16[1024,2048]{1,0:T(8,128)(2,1)} %get-tuple-element.319.slope_ref), custom_call_target="tpu_custom_call" | custom-call | flops 4294967296 | bytes 14680064 | tf_op jit(solution)/shard_map/pallas_call | solution.py:394
  248.3 7.1 %convolution_convert_fusion = bf16[1024,2048]{1,0:T(8,128)(2,1)S(1)} fusion(bf16[1024,1024]{1,0:T(8,128)(2,1)S(1)} %copy-done.64, bf16[1024,2048]{1,0:T(8,128)(2,1)} %get-tuple-element.331.refs_1_), kind=kOutput, calls=%fused_computation.1 | convolution fusion | flops 4297064448 | bytes 10485760 | tf_op jit(solution)/shard_map/dot_general | solution.py:32
  255.4 4.8 convolution_convert_fusion.1
  260.2 2.3 collective-permute-done.10
  267.5 2.0 collective-permute-start.19
  269.4 17.6 %shard_map.339 = (bf16[1024,1024]{1,0:T(8,128)(2,1)}, f32[8,1024]{1,0:T(8,128)}) custom-call(f32[1024,1024]{1,0:T(8,128)} %get-tuple-element.300.r_ref, bf16[1024,1024]{1,0:T(8,128)(2,1)} %broadcast_select_fusion.2.g_ref, f32[1,1024]{1,0:T(1,128)} %bitcast.155, bf16[1024,2048]{1,0:T(8,128)(2,1)} %get-tuple-element.330.refs_0_, ...), custom_call_target="tpu_custom_call" | custom-call | flops 8589934592 | bytes 25165824 | tf_op jit(solution)/shard_map/pallas_call | solution.py:516
  288.0 2.9 fusion.1
  297.0 2.3 convolution_convert_fusion.4.refs_1_
  300.0 6.6 %shard_map.340 = (bf16[4,64,2048]{2,1,0:T(8,128)(2,1)}, bf16[4,64,2048]{2,1,0:T(8,128)(2,1)}, bf16[2,4,64,2048]{3,2,1,0:T(8,128)(2,1)}) custom-call(s32[9]{0:T(128)} %pad_add_fusion.t_ref, bf16[8,2,64,2048]{3,2,1,0:T(8,128)(2,1)} %bitcast.122, bf16[8,2,64,2048]{3,2,1,0:T(8,128)(2,1)} %bitcast.123, bf16[8,2,64,2048]{3,2,1,0:T(8,128)(2,1)} %bitcast.119, ...), custom_call_target="tpu_custom_call" | custom-call | flops 2097152 | bytes 12582912 | tf_op jit(solution)/shard_map/pallas_call | solution.py:720
  310.1 2.3 collective-permute-start.15
  312.3 3.1 broadcast_select_fusion.1
  316.9 24.3 %shard_map.341 = (bf16[1024,256]{1,0:T(8,128)(2,1)}, bf16[2,1024,256]{2,1,0:T(8,128)(2,1)}, bf16[2,1024,256]{2,1,0:T(8,128)(2,1)}) custom-call(bf16[1024,512]{1,0:T(8,128)(2,1)} %get-tuple-element.380.refs_0_, bf16[1024,512]{1,0:T(8,128)(2,1)} %convolution_convert_fusion.4.refs_1_, bf16[1024,512]{1,0:T(8,128)(2,1)} %get-tuple-element.382.refs_6_.refs_2_, ...), custom_call_target="tpu_custom_call" | custom-call | flops 21474836480 | bytes 6291456 | tf_op jit(solution)/shard_map/pallas_call | solution.py:300
  343.5 4.5 shard_map.342
  350.0 24.1 %shard_map.343 = (bf16[1024,256]{1,0:T(8,128)(2,1)}, bf16[2,1024,256]{2,1,0:T(8,128)(2,1)}, bf16[2,1024,256]{2,1,0:T(8,128)(2,1)}) custom-call(bf16[1024,512]{1,0:T(8,128)(2,1)} %get-tuple-element.380.refs_0_, bf16[1024,512]{1,0:T(8,128)(2,1)} %convolution_convert_fusion.4.refs_1_, bf16[1024,512]{1,0:T(8,128)(2,1)} %get-tuple-element.382.refs_6_.refs_2_, ...), custom_call_target="tpu_custom_call" | custom-call | flops 21474836480 | bytes 6291456 | tf_op jit(solution)/shard_map/pallas_call | solution.py:300
  377.4 24.6 %shard_map.344 = (bf16[1024,256]{1,0:T(8,128)(2,1)}, bf16[2,1024,256]{2,1,0:T(8,128)(2,1)}, bf16[2,1024,256]{2,1,0:T(8,128)(2,1)}) custom-call(bf16[1024,512]{1,0:T(8,128)(2,1)} %get-tuple-element.454.refs_0_, bf16[1024,256]{1,0:T(8,128)(2,1)} %convolution_convert_fusion.7.refs_1_, bf16[1024,256]{1,0:T(8,128)(2,1)} %get-tuple-element.399.refs_4_.refs_2_, ...), custom_call_target="tpu_custom_call" | custom-call | flops 21474836480 | bytes 6291456 | tf_op jit(solution)/shard_map/pallas_call | solution.py:300
  405.4 2.1 collective-permute-start.27
  407.5 10.8 %shard_map.345 = (bf16[8,3,64,512]{3,2,1,0:T(8,128)(2,1)}, bf16[8,3,64,512]{3,2,1,0:T(8,128)(2,1)}, bf16[1024,1536]{1,0:T(8,128)(2,1)}, f32[8,1536]{1,0:T(8,128)}) custom-call(s32[16]{0:T(128)} %pad_add_fusion.1.t_ref, bf16[1024,1024]{1,0:T(8,128)(2,1)} %get-tuple-element.371.nt_ref, f32[1024,128]{1,0:T(8,128)} %get-tuple-element.532.c_ref.refs_4_, ...), custom_call_target="tpu_custom_call" | custom-call | flops 3221225472 | bytes 13631488 | tf_op jit(solution)/shard_map/pallas_call | solution.py:646
  420.9 7.5 %shard_map.346 = (bf16[8,3,64,256]{3,2,1,0:T(8,128)(2,1)}, bf16[8,3,64,256]{3,2,1,0:T(8,128)(2,1)}, bf16[1024,768]{1,0:T(8,128)(2,1)}, f32[8,768]{1,0:T(8,128)}) custom-call(s32[16]{0:T(128)} %pad_add_fusion.1.t_ref, bf16[1024,1024]{1,0:T(8,128)(2,1)} %get-tuple-element.371.nt_ref, f32[1024,128]{1,0:T(8,128)} %get-tuple-element.532.c_ref.refs_4_, ...), custom_call_target="tpu_custom_call" | custom-call | flops 1610612736 | bytes 7864320 | tf_op jit(solution)/shard_map/pallas_call | solution.py:646
  429.5 1.7 collective-permute-start.31
  431.2 24.1 %shard_map.347 = (bf16[1024,256]{1,0:T(8,128)(2,1)}, bf16[2,1024,256]{2,1,0:T(8,128)(2,1)}, bf16[2,1024,256]{2,1,0:T(8,128)(2,1)}) custom-call(bf16[1024,512]{1,0:T(8,128)(2,1)} %get-tuple-element.454.refs_0_, bf16[1024,256]{1,0:T(8,128)(2,1)} %convolution_convert_fusion.6.refs_1_, bf16[1024,256]{1,0:T(8,128)(2,1)} %get-tuple-element.456.refs_5_.refs_2_, ...), custom_call_target="tpu_custom_call" | custom-call | flops 21474836480 | bytes 6291456 | tf_op jit(solution)/shard_map/pallas_call | solution.py:300
  458.9 10.4 %shard_map.348.part_ref = f32[1024,1024]{1,0:T(8,128)} custom-call(bf16[1,3,1024,512]{3,2,1,0:T(8,128)(2,1)} %bitcast.135, bf16[16,3,64,512]{3,2,1,0:T(8,128)(2,1)} %bitcast.160, bf16[1024,768]{1,0:T(8,128)(2,1)} %get-tuple-element.475.own_rows, bf16[1024,1536]{1,0:T(8,128)(2,1)} %get-tuple-element.476.oth_rows), custom_call_target="tpu_custom_call" | custom-call | flops 4831838208 | bytes 13631488 | tf_op jit(solution)/shard_map/pallas_call | solution.py:566
  470.2 7.5 %shard_map.349 = (bf16[8,3,64,256]{3,2,1,0:T(8,128)(2,1)}, bf16[8,3,64,256]{3,2,1,0:T(8,128)(2,1)}, bf16[1024,768]{1,0:T(8,128)(2,1)}, f32[8,768]{1,0:T(8,128)}) custom-call(s32[16]{0:T(128)} %pad_add_fusion.1.t_ref, bf16[1024,1024]{1,0:T(8,128)(2,1)} %get-tuple-element.371.nt_ref, f32[1024,128]{1,0:T(8,128)} %get-tuple-element.532.c_ref.refs_4_, ...), custom_call_target="tpu_custom_call" | custom-call | flops 1610612736 | bytes 7864320 | tf_op jit(solution)/shard_map/pallas_call | solution.py:646
  480.3 2.0 collective-permute-start.37
  482.3 9.0 %shard_map.350 = (bf16[1024,1024]{1,0:T(8,128)(2,1)}, f32[8,1024]{1,0:T(8,128)}) custom-call(bf16[1024,1024]{1,0:T(8,128)(2,1)} %broadcast_select_fusion.3.x_ref.refs_0_, bf16[1024,1024]{1,0:T(8,128)(2,1)} %get-tuple-element.340.g_ref, f32[1,1024]{1,0:T(1,128)} %bitcast.145, f32[1024,1024]{1,0:T(8,128)} %shard_map.348.part_ref, ...), custom_call_target="tpu_custom_call" | custom-call | flops 1610612736 | bytes 13631488 | tf_op jit(solution)/shard_map/pallas_call | solution.py:583
  491.3 3.5 collective-permute-done.37
  499.4 2.6 collective-permute-done.40
  502.9 4.2 collective-permute-done.41
  507.4 6.6 %convert_element_type.89 = f32[2048,1024]{1,0:T(8,128)} convert(bf16[2048,1024]{1,0:T(8,128)(2,1)} %bitcast.133) | non-fusion elementwise | flops 2097152 | bytes 12582912 | tf_op jit(solution)/shard_map/convert_element_type | solution.py:1163
  515.5 1.9 collective-permute-start.46
  518.0 2.6 collective-permute-start.44
  522.3 3.0 collective-permute-start.47
  526.0 4.7 collective-permute-done.47
  533.2 2.1 collective-permute-start.38
  535.2 2.7 collective-permute-done.48
  538.7 2.5 slice.243
  541.2 4.1 collective-permute-done.49
  546.0 4.7 bitcast_convert_fusion
  550.8 8.1 %collective-permute-done.50 = bf16[4,3,64,256]{3,2,1,0:T(8,128)(2,1)S(1)} collective-permute-done((bf16[4,3,64,256]{3,2,1,0:T(8,128)(2,1)S(1)}, bf16[4,3,64,256]{3,2,1,0:T(8,128)(2,1)S(1)}, u32[]{:S(2)}, u32[]{:S(2)}) %collective-permute-start.50) | collective-permute-done | bytes 393248 | tf_op jit(solution)/shard_map/ppermute | solution.py:760
  564.9 3.3 broadcast_select_fusion
  570.5 5.5 shard_map.351
  (341 shorter events, 88.4 us)
Async XLA Ops:
  7.2 17.3 %copy-start.51 = (f32[128]{0:T(128)S(1)}, f32[128]{0:T(128)}, u32[]{:S(2)}) copy-start(f32[128]{0:T(128)} %constant.162) | copy-start | bytes 1540
  7.3 20.9 %copy-start.10 = (bf16[1024,1024]{1,0:T(8,128)(2,1)S(1)}, bf16[1024,1024]{1,0:T(8,128)(2,1)}, u32[]{:S(2)}) copy-start(bf16[1024,1024]{1,0:T(8,128)(2,1)} %param.23) | copy-start | bytes 6291460
  7.3 81.2 %all-gather.14.cloned.1.call-start = ((), (), s32[]{:S(2)}) async-start(), calls=%async_computation.1 | async-start | bytes 3342336 | tf_op jit(solution)/shard_map/all_gather | solution.py:1017
  8.4 7.9 %collective-permute-start.1 = (bf16[3,64,512]{2,1,0:T(8,128)(2,1)S(1)}, bf16[3,64,512]{2,1,0:T(8,128)(2,1)S(1)}, u32[]{:S(2)}, u32[]{:S(2)}) collective-permute-start(bf16[3,64,512]{2,1,0:T(8,128)(2,1)S(1)} %dynamic-slice_bitcast_fusion.6), channel_id=1, source_target_pairs={{0,1},{1,0},{2,3},{3,2},{4,5},{5,4},{6,7},{7,6},{8,9},{9,8},{10,11... | collective-permute-start | bytes 589832 | tf_op jit(solution)/shard_map/ppermute | solution.py:760
  17.0 125.7 %all-gather.16.cloned.1.call-start = ((), (), s32[]{:S(2)}) async-start(), calls=%async_computation.2 | async-start | bytes 5570560 | tf_op jit(solution)/shard_map/all_gather | solution.py:1026
  17.1 11.1 %collective-permute-start = (bf16[1024,1024]{1,0:T(8,128)(2,1)}, bf16[1024,1024]{1,0:T(8,128)(2,1)}, u32[]{:S(2)}, u32[]{:S(2)}) collective-permute-start(bf16[1024,1024]{1,0:T(8,128)(2,1)} %param.23), channel_id=1, source_target_pairs={{1,2},{2,1},{5,6},{6,5},{9,10},{10,9},{13,14},{14,13},{17,18},{18,... | collective-permute-start | bytes 6291464 | tf_op jit(solution)/shard_map/ppermute | solution.py:760
  29.7 24.9 %copy-start.42 = (bf16[3,512]{1,0:T(4,128)(2,1)S(1)}, bf16[3,512]{1,0:T(4,128)(2,1)}, u32[]{:S(2)}) copy-start(bf16[3,512]{1,0:T(4,128)(2,1)} %param.27) | copy-start | bytes 9220
  34.8 33.5 %collective-permute-start.3 = (bf16[160,1024]{1,0:T(8,128)(2,1)S(1)}, bf16[160,1024]{1,0:T(8,128)(2,1)S(1)}, u32[]{:S(2)}, u32[]{:S(2)}) collective-permute-start(bf16[160,1024]{1,0:T(8,128)(2,1)S(1)} %pad_maximum_fusion.3), channel_id=1, source_target_pairs={{0,1},{1,0},{2,3},{3,2},{4,5},{5,4},{6,7},{7,6},{8,9},{9,8},{10,11... | collective-permute-start | bytes 983048 | tf_op jit(solution)/shard_map/ppermute | solution.py:760
  55.3 13.0 %collective-permute-start.2 = (bf16[64,2048]{1,0:T(8,128)(2,1)S(1)}, bf16[64,2048]{1,0:T(8,128)(2,1)S(1)}, u32[]{:S(2)}, u32[]{:S(2)}) collective-permute-start(bf16[64,2048]{1,0:T(8,128)(2,1)S(1)} %constant_dynamic-slice_fusion.4), channel_id=1, source_target_pairs={{0,1},{1,0},{2,3},{3,2},{4,5},{5,4},{6,7},{7,6},{8,9},{9,8},{10,11... | collective-permute-start | bytes 786440 | tf_op jit(solution)/shard_map/ppermute | solution.py:760
  69.1 108.0 %all-gather.18.cloned.1.call-start = ((), (), s32[]{:S(2)}) async-start(), calls=%async_computation.3 | async-start | bytes 4456448 | tf_op jit(solution)/shard_map/all_gather | solution.py:1026
  69.1 5.3 collective-permute-start.4
  69.8 359.4 %all-gather.20.cloned.1.call-start = ((), (), s32[]{:S(2)}) async-start(), calls=%async_computation.4 | async-start | bytes 4456448 | tf_op jit(solution)/shard_map/all_gather | solution.py:810
  70.1 3.7 collective-permute-start.5
  99.2 18.5 %collective-permute-start.6 = (bf16[1024,1024]{1,0:T(8,128)(2,1)}, bf16[1024,1024]{1,0:T(8,128)(2,1)}, u32[]{:S(2)}, u32[]{:S(2)}) collective-permute-start(bf16[1024,1024]{1,0:T(8,128)(2,1)} %get-tuple-element.384.refs_1_.refs_3_.refs_7_.refs_9_), channel_id=1, source_target_pairs={{0,2},{1,3},{2,0},{3,1},{4,6},{5,7},{6,4},{7,5},{8,10},{9,11},{10,... | collective-permute-start | bytes 6291464 | tf_op jit(solution)/shard_map/ppermute | solution.py:760
  103.9 37.4 %collective-permute-start.7 = (bf16[1024,1024]{1,0:T(8,128)(2,1)S(1)}, bf16[1024,1024]{1,0:T(8,128)(2,1)S(1)}, u32[]{:S(2)}, u32[]{:S(2)}) collective-permute-start(bf16[1024,1024]{1,0:T(8,128)(2,1)S(1)} %copy-done.11), channel_id=1, source_target_pairs={{1,2},{2,1},{5,6},{6,5},{9,10},{10,9},{13,14},{14,13},{17,18},{18,... | collective-permute-start | bytes 6291464 | tf_op jit(solution)/shard_map/ppermute | solution.py:760
  217.6 10.9 %collective-permute-start.8 = (bf16[8,128,1024]{2,1,0:T(8,128)(2,1)}, bf16[8,128,1024]{2,1,0:T(8,128)(2,1)S(1)}, u32[]{:S(2)}, u32[]{:S(2)}) collective-permute-start(bf16[8,128,1024]{2,1,0:T(8,128)(2,1)} %dynamic-slice_bitcast_fusion.3), channel_id=1, source_target_pairs={{0,2},{1,3},{2,0},{3,1},{4,6},{5,7},{6,4},{7,5},{8,10},{9,11},{10,... | collective-permute-start | bytes 6291464 | tf_op jit(solution)/shard_map/ppermute | solution.py:760
  217.8 10.6 %collective-permute-start.9 = (bf16[8,128,1024]{2,1,0:T(8,128)(2,1)}, bf16[8,128,1024]{2,1,0:T(8,128)(2,1)}, u32[]{:S(2)}, u32[]{:S(2)}) collective-permute-start(bf16[8,128,1024]{2,1,0:T(8,128)(2,1)} %dynamic-slice_bitcast_fusion.2), channel_id=1, source_target_pairs={{0,2},{1,3},{2,0},{3,1},{4,6},{5,7},{6,4},{7,5},{8,10},{9,11},{10,... | collective-permute-start | bytes 6291464 | tf_op jit(solution)/shard_map/ppermute | solution.py:760
  236.3 26.2 %collective-permute-start.10 = (bf16[2,4,128,1024]{3,2,1,0:T(8,128)(2,1)}, bf16[2,4,128,1024]{3,2,1,0:T(8,128)(2,1)S(1)}, u32[]{:S(2)}, u32[]{:S(2)}) collective-permute-start(bf16[2,4,128,1024]{3,2,1,0:T(8,128)(2,1)} %get-tuple-element.324), channel_id=1, source_target_pairs={{0,1},{1,0},{2,6},{3,7},{4,5},{5,4},{6,2},{7,3},{8,9},{9,8},{10,14... | collective-permute-start | bytes 6291464 | tf_op jit(solution)/shard_map/ppermute | solution.py:760
  266.4 20.6 %collective-permute-start.11 = (bf16[8,64,2048]{2,1,0:T(8,128)(2,1)}, bf16[8,64,2048]{2,1,0:T(8,128)(2,1)S(1)}, u32[]{:S(2)}, u32[]{:S(2)}) collective-permute-start(bf16[8,64,2048]{2,1,0:T(8,128)(2,1)} %dynamic-slice_bitcast_fusion.1), channel_id=1, source_target_pairs={{0,2},{1,3},{2,0},{3,1},{4,6},{5,7},{6,4},{7,5},{8,10},{9,11},{10,... | collective-permute-start | bytes 6291464 | tf_op jit(solution)/shard_map/ppermute | solution.py:760
  266.4 20.7 %collective-permute-start.12 = (bf16[8,64,2048]{2,1,0:T(8,128)(2,1)S(1)}, bf16[8,64,2048]{2,1,0:T(8,128)(2,1)S(1)}, u32[]{:S(2)}, u32[]{:S(2)}) collective-permute-start(bf16[8,64,2048]{2,1,0:T(8,128)(2,1)S(1)} %dynamic-slice_bitcast_fusion), channel_id=1, source_target_pairs={{0,2},{1,3},{2,0},{3,1},{4,6},{5,7},{6,4},{7,5},{8,10},{9,11},{10,... | collective-permute-start | bytes 6291464 | tf_op jit(solution)/shard_map/ppermute | solution.py:760
  266.9 20.1 %collective-permute-start.13 = (bf16[4,128,1024]{2,1,0:T(8,128)(2,1)}, bf16[4,128,1024]{2,1,0:T(8,128)(2,1)S(1)}, u32[]{:S(2)}, u32[]{:S(2)}) collective-permute-start(bf16[4,128,1024]{2,1,0:T(8,128)(2,1)} %bitcast_add_fusion.2), channel_id=1, source_target_pairs={{0,4},{1,5},{2,3},{3,2},{4,0},{5,1},{6,7},{7,6},{8,12},{9,13},{10,... | collective-permute-start | bytes 3145736 | tf_op jit(solution)/shard_map/ppermute | solution.py:760
  267.5 44.9 %collective-permute-start.19 = (bf16[1024,1024]{1,0:T(8,128)(2,1)}, bf16[1024,1024]{1,0:T(8,128)(2,1)}, u32[]{:S(2)}, u32[]{:S(2)}) collective-permute-start(bf16[1024,1024]{1,0:T(8,128)(2,1)} %shard_map.335), channel_id=1, source_target_pairs={{1,2},{2,1},{5,6},{6,5},{9,10},{10,9},{13,14},{14,13},{17,18},{18,... | collective-permute-start | bytes 6291464 | tf_op jit(solution)/shard_map/ppermute | solution.py:760
  294.8 14.3 %collective-permute-start.14 = (bf16[2,128,1024]{2,1,0:T(8,128)(2,1)S(1)}, bf16[2,128,1024]{2,1,0:T(8,128)(2,1)S(1)}, u32[]{:S(2)}, u32[]{:S(2)}) collective-permute-start(bf16[2,128,1024]{2,1,0:T(8,128)(2,1)S(1)} %slice.251), channel_id=1, source_target_pairs={{0,8},{1,9},{2,10},{3,11},{4,12},{5,13},{6,14},{7,15},{8,0},{9,1},... | collective-permute-start | bytes 1572872 | tf_op jit(solution)/shard_map/ppermute | solution.py:760
  310.1 31.1 %collective-permute-start.15 = (bf16[2,4,64,2048]{3,2,1,0:T(8,128)(2,1)}, bf16[2,4,64,2048]{3,2,1,0:T(8,128)(2,1)S(1)}, u32[]{:S(2)}, u32[]{:S(2)}) collective-permute-start(bf16[2,4,64,2048]{3,2,1,0:T(8,128)(2,1)} %get-tuple-element.361), channel_id=1, source_target_pairs={{0,1},{1,0},{2,6},{3,7},{4,5},{5,4},{6,2},{7,3},{8,9},{9,8},{10,14... | collective-permute-start | bytes 6291464 | tf_op jit(solution)/shard_map/ppermute | solution.py:760
  315.5 25.7 %collective-permute-start.16 = (bf16[1,128,1024]{2,1,0:T(8,128)(2,1)S(1)}, bf16[1,128,1024]{2,1,0:T(8,128)(2,1)S(1)}, u32[]{:S(2)}, u32[]{:S(2)}) collective-permute-start(bf16[1,128,1024]{2,1,0:T(8,128)(2,1)S(1)} %slice.253), channel_id=1, source_target_pairs={{0,16},{1,17},{2,18},{3,19},{4,20},{5,21},{6,22},{7,23},{8,24},{9,... | collective-permute-start | bytes 786440 | tf_op jit(solution)/shard_map/ppermute | solution.py:760
  316.4 24.8 %collective-permute-start.17 = (bf16[8,32,1024]{2,1,0:T(8,128)(2,1)S(1)}, bf16[8,32,1024]{2,1,0:T(8,128)(2,1)S(1)}, u32[]{:S(2)}, u32[]{:S(2)}) collective-permute-start(bf16[8,32,1024]{2,1,0:T(8,128)(2,1)S(1)} %dynamic-slice_bitcast_fusion.5), channel_id=1, source_target_pairs={{0,2},{1,3},{2,0},{3,1},{4,6},{5,7},{6,4},{7,5},{8,10},{9,11},{10,... | collective-permute-start | bytes 1572872 | tf_op jit(solution)/shard_map/ppermute | solution.py:760
  316.5 24.7 %collective-permute-start.18 = (bf16[8,32,1024]{2,1,0:T(8,128)(2,1)S(1)}, bf16[8,32,1024]{2,1,0:T(8,128)(2,1)S(1)}, u32[]{:S(2)}, u32[]{:S(2)}) collective-permute-start(bf16[8,32,1024]{2,1,0:T(8,128)(2,1)S(1)} %dynamic-slice_bitcast_fusion.4), channel_id=1, source_target_pairs={{0,2},{1,3},{2,0},{3,1},{4,6},{5,7},{6,4},{7,5},{8,10},{9,11},{10,... | collective-permute-start | bytes 1572872 | tf_op jit(solution)/shard_map/ppermute | solution.py:760
  342.1 155.8 %all-gather.22.cloned.1.call-start = ((), (), s32[]{:S(2)}) async-start(), calls=%async_computation.5 | async-start | bytes 5570560 | tf_op jit(solution)/shard_map/all_gather | solution.py:1117
  348.0 26.2 %copy-start.26 = (bf16[4,64,2048]{2,1,0:T(8,128)(2,1)S(1)}, bf16[4,64,2048]{2,1,0:T(8,128)(2,1)}, u32[]{:S(2)}) copy-start(bf16[4,64,2048]{2,1,0:T(8,128)(2,1)} %get-tuple-element.393) | copy-start | bytes 3145732
  348.0 26.1 %collective-permute-start.22 = (bf16[2,4,32,1024]{3,2,1,0:T(8,128)(2,1)}, bf16[2,4,32,1024]{3,2,1,0:T(8,128)(2,1)S(1)}, u32[]{:S(2)}, u32[]{:S(2)}) collective-permute-start(bf16[2,4,32,1024]{3,2,1,0:T(8,128)(2,1)} %get-tuple-element.391), channel_id=1, source_target_pairs={{0,1},{1,0},{2,6},{3,7},{4,5},{5,4},{6,2},{7,3},{8,9},{9,8},{10,14... | collective-permute-start | bytes 1572872 | tf_op jit(solution)/shard_map/ppermute | solution.py:760
  348.1 26.0 %collective-permute-start.20 = (bf16[2,1024,256]{2,1,0:T(8,128)(2,1)}, bf16[2,1024,256]{2,1,0:T(8,128)(2,1)S(1)}, u32[]{:S(2)}, u32[]{:S(2)}) collective-permute-start(bf16[2,1024,256]{2,1,0:T(8,128)(2,1)} %get-tuple-element.389), channel_id=1, source_target_pairs={{0,2},{1,3},{2,0},{3,1},{4,6},{5,7},{6,4},{7,5},{8,10},{9,11},{10,... | collective-permute-start | bytes 3145736 | tf_op jit(solution)/shard_map/ppermute | solution.py:760
  348.5 25.7 %collective-permute-start.21 = (bf16[4,64,2048]{2,1,0:T(8,128)(2,1)S(1)}, bf16[4,64,2048]{2,1,0:T(8,128)(2,1)S(1)}, u32[]{:S(2)}, u32[]{:S(2)}) collective-permute-start(bf16[4,64,2048]{2,1,0:T(8,128)(2,1)S(1)} %bitcast_add_fusion.1), channel_id=1, source_target_pairs={{0,4},{1,5},{2,3},{3,2},{4,0},{5,1},{6,7},{7,6},{8,12},{9,13},{10,... | collective-permute-start | bytes 3145736 | tf_op jit(solution)/shard_map/ppermute | solution.py:760
  375.3 26.7 %copy-start.37 = (bf16[4,32,1024]{2,1,0:T(8,128)(2,1)S(1)}, bf16[4,32,1024]{2,1,0:T(8,128)(2,1)}, u32[]{:S(2)}) copy-start(bf16[4,32,1024]{2,1,0:T(8,128)(2,1)} %get-tuple-element.419) | copy-start | bytes 786436
  375.4 26.7 %collective-permute-start.25 = (bf16[4,32,1024]{2,1,0:T(8,128)(2,1)S(1)}, bf16[4,32,1024]{2,1,0:T(8,128)(2,1)S(1)}, u32[]{:S(2)}, u32[]{:S(2)}) collective-permute-start(bf16[4,32,1024]{2,1,0:T(8,128)(2,1)S(1)} %bitcast_add_fusion.5), channel_id=1, source_target_pairs={{0,4},{1,5},{2,3},{3,2},{4,0},{5,1},{6,7},{7,6},{8,12},{9,13},{10,... | collective-permute-start | bytes 786440 | tf_op jit(solution)/shard_map/ppermute | solution.py:760
  376.0 26.1 %collective-permute-start.24 = (bf16[2,64,2048]{2,1,0:T(8,128)(2,1)S(1)}, bf16[2,64,2048]{2,1,0:T(8,128)(2,1)S(1)}, u32[]{:S(2)}, u32[]{:S(2)}) collective-permute-start(bf16[2,64,2048]{2,1,0:T(8,128)(2,1)S(1)} %slice.254), channel_id=1, source_target_pairs={{0,8},{1,9},{2,10},{3,11},{4,12},{5,13},{6,14},{7,15},{8,0},{9,1},... | collective-permute-start | bytes 1572872 | tf_op jit(solution)/shard_map/ppermute | solution.py:760
  377.4 24.6 %collective-permute-start.23 = (bf16[2,1024,256]{2,1,0:T(8,128)(2,1)}, bf16[2,1024,256]{2,1,0:T(8,128)(2,1)S(1)}, u32[]{:S(2)}, u32[]{:S(2)}) collective-permute-start(bf16[2,1024,256]{2,1,0:T(8,128)(2,1)} %get-tuple-element.406), channel_id=1, source_target_pairs={{0,2},{1,3},{2,0},{3,1},{4,6},{5,7},{6,4},{7,5},{8,10},{9,11},{10,... | collective-permute-start | bytes 3145736 | tf_op jit(solution)/shard_map/ppermute | solution.py:760
  403.6 16.3 %collective-permute-start.26 = (bf16[2,1024,256]{2,1,0:T(8,128)(2,1)S(1)}, bf16[2,1024,256]{2,1,0:T(8,128)(2,1)S(1)}, u32[]{:S(2)}, u32[]{:S(2)}) collective-permute-start(bf16[2,1024,256]{2,1,0:T(8,128)(2,1)S(1)} %copy-done.61), channel_id=1, source_target_pairs={{0,2},{1,3},{2,0},{3,1},{4,6},{5,7},{6,4},{7,5},{8,10},{9,11},{10,... | collective-permute-start | bytes 3145736 | tf_op jit(solution)/shard_map/ppermute | solution.py:760
  404.8 13.6 %collective-permute-start.28 = (bf16[2,32,1024]{2,1,0:T(8,128)(2,1)S(1)}, bf16[2,32,1024]{2,1,0:T(8,128)(2,1)S(1)}, u32[]{:S(2)}, u32[]{:S(2)}) collective-permute-start(bf16[2,32,1024]{2,1,0:T(8,128)(2,1)S(1)} %slice.257), channel_id=1, source_target_pairs={{0,8},{1,9},{2,10},{3,11},{4,12},{5,13},{6,14},{7,15},{8,0},{9,1},... | collective-permute-start | bytes 393224 | tf_op jit(solution)/shard_map/ppermute | solution.py:760
  405.4 14.5 %collective-permute-start.27 = (bf16[1,64,2048]{2,1,0:T(8,128)(2,1)S(1)}, bf16[1,64,2048]{2,1,0:T(8,128)(2,1)S(1)}, u32[]{:S(2)}, u32[]{:S(2)}) collective-permute-start(bf16[1,64,2048]{2,1,0:T(8,128)(2,1)S(1)} %slice.256), channel_id=1, source_target_pairs={{0,16},{1,17},{2,18},{3,19},{4,20},{5,21},{6,22},{7,23},{8,24},{9,... | collective-permute-start | bytes 786440 | tf_op jit(solution)/shard_map/ppermute | solution.py:760
  419.9 8.5 %collective-permute-start.29 = (bf16[8,3,64,512]{3,2,1,0:T(8,128)(2,1)}, bf16[8,3,64,512]{3,2,1,0:T(8,128)(2,1)S(1)}, u32[]{:S(2)}, u32[]{:S(2)}) collective-permute-start(bf16[8,3,64,512]{3,2,1,0:T(8,128)(2,1)} %get-tuple-element.444), channel_id=1, source_target_pairs={{0,2},{1,3},{2,0},{3,1},{4,6},{5,7},{6,4},{7,5},{8,10},{9,11},{10,... | collective-permute-start | bytes 4718600 | tf_op jit(solution)/shard_map/ppermute | solution.py:760
  420.0 8.4 %collective-permute-start.30 = (bf16[1,32,1024]{2,1,0:T(8,128)(2,1)S(1)}, bf16[1,32,1024]{2,1,0:T(8,128)(2,1)S(1)}, u32[]{:S(2)}, u32[]{:S(2)}) collective-permute-start(bf16[1,32,1024]{2,1,0:T(8,128)(2,1)S(1)} %slice.259), channel_id=1, source_target_pairs={{0,16},{1,17},{2,18},{3,19},{4,20},{5,21},{6,22},{7,23},{8,24},{9,... | collective-permute-start | bytes 196616 | tf_op jit(solution)/shard_map/ppermute | solution.py:760
  429.3 140.2 %all-gather.12.cloned.1.call-start = ((), (), s32[]{:S(2)}) async-start(), calls=%async_computation | async-start | bytes 1671168 | tf_op jit(solution)/shard_map/all_gather | solution.py:1144
  429.5 25.8 %copy-start.29 = (bf16[8,3,64,256]{3,2,1,0:T(8,128)(2,1)S(1)}, bf16[8,3,64,256]{3,2,1,0:T(8,128)(2,1)}, u32[]{:S(2)}) copy-start(bf16[8,3,64,256]{3,2,1,0:T(8,128)(2,1)} %get-tuple-element.472) | copy-start | bytes 2359300
  429.5 25.8 %collective-permute-start.31 = (bf16[8,3,64,256]{3,2,1,0:T(8,128)(2,1)S(1)}, bf16[8,3,64,256]{3,2,1,0:T(8,128)(2,1)S(1)}, u32[]{:S(2)}, u32[]{:S(2)}) collective-permute-start(bf16[8,3,64,256]{3,2,1,0:T(8,128)(2,1)S(1)} %get-tuple-element.453), channel_id=1, source_target_pairs={{0,1},{1,0},{2,3},{3,2},{4,5},{5,4},{6,7},{7,6},{8,9},{9,8},{10,11... | collective-permute-start | bytes 2359304 | tf_op jit(solution)/shard_map/ppermute | solution.py:760
  431.2 24.1 %collective-permute-start.32 = (bf16[8,3,64,256]{3,2,1,0:T(8,128)(2,1)}, bf16[8,3,64,256]{3,2,1,0:T(8,128)(2,1)S(1)}, u32[]{:S(2)}, u32[]{:S(2)}) collective-permute-start(bf16[8,3,64,256]{3,2,1,0:T(8,128)(2,1)} %get-tuple-element.463), channel_id=1, source_target_pairs={{0,2},{1,3},{2,0},{3,1},{4,6},{5,7},{6,4},{7,5},{8,10},{9,11},{10,... | collective-permute-start | bytes 2359304 | tf_op jit(solution)/shard_map/ppermute | solution.py:760
  456.5 12.8 %collective-permute-start.33 = (bf16[2,1024,256]{2,1,0:T(8,128)(2,1)S(1)}, bf16[2,1024,256]{2,1,0:T(8,128)(2,1)S(1)}, u32[]{:S(2)}, u32[]{:S(2)}) collective-permute-start(bf16[2,1024,256]{2,1,0:T(8,128)(2,1)S(1)} %copy-done.63), channel_id=1, source_target_pairs={{0,2},{1,3},{2,0},{3,1},{4,6},{5,7},{6,4},{7,5},{8,10},{9,11},{10,... | collective-permute-start | bytes 3145736 | tf_op jit(solution)/shard_map/ppermute | solution.py:760
  457.2 20.6 %collective-permute-start.35 = (bf16[8,3,64,256]{3,2,1,0:T(8,128)(2,1)S(1)}, bf16[8,3,64,256]{3,2,1,0:T(8,128)(2,1)S(1)}, u32[]{:S(2)}, u32[]{:S(2)}) collective-permute-start(bf16[8,3,64,256]{3,2,1,0:T(8,128)(2,1)S(1)} %get-tuple-element.489), channel_id=1, source_target_pairs={{0,1},{1,0},{2,3},{3,2},{4,5},{5,4},{6,7},{7,6},{8,9},{9,8},{10,11... | collective-permute-start | bytes 2359304 | tf_op jit(solution)/shard_map/ppermute | solution.py:760
  457.4 20.3 %collective-permute-start.34 = (bf16[4,3,64,256]{3,2,1,0:T(8,128)(2,1)S(1)}, bf16[4,3,64,256]{3,2,1,0:T(8,128)(2,1)S(1)}, u32[]{:S(2)}, u32[]{:S(2)}) collective-permute-start(bf16[4,3,64,256]{3,2,1,0:T(8,128)(2,1)S(1)} %slice.262), channel_id=1, source_target_pairs={{0,4},{1,5},{2,6},{3,7},{4,0},{5,1},{6,2},{7,3},{8,12},{9,13},{10,... | collective-permute-start | bytes 1179656 | tf_op jit(solution)/shard_map/ppermute | solution.py:760
  477.8 17.0 %collective-permute-start.36 = (bf16[8,3,64,256]{3,2,1,0:T(8,128)(2,1)}, bf16[8,3,64,256]{3,2,1,0:T(8,128)(2,1)S(1)}, u32[]{:S(2)}, u32[]{:S(2)}) collective-permute-start(bf16[8,3,64,256]{3,2,1,0:T(8,128)(2,1)} %get-tuple-element.496), channel_id=1, source_target_pairs={{0,2},{1,3},{2,0},{3,1},{4,6},{5,7},{6,4},{7,5},{8,10},{9,11},{10,... | collective-permute-start | bytes 2359304 | tf_op jit(solution)/shard_map/ppermute | solution.py:760
  480.3 14.5 %collective-permute-start.37 = (bf16[2,3,64,256]{3,2,1,0:T(8,128)(2,1)S(1)}, bf16[2,3,64,256]{3,2,1,0:T(8,128)(2,1)S(1)}, u32[]{:S(2)}, u32[]{:S(2)}) collective-permute-start(bf16[2,3,64,256]{3,2,1,0:T(8,128)(2,1)S(1)} %slice.264), channel_id=1, source_target_pairs={{0,8},{1,9},{2,10},{3,11},{4,12},{5,13},{6,14},{7,15},{8,0},{9,1},... | collective-permute-start | bytes 589832 | tf_op jit(solution)/shard_map/ppermute | solution.py:760
  495.8 1.3 collective-permute-start.39
  497.1 4.9 collective-permute-start.40
  497.9 17.5 %collective-permute-start.45 = (bf16[4,3,64,256]{3,2,1,0:T(8,128)(2,1)S(1)}, bf16[4,3,64,256]{3,2,1,0:T(8,128)(2,1)S(1)}, u32[]{:S(2)}, u32[]{:S(2)}) collective-permute-start(bf16[4,3,64,256]{3,2,1,0:T(8,128)(2,1)S(1)} %slice.267), channel_id=1, source_target_pairs={{0,4},{1,5},{2,6},{3,7},{4,0},{5,1},{6,2},{7,3},{8,12},{9,13},{10,... | collective-permute-start | bytes 1179656 | tf_op jit(solution)/shard_map/ppermute | solution.py:760
  502.8 4.2 collective-permute-start.41
  507.1 7.0 %collective-permute-start.42 = (f32[2,52,128]{2,1,0:T(8,128)S(1)}, f32[2,52,128]{2,1,0:T(8,128)S(1)}, u32[]{:S(2)}, u32[]{:S(2)}) collective-permute-start(f32[2,52,128]{2,1,0:T(8,128)S(1)} %add.249), channel_id=1, source_target_pairs={{0,16},{1,17},{2,18},{3,19},{4,20},{5,21},{6,22},{7,23},{8,24},{9,... | collective-permute-start | bytes 159752 | tf_op jit(solution)/shard_map/ppermute | solution.py:760
  514.1 3.9 collective-permute-start.43
  515.5 6.8 %collective-permute-start.46 = (bf16[2,3,64,256]{3,2,1,0:T(8,128)(2,1)S(1)}, bf16[2,3,64,256]{3,2,1,0:T(8,128)(2,1)S(1)}, u32[]{:S(2)}, u32[]{:S(2)}) collective-permute-start(bf16[2,3,64,256]{3,2,1,0:T(8,128)(2,1)S(1)} %slice.275), channel_id=1, source_target_pairs={{0,8},{1,9},{2,10},{3,11},{4,12},{5,13},{6,14},{7,15},{8,0},{9,1},... | collective-permute-start | bytes 589832 | tf_op jit(solution)/shard_map/ppermute | solution.py:760
  518.0 7.3 %collective-permute-start.44 = (bf16[1,3,64,256]{3,2,1,0:T(8,128)(2,1)S(1)}, bf16[1,3,64,256]{3,2,1,0:T(8,128)(2,1)S(1)}, u32[]{:S(2)}, u32[]{:S(2)}) collective-permute-start(bf16[1,3,64,256]{3,2,1,0:T(8,128)(2,1)S(1)} %slice.266), channel_id=1, source_target_pairs={{0,16},{1,17},{2,18},{3,19},{4,20},{5,21},{6,22},{7,23},{8,24},{9,... | collective-permute-start | bytes 294920 | tf_op jit(solution)/shard_map/ppermute | solution.py:760
  522.3 8.3 %collective-permute-start.47 = (bf16[1,3,64,256]{3,2,1,0:T(8,128)(2,1)S(1)}, bf16[1,3,64,256]{3,2,1,0:T(8,128)(2,1)S(1)}, u32[]{:S(2)}, u32[]{:S(2)}) collective-permute-start(bf16[1,3,64,256]{3,2,1,0:T(8,128)(2,1)S(1)} %slice.277), channel_id=1, source_target_pairs={{0,16},{1,17},{2,18},{3,19},{4,20},{5,21},{6,22},{7,23},{8,24},{9,... | collective-permute-start | bytes 294920 | tf_op jit(solution)/shard_map/ppermute | solution.py:760
  531.3 6.6 %collective-permute-start.48 = (bf16[1,3,64,256]{3,2,1,0:T(8,128)(2,1)S(1)}, bf16[1,3,64,256]{3,2,1,0:T(8,128)(2,1)S(1)}, u32[]{:S(2)}, u32[]{:S(2)}) collective-permute-start(bf16[1,3,64,256]{3,2,1,0:T(8,128)(2,1)S(1)} %get-tuple-element.517), channel_id=1, source_target_pairs={{0,16},{1,17},{2,18},{3,19},{4,20},{5,21},{6,22},{7,23},{8,24},{9,... | collective-permute-start | bytes 294920 | tf_op jit(solution)/shard_map/ppermute | solution.py:760
  533.2 31.8 %collective-permute-start.38 = (bf16[1024,1024]{1,0:T(8,128)(2,1)}, bf16[1024,1024]{1,0:T(8,128)(2,1)}, u32[]{:S(2)}, u32[]{:S(2)}) collective-permute-start(bf16[1024,1024]{1,0:T(8,128)(2,1)} %get-tuple-element.504), channel_id=1, source_target_pairs={{1,2},{2,1},{5,6},{6,5},{9,10},{10,9},{13,14},{14,13},{17,18},{18,... | collective-permute-start | bytes 6291464 | tf_op jit(solution)/shard_map/ppermute | solution.py:760
  538.0 7.3 %collective-permute-start.49 = (bf16[2,3,64,256]{3,2,1,0:T(8,128)(2,1)S(1)}, bf16[2,3,64,256]{3,2,1,0:T(8,128)(2,1)S(1)}, u32[]{:S(2)}, u32[]{:S(2)}) collective-permute-start(bf16[2,3,64,256]{3,2,1,0:T(8,128)(2,1)S(1)} %pad_maximum_fusion.5), channel_id=1, source_target_pairs={{0,8},{1,9},{2,10},{3,11},{4,12},{5,13},{6,14},{7,15},{8,0},{9,1},... | collective-permute-start | bytes 589832 | tf_op jit(solution)/shard_map/ppermute | solution.py:760
  545.3 13.6 %collective-permute-start.50 = (bf16[4,3,64,256]{3,2,1,0:T(8,128)(2,1)S(1)}, bf16[4,3,64,256]{3,2,1,0:T(8,128)(2,1)S(1)}, u32[]{:S(2)}, u32[]{:S(2)}) collective-permute-start(bf16[4,3,64,256]{3,2,1,0:T(8,128)(2,1)S(1)} %pad_maximum_fusion.2), channel_id=1, source_target_pairs={{0,4},{1,5},{2,6},{3,7},{4,0},{5,1},{6,2},{7,3},{8,12},{9,13},{10,... | collective-permute-start | bytes 1179656 | tf_op jit(solution)/shard_map/ppermute | solution.py:760
  559.9 8.4 %collective-permute-start.51 = (bf16[8,3,64,256]{3,2,1,0:T(8,128)(2,1)}, bf16[8,3,64,256]{3,2,1,0:T(8,128)(2,1)}, u32[]{:S(2)}, u32[]{:S(2)}) collective-permute-start(bf16[8,3,64,256]{3,2,1,0:T(8,128)(2,1)} %pad_maximum_fusion.1), channel_id=1, source_target_pairs={{0,2},{1,3},{2,0},{3,1},{4,6},{5,7},{6,4},{7,5},{8,10},{9,11},{10,... | collective-permute-start | bytes 2359304 | tf_op jit(solution)/shard_map/ppermute | solution.py:760
  (62 other events, 371.2 us)
Sparse Core Ops, SparseCore 0:
  17.2 46.8 all-gather.13
  69.2 56.2 all-gather.15
  127.7 49.2 all-gather.17
  342.2 55.6 all-gather.19
  429.4 66.8 all-gather.21
  526.1 40.2 all-gather.11

commit v6 on v5

--- a/solution.py
+++ b/solution.py
@@ -80,29 +80,34 @@
     )
 
 
-def norm_kernel(x_ref, scale_ref, shift_ref, n_ref, nt_ref):
-    normed, _, _ = norm_parts(x_ref[...].astype(F32), scale_ref[...], shift_ref[...])
+def norm_kernel(stay_ref, x_ref, got_ref, scale_ref, shift_ref, rows_ref, n_ref, nt_ref):
+    rows = jnp.where(stay_ref[0] == 1, x_ref[...].astype(F32), got_ref[...].astype(F32))
+    rows_ref[...] = rows.astype(BF)
+    normed, _, _ = norm_parts(rows, scale_ref[...], shift_ref[...])
     n_ref[...] = normed.astype(BF)
     nt_ref[...] = normed.T.astype(BF)
 
 
-def norm_rows(x, scale, shift):
+def norm_rows(stay, x, got, scale, shift):
     tokens, width = x.shape
     rows = min(256, tokens)
-    vector = pl.BlockSpec((1, width), lambda i: (0, 0))
-    tile = pl.BlockSpec((rows, width), lambda i: (i, 0))
-    return call(
+    vector = pl.BlockSpec((1, width), lambda i, t: (0, 0))
+    tile = pl.BlockSpec((rows, width), lambda i, t: (i, 0))
+    return pl.pallas_call(
         norm_kernel,
-        10 * tokens * width,
-        6 * tokens * width,
-        grid=(tokens // rows,),
-        in_specs=[tile, vector, vector],
-        out_specs=[tile, pl.BlockSpec((width, rows), lambda i: (0, i))],
-        out_shape=[
-            jax.ShapeDtypeStruct((tokens, width), BF),
-            jax.ShapeDtypeStruct((width, tokens), BF),
-        ],
-    )(x, scale, shift)
+        grid_spec=pltpu.PrefetchScalarGridSpec(
+            num_scalar_prefetch=1,
+            grid=(tokens // rows,),
+            in_specs=[tile, tile, vector, vector],
+            out_specs=[tile, tile, pl.BlockSpec((width, rows), lambda i, t: (0, i))],
+        ),
+        out_shape=[jax.ShapeDtypeStruct((tokens, width), BF)] * 2
+        + [jax.ShapeDtypeStruct((width, tokens), BF)],
+        compiler_params=pltpu.CompilerParams(vmem_limit_bytes=VMEM_BYTES),
+        cost_estimate=pl.CostEstimate(
+            flops=10 * tokens * width, bytes_accessed=10 * tokens * width, transcendentals=0
+        ),
+    )(stay, x, got, scale, shift)
 
 
 def qkv_kernel(n_ref, w_ref, b_ref, c_ref, sa_ref, sb_ref, q_ref, kv_ref, *, q_steps):
@@ -537,9 +542,10 @@
     return total
 
 
-def early_kernel(own_ref, oth_ref, own_rows, oth_rows, out_ref):
-    total = add_parts(jnp.zeros(out_ref.shape, F32), oth_ref, oth_rows, 0)
-    out_ref[...] = add_parts(total, own_ref, own_rows, 0)
+def early_kernel(*refs):
+    w_ref, rows_ref, out_ref = refs[0], refs[1], refs[-1]
+    total = refs[2][...] if len(refs) == 4 else jnp.zeros(out_ref.shape, F32)
+    out_ref[...] = add_parts(total, w_ref, rows_ref, 0)
 
 
 def last_kernel(x_ref, g_ref, scale_ref, part_ref, own_ref, rows_ref, in_grad_ref, sums_ref):
@@ -559,20 +565,25 @@
         sums_ref[...] += sums
 
 
-def early_rows(own, oth, own_rows, oth_rows):
-    tokens, deep = own_rows.shape[0], own_rows.shape[1] + oth_rows.shape[1]
-    width = own.shape[0] * own.shape[2]
+def early_rows(weight, rows_grad, *before):
+    tokens, deep = rows_grad.shape
+    width = weight.shape[0] * weight.shape[2]
     rows = min(512, tokens)
+    block = (weight.shape[0], 3, weight.shape[2], deep // 3)
+    tile = pl.BlockSpec((rows, width), lambda i: (i, 0))
     return call(
         early_kernel,
         2 * tokens * width * deep,
         2 * (tokens * deep + width * deep + 2 * tokens * width),
         grid=(tokens // rows,),
-        in_specs=[pl.BlockSpec(w.shape, lambda i: (0, 0, 0, 0)) for w in (own, oth)]
-        + [pl.BlockSpec((rows, p.shape[1]), lambda i: (i, 0)) for p in (own_rows, oth_rows)],
-        out_specs=pl.BlockSpec((rows, width), lambda i: (i, 0)),
+        in_specs=[
+            pl.BlockSpec(block, lambda i: (0, 0, 0, 0)),
+            pl.BlockSpec((rows, deep), lambda i: (i, 0)),
+        ]
+        + [tile for _ in before],
+        out_specs=tile,
         out_shape=jax.ShapeDtypeStruct((tokens, width), F32),
-    )(own, oth, own_rows, oth_rows)
+    )(weight, rows_grad, *before)
 
 
 def last_rows(x, branch_grad, scale, partial, own, own_rows):
@@ -759,8 +770,10 @@
                     pairs.append((dp * 2 + y, a * 2 + b))
         return lax.ppermute(x, ("dp", "tensor"), pairs)
 
-    def swap_rows(self, rows):
-        got = self.move(rows, lambda dp, y: (dp - dp % 2 + y, dp % 2))
+    def swap(self, rows):
+        return self.move(rows, lambda dp, y: (dp - dp % 2 + y, dp % 2))
+
+    def stays(self, rows, got):
         return jnp.where(self.core == self.me_y, rows, got)
 
     def over_y(self, x):
@@ -1004,41 +1017,47 @@
     table = move.table()
     low_product = lambda a, b: dot_tn(a, b).astype(BF)
 
+    block_got = move.swap(block_in)
     qkv_own = jnp.transpose(qkv_weight, (1, 0, 2))
     small = jnp.concatenate([qkv_bias.reshape(3 * part), up_bias])
-    qkv_piece = move.piece(qkv_own, 1)
-    block_in = move.swap_rows(block_in)
-    tables = rotary_tables(move.first, tokens)
-    qkv_got = move.over_y(qkv_piece)
+    out_piece = move.piece(out_weight)
+    out_piece = jnp.concatenate([out_piece[:, at : at + part] for at in range(0, width, part)])
+    first_piece = jnp.concatenate([move.piece(qkv_own, 1), out_piece[None]])
+    first_got = move.over_y(first_piece)
     small_got = move.over_y(small)
     qkv_bs = [row(v[: 3 * part]) for v in (small, small_got)]
     up_bs = [row(v[3 * part :]) for v in (small, small_got)]
+    tables = rotary_tables(move.first, tokens)
     qkv_own = qkv_own[None]
-    qkv_oth = lax.all_gather(qkv_got, "dp")
-    rest = [move.piece(up_weight), jnp.concatenate([move.piece(w) for w in (out_weight, down_weight)])]
-    normed1, normed1_t = norm_rows(block_in, row(ln1_scale), row(ln1_shift))
+    qkv_oth = lax.all_gather(first_got, "dp")
+    rest = [move.piece(w) for w in (up_weight, down_weight)]
+    stay = jnp.stack([(move.core == move.me_y).astype(jnp.int32)])
+    block_in, normed1, normed1_t = norm_rows(
+        stay, block_in, block_got, row(ln1_scale), row(ln1_shift)
+    )
     (q_own, kv_own), (rest,) = beside(
         lambda n: qkv_rows(n, qkv_own, qkv_bs[0], tables),
         (normed1,),
         (lambda ws: [move.over_y(w) for w in ws], rest),
     )
     kvs_own = [kv_own, move.over_core(kv_own)]
-    up_got, mixed_got = (lax.all_gather(got, "dp") for got in rest)
+    up_got, down_got = (move.gather(got[None]) for got in rest)
     (out_a, log_a), _ = beside(lambda q, kvs: attend(q, kvs, 0, half), (q_own, kvs_own))
     qkv_oth, out_a, out_grad = tie(qkv_oth, out_a, out_grad)
     q_oth, kv_oth = qkv_rows(normed1, qkv_oth, qkv_bs[1], tables)
-    (out_b, log_b), (kv_got, grad_low) = beside(
+    (out_b, log_b), (kv_got, grad_got) = beside(
         lambda q, kvs: attend(q, kvs, half, half),
         (q_own, kvs_own),
         (move.over_core, kv_oth),
-        late=[(move.swap_rows, out_grad)],
+        late=[(move.swap, out_grad)],
     )
     kvs_oth = [kv_oth, kv_got]
     (out_oth, log_oth), _ = beside(attend, (q_oth, kvs_oth))
-    out_rows = part // n_dp
-    out_got = mixed_got[:, :out_rows].reshape(part, width)
-    up_ws = [up_weight, up_got.reshape(up_weight.shape)]
-    down_ws = [(down_weight[None], 0), (mixed_got, out_rows)]
+    grad_low = move.stays(out_grad, grad_got)
+    out_got = qkv_oth[:, 3].reshape(n_dp, width // part, part // n_dp, part)
+    out_got = out_got.transpose(0, 2, 1, 3).reshape(part, width)
+    up_ws = [up_weight, up_got]
+    down_ws = [(w[None], 0) for w in (down_weight, down_got)]
     outs = [out_a, out_b, out_oth]
     out_ws = [out_weight[:cols], out_weight[cols:], out_got]
 
@@ -1047,10 +1066,10 @@
     )
     acts, slopes = zip(*[up_rows(normed2, w, b) for w, b in zip(up_ws, up_bs)])
     block_out = down_rows(resid, row(down_bias), acts, down_ws)
-    down_grads, (block_out,) = beside(
+    down_grads, (block_got,) = beside(
         lambda xs, g: [low_product(a, g) for a in xs],
         (acts, grad_low),
-        late=[(move.swap_rows, block_out)],
+        late=[(move.swap, block_out)],
     )
     down = Reduction(move, table, *down_grads)
     (hg_own, up_b_own), _ = beside(
@@ -1073,6 +1092,7 @@
         return out_w_grads, [dot_nt(g, w).astype(BF) for w in out_ws]
 
     (out_w_grads, out_gs), _ = beside(projected, (outs, branch_grad), down)
+    out_gs, block_got = tie(out_gs, block_got)
     proj = Reduction(move, table, *out_w_grads)
 
     def back(which):
@@ -1096,13 +1116,22 @@
             move.blocks, normed1_t, tables, [x[0] for x in xs], [x[1][0] for x in xs], gots
         )
 
-    level = lambda n: functools.partial(move.over_chip, level=n)
+    over_x = functools.partial(move.over_chip, level=0)
+    others_z = (8, 4, 12)
+
+    def over_z(parts):
+        return [
+            move.move(p, lambda dp, y, far=far: (dp ^ far, y)) for p, far in zip(parts, others_z)
+        ]
+
+    def z_parts(total):
+        return total[:1], [total[n : n + 1] for n in range(1, 4)]
 
     def halves(total):
         return total[: total.shape[0] // 2], total[total.shape[0] // 2 :]
 
     oth_a, _ = beside(*back(0), up, down, proj)
-    down_block, oth_a, block_out = tie(down.done, oth_a, block_out)
+    down_block, oth_a = tie(down.done, oth_a)
     down_all = move.gather(down_block)
     oth_b, (got_a,) = beside(*back(1), keys_of(oth_a), up, proj)
     own_a, (got_b,) = beside(*back(2), keys_of(oth_b), up, proj)
@@ -1122,33 +1151,30 @@
     y_got_a, own_b = tie(y_got_a, own_b)
     keep_a, send_a = halves(keep_a + core_got_a + y_got_a)
     partial, (key_got, a_got) = beside(
-        lambda *xs: early_rows(qkv_own, qkv_oth, *xs),
-        (rows_a, rows_oth),
-        keys_of(own_b),
-        late=[(level(0), send_a)],
+        early_rows, (qkv_oth, rows_oth), keys_of(own_b), late=[(over_x, send_a)]
     )
     (keep_b, send_b, rows_b, bias_b), _ = beside(unit, ((own_b,), (key_got,)))
     keep_b, a_got, y_got_b = tie(keep_b, a_got, y_got_b)
-    keep_a, send_a = halves(keep_a + a_got)
-    (in_grad, sums_one), (core_got, a_got) = beside(
+    keep_a, send_a = z_parts(keep_a + a_got)
+    partial, (core_got, a_got) = beside(
+        early_rows, (qkv_own, rows_a, partial), (move.over_core, send_b), (over_z, send_a)
+    )
+    total_a = keep_a + sum(a_got)
+    keep_b, send_b = halves(keep_b + core_got + y_got_b)
+    mixed_all, partial, total_a = tie(mixed_all, partial, total_a)
+    unit_a = lax.all_gather(total_a[0], "dp")
+    (in_grad, sums_one), (b_got,) = beside(
         lambda *xs: last_rows(block_in, branch_grad, row(ln1_scale), *xs),
         (partial, qkv_own, rows_b),
-        (move.over_core, send_b),
-        (level(1), send_a),
-    )
-    keep_a, send_a = halves(keep_a + a_got)
-    keep_b, send_b = halves(keep_b + core_got + y_got_b)
-    in_grad, send_a, send_b, mixed_all = tie(in_grad, send_a, send_b, mixed_all)
-    in_grad = move.swap_rows(in_grad)
-    total_a = keep_a + move.over_chip(send_a, 2)
-    unit_a = lax.all_gather(total_a[0], "dp")
-    total_b = keep_b + move.over_chip(send_b, 0)
-    levels = (n_dp // 2).bit_length() - 1
-    for n in range(1, levels):
-        keep_b, send_b = halves(total_b)
-        total_b = keep_b + move.over_chip(send_b, n)
-    for n in reversed(range(levels)):
-        total_b = jnp.concatenate([total_b, move.over_chip(total_b, n)])
+        (over_x, send_b),
+    )
+    in_grad, mixed_all, block_got, down_all = tie(in_grad, mixed_all, block_got, down_all)
+    in_grad_got = move.swap(in_grad)
+    keep_b, send_b = z_parts(keep_b + b_got)
+    total_b = keep_b + sum(over_z(send_b))
+    total_b = jnp.concatenate([total_b] + over_z([total_b] * 3))
+    total_b, unit_a = tie(total_b, unit_a)
+    total_b = jnp.concatenate([total_b, over_x(total_b)])
     total_b = jnp.concatenate([total_b, move.over_core(total_b)])
     qkv_g = jnp.transpose(widen(move.blocks, unit_a, total_b), (1, 0, 2))
     up_rows_each = width // n_dp
@@ -1162,8 +1188,8 @@
     )
     f32 = lambda v: v.astype(F32)
     return (
-        block_out,
-        in_grad,
+        move.stays(block_out, block_got),
+        move.stays(in_grad, in_grad_got),
         vec[0],
         vec[1],
         qkv_g,
@@ -1247,7 +1273,7 @@
         P(),
         rows,
     )
-    paired = n_tensor == 2 and n_dp >= 8 and n_dp & (n_dp - 1) == 0
+    paired = n_tensor == 2 and n_dp == 16
     return jax.shard_map(
         functools.partial(paired_device, n_dp) if paired else spread_device,
         mesh=mesh,

time: 591 us -> 579 us (0.980)
  waiting for transfers between devices: 61.3 us -> 49.1 us
    all_gather x3 -> x1, waiting for transfers between devices: 13 us -> 0.01 us  [paired_device(): qkv_oth = lax.all_gather(first_got, 'dp')]
    ppermute x52 -> x55, waiting for transfers between devices: 47.6 us -> 41.4 us  [move(): return lax.ppermute(x, ('dp', 'tensor'), pairs)]
    unnamed x140 -> x124, local copies, waits for them, and re-layouts: 18.7 us -> 13.3 us
    ppermute x52 -> x55, starting transfers between devices: 65.2 us -> 69 us  [move(): return lax.ppermute(x, ('dp', 'tensor'), pairs)]
    pallas_call x1 -> x2, Pallas kernels: 10.4 us -> 13.2 us  [early_rows(): call(early_kernel, 2 * tokens * width * deep, 2 * (tokens * deep + width...]
  transfers between devices with their start and end apart: 58 -> 61, of which waited for: 16 -> 14; matrix products, arithmetic and copies ran while one was open for 14% -> 14% of each run, Pallas kernels for 49% -> 54%
where the time goes in v6:
time: 579 us; the launch traced here: 572 us
  Pallas kernels  328 us (57%)
  starting transfers between devices  69.7 us (12%)
  waiting for transfers between devices  49.1 us (8%)
  other arithmetic  42.6 us (7%)
  local copies, waits for them, and re-layouts  37.3 us (6%)
  matrix products  29.8 us (5%)
  between operations  15.6 us (3%)
    pallas_call x4, Pallas kernels, attend_back(): call(functools.partial(attend_back_kernel, sources=len(kvs), keys_at=1024...  97.8 us
    ppermute x55, starting transfers between devices, move(): return lax.ppermute(x, ('dp', 'tensor'), pairs)  69 us
    pallas_call x3, Pallas kernels, attend(): call(functools.partial(attend_kernel, sources=len(kvs), rows_at=min(512,...  48.9 us
    ppermute x55, waiting for transfers between devices, move(): return lax.ppermute(x, ('dp', 'tensor'), pairs)  41.4 us
    pallas_call x3, Pallas kernels, unit_grads(): pl.pallas_call(functools.partial(unit_kernel, chips=chips, parts=parts),...  25.8 us
    pallas_call x2, Pallas kernels, up_rows(): call(up_kernel, 2 * tokens * width * cols, 2 * (tokens * width + width *...  22.9 us
    pallas_call x2, Pallas kernels, qkv_rows(): call(functools.partial(qkv_kernel, q_steps=q_steps), 2 * tokens * width *...  21.3 us
    pallas_call x2, Pallas kernels, hidden_grads(): call(functools.partial(hidden_grad_kernel, skip=skip), 2 * tokens * width...  19.7 us
  transfers between devices with their start and end apart: 61, of which 14 were waited for; matrix products, arithmetic and copies ran while one was open for 14% of the time, Pallas kernels for 54%

profile of v6, /device:TPU:0, one launch (start us, length us, event | category | flops | bytes accessed | tf_op | source)
XLA Modules:
  0.0 572.5 jit_solution(8492979951332343517)
XLA Ops:
  9.1 3.0 collective-permute-start.1
  12.1 6.3 %collective-permute-done.1 = bf16[4,64,512]{2,1,0:T(8,128)(2,1)S(1)} collective-permute-done((bf16[4,64,512]{2,1,0:T(8,128)(2,1)S(1)}, bf16[4,64,512]{2,1,0:T(8,128)(2,1)S(1)}, u32[]{:S(2)}, u32[]{:S(2)}) %collective-permute-start.1) | collective-permute-done | bytes 262176 | tf_op jit(solution)/shard_map/ppermute | solution.py:771
  25.9 3.6 fusion.3
  30.9 5.8 %shard_map.326 = (bf16[1024,1024]{1,0:T(8,128)(2,1)}, bf16[1024,1024]{1,0:T(8,128)(2,1)}, bf16[1024,1024]{1,0:T(8,128)(2,1)}) custom-call(s32[1]{0:T(128)} %bitcast.stay_ref, bf16[1024,1024]{1,0:T(8,128)(2,1)} %x_ref.1, bf16[1024,1024]{1,0:T(8,128)(2,1)} %copy-done.15, f32[1,1024]{1,0:T(1,128)} %bitcast.156, f32[1,1024]{1,0:T(1,128)} %bitcast.160), custom_call_target="tpu_custom_call" | custom-call | flops 10485760 | bytes 10485760 | tf_op jit(solution)/shard_map/pallas_call | solution.py:96
  36.7 19.0 %collective-permute-start.2 = (bf16[64,2048]{1,0:T(8,128)(2,1)S(1)}, bf16[64,2048]{1,0:T(8,128)(2,1)S(1)}, u32[]{:S(2)}, u32[]{:S(2)}) collective-permute-start(bf16[64,2048]{1,0:T(8,128)(2,1)S(1)} %constant_dynamic-slice_fusion.4), channel_id=1, source_target_pairs={{0,1},{1,0},{2,3},{3,2},{4,5},{5,4},{6,7},{7,6},{8,9},{9,8},{10,11... | collective-permute-start | bytes 786440 | tf_op jit(solution)/shard_map/ppermute | solution.py:771
  55.7 10.6 %shard_map.327 = (bf16[1024,512]{1,0:T(8,128)(2,1)}, bf16[1024,1024]{1,0:T(8,128)(2,1)}) custom-call(bf16[1024,1024]{1,0:T(8,128)(2,1)} %get-tuple-element.286.n_ref, bf16[1,3,1024,512]{3,2,1,0:T(8,128)(2,1)} %bitcast.132, f32[1,1536]{1,0:T(1,128)} %bitcast.165, f32[1024,128]{1,0:T(8,128)} %get-tuple-element.576.c_ref.refs_4_, ...), custom_call_target="tpu_custom_call" | custom-call | flops 3221225472 | bytes 8388608 | tf_op jit(solution)/shard_map/pallas_call | solution.py:145
  70.3 2.6 collective-permute-done.5
  73.5 12.7 %shard_map.328 = (bf16[1024,256]{1,0:T(8,128)(2,1)}, f32[2,2,1024]{2,1,0:T(2,128)}) custom-call(bf16[1024,512]{1,0:T(8,128)(2,1)} %get-tuple-element.481.refs_0_, bf16[1024,1024]{1,0:T(8,128)(2,1)} %get-tuple-element.485.refs_1_.refs_3_.refs_7_.refs_9_, bf16[1024,1024]{1,0:T(8,128)(2,1)} %collective-permute-done.4.refs_2_.refs_4_.refs_8_.refs_10_, ...), custom_call_target="tpu_custom_call" | custom-call | flops 8589934592 | bytes 3145728 | tf_op jit(solution)/shard_map/pallas_call | solution.py:213
  86.3 10.7 %shard_map.329 = (bf16[1024,512]{1,0:T(8,128)(2,1)}, bf16[1024,1024]{1,0:T(8,128)(2,1)}) custom-call(bf16[1024,1024]{1,0:T(8,128)(2,1)} %get-tuple-element.286.n_ref, bf16[16,4,64,512]{3,2,1,0:T(8,128)(2,1)} %bitcast.151, f32[1,1536]{1,0:T(1,128)} %reshape.234.b_ref, f32[1024,128]{1,0:T(8,128)} %get-tuple-element.576.c_ref.refs_4_, ...), custom_call_target="tpu_custom_call" | custom-call | flops 3221225472 | bytes 8388608 | tf_op jit(solution)/shard_map/pallas_call | solution.py:145
  105.3 2.1 collective-permute-start.7
  107.4 12.7 %shard_map.330 = (bf16[1024,256]{1,0:T(8,128)(2,1)}, f32[2,2,1024]{2,1,0:T(2,128)}) custom-call(bf16[1024,512]{1,0:T(8,128)(2,1)} %get-tuple-element.481.refs_0_, bf16[1024,1024]{1,0:T(8,128)(2,1)} %get-tuple-element.485.refs_1_.refs_3_.refs_7_.refs_9_, bf16[1024,1024]{1,0:T(8,128)(2,1)} %collective-permute-done.4.refs_2_.refs_4_.refs_8_.refs_10_, ...), custom_call_target="tpu_custom_call" | custom-call | flops 8589934592 | bytes 3145728 | tf_op jit(solution)/shard_map/pallas_call | solution.py:213
  120.1 23.5 %shard_map.331 = (bf16[1024,512]{1,0:T(8,128)(2,1)}, f32[4,2,1024]{2,1,0:T(2,128)}) custom-call(bf16[1024,512]{1,0:T(8,128)(2,1)} %get-tuple-element.400.refs_0_, bf16[1024,1024]{1,0:T(8,128)(2,1)} %get-tuple-element.404.refs_1_.refs_3_.refs_7_.refs_9_, bf16[1024,1024]{1,0:T(8,128)(2,1)} %collective-permute-done.6.refs_2_.refs_4_.refs_8_.refs_10_, ...), custom_call_target="tpu_custom_call" | custom-call | flops 17179869184 | bytes 6291456 | tf_op jit(solution)/shard_map/pallas_call | solution.py:213
  143.6 7.9 %shard_map.332 = (f32[1024,1024]{1,0:T(8,128)}, bf16[1024,1024]{1,0:T(8,128)(2,1)}, bf16[1024,1024]{1,0:T(8,128)(2,1)}) custom-call(bf16[1024,1024]{1,0:T(8,128)(2,1)} %get-tuple-element.284.refs_0_.x_ref, f32[1,1024]{1,0:T(1,128)} %bitcast.169, f32[1,1024]{1,0:T(1,128)} %bitcast.166, f32[1,1024]{1,0:T(1,128)} %bitcast.170, ...), custom_call_target="tpu_custom_call" | custom-call | flops 2147483648 | bytes 14680064 | tf_op jit(solution)/shard_map/pallas_call | solution.py:452
  151.5 11.9 %shard_map.333 = (bf16[1024,2048]{1,0:T(8,128)(2,1)}, bf16[1024,2048]{1,0:T(8,128)(2,1)}) custom-call(bf16[1024,1024]{1,0:T(8,128)(2,1)} %get-tuple-element.315.n_ref, bf16[1024,2048]{1,0:T(8,128)(2,1)} %refs_2_.1, f32[1,2048]{1,0:T(1,128)} %bitcast.163), custom_call_target="tpu_custom_call" | custom-call | flops 4294967296 | bytes 14680064 | tf_op jit(solution)/shard_map/pallas_call | solution.py:364
  163.4 11.1 %shard_map.334 = (bf16[1024,2048]{1,0:T(8,128)(2,1)}, bf16[1024,2048]{1,0:T(8,128)(2,1)}) custom-call(bf16[1024,1024]{1,0:T(8,128)(2,1)} %get-tuple-element.315.n_ref, bf16[1024,2048]{1,0:T(8,128)(2,1)} %all-gather.10.cloned.1.call-done.w_ref.refs_3_, f32[1,2048]{1,0:T(1,128)} %bitcast.164), custom_call_target="tpu_custom_call" | custom-call | flops 4294967296 | bytes 14680064 | tf_op jit(solution)/shard_map/pallas_call | solution.py:364
  174.5 2.2 all-gather.12.cloned.1.call-done
  176.7 15.2 %shard_map.335 = bf16[1024,1024]{1,0:T(8,128)(2,1)} custom-call(f32[1024,1024]{1,0:T(8,128)} %get-tuple-element.314.r_ref, f32[1,1024]{1,0:T(1,128)} %bitcast.168, bf16[1024,2048]{1,0:T(8,128)(2,1)} %get-tuple-element.322.refs_0_, bf16[1024,2048]{1,0:T(8,128)(2,1)} %get-tuple-element.324.refs_1_, bf16[1,2048,1024]{2,1,0:T(8,128)(2,1)} %bitcast.158, ...), custom_call_target="tpu_custom_call" | custom-call | flops 8589934592 | bytes 23068672 | tf_op jit(solution)/shard_map/pallas_call | solution.py:482
  192.2 1.9 copy-done.58
  194.2 4.9 convolution_convert_fusion.2
  199.1 4.9 convolution_convert_fusion.3
  204.1 1.8 dynamic-slice_bitcast_fusion.2
  209.8 9.7 %shard_map.336 = (bf16[1024,2048]{1,0:T(8,128)(2,1)}, f32[1,2048]{1,0:T(1,128)}) custom-call(bf16[1024,1024]{1,0:T(8,128)(2,1)} %copy-done.12, bf16[1,2048,1024]{2,1,0:T(8,128)(2,1)} %bitcast.159, bf16[1024,2048]{1,0:T(8,128)(2,1)} %get-tuple-element.328.slope_ref), custom_call_target="tpu_custom_call" | custom-call | flops 4294967296 | bytes 14680064 | tf_op jit(solution)/shard_map/pallas_call | solution.py:399
  220.9 6.5 %shard_map.337 = (bf16[4,128,1024]{2,1,0:T(8,128)(2,1)}, bf16[4,128,1024]{2,1,0:T(8,128)(2,1)}, bf16[2,4,128,1024]{3,2,1,0:T(8,128)(2,1)}) custom-call(s32[9]{0:T(128)} %pad_add_fusion.t_ref, bf16[8,2,128,1024]{3,2,1,0:T(8,128)(2,1)} %bitcast.124, bf16[8,2,128,1024]{3,2,1,0:T(8,128)(2,1)} %bitcast.125, bf16[8,2,128,1024]{3,2,1,0:T(8,128)(2,1)} %bitcast.121, ...), custom_call_target="tpu_custom_call" | custom-call | flops 2097152 | bytes 12582912 | tf_op jit(solution)/shard_map/pallas_call | solution.py:731
  229.1 10.0 %shard_map.338 = (bf16[1024,2048]{1,0:T(8,128)(2,1)}, f32[1,2048]{1,0:T(1,128)}) custom-call(bf16[1024,1024]{1,0:T(8,128)(2,1)} %copy-done.12, bf16[1,2048,1024]{2,1,0:T(8,128)(2,1)} %bitcast.172, bf16[1024,2048]{1,0:T(8,128)(2,1)} %get-tuple-element.338.slope_ref), custom_call_target="tpu_custom_call" | custom-call | flops 4294967296 | bytes 14680064 | tf_op jit(solution)/shard_map/pallas_call | solution.py:399
  239.1 7.1 %convolution_convert_fusion = bf16[1024,2048]{1,0:T(8,128)(2,1)S(1)} fusion(bf16[1024,1024]{1,0:T(8,128)(2,1)S(1)} %copy-done.55, bf16[1024,2048]{1,0:T(8,128)(2,1)} %get-tuple-element.350.refs_1_), kind=kOutput, calls=%fused_computation.1 | convolution fusion | flops 4297064448 | bytes 10485760 | tf_op jit(solution)/shard_map/dot_general | solution.py:32
  246.2 4.8 convolution_convert_fusion.1
  251.0 2.6 collective-permute-done.10
  258.1 2.0 collective-permute-start.15
  260.1 17.6 %shard_map.339 = (bf16[1024,1024]{1,0:T(8,128)(2,1)}, f32[8,1024]{1,0:T(8,128)}) custom-call(f32[1024,1024]{1,0:T(8,128)} %get-tuple-element.314.r_ref, bf16[1024,1024]{1,0:T(8,128)(2,1)} %copy-done.12, f32[1,1024]{1,0:T(1,128)} %bitcast.167, bf16[1024,2048]{1,0:T(8,128)(2,1)} %get-tuple-element.349.refs_0_, bf16[1024,2048]{1,0:T(8,128)(2,1)} %get-tuple-element.350.refs_1_, ...), custom_call_target="tpu_custom_call" | custom-call | flops 8589934592 | bytes 25165824 | tf_op jit(solution)/shard_map/pallas_call | solution.py:521
  277.7 3.5 fusion.1
  288.0 2.3 convolution_convert_fusion.4.refs_1_
  291.0 6.6 %shard_map.340 = (bf16[4,64,2048]{2,1,0:T(8,128)(2,1)}, bf16[4,64,2048]{2,1,0:T(8,128)(2,1)}, bf16[2,4,64,2048]{3,2,1,0:T(8,128)(2,1)}) custom-call(s32[9]{0:T(128)} %pad_add_fusion.t_ref, bf16[8,2,64,2048]{3,2,1,0:T(8,128)(2,1)} %bitcast.130, bf16[8,2,64,2048]{3,2,1,0:T(8,128)(2,1)} %bitcast.131, bf16[8,2,64,2048]{3,2,1,0:T(8,128)(2,1)} %bitcast.127, ...), custom_call_target="tpu_custom_call" | custom-call | flops 2097152 | bytes 12582912 | tf_op jit(solution)/shard_map/pallas_call | solution.py:731
  301.1 2.5 collective-permute-start.16
  305.0 24.3 %shard_map.341 = (bf16[1024,256]{1,0:T(8,128)(2,1)}, bf16[2,1024,256]{2,1,0:T(8,128)(2,1)}, bf16[2,1024,256]{2,1,0:T(8,128)(2,1)}) custom-call(bf16[1024,512]{1,0:T(8,128)(2,1)} %get-tuple-element.400.refs_0_, bf16[1024,512]{1,0:T(8,128)(2,1)} %convolution_convert_fusion.4.refs_1_, bf16[1024,512]{1,0:T(8,128)(2,1)} %get-tuple-element.402.refs_6_.refs_2_, ...), custom_call_target="tpu_custom_call" | custom-call | flops 21474836480 | bytes 6291456 | tf_op jit(solution)/shard_map/pallas_call | solution.py:305
  330.4 4.4 shard_map.342
  336.3 24.6 %shard_map.343 = (bf16[1024,256]{1,0:T(8,128)(2,1)}, bf16[2,1024,256]{2,1,0:T(8,128)(2,1)}, bf16[2,1024,256]{2,1,0:T(8,128)(2,1)}) custom-call(bf16[1024,512]{1,0:T(8,128)(2,1)} %get-tuple-element.400.refs_0_, bf16[1024,512]{1,0:T(8,128)(2,1)} %convolution_convert_fusion.4.refs_1_, bf16[1024,512]{1,0:T(8,128)(2,1)} %get-tuple-element.402.refs_6_.refs_2_, ...), custom_call_target="tpu_custom_call" | custom-call | flops 21474836480 | bytes 6291456 | tf_op jit(solution)/shard_map/pallas_call | solution.py:305
  366.0 24.3 %shard_map.344 = (bf16[1024,256]{1,0:T(8,128)(2,1)}, bf16[2,1024,256]{2,1,0:T(8,128)(2,1)}, bf16[2,1024,256]{2,1,0:T(8,128)(2,1)}) custom-call(bf16[1024,512]{1,0:T(8,128)(2,1)} %get-tuple-element.481.refs_0_, bf16[1024,256]{1,0:T(8,128)(2,1)} %convolution_convert_fusion.7.refs_1_, bf16[1024,256]{1,0:T(8,128)(2,1)} %get-tuple-element.420.refs_4_.refs_2_, ...), custom_call_target="tpu_custom_call" | custom-call | flops 21474836480 | bytes 6291456 | tf_op jit(solution)/shard_map/pallas_call | solution.py:305
  390.4 4.4 collective-permute-done.24
  396.8 2.4 collective-permute-start.28
  399.2 10.7 %shard_map.345 = (bf16[8,3,64,512]{3,2,1,0:T(8,128)(2,1)}, bf16[8,3,64,512]{3,2,1,0:T(8,128)(2,1)}, bf16[1024,1536]{1,0:T(8,128)(2,1)}, f32[8,1536]{1,0:T(8,128)}) custom-call(s32[16]{0:T(128)} %pad_add_fusion.1.t_ref, bf16[1024,1024]{1,0:T(8,128)(2,1)} %get-tuple-element.431.nt_ref, f32[1024,128]{1,0:T(8,128)} %get-tuple-element.576.c_ref.refs_4_, ...), custom_call_target="tpu_custom_call" | custom-call | flops 3221225472 | bytes 13631488 | tf_op jit(solution)/shard_map/pallas_call | solution.py:657
  412.2 7.6 %shard_map.346 = (bf16[8,3,64,256]{3,2,1,0:T(8,128)(2,1)}, bf16[8,3,64,256]{3,2,1,0:T(8,128)(2,1)}, bf16[1024,768]{1,0:T(8,128)(2,1)}, f32[8,768]{1,0:T(8,128)}) custom-call(s32[16]{0:T(128)} %pad_add_fusion.1.t_ref, bf16[1024,1024]{1,0:T(8,128)(2,1)} %get-tuple-element.431.nt_ref, f32[1024,128]{1,0:T(8,128)} %get-tuple-element.576.c_ref.refs_4_, ...), custom_call_target="tpu_custom_call" | custom-call | flops 1610612736 | bytes 7864320 | tf_op jit(solution)/shard_map/pallas_call | solution.py:657
  422.7 24.5 %shard_map.347 = (bf16[1024,256]{1,0:T(8,128)(2,1)}, bf16[2,1024,256]{2,1,0:T(8,128)(2,1)}, bf16[2,1024,256]{2,1,0:T(8,128)(2,1)}) custom-call(bf16[1024,512]{1,0:T(8,128)(2,1)} %get-tuple-element.481.refs_0_, bf16[1024,256]{1,0:T(8,128)(2,1)} %convolution_convert_fusion.6.refs_1_, bf16[1024,256]{1,0:T(8,128)(2,1)} %get-tuple-element.483.refs_5_.refs_2_, ...), custom_call_target="tpu_custom_call" | custom-call | flops 21474836480 | bytes 6291456 | tf_op jit(solution)/shard_map/pallas_call | solution.py:305
  449.3 7.3 %shard_map.348.refs_2_ = f32[1024,1024]{1,0:T(8,128)} custom-call(bf16[16,4,64,512]{3,2,1,0:T(8,128)(2,1)} %bitcast.153, bf16[1024,1536]{1,0:T(8,128)(2,1)} %get-tuple-element.499.refs_1_), custom_call_target="tpu_custom_call" | custom-call | flops 3221225472 | bytes 10485760 | tf_op jit(solution)/shard_map/pallas_call | solution.py:574
  457.7 7.6 %shard_map.349 = (bf16[8,3,64,256]{3,2,1,0:T(8,128)(2,1)}, bf16[8,3,64,256]{3,2,1,0:T(8,128)(2,1)}, bf16[1024,768]{1,0:T(8,128)(2,1)}, f32[8,768]{1,0:T(8,128)}) custom-call(s32[16]{0:T(128)} %pad_add_fusion.1.t_ref, bf16[1024,1024]{1,0:T(8,128)(2,1)} %get-tuple-element.431.nt_ref, f32[1024,128]{1,0:T(8,128)} %get-tuple-element.576.c_ref.refs_4_, ...), custom_call_target="tpu_custom_call" | custom-call | flops 1610612736 | bytes 7864320 | tf_op jit(solution)/shard_map/pallas_call | solution.py:657
  465.2 2.2 collective-permute-done.35
  468.8 2.1 collective-permute-start.37
  471.0 2.2 collective-permute-start.39
  473.3 5.8 %shard_map.350.part_ref = f32[1024,1024]{1,0:T(8,128)} custom-call(bf16[1,3,1024,512]{3,2,1,0:T(8,128)(2,1)} %bitcast.133, bf16[1024,768]{1,0:T(8,128)(2,1)} %get-tuple-element.514.refs_1_, f32[1024,1024]{1,0:T(8,128)} %shard_map.348.refs_2_), custom_call_target="tpu_custom_call" | custom-call | flops 1610612736 | bytes 7340032 | tf_op jit(solution)/shard_map/pallas_call | solution.py:574
  479.1 3.7 collective-permute-done.37
  482.8 2.9 collective-permute-done.39
  486.5 5.3 all-gather.20.cloned.1.call-done
  494.4 9.1 %shard_map.351 = (bf16[1024,1024]{1,0:T(8,128)(2,1)}, f32[8,1024]{1,0:T(8,128)}) custom-call(bf16[1024,1024]{1,0:T(8,128)(2,1)} %get-tuple-element.284.refs_0_.x_ref, bf16[1024,1024]{1,0:T(8,128)(2,1)} %get-tuple-element.363.g_ref, f32[1,1024]{1,0:T(1,128)} %bitcast.157, f32[1024,1024]{1,0:T(8,128)} %shard_map.350.part_ref, ...), custom_call_target="tpu_custom_call" | custom-call | flops 1610612736 | bytes 13631488 | tf_op jit(solution)/shard_map/pallas_call | solution.py:594
  505.4 2.6 collective-permute-start.49
  508.1 2.3 slice.251
  511.4 6.7 %bitcast_convert_fusion = f32[1024,2048]{1,0:T(8,128)} fusion(bf16[16,64,2048]{2,1,0:T(8,128)(2,1)} %slice.251), kind=kLoop, calls=%fused_computation | loop fusion | flops 2097152 | bytes 12582912 | tf_op jit(solution)/shard_map/convert_element_type | solution.py:1189
  518.0 2.0 collective-permute-start.41
  521.2 2.1 collective-permute-start.51
  523.4 2.2 collective-permute-start.52
  527.2 9.2 %collective-permute-done.44 = f32[2,52,128]{2,1,0:T(8,128)S(1)} collective-permute-done((f32[2,52,128]{2,1,0:T(8,128)S(1)}, f32[2,52,128]{2,1,0:T(8,128)S(1)}, u32[]{:S(2)}, u32[]{:S(2)}) %collective-permute-start.44) | collective-permute-done | bytes 53280 | tf_op jit(solution)/shard_map/ppermute | solution.py:771
  538.1 4.1 collective-permute-done.45
  544.4 3.1 broadcast_select_fusion.1
  547.6 4.4 convert_element_type.90
  555.5 3.1 broadcast_select_fusion
  559.9 5.5 shard_map.352
  (329 shorter events, 84.2 us)
Async XLA Ops:
  7.3 78.9 %all-gather.16.cloned.1.call-start = ((), (), s32[]{:S(2)}) async-start(), calls=%async_computation.3 | async-start | bytes 4456448 | tf_op jit(solution)/shard_map/all_gather | solution.py:1032
  9.1 9.3 %collective-permute-start.1 = (bf16[4,64,512]{2,1,0:T(8,128)(2,1)S(1)}, bf16[4,64,512]{2,1,0:T(8,128)(2,1)S(1)}, u32[]{:S(2)}, u32[]{:S(2)}) collective-permute-start(bf16[4,64,512]{2,1,0:T(8,128)(2,1)S(1)} %pad_maximum_fusion.5), channel_id=1, source_target_pairs={{0,1},{1,0},{2,3},{3,2},{4,5},{5,4},{6,7},{7,6},{8,9},{9,8},{10,11... | collective-permute-start | bytes 786440 | tf_op jit(solution)/shard_map/ppermute | solution.py:771
  19.2 144.2 %all-gather.10.cloned.1.call-start = ((), (), s32[]{:S(2)}) async-start(), calls=%async_computation | async-start | bytes 4456448 | tf_op jit(solution)/shard_map/all_gather | solution.py:823
  19.2 10.3 %collective-permute-start = (bf16[1024,1024]{1,0:T(8,128)(2,1)}, bf16[1024,1024]{1,0:T(8,128)(2,1)S(1)}, u32[]{:S(2)}, u32[]{:S(2)}) collective-permute-start(bf16[1024,1024]{1,0:T(8,128)(2,1)} %x_ref.1), channel_id=1, source_target_pairs={{1,2},{2,1},{5,6},{6,5},{9,10},{10,9},{13,14},{14,13},{17,18},{18,... | collective-permute-start | bytes 6291464 | tf_op jit(solution)/shard_map/ppermute | solution.py:771
  36.7 29.6 %collective-permute-start.2 = (bf16[64,2048]{1,0:T(8,128)(2,1)S(1)}, bf16[64,2048]{1,0:T(8,128)(2,1)S(1)}, u32[]{:S(2)}, u32[]{:S(2)}) collective-permute-start(bf16[64,2048]{1,0:T(8,128)(2,1)S(1)} %constant_dynamic-slice_fusion.4), channel_id=1, source_target_pairs={{0,1},{1,0},{2,3},{3,2},{4,5},{5,4},{6,7},{7,6},{8,9},{9,8},{10,11... | collective-permute-start | bytes 786440 | tf_op jit(solution)/shard_map/ppermute | solution.py:771
  55.7 12.2 %collective-permute-start.3 = (bf16[128,1024]{1,0:T(8,128)(2,1)S(1)}, bf16[128,1024]{1,0:T(8,128)(2,1)S(1)}, u32[]{:S(2)}, u32[]{:S(2)}) collective-permute-start(bf16[128,1024]{1,0:T(8,128)(2,1)S(1)} %constant_dynamic-slice_fusion.3), channel_id=1, source_target_pairs={{0,1},{1,0},{2,3},{3,2},{4,5},{5,4},{6,7},{7,6},{8,9},{9,8},{10,11... | collective-permute-start | bytes 786440 | tf_op jit(solution)/shard_map/ppermute | solution.py:771
  67.9 108.8 %all-gather.12.cloned.1.call-start = ((), (), s32[]{:S(2)}) async-start(), calls=%async_computation.1 | async-start | bytes 4456448 | tf_op jit(solution)/shard_map/all_gather | solution.py:823
  68.0 5.6 collective-permute-start.4
  68.6 352.0 %all-gather.18.cloned.1.call-start = ((), (), s32[]{:S(2)}) async-start(), calls=%async_computation.4 | async-start | bytes 4456448 | tf_op jit(solution)/shard_map/all_gather | solution.py:823
  69.2 3.7 collective-permute-start.5
  97.0 23.1 %collective-permute-start.6 = (bf16[1024,1024]{1,0:T(8,128)(2,1)}, bf16[1024,1024]{1,0:T(8,128)(2,1)}, u32[]{:S(2)}, u32[]{:S(2)}) collective-permute-start(bf16[1024,1024]{1,0:T(8,128)(2,1)} %get-tuple-element.404.refs_1_.refs_3_.refs_7_.refs_9_), channel_id=1, source_target_pairs={{0,2},{1,3},{2,0},{3,1},{4,6},{5,7},{6,4},{7,5},{8,10},{9,11},{10,... | collective-permute-start | bytes 6291464 | tf_op jit(solution)/shard_map/ppermute | solution.py:771
  105.3 86.7 %collective-permute-start.7 = (bf16[1024,1024]{1,0:T(8,128)(2,1)S(1)}, bf16[1024,1024]{1,0:T(8,128)(2,1)}, u32[]{:S(2)}, u32[]{:S(2)}) collective-permute-start(bf16[1024,1024]{1,0:T(8,128)(2,1)S(1)} %copy-done.11), channel_id=1, source_target_pairs={{1,2},{2,1},{5,6},{6,5},{9,10},{10,9},{13,14},{14,13},{17,18},{18,... | collective-permute-start | bytes 6291464 | tf_op jit(solution)/shard_map/ppermute | solution.py:771
  208.3 11.2 %collective-permute-start.8 = (bf16[8,128,1024]{2,1,0:T(8,128)(2,1)}, bf16[8,128,1024]{2,1,0:T(8,128)(2,1)S(1)}, u32[]{:S(2)}, u32[]{:S(2)}) collective-permute-start(bf16[8,128,1024]{2,1,0:T(8,128)(2,1)} %dynamic-slice_bitcast_fusion.3), channel_id=1, source_target_pairs={{0,2},{1,3},{2,0},{3,1},{4,6},{5,7},{6,4},{7,5},{8,10},{9,11},{10,... | collective-permute-start | bytes 6291464 | tf_op jit(solution)/shard_map/ppermute | solution.py:771
  209.2 10.4 %collective-permute-start.9 = (bf16[8,128,1024]{2,1,0:T(8,128)(2,1)}, bf16[8,128,1024]{2,1,0:T(8,128)(2,1)}, u32[]{:S(2)}, u32[]{:S(2)}) collective-permute-start(bf16[8,128,1024]{2,1,0:T(8,128)(2,1)} %dynamic-slice_bitcast_fusion.2), channel_id=1, source_target_pairs={{0,2},{1,3},{2,0},{3,1},{4,6},{5,7},{6,4},{7,5},{8,10},{9,11},{10,... | collective-permute-start | bytes 6291464 | tf_op jit(solution)/shard_map/ppermute | solution.py:771
  227.4 26.2 %collective-permute-start.10 = (bf16[2,4,128,1024]{3,2,1,0:T(8,128)(2,1)}, bf16[2,4,128,1024]{3,2,1,0:T(8,128)(2,1)S(1)}, u32[]{:S(2)}, u32[]{:S(2)}) collective-permute-start(bf16[2,4,128,1024]{3,2,1,0:T(8,128)(2,1)} %get-tuple-element.343), channel_id=1, source_target_pairs={{0,1},{1,0},{2,6},{3,7},{4,5},{5,4},{6,2},{7,3},{8,9},{9,8},{10,14... | collective-permute-start | bytes 6291464 | tf_op jit(solution)/shard_map/ppermute | solution.py:771
  257.0 20.7 %collective-permute-start.11 = (bf16[8,64,2048]{2,1,0:T(8,128)(2,1)}, bf16[8,64,2048]{2,1,0:T(8,128)(2,1)S(1)}, u32[]{:S(2)}, u32[]{:S(2)}) collective-permute-start(bf16[8,64,2048]{2,1,0:T(8,128)(2,1)} %dynamic-slice_bitcast_fusion.1), channel_id=1, source_target_pairs={{0,2},{1,3},{2,0},{3,1},{4,6},{5,7},{6,4},{7,5},{8,10},{9,11},{10,... | collective-permute-start | bytes 6291464 | tf_op jit(solution)/shard_map/ppermute | solution.py:771
  257.1 20.7 %collective-permute-start.12 = (bf16[8,64,2048]{2,1,0:T(8,128)(2,1)}, bf16[8,64,2048]{2,1,0:T(8,128)(2,1)S(1)}, u32[]{:S(2)}, u32[]{:S(2)}) collective-permute-start(bf16[8,64,2048]{2,1,0:T(8,128)(2,1)} %dynamic-slice_bitcast_fusion), channel_id=1, source_target_pairs={{0,2},{1,3},{2,0},{3,1},{4,6},{5,7},{6,4},{7,5},{8,10},{9,11},{10,... | collective-permute-start | bytes 6291464 | tf_op jit(solution)/shard_map/ppermute | solution.py:771
  257.6 20.1 %collective-permute-start.13 = (bf16[4,128,1024]{2,1,0:T(8,128)(2,1)S(1)}, bf16[4,128,1024]{2,1,0:T(8,128)(2,1)}, u32[]{:S(2)}, u32[]{:S(2)}) collective-permute-start(bf16[4,128,1024]{2,1,0:T(8,128)(2,1)S(1)} %bitcast_add_fusion.3), channel_id=1, source_target_pairs={{0,4},{1,5},{2,3},{3,2},{4,0},{5,1},{6,7},{7,6},{8,12},{9,13},{10,... | collective-permute-start | bytes 3145736 | tf_op jit(solution)/shard_map/ppermute | solution.py:771
  258.1 42.1 %collective-permute-start.15 = (bf16[1024,1024]{1,0:T(8,128)(2,1)}, bf16[1024,1024]{1,0:T(8,128)(2,1)}, u32[]{:S(2)}, u32[]{:S(2)}) collective-permute-start(bf16[1024,1024]{1,0:T(8,128)(2,1)} %shard_map.335), channel_id=1, source_target_pairs={{1,2},{2,1},{5,6},{6,5},{9,10},{10,9},{13,14},{14,13},{17,18},{18,... | collective-permute-start | bytes 6291464 | tf_op jit(solution)/shard_map/ppermute | solution.py:771
  282.1 17.9 %collective-permute-start.14 = (bf16[2,128,1024]{2,1,0:T(8,128)(2,1)}, bf16[2,128,1024]{2,1,0:T(8,128)(2,1)S(1)}, u32[]{:S(2)}, u32[]{:S(2)}) collective-permute-start(bf16[2,128,1024]{2,1,0:T(8,128)(2,1)} %slice.257), channel_id=1, source_target_pairs={{0,8},{1,9},{2,10},{3,11},{4,12},{5,13},{6,14},{7,15},{8,0},{9,1},... | collective-permute-start | bytes 1572872 | tf_op jit(solution)/shard_map/ppermute | solution.py:771
  301.1 28.3 %collective-permute-start.16 = (bf16[2,4,64,2048]{3,2,1,0:T(8,128)(2,1)}, bf16[2,4,64,2048]{3,2,1,0:T(8,128)(2,1)S(1)}, u32[]{:S(2)}, u32[]{:S(2)}) collective-permute-start(bf16[2,4,64,2048]{3,2,1,0:T(8,128)(2,1)} %get-tuple-element.386), channel_id=1, source_target_pairs={{0,1},{1,0},{2,6},{3,7},{4,5},{5,4},{6,2},{7,3},{8,9},{9,8},{10,14... | collective-permute-start | bytes 6291464 | tf_op jit(solution)/shard_map/ppermute | solution.py:771
  303.6 25.7 %collective-permute-start.18 = (bf16[8,32,1024]{2,1,0:T(8,128)(2,1)S(1)}, bf16[8,32,1024]{2,1,0:T(8,128)(2,1)S(1)}, u32[]{:S(2)}, u32[]{:S(2)}) collective-permute-start(bf16[8,32,1024]{2,1,0:T(8,128)(2,1)S(1)} %dynamic-slice_bitcast_fusion.5), channel_id=1, source_target_pairs={{0,2},{1,3},{2,0},{3,1},{4,6},{5,7},{6,4},{7,5},{8,10},{9,11},{10,... | collective-permute-start | bytes 1572872 | tf_op jit(solution)/shard_map/ppermute | solution.py:771
  303.8 25.6 %collective-permute-start.19 = (bf16[8,32,1024]{2,1,0:T(8,128)(2,1)S(1)}, bf16[8,32,1024]{2,1,0:T(8,128)(2,1)S(1)}, u32[]{:S(2)}, u32[]{:S(2)}) collective-permute-start(bf16[8,32,1024]{2,1,0:T(8,128)(2,1)S(1)} %dynamic-slice_bitcast_fusion.4), channel_id=1, source_target_pairs={{0,2},{1,3},{2,0},{3,1},{4,6},{5,7},{6,4},{7,5},{8,10},{9,11},{10,... | collective-permute-start | bytes 1572872 | tf_op jit(solution)/shard_map/ppermute | solution.py:771
  304.1 25.2 %collective-permute-start.17 = (bf16[1,128,1024]{2,1,0:T(8,128)(2,1)S(1)}, bf16[1,128,1024]{2,1,0:T(8,128)(2,1)S(1)}, u32[]{:S(2)}, u32[]{:S(2)}) collective-permute-start(bf16[1,128,1024]{2,1,0:T(8,128)(2,1)S(1)} %slice.259), channel_id=1, source_target_pairs={{0,16},{1,17},{2,18},{3,19},{4,20},{5,21},{6,22},{7,23},{8,24},{9,... | collective-permute-start | bytes 786440 | tf_op jit(solution)/shard_map/ppermute | solution.py:771
  335.0 26.0 %collective-permute-start.20 = (bf16[2,1024,256]{2,1,0:T(8,128)(2,1)}, bf16[2,1024,256]{2,1,0:T(8,128)(2,1)}, u32[]{:S(2)}, u32[]{:S(2)}) collective-permute-start(bf16[2,1024,256]{2,1,0:T(8,128)(2,1)} %get-tuple-element.409), channel_id=1, source_target_pairs={{0,2},{1,3},{2,0},{3,1},{4,6},{5,7},{6,4},{7,5},{8,10},{9,11},{10,... | collective-permute-start | bytes 3145736 | tf_op jit(solution)/shard_map/ppermute | solution.py:771
  335.0 26.0 %collective-permute-start.21 = (bf16[4,64,2048]{2,1,0:T(8,128)(2,1)S(1)}, bf16[4,64,2048]{2,1,0:T(8,128)(2,1)}, u32[]{:S(2)}, u32[]{:S(2)}) collective-permute-start(bf16[4,64,2048]{2,1,0:T(8,128)(2,1)S(1)} %bitcast_add_fusion), channel_id=1, source_target_pairs={{0,4},{1,5},{2,3},{3,2},{4,0},{5,1},{6,7},{7,6},{8,12},{9,13},{10,... | collective-permute-start | bytes 3145736 | tf_op jit(solution)/shard_map/ppermute | solution.py:771
  336.3 24.7 %collective-permute-start.22 = (bf16[2,4,32,1024]{3,2,1,0:T(8,128)(2,1)}, bf16[2,4,32,1024]{3,2,1,0:T(8,128)(2,1)}, u32[]{:S(2)}, u32[]{:S(2)}) collective-permute-start(bf16[2,4,32,1024]{3,2,1,0:T(8,128)(2,1)} %get-tuple-element.411), channel_id=1, source_target_pairs={{0,1},{1,0},{2,6},{3,7},{4,5},{5,4},{6,2},{7,3},{8,9},{9,8},{10,14... | collective-permute-start | bytes 1572872 | tf_op jit(solution)/shard_map/ppermute | solution.py:771
  336.3 155.5 %all-gather.20.cloned.1.call-start = ((), (), s32[]{:S(2)}) async-start(), calls=%async_computation.5 | async-start | bytes 5570560 | tf_op jit(solution)/shard_map/all_gather | solution.py:1146
  336.3 24.7 %copy-start.26 = (bf16[4,64,2048]{2,1,0:T(8,128)(2,1)S(1)}, bf16[4,64,2048]{2,1,0:T(8,128)(2,1)}, u32[]{:S(2)}) copy-start(bf16[4,64,2048]{2,1,0:T(8,128)(2,1)} %get-tuple-element.359) | copy-start | bytes 3145732
  363.5 31.3 %copy-start.35 = (bf16[4,32,1024]{2,1,0:T(8,128)(2,1)S(1)}, bf16[4,32,1024]{2,1,0:T(8,128)(2,1)}, u32[]{:S(2)}) copy-start(bf16[4,32,1024]{2,1,0:T(8,128)(2,1)} %get-tuple-element.439) | copy-start | bytes 786436
  363.5 31.3 %collective-permute-start.23 = (bf16[2,1024,256]{2,1,0:T(8,128)(2,1)}, bf16[2,1024,256]{2,1,0:T(8,128)(2,1)S(1)}, u32[]{:S(2)}, u32[]{:S(2)}) collective-permute-start(bf16[2,1024,256]{2,1,0:T(8,128)(2,1)} %get-tuple-element.427), channel_id=1, source_target_pairs={{0,2},{1,3},{2,0},{3,1},{4,6},{5,7},{6,4},{7,5},{8,10},{9,11},{10,... | collective-permute-start | bytes 3145736 | tf_op jit(solution)/shard_map/ppermute | solution.py:771
  363.7 31.0 %collective-permute-start.24 = (bf16[2,64,2048]{2,1,0:T(8,128)(2,1)S(1)}, bf16[2,64,2048]{2,1,0:T(8,128)(2,1)S(1)}, u32[]{:S(2)}, u32[]{:S(2)}) collective-permute-start(bf16[2,64,2048]{2,1,0:T(8,128)(2,1)S(1)} %slice.262), channel_id=1, source_target_pairs={{0,8},{1,9},{2,10},{3,11},{4,12},{5,13},{6,14},{7,15},{8,0},{9,1},... | collective-permute-start | bytes 1572872 | tf_op jit(solution)/shard_map/ppermute | solution.py:771
  364.9 25.5 %collective-permute-start.25 = (bf16[4,32,1024]{2,1,0:T(8,128)(2,1)S(1)}, bf16[4,32,1024]{2,1,0:T(8,128)(2,1)S(1)}, u32[]{:S(2)}, u32[]{:S(2)}) collective-permute-start(bf16[4,32,1024]{2,1,0:T(8,128)(2,1)S(1)} %bitcast_add_fusion.5), channel_id=1, source_target_pairs={{0,4},{1,5},{2,3},{3,2},{4,0},{5,1},{6,7},{7,6},{8,12},{9,13},{10,... | collective-permute-start | bytes 786440 | tf_op jit(solution)/shard_map/ppermute | solution.py:771
  396.0 15.2 %collective-permute-start.26 = (bf16[2,1024,256]{2,1,0:T(8,128)(2,1)S(1)}, bf16[2,1024,256]{2,1,0:T(8,128)(2,1)S(1)}, u32[]{:S(2)}, u32[]{:S(2)}) collective-permute-start(bf16[2,1024,256]{2,1,0:T(8,128)(2,1)S(1)} %copy-done.54), channel_id=1, source_target_pairs={{0,2},{1,3},{2,0},{3,1},{4,6},{5,7},{6,4},{7,5},{8,10},{9,11},{10,... | collective-permute-start | bytes 3145736 | tf_op jit(solution)/shard_map/ppermute | solution.py:771
  396.8 14.4 %collective-permute-start.27 = (bf16[1,64,2048]{2,1,0:T(8,128)(2,1)S(1)}, bf16[1,64,2048]{2,1,0:T(8,128)(2,1)S(1)}, u32[]{:S(2)}, u32[]{:S(2)}) collective-permute-start(bf16[1,64,2048]{2,1,0:T(8,128)(2,1)S(1)} %slice.264), channel_id=1, source_target_pairs={{0,16},{1,17},{2,18},{3,19},{4,20},{5,21},{6,22},{7,23},{8,24},{9,... | collective-permute-start | bytes 786440 | tf_op jit(solution)/shard_map/ppermute | solution.py:771
  396.8 13.1 %collective-permute-start.28 = (bf16[2,32,1024]{2,1,0:T(8,128)(2,1)S(1)}, bf16[2,32,1024]{2,1,0:T(8,128)(2,1)S(1)}, u32[]{:S(2)}, u32[]{:S(2)}) collective-permute-start(bf16[2,32,1024]{2,1,0:T(8,128)(2,1)S(1)} %slice.265), channel_id=1, source_target_pairs={{0,8},{1,9},{2,10},{3,11},{4,12},{5,13},{6,14},{7,15},{8,0},{9,1},... | collective-permute-start | bytes 393224 | tf_op jit(solution)/shard_map/ppermute | solution.py:771
  411.2 8.6 %collective-permute-start.29 = (bf16[8,3,64,512]{3,2,1,0:T(8,128)(2,1)}, bf16[8,3,64,512]{3,2,1,0:T(8,128)(2,1)S(1)}, u32[]{:S(2)}, u32[]{:S(2)}) collective-permute-start(bf16[8,3,64,512]{3,2,1,0:T(8,128)(2,1)} %get-tuple-element.467), channel_id=1, source_target_pairs={{0,2},{1,3},{2,0},{3,1},{4,6},{5,7},{6,4},{7,5},{8,10},{9,11},{10,... | collective-permute-start | bytes 4718600 | tf_op jit(solution)/shard_map/ppermute | solution.py:771
  411.4 8.4 %collective-permute-start.30 = (bf16[1,32,1024]{2,1,0:T(8,128)(2,1)S(1)}, bf16[1,32,1024]{2,1,0:T(8,128)(2,1)S(1)}, u32[]{:S(2)}, u32[]{:S(2)}) collective-permute-start(bf16[1,32,1024]{2,1,0:T(8,128)(2,1)S(1)} %slice.268), channel_id=1, source_target_pairs={{0,16},{1,17},{2,18},{3,19},{4,20},{5,21},{6,22},{7,23},{8,24},{9,... | collective-permute-start | bytes 196616 | tf_op jit(solution)/shard_map/ppermute | solution.py:771
  420.6 122.3 %all-gather.14.cloned.1.call-start = ((), (), s32[]{:S(2)}) async-start(), calls=%async_computation.2 | async-start | bytes 1671168 | tf_op jit(solution)/shard_map/all_gather | solution.py:1165
  420.9 26.4 %copy-start.28 = (bf16[8,3,64,256]{3,2,1,0:T(8,128)(2,1)S(1)}, bf16[8,3,64,256]{3,2,1,0:T(8,128)(2,1)}, u32[]{:S(2)}) copy-start(bf16[8,3,64,256]{3,2,1,0:T(8,128)(2,1)} %get-tuple-element.495) | copy-start | bytes 2359300
  420.9 26.3 %collective-permute-start.32 = (bf16[8,3,64,256]{3,2,1,0:T(8,128)(2,1)}, bf16[8,3,64,256]{3,2,1,0:T(8,128)(2,1)S(1)}, u32[]{:S(2)}, u32[]{:S(2)}) collective-permute-start(bf16[8,3,64,256]{3,2,1,0:T(8,128)(2,1)} %get-tuple-element.490), channel_id=1, source_target_pairs={{0,2},{1,3},{2,0},{3,1},{4,6},{5,7},{6,4},{7,5},{8,10},{9,11},{10,... | collective-permute-start | bytes 2359304 | tf_op jit(solution)/shard_map/ppermute | solution.py:771
  421.0 26.2 %collective-permute-start.31 = (bf16[8,3,64,256]{3,2,1,0:T(8,128)(2,1)S(1)}, bf16[8,3,64,256]{3,2,1,0:T(8,128)(2,1)S(1)}, u32[]{:S(2)}, u32[]{:S(2)}) collective-permute-start(bf16[8,3,64,256]{3,2,1,0:T(8,128)(2,1)S(1)} %get-tuple-element.480), channel_id=1, source_target_pairs={{0,1},{1,0},{2,3},{3,2},{4,5},{5,4},{6,7},{7,6},{8,9},{9,8},{10,11... | collective-permute-start | bytes 2359304 | tf_op jit(solution)/shard_map/ppermute | solution.py:771
  447.4 9.3 %collective-permute-start.33 = (bf16[2,1024,256]{2,1,0:T(8,128)(2,1)}, bf16[2,1024,256]{2,1,0:T(8,128)(2,1)S(1)}, u32[]{:S(2)}, u32[]{:S(2)}) collective-permute-start(bf16[2,1024,256]{2,1,0:T(8,128)(2,1)} %get-tuple-element.500), channel_id=1, source_target_pairs={{0,2},{1,3},{2,0},{3,1},{4,6},{5,7},{6,4},{7,5},{8,10},{9,11},{10,... | collective-permute-start | bytes 3145736 | tf_op jit(solution)/shard_map/ppermute | solution.py:771
  447.6 19.8 %collective-permute-start.35 = (bf16[8,3,64,256]{3,2,1,0:T(8,128)(2,1)S(1)}, bf16[8,3,64,256]{3,2,1,0:T(8,128)(2,1)S(1)}, u32[]{:S(2)}, u32[]{:S(2)}) collective-permute-start(bf16[8,3,64,256]{3,2,1,0:T(8,128)(2,1)S(1)} %get-tuple-element.511), channel_id=1, source_target_pairs={{0,1},{1,0},{2,3},{3,2},{4,5},{5,4},{6,7},{7,6},{8,9},{9,8},{10,11... | collective-permute-start | bytes 2359304 | tf_op jit(solution)/shard_map/ppermute | solution.py:771
  448.0 19.8 %collective-permute-start.34 = (bf16[4,3,64,256]{3,2,1,0:T(8,128)(2,1)S(1)}, bf16[4,3,64,256]{3,2,1,0:T(8,128)(2,1)S(1)}, u32[]{:S(2)}, u32[]{:S(2)}) collective-permute-start(bf16[4,3,64,256]{3,2,1,0:T(8,128)(2,1)S(1)} %slice.269), channel_id=1, source_target_pairs={{0,4},{1,5},{2,6},{3,7},{4,0},{5,1},{6,2},{7,3},{8,12},{9,13},{10,... | collective-permute-start | bytes 1179656 | tf_op jit(solution)/shard_map/ppermute | solution.py:771
  467.9 17.8 %collective-permute-start.36 = (bf16[8,3,64,256]{3,2,1,0:T(8,128)(2,1)}, bf16[8,3,64,256]{3,2,1,0:T(8,128)(2,1)S(1)}, u32[]{:S(2)}, u32[]{:S(2)}) collective-permute-start(bf16[8,3,64,256]{3,2,1,0:T(8,128)(2,1)} %get-tuple-element.516), channel_id=1, source_target_pairs={{0,2},{1,3},{2,0},{3,1},{4,6},{5,7},{6,4},{7,5},{8,10},{9,11},{10,... | collective-permute-start | bytes 2359304 | tf_op jit(solution)/shard_map/ppermute | solution.py:771
  468.8 14.0 %collective-permute-start.37 = (bf16[1,3,64,256]{3,2,1,0:T(8,128)(2,1)S(1)}, bf16[1,3,64,256]{3,2,1,0:T(8,128)(2,1)S(1)}, u32[]{:S(2)}, u32[]{:S(2)}) collective-permute-start(bf16[1,3,64,256]{3,2,1,0:T(8,128)(2,1)S(1)} %get-tuple-element.517), channel_id=1, source_target_pairs={{0,16},{1,17},{2,18},{3,19},{4,20},{5,21},{6,22},{7,23},{8,24},{9,... | collective-permute-start | bytes 294920 | tf_op jit(solution)/shard_map/ppermute | solution.py:771
  470.9 11.9 %collective-permute-start.38 = (bf16[1,3,64,256]{3,2,1,0:T(8,128)(2,1)S(1)}, bf16[1,3,64,256]{3,2,1,0:T(8,128)(2,1)S(1)}, u32[]{:S(2)}, u32[]{:S(2)}) collective-permute-start(bf16[1,3,64,256]{3,2,1,0:T(8,128)(2,1)S(1)} %get-tuple-element.518), channel_id=1, source_target_pairs={{0,8},{1,9},{2,10},{3,11},{4,12},{5,13},{6,14},{7,15},{8,0},{9,1},... | collective-permute-start | bytes 294920 | tf_op jit(solution)/shard_map/ppermute | solution.py:771
  471.0 14.7 %collective-permute-start.39 = (bf16[1,3,64,256]{3,2,1,0:T(8,128)(2,1)S(1)}, bf16[1,3,64,256]{3,2,1,0:T(8,128)(2,1)S(1)}, u32[]{:S(2)}, u32[]{:S(2)}) collective-permute-start(bf16[1,3,64,256]{3,2,1,0:T(8,128)(2,1)S(1)} %get-tuple-element.519), channel_id=1, source_target_pairs={{0,24},{1,25},{2,26},{3,27},{4,28},{5,29},{6,30},{7,31},{8,16},{9,... | collective-permute-start | bytes 294920 | tf_op jit(solution)/shard_map/ppermute | solution.py:771
  491.8 11.7 %collective-permute-start.40 = (bf16[4,3,64,256]{3,2,1,0:T(8,128)(2,1)S(1)}, bf16[4,3,64,256]{3,2,1,0:T(8,128)(2,1)S(1)}, u32[]{:S(2)}, u32[]{:S(2)}) collective-permute-start(bf16[4,3,64,256]{3,2,1,0:T(8,128)(2,1)S(1)} %slice.275), channel_id=1, source_target_pairs={{0,4},{1,5},{2,6},{3,7},{4,0},{5,1},{6,2},{7,3},{8,12},{9,13},{10,... | collective-permute-start | bytes 1179656 | tf_op jit(solution)/shard_map/ppermute | solution.py:771
  503.6 17.5 %collective-permute-start.47 = (bf16[1,3,64,256]{3,2,1,0:T(8,128)(2,1)S(1)}, bf16[1,3,64,256]{3,2,1,0:T(8,128)(2,1)S(1)}, u32[]{:S(2)}, u32[]{:S(2)}) collective-permute-start(bf16[1,3,64,256]{3,2,1,0:T(8,128)(2,1)S(1)} %get-tuple-element.562), channel_id=1, source_target_pairs={{0,16},{1,17},{2,18},{3,19},{4,20},{5,21},{6,22},{7,23},{8,24},{9,... | collective-permute-start | bytes 294920 | tf_op jit(solution)/shard_map/ppermute | solution.py:771
  503.7 17.4 %collective-permute-start.48 = (bf16[1,3,64,256]{3,2,1,0:T(8,128)(2,1)S(1)}, bf16[1,3,64,256]{3,2,1,0:T(8,128)(2,1)S(1)}, u32[]{:S(2)}, u32[]{:S(2)}) collective-permute-start(bf16[1,3,64,256]{3,2,1,0:T(8,128)(2,1)S(1)} %get-tuple-element.560), channel_id=1, source_target_pairs={{0,8},{1,9},{2,10},{3,11},{4,12},{5,13},{6,14},{7,15},{8,0},{9,1},... | collective-permute-start | bytes 294920 | tf_op jit(solution)/shard_map/ppermute | solution.py:771
  505.4 15.7 %collective-permute-start.49 = (bf16[1,3,64,256]{3,2,1,0:T(8,128)(2,1)S(1)}, bf16[1,3,64,256]{3,2,1,0:T(8,128)(2,1)S(1)}, u32[]{:S(2)}, u32[]{:S(2)}) collective-permute-start(bf16[1,3,64,256]{3,2,1,0:T(8,128)(2,1)S(1)} %get-tuple-element.561), channel_id=1, source_target_pairs={{0,24},{1,25},{2,26},{3,27},{4,28},{5,29},{6,30},{7,31},{8,16},{9,... | collective-permute-start | bytes 294920 | tf_op jit(solution)/shard_map/ppermute | solution.py:771
  511.3 8.7 %collective-permute-start.42 = (f32[2,52,128]{2,1,0:T(8,128)S(1)}, f32[2,52,128]{2,1,0:T(8,128)S(1)}, u32[]{:S(2)}, u32[]{:S(2)}) collective-permute-start(f32[2,52,128]{2,1,0:T(8,128)S(1)} %pad_maximum_fusion.6), channel_id=1, source_target_pairs={{0,2},{1,3},{2,0},{3,1},{4,6},{5,7},{6,4},{7,5},{8,10},{9,11},{10,... | collective-permute-start | bytes 159752 | tf_op jit(solution)/shard_map/ppermute | solution.py:771
  518.0 37.5 %collective-permute-start.41 = (bf16[1024,1024]{1,0:T(8,128)(2,1)}, bf16[1024,1024]{1,0:T(8,128)(2,1)}, u32[]{:S(2)}, u32[]{:S(2)}) collective-permute-start(bf16[1024,1024]{1,0:T(8,128)(2,1)} %get-tuple-element.540), channel_id=1, source_target_pairs={{1,2},{2,1},{5,6},{6,5},{9,10},{10,9},{13,14},{14,13},{17,18},{18,... | collective-permute-start | bytes 6291464 | tf_op jit(solution)/shard_map/ppermute | solution.py:771
  520.0 5.6 collective-permute-start.43
  521.2 16.9 %collective-permute-start.50 = (bf16[1,3,64,256]{3,2,1,0:T(8,128)(2,1)S(1)}, bf16[1,3,64,256]{3,2,1,0:T(8,128)(2,1)S(1)}, u32[]{:S(2)}, u32[]{:S(2)}) collective-permute-start(bf16[1,3,64,256]{3,2,1,0:T(8,128)(2,1)S(1)} %slice_add_fusion.9), channel_id=1, source_target_pairs={{0,16},{1,17},{2,18},{3,19},{4,20},{5,21},{6,22},{7,23},{8,24},{9,... | collective-permute-start | bytes 294920 | tf_op jit(solution)/shard_map/ppermute | solution.py:771
  521.2 16.8 %collective-permute-start.51 = (bf16[1,3,64,256]{3,2,1,0:T(8,128)(2,1)S(1)}, bf16[1,3,64,256]{3,2,1,0:T(8,128)(2,1)S(1)}, u32[]{:S(2)}, u32[]{:S(2)}) collective-permute-start(bf16[1,3,64,256]{3,2,1,0:T(8,128)(2,1)S(1)} %slice_add_fusion.9), channel_id=1, source_target_pairs={{0,8},{1,9},{2,10},{3,11},{4,12},{5,13},{6,14},{7,15},{8,0},{9,1},... | collective-permute-start | bytes 294920 | tf_op jit(solution)/shard_map/ppermute | solution.py:771
  523.4 14.7 %collective-permute-start.52 = (bf16[1,3,64,256]{3,2,1,0:T(8,128)(2,1)S(1)}, bf16[1,3,64,256]{3,2,1,0:T(8,128)(2,1)S(1)}, u32[]{:S(2)}, u32[]{:S(2)}) collective-permute-start(bf16[1,3,64,256]{3,2,1,0:T(8,128)(2,1)S(1)} %slice_add_fusion.9), channel_id=1, source_target_pairs={{0,24},{1,25},{2,26},{3,27},{4,28},{5,29},{6,30},{7,31},{8,16},{9,... | collective-permute-start | bytes 294920 | tf_op jit(solution)/shard_map/ppermute | solution.py:771
  525.7 10.8 %collective-permute-start.44 = (f32[2,52,128]{2,1,0:T(8,128)S(1)}, f32[2,52,128]{2,1,0:T(8,128)S(1)}, u32[]{:S(2)}, u32[]{:S(2)}) collective-permute-start(f32[2,52,128]{2,1,0:T(8,128)S(1)} %fusion.41), channel_id=1, source_target_pairs={{0,8},{1,9},{2,10},{3,11},{4,12},{5,13},{6,14},{7,15},{8,0},{9,1},... | collective-permute-start | bytes 159752 | tf_op jit(solution)/shard_map/ppermute | solution.py:771
  536.5 5.7 collective-permute-start.45
  542.2 11.3 %collective-permute-start.46 = (f32[52,128]{1,0:T(8,128)S(1)}, f32[52,128]{1,0:T(8,128)S(1)}, u32[]{:S(2)}, u32[]{:S(2)}) collective-permute-start(f32[52,128]{1,0:T(8,128)S(1)} %slice_bitcast_fusion), channel_id=1, source_target_pairs={{0,1},{1,0},{2,3},{3,2},{4,5},{5,4},{6,7},{7,6},{8,9},{9,8},{10,11... | collective-permute-start | bytes 79880 | tf_op jit(solution)/shard_map/ppermute | solution.py:771
  543.0 11.1 %collective-permute-start.53 = (bf16[4,3,64,256]{3,2,1,0:T(8,128)(2,1)S(1)}, bf16[4,3,64,256]{3,2,1,0:T(8,128)(2,1)S(1)}, u32[]{:S(2)}, u32[]{:S(2)}) collective-permute-start(bf16[4,3,64,256]{3,2,1,0:T(8,128)(2,1)S(1)} %pad_maximum_fusion.3), channel_id=1, source_target_pairs={{0,4},{1,5},{2,6},{3,7},{4,0},{5,1},{6,2},{7,3},{8,12},{9,13},{10,... | collective-permute-start | bytes 1179656 | tf_op jit(solution)/shard_map/ppermute | solution.py:771
  554.2 4.4 collective-permute-start.54
  (58 other events, 420.0 us)
Sparse Core Ops, SparseCore 0:
  19.3 53.4 all-gather.15
  75.0 50.1 all-gather.9
  127.4 49.2 all-gather.11
  336.4 59.0 all-gather.17
  420.8 71.0 all-gather.19
  494.5 43.8 all-gather.13

commit v7 on v6

--- a/solution.py
+++ b/solution.py
@@ -1141,9 +1141,8 @@
     (keep_a, send_a, rows_a, bias_a), (core_got,) = beside(
         unit, ((own_a,), (key_got,)), (move.over_core, send), proj
     )
-    mixed = jnp.concatenate([up.done[0], proj.done[0].reshape(-1, up.done.shape[2])])
-    mixed, keep_a, down_all = tie(mixed, keep_a, down_all)
-    mixed_all = lax.all_gather(mixed, "dp")
+    up_block, keep_a, down_all = tie(up.done, keep_a, down_all)
+    up_all = move.gather(up_block)
     y_sends = [keep_oth[..., at : at + cols] + core_got[..., at : at + cols] for at in (0, cols)]
     own_b, (core_got_a, y_got_a, y_got_b) = beside(
         *back(3), (move.over_core, send_a), late=[(move.over_y, y) for y in y_sends]
@@ -1161,46 +1160,53 @@
     )
     total_a = keep_a + sum(a_got)
     keep_b, send_b = halves(keep_b + core_got + y_got_b)
-    mixed_all, partial, total_a = tie(mixed_all, partial, total_a)
-    unit_a = lax.all_gather(total_a[0], "dp")
+    up_all, partial, total_a = tie(up_all, partial, total_a)
+    unit_a = lax.all_gather(
+        jnp.concatenate([total_a[0], proj.done.reshape(-1, *total_a.shape[2:])]), "dp"
+    )
+    f32 = lambda v: v.astype(F32)
     (in_grad, sums_one), (b_got,) = beside(
         lambda *xs: last_rows(block_in, branch_grad, row(ln1_scale), *xs),
         (partial, qkv_own, rows_b),
         (over_x, send_b),
     )
-    in_grad, mixed_all, block_got, down_all = tie(in_grad, mixed_all, block_got, down_all)
+    in_grad, block_got, down_all, up_all = tie(in_grad, block_got, down_all, up_all)
     in_grad_got = move.swap(in_grad)
     keep_b, send_b = z_parts(keep_b + b_got)
-    total_b = keep_b + sum(over_z(send_b))
-    total_b = jnp.concatenate([total_b] + over_z([total_b] * 3))
-    total_b, unit_a = tie(total_b, unit_a)
-    total_b = jnp.concatenate([total_b, over_x(total_b)])
+    b_got = over_z(send_b)
+    total_b = keep_b + sum(b_got)
+    b_got = over_z([total_b] * 3)
+    b_got[0], down_all, up_all = tie(b_got[0], down_all, up_all)
+    down_g, up_g = f32(down_all), f32(up_all)
+    b_got, down_g, up_g = tie(b_got, down_g, up_g)
+    total_b = jnp.concatenate([total_b] + b_got)
+    b_got = over_x(total_b)
+    block_out = move.stays(block_out, block_got)
+    b_got, block_out = tie(b_got, block_out)
+    total_b = jnp.concatenate([total_b, b_got])
     total_b = jnp.concatenate([total_b, move.over_core(total_b)])
+    out_g = f32(unit_a[:, 3:].reshape(part, width))
     qkv_g = jnp.transpose(widen(move.blocks, unit_a, total_b), (1, 0, 2))
-    up_rows_each = width // n_dp
-    up_all = mixed_all[:, :up_rows_each].reshape(width, -1)
-    out_all = mixed_all[:, up_rows_each:].reshape(part, width)
     side = lambda a, b: jnp.concatenate([a.reshape(3, cols), b.reshape(3, cols)], axis=1).reshape(-1)
     vec, flat = move.reduce_vectors(
         jnp.concatenate([sums_one[:2], sums_two[:4]]),
         jnp.concatenate([side(bias_a[0], bias_b[0]), up_b_own[0]]),
         jnp.concatenate([bias_oth[0], up_b_oth[0]]),
     )
-    f32 = lambda v: v.astype(F32)
     return (
-        move.stays(block_out, block_got),
+        block_out,
         move.stays(in_grad, in_grad_got),
         vec[0],
         vec[1],
         qkv_g,
         flat[: 3 * part].reshape(3, part),
-        f32(out_all),
+        out_g,
         vec[4],
         vec[2],
         vec[3],
-        f32(up_all),
+        up_g,
         flat[3 * part :],
-        f32(down_all),
+        down_g,
         vec[5],
     )
 

time: 579 us -> 573 us (0.990)
  waiting for transfers between devices: 49.1 us -> 41.7 us
    unnamed x124 -> x132, local copies, waits for them, and re-layouts: 13.3 us -> 17.8 us
  transfers between devices with their start and end apart: 61 -> 61, of which waited for: 14 -> 15; matrix products, arithmetic and copies ran while one was open for 14% -> 13% of each run, Pallas kernels for 54% -> 55%
where the time goes in v7:
time: 573 us; the launch traced here: 565 us
  Pallas kernels  328 us (57%)
  starting transfers between devices  70.5 us (12%)
  waiting for transfers between devices  41.7 us (7%)
  local copies, waits for them, and re-layouts  40.3 us (7%)
  other arithmetic  39.3 us (7%)
  matrix products  29.8 us (5%)
  between operations  15.6 us (3%)
    pallas_call x4, Pallas kernels, attend_back(): call(functools.partial(attend_back_kernel, sources=len(kvs), keys_at=1024...  97.5 us
    ppermute x55, starting transfers between devices, move(): return lax.ppermute(x, ('dp', 'tensor'), pairs)  70.1 us
    pallas_call x3, Pallas kernels, attend(): call(functools.partial(attend_kernel, sources=len(kvs), rows_at=min(512,...  48.9 us
    ppermute x55, waiting for transfers between devices, move(): return lax.ppermute(x, ('dp', 'tensor'), pairs)  39.3 us
    pallas_call x3, Pallas kernels, unit_grads(): pl.pallas_call(functools.partial(unit_kernel, chips=chips, parts=parts),...  26.2 us
    pallas_call x2, Pallas kernels, up_rows(): call(up_kernel, 2 * tokens * width * cols, 2 * (tokens * width + width *...  22.6 us
    pallas_call x2, Pallas kernels, qkv_rows(): call(functools.partial(qkv_kernel, q_steps=q_steps), 2 * tokens * width *...  21.3 us
    pallas_call x2, Pallas kernels, hidden_grads(): call(functools.partial(hidden_grad_kernel, skip=skip), 2 * tokens * width...  20.1 us
  transfers between devices with their start and end apart: 61, of which 15 were waited for; matrix products, arithmetic and copies ran while one was open for 13% of the time, Pallas kernels for 55%

profile of v7, /device:TPU:0, one launch (start us, length us, event | category | flops | bytes accessed | tf_op | source)
XLA Modules:
  0.0 565.2 jit_solution(5896711779616489495)
XLA Ops:
  9.1 3.0 collective-permute-start.3
  12.1 6.3 %collective-permute-done.3 = bf16[4,64,512]{2,1,0:T(8,128)(2,1)S(1)} collective-permute-done((bf16[4,64,512]{2,1,0:T(8,128)(2,1)S(1)}, bf16[4,64,512]{2,1,0:T(8,128)(2,1)S(1)}, u32[]{:S(2)}, u32[]{:S(2)}) %collective-permute-start.3) | collective-permute-done | bytes 262176 | tf_op jit(solution)/shard_map/ppermute | solution.py:771
  25.9 3.7 fusion.3
  30.9 5.8 %shard_map.326 = (bf16[1024,1024]{1,0:T(8,128)(2,1)}, bf16[1024,1024]{1,0:T(8,128)(2,1)}, bf16[1024,1024]{1,0:T(8,128)(2,1)}) custom-call(s32[1]{0:T(128)} %bitcast.stay_ref, bf16[1024,1024]{1,0:T(8,128)(2,1)} %x_ref.1, bf16[1024,1024]{1,0:T(8,128)(2,1)} %copy-done.17, f32[1,1024]{1,0:T(1,128)} %bitcast.155, f32[1,1024]{1,0:T(1,128)} %bitcast.159), custom_call_target="tpu_custom_call" | custom-call | flops 10485760 | bytes 10485760 | tf_op jit(solution)/shard_map/pallas_call | solution.py:96
  36.8 18.9 %collective-permute-start.1 = (bf16[64,2048]{1,0:T(8,128)(2,1)S(1)}, bf16[64,2048]{1,0:T(8,128)(2,1)S(1)}, u32[]{:S(2)}, u32[]{:S(2)}) collective-permute-start(bf16[64,2048]{1,0:T(8,128)(2,1)S(1)} %constant_dynamic-slice_fusion.4), channel_id=1, source_target_pairs={{0,1},{1,0},{2,3},{3,2},{4,5},{5,4},{6,7},{7,6},{8,9},{9,8},{10,11... | collective-permute-start | bytes 786440 | tf_op jit(solution)/shard_map/ppermute | solution.py:771
  55.7 10.6 %shard_map.327 = (bf16[1024,512]{1,0:T(8,128)(2,1)}, bf16[1024,1024]{1,0:T(8,128)(2,1)}) custom-call(bf16[1024,1024]{1,0:T(8,128)(2,1)} %get-tuple-element.294.n_ref, bf16[1,3,1024,512]{3,2,1,0:T(8,128)(2,1)} %bitcast.131, f32[1,1536]{1,0:T(1,128)} %bitcast.164, f32[1024,128]{1,0:T(8,128)} %get-tuple-element.602.c_ref.refs_4_, ...), custom_call_target="tpu_custom_call" | custom-call | flops 3221225472 | bytes 8388608 | tf_op jit(solution)/shard_map/pallas_call | solution.py:145
  70.1 2.6 collective-permute-done.5
  73.3 12.7 %shard_map.328 = (bf16[1024,256]{1,0:T(8,128)(2,1)}, f32[2,2,1024]{2,1,0:T(2,128)}) custom-call(bf16[1024,512]{1,0:T(8,128)(2,1)} %get-tuple-element.482.refs_0_, bf16[1024,1024]{1,0:T(8,128)(2,1)} %get-tuple-element.486.refs_1_.refs_3_.refs_7_.refs_9_, bf16[1024,1024]{1,0:T(8,128)(2,1)} %collective-permute-done.4.refs_2_.refs_4_.refs_8_.refs_10_, ...), custom_call_target="tpu_custom_call" | custom-call | flops 8589934592 | bytes 3145728 | tf_op jit(solution)/shard_map/pallas_call | solution.py:213
  86.1 10.7 %shard_map.329 = (bf16[1024,512]{1,0:T(8,128)(2,1)}, bf16[1024,1024]{1,0:T(8,128)(2,1)}) custom-call(bf16[1024,1024]{1,0:T(8,128)(2,1)} %get-tuple-element.294.n_ref, bf16[16,4,64,512]{3,2,1,0:T(8,128)(2,1)} %bitcast.150, f32[1,1536]{1,0:T(1,128)} %reshape.232.b_ref, f32[1024,128]{1,0:T(8,128)} %get-tuple-element.602.c_ref.refs_4_, ...), custom_call_target="tpu_custom_call" | custom-call | flops 3221225472 | bytes 8388608 | tf_op jit(solution)/shard_map/pallas_call | solution.py:145
  105.0 2.4 collective-permute-start.7
  107.5 12.7 %shard_map.330 = (bf16[1024,256]{1,0:T(8,128)(2,1)}, f32[2,2,1024]{2,1,0:T(2,128)}) custom-call(bf16[1024,512]{1,0:T(8,128)(2,1)} %get-tuple-element.482.refs_0_, bf16[1024,1024]{1,0:T(8,128)(2,1)} %get-tuple-element.486.refs_1_.refs_3_.refs_7_.refs_9_, bf16[1024,1024]{1,0:T(8,128)(2,1)} %collective-permute-done.4.refs_2_.refs_4_.refs_8_.refs_10_, ...), custom_call_target="tpu_custom_call" | custom-call | flops 8589934592 | bytes 3145728 | tf_op jit(solution)/shard_map/pallas_call | solution.py:213
  120.2 23.5 %shard_map.331 = (bf16[1024,512]{1,0:T(8,128)(2,1)}, f32[4,2,1024]{2,1,0:T(2,128)}) custom-call(bf16[1024,512]{1,0:T(8,128)(2,1)} %get-tuple-element.412.refs_0_, bf16[1024,1024]{1,0:T(8,128)(2,1)} %get-tuple-element.416.refs_1_.refs_3_.refs_7_.refs_9_, bf16[1024,1024]{1,0:T(8,128)(2,1)} %collective-permute-done.6.refs_2_.refs_4_.refs_8_.refs_10_, ...), custom_call_target="tpu_custom_call" | custom-call | flops 17179869184 | bytes 6291456 | tf_op jit(solution)/shard_map/pallas_call | solution.py:213
  143.7 7.9 %shard_map.332 = (f32[1024,1024]{1,0:T(8,128)}, bf16[1024,1024]{1,0:T(8,128)(2,1)}, bf16[1024,1024]{1,0:T(8,128)(2,1)}) custom-call(bf16[1024,1024]{1,0:T(8,128)(2,1)} %get-tuple-element.322.refs_0_.x_ref, f32[1,1024]{1,0:T(1,128)} %bitcast.169, f32[1,1024]{1,0:T(1,128)} %bitcast.165, f32[1,1024]{1,0:T(1,128)} %bitcast.168, ...), custom_call_target="tpu_custom_call" | custom-call | flops 2147483648 | bytes 14680064 | tf_op jit(solution)/shard_map/pallas_call | solution.py:452
  151.6 11.5 %shard_map.333 = (bf16[1024,2048]{1,0:T(8,128)(2,1)}, bf16[1024,2048]{1,0:T(8,128)(2,1)}) custom-call(bf16[1024,1024]{1,0:T(8,128)(2,1)} %get-tuple-element.325.n_ref, bf16[1024,2048]{1,0:T(8,128)(2,1)} %refs_2_.1, f32[1,2048]{1,0:T(1,128)} %bitcast.162), custom_call_target="tpu_custom_call" | custom-call | flops 4294967296 | bytes 14680064 | tf_op jit(solution)/shard_map/pallas_call | solution.py:364
  163.1 11.1 %shard_map.334 = (bf16[1024,2048]{1,0:T(8,128)(2,1)}, bf16[1024,2048]{1,0:T(8,128)(2,1)}) custom-call(bf16[1024,1024]{1,0:T(8,128)(2,1)} %get-tuple-element.325.n_ref, bf16[1024,2048]{1,0:T(8,128)(2,1)} %all-gather.11.cloned.1.call-done.w_ref.refs_3_, f32[1,2048]{1,0:T(1,128)} %bitcast.163), custom_call_target="tpu_custom_call" | custom-call | flops 4294967296 | bytes 14680064 | tf_op jit(solution)/shard_map/pallas_call | solution.py:364
  174.2 2.2 all-gather.13.cloned.1.call-done
  176.4 15.2 %shard_map.335 = bf16[1024,1024]{1,0:T(8,128)(2,1)} custom-call(f32[1024,1024]{1,0:T(8,128)} %get-tuple-element.323.r_ref, f32[1,1024]{1,0:T(1,128)} %bitcast.167, bf16[1024,2048]{1,0:T(8,128)(2,1)} %get-tuple-element.331.refs_0_, bf16[1024,2048]{1,0:T(8,128)(2,1)} %get-tuple-element.333.refs_1_, bf16[1,2048,1024]{2,1,0:T(8,128)(2,1)} %bitcast.157, ...), custom_call_target="tpu_custom_call" | custom-call | flops 8589934592 | bytes 23068672 | tf_op jit(solution)/shard_map/pallas_call | solution.py:482
  191.9 1.9 copy-done.62
  193.8 4.9 convolution_convert_fusion.2
  198.8 4.9 convolution_convert_fusion.3
  203.7 1.8 dynamic-slice_bitcast_fusion.2
  209.4 9.7 %shard_map.336 = (bf16[1024,2048]{1,0:T(8,128)(2,1)}, f32[1,2048]{1,0:T(1,128)}) custom-call(bf16[1024,1024]{1,0:T(8,128)(2,1)} %copy-done.14, bf16[1,2048,1024]{2,1,0:T(8,128)(2,1)} %bitcast.158, bf16[1024,2048]{1,0:T(8,128)(2,1)} %get-tuple-element.337.slope_ref), custom_call_target="tpu_custom_call" | custom-call | flops 4294967296 | bytes 14680064 | tf_op jit(solution)/shard_map/pallas_call | solution.py:399
  220.5 6.5 %shard_map.337 = (bf16[4,128,1024]{2,1,0:T(8,128)(2,1)}, bf16[4,128,1024]{2,1,0:T(8,128)(2,1)}, bf16[2,4,128,1024]{3,2,1,0:T(8,128)(2,1)}) custom-call(s32[9]{0:T(128)} %pad_add_fusion.1.t_ref, bf16[8,2,128,1024]{3,2,1,0:T(8,128)(2,1)} %bitcast.123, bf16[8,2,128,1024]{3,2,1,0:T(8,128)(2,1)} %bitcast.124, bf16[8,2,128,1024]{3,2,1,0:T(8,128)(2,1)} %bitcast.120, ...), custom_call_target="tpu_custom_call" | custom-call | flops 2097152 | bytes 12582912 | tf_op jit(solution)/shard_map/pallas_call | solution.py:731
  228.7 10.3 %shard_map.338 = (bf16[1024,2048]{1,0:T(8,128)(2,1)}, f32[1,2048]{1,0:T(1,128)}) custom-call(bf16[1024,1024]{1,0:T(8,128)(2,1)} %copy-done.14, bf16[1,2048,1024]{2,1,0:T(8,128)(2,1)} %bitcast.171, bf16[1024,2048]{1,0:T(8,128)(2,1)} %get-tuple-element.347.slope_ref), custom_call_target="tpu_custom_call" | custom-call | flops 4294967296 | bytes 14680064 | tf_op jit(solution)/shard_map/pallas_call | solution.py:399
  239.1 7.1 %convolution_convert_fusion = bf16[1024,2048]{1,0:T(8,128)(2,1)S(1)} fusion(bf16[1024,1024]{1,0:T(8,128)(2,1)S(1)} %copy-done.59, bf16[1024,2048]{1,0:T(8,128)(2,1)} %get-tuple-element.359.refs_1_), kind=kOutput, calls=%fused_computation | convolution fusion | flops 4297064448 | bytes 10485760 | tf_op jit(solution)/shard_map/dot_general | solution.py:32
  246.1 4.8 convolution_convert_fusion.1
  250.9 2.3 collective-permute-done.10
  257.6 2.0 collective-permute-start.15
  259.6 17.6 %shard_map.339 = (bf16[1024,1024]{1,0:T(8,128)(2,1)}, f32[8,1024]{1,0:T(8,128)}) custom-call(f32[1024,1024]{1,0:T(8,128)} %get-tuple-element.323.r_ref, bf16[1024,1024]{1,0:T(8,128)(2,1)} %copy-done.14, f32[1,1024]{1,0:T(1,128)} %bitcast.166, bf16[1024,2048]{1,0:T(8,128)(2,1)} %get-tuple-element.358.refs_0_, bf16[1024,2048]{1,0:T(8,128)(2,1)} %get-tuple-element.359.refs_1_, ...), custom_call_target="tpu_custom_call" | custom-call | flops 8589934592 | bytes 25165824 | tf_op jit(solution)/shard_map/pallas_call | solution.py:521
  277.2 3.5 fusion.1
  287.6 2.3 convolution_convert_fusion.4.refs_1_
  290.6 6.6 %shard_map.340 = (bf16[4,64,2048]{2,1,0:T(8,128)(2,1)}, bf16[4,64,2048]{2,1,0:T(8,128)(2,1)}, bf16[2,4,64,2048]{3,2,1,0:T(8,128)(2,1)}) custom-call(s32[9]{0:T(128)} %pad_add_fusion.1.t_ref, bf16[8,2,64,2048]{3,2,1,0:T(8,128)(2,1)} %bitcast.129, bf16[8,2,64,2048]{3,2,1,0:T(8,128)(2,1)} %bitcast.130, bf16[8,2,64,2048]{3,2,1,0:T(8,128)(2,1)} %bitcast.126, ...), custom_call_target="tpu_custom_call" | custom-call | flops 2097152 | bytes 12582912 | tf_op jit(solution)/shard_map/pallas_call | solution.py:731
  300.6 2.5 collective-permute-start.16
  304.5 24.3 %shard_map.341 = (bf16[1024,256]{1,0:T(8,128)(2,1)}, bf16[2,1024,256]{2,1,0:T(8,128)(2,1)}, bf16[2,1024,256]{2,1,0:T(8,128)(2,1)}) custom-call(bf16[1024,512]{1,0:T(8,128)(2,1)} %get-tuple-element.412.refs_0_, bf16[1024,512]{1,0:T(8,128)(2,1)} %convolution_convert_fusion.4.refs_1_, bf16[1024,512]{1,0:T(8,128)(2,1)} %get-tuple-element.414.refs_6_.refs_2_, ...), custom_call_target="tpu_custom_call" | custom-call | flops 21474836480 | bytes 6291456 | tf_op jit(solution)/shard_map/pallas_call | solution.py:305
  329.9 4.4 shard_map.342
  336.0 24.6 %shard_map.343 = (bf16[1024,256]{1,0:T(8,128)(2,1)}, bf16[2,1024,256]{2,1,0:T(8,128)(2,1)}, bf16[2,1024,256]{2,1,0:T(8,128)(2,1)}) custom-call(bf16[1024,512]{1,0:T(8,128)(2,1)} %get-tuple-element.412.refs_0_, bf16[1024,512]{1,0:T(8,128)(2,1)} %convolution_convert_fusion.4.refs_1_, bf16[1024,512]{1,0:T(8,128)(2,1)} %get-tuple-element.414.refs_6_.refs_2_, ...), custom_call_target="tpu_custom_call" | custom-call | flops 21474836480 | bytes 6291456 | tf_op jit(solution)/shard_map/pallas_call | solution.py:305
  365.4 24.3 %shard_map.344 = (bf16[1024,256]{1,0:T(8,128)(2,1)}, bf16[2,1024,256]{2,1,0:T(8,128)(2,1)}, bf16[2,1024,256]{2,1,0:T(8,128)(2,1)}) custom-call(bf16[1024,512]{1,0:T(8,128)(2,1)} %get-tuple-element.482.refs_0_, bf16[1024,256]{1,0:T(8,128)(2,1)} %convolution_convert_fusion.7.refs_1_, bf16[1024,256]{1,0:T(8,128)(2,1)} %get-tuple-element.431.refs_4_.refs_2_, ...), custom_call_target="tpu_custom_call" | custom-call | flops 21474836480 | bytes 6291456 | tf_op jit(solution)/shard_map/pallas_call | solution.py:305
  389.8 4.5 collective-permute-done.24
  396.3 2.3 collective-permute-start.28
  398.6 10.7 %shard_map.345 = (bf16[8,3,64,512]{3,2,1,0:T(8,128)(2,1)}, bf16[8,3,64,512]{3,2,1,0:T(8,128)(2,1)}, bf16[1024,1536]{1,0:T(8,128)(2,1)}, f32[8,1536]{1,0:T(8,128)}) custom-call(s32[16]{0:T(128)} %pad_add_fusion.t_ref, bf16[1024,1024]{1,0:T(8,128)(2,1)} %get-tuple-element.292.nt_ref, f32[1024,128]{1,0:T(8,128)} %get-tuple-element.602.c_ref.refs_4_, ...), custom_call_target="tpu_custom_call" | custom-call | flops 3221225472 | bytes 13631488 | tf_op jit(solution)/shard_map/pallas_call | solution.py:657
  412.4 7.6 %shard_map.346 = (bf16[8,3,64,256]{3,2,1,0:T(8,128)(2,1)}, bf16[8,3,64,256]{3,2,1,0:T(8,128)(2,1)}, bf16[1024,768]{1,0:T(8,128)(2,1)}, f32[8,768]{1,0:T(8,128)}) custom-call(s32[16]{0:T(128)} %pad_add_fusion.t_ref, bf16[1024,1024]{1,0:T(8,128)(2,1)} %get-tuple-element.292.nt_ref, f32[1024,128]{1,0:T(8,128)} %get-tuple-element.602.c_ref.refs_4_, ...), custom_call_target="tpu_custom_call" | custom-call | flops 1610612736 | bytes 7864320 | tf_op jit(solution)/shard_map/pallas_call | solution.py:657
  422.5 24.3 %shard_map.347 = (bf16[1024,256]{1,0:T(8,128)(2,1)}, bf16[2,1024,256]{2,1,0:T(8,128)(2,1)}, bf16[2,1024,256]{2,1,0:T(8,128)(2,1)}) custom-call(bf16[1024,512]{1,0:T(8,128)(2,1)} %get-tuple-element.482.refs_0_, bf16[1024,256]{1,0:T(8,128)(2,1)} %convolution_convert_fusion.6.refs_1_, bf16[1024,256]{1,0:T(8,128)(2,1)} %get-tuple-element.484.refs_5_.refs_2_, ...), custom_call_target="tpu_custom_call" | custom-call | flops 21474836480 | bytes 6291456 | tf_op jit(solution)/shard_map/pallas_call | solution.py:305
  449.7 7.4 %shard_map.348.refs_2_ = f32[1024,1024]{1,0:T(8,128)} custom-call(bf16[16,4,64,512]{3,2,1,0:T(8,128)(2,1)} %bitcast.152, bf16[1024,1536]{1,0:T(8,128)(2,1)} %get-tuple-element.506.refs_1_), custom_call_target="tpu_custom_call" | custom-call | flops 3221225472 | bytes 10485760 | tf_op jit(solution)/shard_map/pallas_call | solution.py:574
  458.0 7.9 %shard_map.349 = (bf16[8,3,64,256]{3,2,1,0:T(8,128)(2,1)}, bf16[8,3,64,256]{3,2,1,0:T(8,128)(2,1)}, bf16[1024,768]{1,0:T(8,128)(2,1)}, f32[8,768]{1,0:T(8,128)}) custom-call(s32[16]{0:T(128)} %pad_add_fusion.t_ref, bf16[1024,1024]{1,0:T(8,128)(2,1)} %get-tuple-element.292.nt_ref, f32[1024,128]{1,0:T(8,128)} %get-tuple-element.602.c_ref.refs_4_, ...), custom_call_target="tpu_custom_call" | custom-call | flops 1610612736 | bytes 7864320 | tf_op jit(solution)/shard_map/pallas_call | solution.py:657
  466.0 2.3 collective-permute-done.35
  469.7 2.7 collective-permute-start.37
  472.4 1.9 collective-permute-start.39
  474.3 5.7 %shard_map.350.part_ref = f32[1024,1024]{1,0:T(8,128)} custom-call(bf16[1,3,1024,512]{3,2,1,0:T(8,128)(2,1)} %bitcast.132, bf16[1024,768]{1,0:T(8,128)(2,1)} %get-tuple-element.521.refs_1_, f32[1024,1024]{1,0:T(8,128)} %shard_map.348.refs_2_), custom_call_target="tpu_custom_call" | custom-call | flops 1610612736 | bytes 7340032 | tf_op jit(solution)/shard_map/pallas_call | solution.py:574
  479.9 2.2 collective-permute-done.37
  482.1 3.9 collective-permute-done.39
  489.0 9.0 %shard_map.351 = (bf16[1024,1024]{1,0:T(8,128)(2,1)}, f32[8,1024]{1,0:T(8,128)}) custom-call(bf16[1024,1024]{1,0:T(8,128)(2,1)} %get-tuple-element.322.refs_0_.x_ref, bf16[1024,1024]{1,0:T(8,128)(2,1)} %get-tuple-element.369.g_ref, f32[1,1024]{1,0:T(1,128)} %bitcast.156, f32[1024,1024]{1,0:T(8,128)} %shard_map.350.part_ref, ...), custom_call_target="tpu_custom_call" | custom-call | flops 1610612736 | bytes 13631488 | tf_op jit(solution)/shard_map/pallas_call | solution.py:594
  499.6 1.9 collective-permute-start.42
  503.6 3.3 broadcast_select_fusion.1
  506.9 2.0 collective-permute-start.48
  510.5 1.8 collective-permute-done.41
  512.9 2.4 collective-permute-start.44
  515.3 2.0 collective-permute-start.46
  518.4 4.7 collective-permute-done.44
  523.1 4.4 convert_element_type.83
  527.5 4.4 convert_element_type.84
  532.0 2.6 collective-permute-start.47
  537.4 3.0 collective-permute-done.52
  542.7 2.6 collective-permute-done.53
  551.1 5.5 shard_map.352
  (335 shorter events, 89.8 us)
Async XLA Ops:
  7.3 78.7 %all-gather.15.cloned.1.call-start = ((), (), s32[]{:S(2)}) async-start(), calls=%async_computation.2 | async-start | bytes 4456448 | tf_op jit(solution)/shard_map/all_gather | solution.py:1032
  9.1 9.3 %collective-permute-start.3 = (bf16[4,64,512]{2,1,0:T(8,128)(2,1)S(1)}, bf16[4,64,512]{2,1,0:T(8,128)(2,1)S(1)}, u32[]{:S(2)}, u32[]{:S(2)}) collective-permute-start(bf16[4,64,512]{2,1,0:T(8,128)(2,1)S(1)} %pad_maximum_fusion.2), channel_id=1, source_target_pairs={{0,1},{1,0},{2,3},{3,2},{4,5},{5,4},{6,7},{7,6},{8,9},{9,8},{10,11... | collective-permute-start | bytes 786440 | tf_op jit(solution)/shard_map/ppermute | solution.py:771
  19.2 144.0 %all-gather.11.cloned.1.call-start = ((), (), s32[]{:S(2)}) async-start(), calls=%async_computation | async-start | bytes 4456448 | tf_op jit(solution)/shard_map/all_gather | solution.py:823
  19.2 10.4 %collective-permute-start = (bf16[1024,1024]{1,0:T(8,128)(2,1)}, bf16[1024,1024]{1,0:T(8,128)(2,1)S(1)}, u32[]{:S(2)}, u32[]{:S(2)}) collective-permute-start(bf16[1024,1024]{1,0:T(8,128)(2,1)} %x_ref.1), channel_id=1, source_target_pairs={{1,2},{2,1},{5,6},{6,5},{9,10},{10,9},{13,14},{14,13},{17,18},{18,... | collective-permute-start | bytes 6291464 | tf_op jit(solution)/shard_map/ppermute | solution.py:771
  36.8 29.5 %collective-permute-start.1 = (bf16[64,2048]{1,0:T(8,128)(2,1)S(1)}, bf16[64,2048]{1,0:T(8,128)(2,1)S(1)}, u32[]{:S(2)}, u32[]{:S(2)}) collective-permute-start(bf16[64,2048]{1,0:T(8,128)(2,1)S(1)} %constant_dynamic-slice_fusion.4), channel_id=1, source_target_pairs={{0,1},{1,0},{2,3},{3,2},{4,5},{5,4},{6,7},{7,6},{8,9},{9,8},{10,11... | collective-permute-start | bytes 786440 | tf_op jit(solution)/shard_map/ppermute | solution.py:771
  55.7 12.2 %collective-permute-start.2 = (bf16[128,1024]{1,0:T(8,128)(2,1)S(1)}, bf16[128,1024]{1,0:T(8,128)(2,1)S(1)}, u32[]{:S(2)}, u32[]{:S(2)}) collective-permute-start(bf16[128,1024]{1,0:T(8,128)(2,1)S(1)} %constant_dynamic-slice_fusion.3), channel_id=1, source_target_pairs={{0,1},{1,0},{2,3},{3,2},{4,5},{5,4},{6,7},{7,6},{8,9},{9,8},{10,11... | collective-permute-start | bytes 786440 | tf_op jit(solution)/shard_map/ppermute | solution.py:771
  67.9 108.5 %all-gather.13.cloned.1.call-start = ((), (), s32[]{:S(2)}) async-start(), calls=%async_computation.1 | async-start | bytes 4456448 | tf_op jit(solution)/shard_map/all_gather | solution.py:823
  68.0 5.4 collective-permute-start.4
  68.7 351.4 %all-gather.17.cloned.1.call-start = ((), (), s32[]{:S(2)}) async-start(), calls=%async_computation.3 | async-start | bytes 4456448 | tf_op jit(solution)/shard_map/all_gather | solution.py:823
  69.0 3.7 collective-permute-start.5
  96.7 23.4 %collective-permute-start.6 = (bf16[1024,1024]{1,0:T(8,128)(2,1)}, bf16[1024,1024]{1,0:T(8,128)(2,1)}, u32[]{:S(2)}, u32[]{:S(2)}) collective-permute-start(bf16[1024,1024]{1,0:T(8,128)(2,1)} %get-tuple-element.416.refs_1_.refs_3_.refs_7_.refs_9_), channel_id=1, source_target_pairs={{0,2},{1,3},{2,0},{3,1},{4,6},{5,7},{6,4},{7,5},{8,10},{9,11},{10,... | collective-permute-start | bytes 6291464 | tf_op jit(solution)/shard_map/ppermute | solution.py:771
  105.0 86.6 %collective-permute-start.7 = (bf16[1024,1024]{1,0:T(8,128)(2,1)S(1)}, bf16[1024,1024]{1,0:T(8,128)(2,1)}, u32[]{:S(2)}, u32[]{:S(2)}) collective-permute-start(bf16[1024,1024]{1,0:T(8,128)(2,1)S(1)} %copy-done.12), channel_id=1, source_target_pairs={{1,2},{2,1},{5,6},{6,5},{9,10},{10,9},{13,14},{14,13},{17,18},{18,... | collective-permute-start | bytes 6291464 | tf_op jit(solution)/shard_map/ppermute | solution.py:771
  207.9 11.2 %collective-permute-start.8 = (bf16[8,128,1024]{2,1,0:T(8,128)(2,1)}, bf16[8,128,1024]{2,1,0:T(8,128)(2,1)S(1)}, u32[]{:S(2)}, u32[]{:S(2)}) collective-permute-start(bf16[8,128,1024]{2,1,0:T(8,128)(2,1)} %dynamic-slice_bitcast_fusion.3), channel_id=1, source_target_pairs={{0,2},{1,3},{2,0},{3,1},{4,6},{5,7},{6,4},{7,5},{8,10},{9,11},{10,... | collective-permute-start | bytes 6291464 | tf_op jit(solution)/shard_map/ppermute | solution.py:771
  208.8 10.4 %collective-permute-start.9 = (bf16[8,128,1024]{2,1,0:T(8,128)(2,1)}, bf16[8,128,1024]{2,1,0:T(8,128)(2,1)}, u32[]{:S(2)}, u32[]{:S(2)}) collective-permute-start(bf16[8,128,1024]{2,1,0:T(8,128)(2,1)} %dynamic-slice_bitcast_fusion.2), channel_id=1, source_target_pairs={{0,2},{1,3},{2,0},{3,1},{4,6},{5,7},{6,4},{7,5},{8,10},{9,11},{10,... | collective-permute-start | bytes 6291464 | tf_op jit(solution)/shard_map/ppermute | solution.py:771
  227.0 26.2 %collective-permute-start.10 = (bf16[2,4,128,1024]{3,2,1,0:T(8,128)(2,1)}, bf16[2,4,128,1024]{3,2,1,0:T(8,128)(2,1)S(1)}, u32[]{:S(2)}, u32[]{:S(2)}) collective-permute-start(bf16[2,4,128,1024]{3,2,1,0:T(8,128)(2,1)} %get-tuple-element.352), channel_id=1, source_target_pairs={{0,1},{1,0},{2,6},{3,7},{4,5},{5,4},{6,2},{7,3},{8,9},{9,8},{10,14... | collective-permute-start | bytes 6291464 | tf_op jit(solution)/shard_map/ppermute | solution.py:771
  256.5 20.6 %collective-permute-start.11 = (bf16[8,64,2048]{2,1,0:T(8,128)(2,1)}, bf16[8,64,2048]{2,1,0:T(8,128)(2,1)S(1)}, u32[]{:S(2)}, u32[]{:S(2)}) collective-permute-start(bf16[8,64,2048]{2,1,0:T(8,128)(2,1)} %dynamic-slice_bitcast_fusion.1), channel_id=1, source_target_pairs={{0,2},{1,3},{2,0},{3,1},{4,6},{5,7},{6,4},{7,5},{8,10},{9,11},{10,... | collective-permute-start | bytes 6291464 | tf_op jit(solution)/shard_map/ppermute | solution.py:771
  256.5 20.6 %collective-permute-start.12 = (bf16[8,64,2048]{2,1,0:T(8,128)(2,1)S(1)}, bf16[8,64,2048]{2,1,0:T(8,128)(2,1)S(1)}, u32[]{:S(2)}, u32[]{:S(2)}) collective-permute-start(bf16[8,64,2048]{2,1,0:T(8,128)(2,1)S(1)} %dynamic-slice_bitcast_fusion), channel_id=1, source_target_pairs={{0,2},{1,3},{2,0},{3,1},{4,6},{5,7},{6,4},{7,5},{8,10},{9,11},{10,... | collective-permute-start | bytes 6291464 | tf_op jit(solution)/shard_map/ppermute | solution.py:771
  257.0 20.1 %collective-permute-start.13 = (bf16[4,128,1024]{2,1,0:T(8,128)(2,1)}, bf16[4,128,1024]{2,1,0:T(8,128)(2,1)}, u32[]{:S(2)}, u32[]{:S(2)}) collective-permute-start(bf16[4,128,1024]{2,1,0:T(8,128)(2,1)} %bitcast_add_fusion.3), channel_id=1, source_target_pairs={{0,4},{1,5},{2,3},{3,2},{4,0},{5,1},{6,7},{7,6},{8,12},{9,13},{10,... | collective-permute-start | bytes 3145736 | tf_op jit(solution)/shard_map/ppermute | solution.py:771
  257.6 42.1 %collective-permute-start.15 = (bf16[1024,1024]{1,0:T(8,128)(2,1)}, bf16[1024,1024]{1,0:T(8,128)(2,1)}, u32[]{:S(2)}, u32[]{:S(2)}) collective-permute-start(bf16[1024,1024]{1,0:T(8,128)(2,1)} %shard_map.335), channel_id=1, source_target_pairs={{1,2},{2,1},{5,6},{6,5},{9,10},{10,9},{13,14},{14,13},{17,18},{18,... | collective-permute-start | bytes 6291464 | tf_op jit(solution)/shard_map/ppermute | solution.py:771
  281.6 18.0 %collective-permute-start.14 = (bf16[2,128,1024]{2,1,0:T(8,128)(2,1)}, bf16[2,128,1024]{2,1,0:T(8,128)(2,1)S(1)}, u32[]{:S(2)}, u32[]{:S(2)}) collective-permute-start(bf16[2,128,1024]{2,1,0:T(8,128)(2,1)} %slice.253), channel_id=1, source_target_pairs={{0,8},{1,9},{2,10},{3,11},{4,12},{5,13},{6,14},{7,15},{8,0},{9,1},... | collective-permute-start | bytes 1572872 | tf_op jit(solution)/shard_map/ppermute | solution.py:771
  300.6 28.3 %collective-permute-start.16 = (bf16[2,4,64,2048]{3,2,1,0:T(8,128)(2,1)}, bf16[2,4,64,2048]{3,2,1,0:T(8,128)(2,1)S(1)}, u32[]{:S(2)}, u32[]{:S(2)}) collective-permute-start(bf16[2,4,64,2048]{3,2,1,0:T(8,128)(2,1)} %get-tuple-element.398), channel_id=1, source_target_pairs={{0,1},{1,0},{2,6},{3,7},{4,5},{5,4},{6,2},{7,3},{8,9},{9,8},{10,14... | collective-permute-start | bytes 6291464 | tf_op jit(solution)/shard_map/ppermute | solution.py:771
  303.0 25.8 %collective-permute-start.18 = (bf16[8,32,1024]{2,1,0:T(8,128)(2,1)S(1)}, bf16[8,32,1024]{2,1,0:T(8,128)(2,1)S(1)}, u32[]{:S(2)}, u32[]{:S(2)}) collective-permute-start(bf16[8,32,1024]{2,1,0:T(8,128)(2,1)S(1)} %dynamic-slice_bitcast_fusion.5), channel_id=1, source_target_pairs={{0,2},{1,3},{2,0},{3,1},{4,6},{5,7},{6,4},{7,5},{8,10},{9,11},{10,... | collective-permute-start | bytes 1572872 | tf_op jit(solution)/shard_map/ppermute | solution.py:771
  303.3 25.6 %collective-permute-start.19 = (bf16[8,32,1024]{2,1,0:T(8,128)(2,1)S(1)}, bf16[8,32,1024]{2,1,0:T(8,128)(2,1)S(1)}, u32[]{:S(2)}, u32[]{:S(2)}) collective-permute-start(bf16[8,32,1024]{2,1,0:T(8,128)(2,1)S(1)} %dynamic-slice_bitcast_fusion.4), channel_id=1, source_target_pairs={{0,2},{1,3},{2,0},{3,1},{4,6},{5,7},{6,4},{7,5},{8,10},{9,11},{10,... | collective-permute-start | bytes 1572872 | tf_op jit(solution)/shard_map/ppermute | solution.py:771
  303.6 25.2 %collective-permute-start.17 = (bf16[1,128,1024]{2,1,0:T(8,128)(2,1)S(1)}, bf16[1,128,1024]{2,1,0:T(8,128)(2,1)S(1)}, u32[]{:S(2)}, u32[]{:S(2)}) collective-permute-start(bf16[1,128,1024]{2,1,0:T(8,128)(2,1)S(1)} %slice.256), channel_id=1, source_target_pairs={{0,16},{1,17},{2,18},{3,19},{4,20},{5,21},{6,22},{7,23},{8,24},{9,... | collective-permute-start | bytes 786440 | tf_op jit(solution)/shard_map/ppermute | solution.py:771
  334.4 26.2 %collective-permute-start.20 = (bf16[2,1024,256]{2,1,0:T(8,128)(2,1)}, bf16[2,1024,256]{2,1,0:T(8,128)(2,1)}, u32[]{:S(2)}, u32[]{:S(2)}) collective-permute-start(bf16[2,1024,256]{2,1,0:T(8,128)(2,1)} %get-tuple-element.421), channel_id=1, source_target_pairs={{0,2},{1,3},{2,0},{3,1},{4,6},{5,7},{6,4},{7,5},{8,10},{9,11},{10,... | collective-permute-start | bytes 3145736 | tf_op jit(solution)/shard_map/ppermute | solution.py:771
  334.5 26.1 %collective-permute-start.21 = (bf16[4,64,2048]{2,1,0:T(8,128)(2,1)S(1)}, bf16[4,64,2048]{2,1,0:T(8,128)(2,1)}, u32[]{:S(2)}, u32[]{:S(2)}) collective-permute-start(bf16[4,64,2048]{2,1,0:T(8,128)(2,1)S(1)} %bitcast_add_fusion.1), channel_id=1, source_target_pairs={{0,4},{1,5},{2,3},{3,2},{4,0},{5,1},{6,7},{7,6},{8,12},{9,13},{10,... | collective-permute-start | bytes 3145736 | tf_op jit(solution)/shard_map/ppermute | solution.py:771
  335.9 24.7 %collective-permute-start.22 = (bf16[2,4,32,1024]{3,2,1,0:T(8,128)(2,1)}, bf16[2,4,32,1024]{3,2,1,0:T(8,128)(2,1)}, u32[]{:S(2)}, u32[]{:S(2)}) collective-permute-start(bf16[2,4,32,1024]{3,2,1,0:T(8,128)(2,1)} %get-tuple-element.423), channel_id=1, source_target_pairs={{0,1},{1,0},{2,6},{3,7},{4,5},{5,4},{6,2},{7,3},{8,9},{9,8},{10,14... | collective-permute-start | bytes 1572872 | tf_op jit(solution)/shard_map/ppermute | solution.py:771
  335.9 150.1 %all-gather.19.cloned.1.call-start = ((), (), s32[]{:S(2)}) async-start(), calls=%async_computation.4 | async-start | bytes 4456448 | tf_op jit(solution)/shard_map/all_gather | solution.py:823
  336.0 24.6 %copy-start.28 = (bf16[4,64,2048]{2,1,0:T(8,128)(2,1)S(1)}, bf16[4,64,2048]{2,1,0:T(8,128)(2,1)}, u32[]{:S(2)}) copy-start(bf16[4,64,2048]{2,1,0:T(8,128)(2,1)} %get-tuple-element.425) | copy-start | bytes 3145732
  363.1 31.1 %copy-start.37 = (bf16[4,32,1024]{2,1,0:T(8,128)(2,1)S(1)}, bf16[4,32,1024]{2,1,0:T(8,128)(2,1)}, u32[]{:S(2)}) copy-start(bf16[4,32,1024]{2,1,0:T(8,128)(2,1)} %get-tuple-element.451) | copy-start | bytes 786436
  363.2 31.1 %collective-permute-start.23 = (bf16[2,1024,256]{2,1,0:T(8,128)(2,1)S(1)}, bf16[2,1024,256]{2,1,0:T(8,128)(2,1)S(1)}, u32[]{:S(2)}, u32[]{:S(2)}) collective-permute-start(bf16[2,1024,256]{2,1,0:T(8,128)(2,1)S(1)} %copy-done.57), channel_id=1, source_target_pairs={{0,2},{1,3},{2,0},{3,1},{4,6},{5,7},{6,4},{7,5},{8,10},{9,11},{10,... | collective-permute-start | bytes 3145736 | tf_op jit(solution)/shard_map/ppermute | solution.py:771
  363.4 30.9 %collective-permute-start.24 = (bf16[2,64,2048]{2,1,0:T(8,128)(2,1)S(1)}, bf16[2,64,2048]{2,1,0:T(8,128)(2,1)S(1)}, u32[]{:S(2)}, u32[]{:S(2)}) collective-permute-start(bf16[2,64,2048]{2,1,0:T(8,128)(2,1)S(1)} %slice.257), channel_id=1, source_target_pairs={{0,8},{1,9},{2,10},{3,11},{4,12},{5,13},{6,14},{7,15},{8,0},{9,1},... | collective-permute-start | bytes 1572872 | tf_op jit(solution)/shard_map/ppermute | solution.py:771
  364.3 25.4 %collective-permute-start.25 = (bf16[4,32,1024]{2,1,0:T(8,128)(2,1)S(1)}, bf16[4,32,1024]{2,1,0:T(8,128)(2,1)S(1)}, u32[]{:S(2)}, u32[]{:S(2)}) collective-permute-start(bf16[4,32,1024]{2,1,0:T(8,128)(2,1)S(1)} %bitcast_add_fusion.5), channel_id=1, source_target_pairs={{0,4},{1,5},{2,3},{3,2},{4,0},{5,1},{6,7},{7,6},{8,12},{9,13},{10,... | collective-permute-start | bytes 786440 | tf_op jit(solution)/shard_map/ppermute | solution.py:771
  395.6 15.0 %collective-permute-start.26 = (bf16[2,1024,256]{2,1,0:T(8,128)(2,1)S(1)}, bf16[2,1024,256]{2,1,0:T(8,128)(2,1)S(1)}, u32[]{:S(2)}, u32[]{:S(2)}) collective-permute-start(bf16[2,1024,256]{2,1,0:T(8,128)(2,1)S(1)} %copy-done.56), channel_id=1, source_target_pairs={{0,2},{1,3},{2,0},{3,1},{4,6},{5,7},{6,4},{7,5},{8,10},{9,11},{10,... | collective-permute-start | bytes 3145736 | tf_op jit(solution)/shard_map/ppermute | solution.py:771
  396.3 14.3 %collective-permute-start.27 = (bf16[1,64,2048]{2,1,0:T(8,128)(2,1)S(1)}, bf16[1,64,2048]{2,1,0:T(8,128)(2,1)S(1)}, u32[]{:S(2)}, u32[]{:S(2)}) collective-permute-start(bf16[1,64,2048]{2,1,0:T(8,128)(2,1)S(1)} %slice.259), channel_id=1, source_target_pairs={{0,16},{1,17},{2,18},{3,19},{4,20},{5,21},{6,22},{7,23},{8,24},{9,... | collective-permute-start | bytes 786440 | tf_op jit(solution)/shard_map/ppermute | solution.py:771
  396.3 13.0 %collective-permute-start.28 = (bf16[2,32,1024]{2,1,0:T(8,128)(2,1)S(1)}, bf16[2,32,1024]{2,1,0:T(8,128)(2,1)S(1)}, u32[]{:S(2)}, u32[]{:S(2)}) collective-permute-start(bf16[2,32,1024]{2,1,0:T(8,128)(2,1)S(1)} %slice.260), channel_id=1, source_target_pairs={{0,8},{1,9},{2,10},{3,11},{4,12},{5,13},{6,14},{7,15},{8,0},{9,1},... | collective-permute-start | bytes 393224 | tf_op jit(solution)/shard_map/ppermute | solution.py:771
  411.6 8.4 %collective-permute-start.29 = (bf16[8,3,64,512]{3,2,1,0:T(8,128)(2,1)}, bf16[8,3,64,512]{3,2,1,0:T(8,128)(2,1)S(1)}, u32[]{:S(2)}, u32[]{:S(2)}) collective-permute-start(bf16[8,3,64,512]{3,2,1,0:T(8,128)(2,1)} %get-tuple-element.476), channel_id=1, source_target_pairs={{0,2},{1,3},{2,0},{3,1},{4,6},{5,7},{6,4},{7,5},{8,10},{9,11},{10,... | collective-permute-start | bytes 4718600 | tf_op jit(solution)/shard_map/ppermute | solution.py:771
  411.7 8.3 %collective-permute-start.30 = (bf16[1,32,1024]{2,1,0:T(8,128)(2,1)S(1)}, bf16[1,32,1024]{2,1,0:T(8,128)(2,1)S(1)}, u32[]{:S(2)}, u32[]{:S(2)}) collective-permute-start(bf16[1,32,1024]{2,1,0:T(8,128)(2,1)S(1)} %slice.262), channel_id=1, source_target_pairs={{0,16},{1,17},{2,18},{3,19},{4,20},{5,21},{6,22},{7,23},{8,24},{9,... | collective-permute-start | bytes 196616 | tf_op jit(solution)/shard_map/ppermute | solution.py:771
  420.1 129.6 %all-gather.21.cloned.1.call-start = ((), (), s32[]{:S(2)}) async-start(), calls=%async_computation.5 | async-start | bytes 2785280 | tf_op jit(solution)/shard_map/all_gather | solution.py:1164
  420.3 26.6 %copy-start.30 = (bf16[8,3,64,256]{3,2,1,0:T(8,128)(2,1)S(1)}, bf16[8,3,64,256]{3,2,1,0:T(8,128)(2,1)}, u32[]{:S(2)}) copy-start(bf16[8,3,64,256]{3,2,1,0:T(8,128)(2,1)} %get-tuple-element.502) | copy-start | bytes 2359300
  420.3 26.5 %collective-permute-start.32 = (bf16[8,3,64,256]{3,2,1,0:T(8,128)(2,1)}, bf16[8,3,64,256]{3,2,1,0:T(8,128)(2,1)S(1)}, u32[]{:S(2)}, u32[]{:S(2)}) collective-permute-start(bf16[8,3,64,256]{3,2,1,0:T(8,128)(2,1)} %get-tuple-element.491), channel_id=1, source_target_pairs={{0,2},{1,3},{2,0},{3,1},{4,6},{5,7},{6,4},{7,5},{8,10},{9,11},{10,... | collective-permute-start | bytes 2359304 | tf_op jit(solution)/shard_map/ppermute | solution.py:771
  420.8 26.1 %collective-permute-start.31 = (bf16[8,3,64,256]{3,2,1,0:T(8,128)(2,1)S(1)}, bf16[8,3,64,256]{3,2,1,0:T(8,128)(2,1)S(1)}, u32[]{:S(2)}, u32[]{:S(2)}) collective-permute-start(bf16[8,3,64,256]{3,2,1,0:T(8,128)(2,1)S(1)} %get-tuple-element.481), channel_id=1, source_target_pairs={{0,1},{1,0},{2,3},{3,2},{4,5},{5,4},{6,7},{7,6},{8,9},{9,8},{10,11... | collective-permute-start | bytes 2359304 | tf_op jit(solution)/shard_map/ppermute | solution.py:771
  448.4 8.7 %collective-permute-start.33 = (bf16[2,1024,256]{2,1,0:T(8,128)(2,1)S(1)}, bf16[2,1024,256]{2,1,0:T(8,128)(2,1)S(1)}, u32[]{:S(2)}, u32[]{:S(2)}) collective-permute-start(bf16[2,1024,256]{2,1,0:T(8,128)(2,1)S(1)} %copy-done.58), channel_id=1, source_target_pairs={{0,2},{1,3},{2,0},{3,1},{4,6},{5,7},{6,4},{7,5},{8,10},{9,11},{10,... | collective-permute-start | bytes 3145736 | tf_op jit(solution)/shard_map/ppermute | solution.py:771
  448.4 20.0 %collective-permute-start.35 = (bf16[8,3,64,256]{3,2,1,0:T(8,128)(2,1)S(1)}, bf16[8,3,64,256]{3,2,1,0:T(8,128)(2,1)S(1)}, u32[]{:S(2)}, u32[]{:S(2)}) collective-permute-start(bf16[8,3,64,256]{3,2,1,0:T(8,128)(2,1)S(1)} %get-tuple-element.514), channel_id=1, source_target_pairs={{0,1},{1,0},{2,3},{3,2},{4,5},{5,4},{6,7},{7,6},{8,9},{9,8},{10,11... | collective-permute-start | bytes 2359304 | tf_op jit(solution)/shard_map/ppermute | solution.py:771
  448.4 20.2 %collective-permute-start.34 = (bf16[4,3,64,256]{3,2,1,0:T(8,128)(2,1)S(1)}, bf16[4,3,64,256]{3,2,1,0:T(8,128)(2,1)S(1)}, u32[]{:S(2)}, u32[]{:S(2)}) collective-permute-start(bf16[4,3,64,256]{3,2,1,0:T(8,128)(2,1)S(1)} %slice.264), channel_id=1, source_target_pairs={{0,4},{1,5},{2,6},{3,7},{4,0},{5,1},{6,2},{7,3},{8,12},{9,13},{10,... | collective-permute-start | bytes 1179656 | tf_op jit(solution)/shard_map/ppermute | solution.py:771
  468.7 17.3 %collective-permute-start.36 = (bf16[8,3,64,256]{3,2,1,0:T(8,128)(2,1)}, bf16[8,3,64,256]{3,2,1,0:T(8,128)(2,1)S(1)}, u32[]{:S(2)}, u32[]{:S(2)}) collective-permute-start(bf16[8,3,64,256]{3,2,1,0:T(8,128)(2,1)} %get-tuple-element.523), channel_id=1, source_target_pairs={{0,2},{1,3},{2,0},{3,1},{4,6},{5,7},{6,4},{7,5},{8,10},{9,11},{10,... | collective-permute-start | bytes 2359304 | tf_op jit(solution)/shard_map/ppermute | solution.py:771
  469.7 12.5 %collective-permute-start.37 = (bf16[1,3,64,256]{3,2,1,0:T(8,128)(2,1)S(1)}, bf16[1,3,64,256]{3,2,1,0:T(8,128)(2,1)S(1)}, u32[]{:S(2)}, u32[]{:S(2)}) collective-permute-start(bf16[1,3,64,256]{3,2,1,0:T(8,128)(2,1)S(1)} %get-tuple-element.524), channel_id=1, source_target_pairs={{0,16},{1,17},{2,18},{3,19},{4,20},{5,21},{6,22},{7,23},{8,24},{9,... | collective-permute-start | bytes 294920 | tf_op jit(solution)/shard_map/ppermute | solution.py:771
  472.4 9.7 %collective-permute-start.38 = (bf16[1,3,64,256]{3,2,1,0:T(8,128)(2,1)S(1)}, bf16[1,3,64,256]{3,2,1,0:T(8,128)(2,1)S(1)}, u32[]{:S(2)}, u32[]{:S(2)}) collective-permute-start(bf16[1,3,64,256]{3,2,1,0:T(8,128)(2,1)S(1)} %get-tuple-element.525), channel_id=1, source_target_pairs={{0,8},{1,9},{2,10},{3,11},{4,12},{5,13},{6,14},{7,15},{8,0},{9,1},... | collective-permute-start | bytes 294920 | tf_op jit(solution)/shard_map/ppermute | solution.py:771
  472.4 13.6 %collective-permute-start.39 = (bf16[1,3,64,256]{3,2,1,0:T(8,128)(2,1)S(1)}, bf16[1,3,64,256]{3,2,1,0:T(8,128)(2,1)S(1)}, u32[]{:S(2)}, u32[]{:S(2)}) collective-permute-start(bf16[1,3,64,256]{3,2,1,0:T(8,128)(2,1)S(1)} %get-tuple-element.526), channel_id=1, source_target_pairs={{0,24},{1,25},{2,26},{3,27},{4,28},{5,29},{6,30},{7,31},{8,16},{9,... | collective-permute-start | bytes 294920 | tf_op jit(solution)/shard_map/ppermute | solution.py:771
  486.9 11.1 %collective-permute-start.40 = (bf16[4,3,64,256]{3,2,1,0:T(8,128)(2,1)S(1)}, bf16[4,3,64,256]{3,2,1,0:T(8,128)(2,1)S(1)}, u32[]{:S(2)}, u32[]{:S(2)}) collective-permute-start(bf16[4,3,64,256]{3,2,1,0:T(8,128)(2,1)S(1)} %slice.271), channel_id=1, source_target_pairs={{0,4},{1,5},{2,6},{3,7},{4,0},{5,1},{6,2},{7,3},{8,12},{9,13},{10,... | collective-permute-start | bytes 1179656 | tf_op jit(solution)/shard_map/ppermute | solution.py:771
  498.1 14.1 %collective-permute-start.41 = (bf16[1,3,64,256]{3,2,1,0:T(8,128)(2,1)S(1)}, bf16[1,3,64,256]{3,2,1,0:T(8,128)(2,1)S(1)}, u32[]{:S(2)}, u32[]{:S(2)}) collective-permute-start(bf16[1,3,64,256]{3,2,1,0:T(8,128)(2,1)S(1)} %get-tuple-element.582), channel_id=1, source_target_pairs={{0,16},{1,17},{2,18},{3,19},{4,20},{5,21},{6,22},{7,23},{8,24},{9,... | collective-permute-start | bytes 294920 | tf_op jit(solution)/shard_map/ppermute | solution.py:771
  499.6 12.6 %collective-permute-start.42 = (bf16[1,3,64,256]{3,2,1,0:T(8,128)(2,1)S(1)}, bf16[1,3,64,256]{3,2,1,0:T(8,128)(2,1)S(1)}, u32[]{:S(2)}, u32[]{:S(2)}) collective-permute-start(bf16[1,3,64,256]{3,2,1,0:T(8,128)(2,1)S(1)} %get-tuple-element.580), channel_id=1, source_target_pairs={{0,8},{1,9},{2,10},{3,11},{4,12},{5,13},{6,14},{7,15},{8,0},{9,1},... | collective-permute-start | bytes 294920 | tf_op jit(solution)/shard_map/ppermute | solution.py:771
  501.5 10.7 %collective-permute-start.43 = (bf16[1,3,64,256]{3,2,1,0:T(8,128)(2,1)S(1)}, bf16[1,3,64,256]{3,2,1,0:T(8,128)(2,1)S(1)}, u32[]{:S(2)}, u32[]{:S(2)}) collective-permute-start(bf16[1,3,64,256]{3,2,1,0:T(8,128)(2,1)S(1)} %get-tuple-element.581), channel_id=1, source_target_pairs={{0,24},{1,25},{2,26},{3,27},{4,28},{5,29},{6,30},{7,31},{8,16},{9,... | collective-permute-start | bytes 294920 | tf_op jit(solution)/shard_map/ppermute | solution.py:771
  503.5 5.3 collective-permute-start.49
  506.9 41.2 %collective-permute-start.48 = (bf16[1024,1024]{1,0:T(8,128)(2,1)S(1)}, bf16[1024,1024]{1,0:T(8,128)(2,1)}, u32[]{:S(2)}, u32[]{:S(2)}) collective-permute-start(bf16[1024,1024]{1,0:T(8,128)(2,1)S(1)} %copy-done.13), channel_id=1, source_target_pairs={{1,2},{2,1},{5,6},{6,5},{9,10},{10,9},{13,14},{14,13},{17,18},{18,... | collective-permute-start | bytes 6291464 | tf_op jit(solution)/shard_map/ppermute | solution.py:771
  508.8 8.5 %collective-permute-start.50 = (f32[2,52,128]{2,1,0:T(8,128)S(1)}, f32[2,52,128]{2,1,0:T(8,128)S(1)}, u32[]{:S(2)}, u32[]{:S(2)}) collective-permute-start(f32[2,52,128]{2,1,0:T(8,128)S(1)} %fusion.16), channel_id=1, source_target_pairs={{0,4},{1,5},{2,6},{3,7},{4,0},{5,1},{6,2},{7,3},{8,12},{9,13},{10,... | collective-permute-start | bytes 159752 | tf_op jit(solution)/shard_map/ppermute | solution.py:771
  512.9 10.1 %collective-permute-start.44 = (bf16[1,3,64,256]{3,2,1,0:T(8,128)(2,1)S(1)}, bf16[1,3,64,256]{3,2,1,0:T(8,128)(2,1)S(1)}, u32[]{:S(2)}, u32[]{:S(2)}) collective-permute-start(bf16[1,3,64,256]{3,2,1,0:T(8,128)(2,1)S(1)} %get-tuple-element.571), channel_id=1, source_target_pairs={{0,16},{1,17},{2,18},{3,19},{4,20},{5,21},{6,22},{7,23},{8,24},{9,... | collective-permute-start | bytes 294920 | tf_op jit(solution)/shard_map/ppermute | solution.py:771
  515.3 16.7 %collective-permute-start.45 = (bf16[1,3,64,256]{3,2,1,0:T(8,128)(2,1)S(1)}, bf16[1,3,64,256]{3,2,1,0:T(8,128)(2,1)S(1)}, u32[]{:S(2)}, u32[]{:S(2)}) collective-permute-start(bf16[1,3,64,256]{3,2,1,0:T(8,128)(2,1)S(1)} %get-tuple-element.571), channel_id=1, source_target_pairs={{0,8},{1,9},{2,10},{3,11},{4,12},{5,13},{6,14},{7,15},{8,0},{9,1},... | collective-permute-start | bytes 294920 | tf_op jit(solution)/shard_map/ppermute | solution.py:771
  515.3 16.7 %collective-permute-start.46 = (bf16[1,3,64,256]{3,2,1,0:T(8,128)(2,1)S(1)}, bf16[1,3,64,256]{3,2,1,0:T(8,128)(2,1)S(1)}, u32[]{:S(2)}, u32[]{:S(2)}) collective-permute-start(bf16[1,3,64,256]{3,2,1,0:T(8,128)(2,1)S(1)} %get-tuple-element.571), channel_id=1, source_target_pairs={{0,24},{1,25},{2,26},{3,27},{4,28},{5,29},{6,30},{7,31},{8,16},{9,... | collective-permute-start | bytes 294920 | tf_op jit(solution)/shard_map/ppermute | solution.py:771
  517.3 17.9 %collective-permute-start.51 = (f32[2,52,128]{2,1,0:T(8,128)S(1)}, f32[2,52,128]{2,1,0:T(8,128)S(1)}, u32[]{:S(2)}, u32[]{:S(2)}) collective-permute-start(f32[2,52,128]{2,1,0:T(8,128)S(1)} %fusion.40), channel_id=1, source_target_pairs={{0,8},{1,9},{2,10},{3,11},{4,12},{5,13},{6,14},{7,15},{8,0},{9,1},... | collective-permute-start | bytes 159752 | tf_op jit(solution)/shard_map/ppermute | solution.py:771
  532.0 8.4 %collective-permute-start.47 = (bf16[4,3,64,256]{3,2,1,0:T(8,128)(2,1)S(1)}, bf16[4,3,64,256]{3,2,1,0:T(8,128)(2,1)S(1)}, u32[]{:S(2)}, u32[]{:S(2)}) collective-permute-start(bf16[4,3,64,256]{3,2,1,0:T(8,128)(2,1)S(1)} %pad_maximum_fusion.1), channel_id=1, source_target_pairs={{0,4},{1,5},{2,6},{3,7},{4,0},{5,1},{6,2},{7,3},{8,12},{9,13},{10,... | collective-permute-start | bytes 1179656 | tf_op jit(solution)/shard_map/ppermute | solution.py:771
  535.3 5.1 collective-permute-start.52
  541.4 5.7 %collective-permute-start.54 = (bf16[8,3,64,256]{3,2,1,0:T(8,128)(2,1)}, bf16[8,3,64,256]{3,2,1,0:T(8,128)(2,1)S(1)}, u32[]{:S(2)}, u32[]{:S(2)}) collective-permute-start(bf16[8,3,64,256]{3,2,1,0:T(8,128)(2,1)} %get-tuple-element.578), channel_id=1, source_target_pairs={{0,2},{1,3},{2,0},{3,1},{4,6},{5,7},{6,4},{7,5},{8,10},{9,11},{10,... | collective-permute-start | bytes 2359304 | tf_op jit(solution)/shard_map/ppermute | solution.py:771
  541.4 3.9 collective-permute-start.53
  (60 other events, 412.8 us)
Sparse Core Ops, SparseCore 0:
  19.3 53.5 all-gather.14
  75.0 50.0 all-gather.10
  127.2 49.0 all-gather.12
  336.0 58.8 all-gather.16
  420.2 65.1 all-gather.18
  488.1 49.7 all-gather.20

commit v8 on v7

--- a/solution.py
+++ b/solution.py
@@ -1184,8 +1184,12 @@
     block_out = move.stays(block_out, block_got)
     b_got, block_out = tie(b_got, block_out)
     total_b = jnp.concatenate([total_b, b_got])
-    total_b = jnp.concatenate([total_b, move.over_core(total_b)])
-    out_g = f32(unit_a[:, 3:].reshape(part, width))
+    (out_g, in_grad), (b_got,) = beside(
+        lambda u, rows, got: (f32(u[:, 3:].reshape(part, width)), move.stays(rows, got)),
+        (unit_a, in_grad, in_grad_got),
+        (move.over_core, total_b),
+    )
+    total_b = jnp.concatenate([total_b, b_got])
     qkv_g = jnp.transpose(widen(move.blocks, unit_a, total_b), (1, 0, 2))
     side = lambda a, b: jnp.concatenate([a.reshape(3, cols), b.reshape(3, cols)], axis=1).reshape(-1)
     vec, flat = move.reduce_vectors(
@@ -1195,7 +1199,7 @@
     )
     return (
         block_out,
-        move.stays(in_grad, in_grad_got),
+        in_grad,
         vec[0],
         vec[1],
         qkv_g,

time: 573 us -> 581 us (1.014)
  waiting for transfers between devices: 41.7 us -> 49.8 us
    ppermute x55, waiting for transfers between devices: 39.3 us -> 46.8 us  [move(): return lax.ppermute(x, ('dp', 'tensor'), pairs)]
    unnamed x132 -> x137, local copies, waits for them, and re-layouts: 17.8 us -> 19.6 us
  transfers between devices with their start and end apart: 61 -> 61, of which waited for: 15 -> 16; matrix products, arithmetic and copies ran while one was open for 13% -> 13% of each run, Pallas kernels for 55% -> 54%
where the time goes in v8:
time: 581 us; the launch traced here: 574 us
  Pallas kernels  328 us (56%)
  starting transfers between devices  69.6 us (12%)
  waiting for transfers between devices  49.8 us (9%)
  local copies, waits for them, and re-layouts  41.2 us (7%)
  other arithmetic  40.2 us (7%)
  matrix products  29.8 us (5%)
  between operations  15.6 us (3%)
    pallas_call x4, Pallas kernels, attend_back(): call(functools.partial(attend_back_kernel, sources=len(kvs), keys_at=1024...  97.8 us
    ppermute x55, starting transfers between devices, move(): return lax.ppermute(x, ('dp', 'tensor'), pairs)  68.9 us
    pallas_call x3, Pallas kernels, attend(): call(functools.partial(attend_kernel, sources=len(kvs), rows_at=min(512,...  48.9 us
    ppermute x55, waiting for transfers between devices, move(): return lax.ppermute(x, ('dp', 'tensor'), pairs)  46.8 us
    pallas_call x3, Pallas kernels, unit_grads(): pl.pallas_call(functools.partial(unit_kernel, chips=chips, parts=parts),...  25.8 us
    pallas_call x2, Pallas kernels, up_rows(): call(up_kernel, 2 * tokens * width * cols, 2 * (tokens * width + width *...  22.9 us
    pallas_call x2, Pallas kernels, qkv_rows(): call(functools.partial(qkv_kernel, q_steps=q_steps), 2 * tokens * width *...  21.3 us
    pallas_call x2, Pallas kernels, hidden_grads(): call(functools.partial(hidden_grad_kernel, skip=skip), 2 * tokens * width...  19.7 us
  transfers between devices with their start and end apart: 61, of which 16 were waited for; matrix products, arithmetic and copies ran while one was open for 13% of the time, Pallas kernels for 54%

profile of v8, /device:TPU:0, one launch (start us, length us, event | category | flops | bytes accessed | tf_op | source)
XLA Modules:
  0.0 574.3 jit_solution(15971234239961243207)
XLA Ops:
  9.1 3.0 collective-permute-start.3
  12.1 6.3 %collective-permute-done.3 = bf16[4,64,512]{2,1,0:T(8,128)(2,1)S(1)} collective-permute-done((bf16[4,64,512]{2,1,0:T(8,128)(2,1)S(1)}, bf16[4,64,512]{2,1,0:T(8,128)(2,1)S(1)}, u32[]{:S(2)}, u32[]{:S(2)}) %collective-permute-start.3) | collective-permute-done | bytes 262176 | tf_op jit(solution)/shard_map/ppermute | solution.py:771
  25.9 3.6 fusion.3
  30.9 5.8 %shard_map.326 = (bf16[1024,1024]{1,0:T(8,128)(2,1)}, bf16[1024,1024]{1,0:T(8,128)(2,1)}, bf16[1024,1024]{1,0:T(8,128)(2,1)}) custom-call(s32[1]{0:T(128)} %bitcast.stay_ref, bf16[1024,1024]{1,0:T(8,128)(2,1)} %x_ref.1, bf16[1024,1024]{1,0:T(8,128)(2,1)} %copy-done.17, f32[1,1024]{1,0:T(1,128)} %bitcast.155, f32[1,1024]{1,0:T(1,128)} %bitcast.159), custom_call_target="tpu_custom_call" | custom-call | flops 10485760 | bytes 10485760 | tf_op jit(solution)/shard_map/pallas_call | solution.py:96
  36.7 18.9 %collective-permute-start.1 = (bf16[64,2048]{1,0:T(8,128)(2,1)S(1)}, bf16[64,2048]{1,0:T(8,128)(2,1)S(1)}, u32[]{:S(2)}, u32[]{:S(2)}) collective-permute-start(bf16[64,2048]{1,0:T(8,128)(2,1)S(1)} %constant_dynamic-slice_fusion.4), channel_id=1, source_target_pairs={{0,1},{1,0},{2,3},{3,2},{4,5},{5,4},{6,7},{7,6},{8,9},{9,8},{10,11... | collective-permute-start | bytes 786440 | tf_op jit(solution)/shard_map/ppermute | solution.py:771
  55.7 10.6 %shard_map.327 = (bf16[1024,512]{1,0:T(8,128)(2,1)}, bf16[1024,1024]{1,0:T(8,128)(2,1)}) custom-call(bf16[1024,1024]{1,0:T(8,128)(2,1)} %get-tuple-element.301.n_ref, bf16[1,3,1024,512]{3,2,1,0:T(8,128)(2,1)} %bitcast.131, f32[1,1536]{1,0:T(1,128)} %bitcast.164, f32[1024,128]{1,0:T(8,128)} %get-tuple-element.616.c_ref.refs_4_, ...), custom_call_target="tpu_custom_call" | custom-call | flops 3221225472 | bytes 8388608 | tf_op jit(solution)/shard_map/pallas_call | solution.py:145
  70.4 2.6 collective-permute-done.5
  73.5 12.7 %shard_map.328 = (bf16[1024,256]{1,0:T(8,128)(2,1)}, f32[2,2,1024]{2,1,0:T(2,128)}) custom-call(bf16[1024,512]{1,0:T(8,128)(2,1)} %get-tuple-element.489.refs_0_, bf16[1024,1024]{1,0:T(8,128)(2,1)} %get-tuple-element.493.refs_1_.refs_3_.refs_7_.refs_9_, bf16[1024,1024]{1,0:T(8,128)(2,1)} %collective-permute-done.4.refs_2_.refs_4_.refs_8_.refs_10_, ...), custom_call_target="tpu_custom_call" | custom-call | flops 8589934592 | bytes 3145728 | tf_op jit(solution)/shard_map/pallas_call | solution.py:213
  86.3 10.7 %shard_map.329 = (bf16[1024,512]{1,0:T(8,128)(2,1)}, bf16[1024,1024]{1,0:T(8,128)(2,1)}) custom-call(bf16[1024,1024]{1,0:T(8,128)(2,1)} %get-tuple-element.301.n_ref, bf16[16,4,64,512]{3,2,1,0:T(8,128)(2,1)} %bitcast.150, f32[1,1536]{1,0:T(1,128)} %reshape.232.b_ref, f32[1024,128]{1,0:T(8,128)} %get-tuple-element.616.c_ref.refs_4_, ...), custom_call_target="tpu_custom_call" | custom-call | flops 3221225472 | bytes 8388608 | tf_op jit(solution)/shard_map/pallas_call | solution.py:145
  105.3 2.1 collective-permute-start.7
  107.4 12.7 %shard_map.330 = (bf16[1024,256]{1,0:T(8,128)(2,1)}, f32[2,2,1024]{2,1,0:T(2,128)}) custom-call(bf16[1024,512]{1,0:T(8,128)(2,1)} %get-tuple-element.489.refs_0_, bf16[1024,1024]{1,0:T(8,128)(2,1)} %get-tuple-element.493.refs_1_.refs_3_.refs_7_.refs_9_, bf16[1024,1024]{1,0:T(8,128)(2,1)} %collective-permute-done.4.refs_2_.refs_4_.refs_8_.refs_10_, ...), custom_call_target="tpu_custom_call" | custom-call | flops 8589934592 | bytes 3145728 | tf_op jit(solution)/shard_map/pallas_call | solution.py:213
  120.1 23.5 %shard_map.331 = (bf16[1024,512]{1,0:T(8,128)(2,1)}, f32[4,2,1024]{2,1,0:T(2,128)}) custom-call(bf16[1024,512]{1,0:T(8,128)(2,1)} %get-tuple-element.419.refs_0_, bf16[1024,1024]{1,0:T(8,128)(2,1)} %get-tuple-element.423.refs_1_.refs_3_.refs_7_.refs_9_, bf16[1024,1024]{1,0:T(8,128)(2,1)} %collective-permute-done.6.refs_2_.refs_4_.refs_8_.refs_10_, ...), custom_call_target="tpu_custom_call" | custom-call | flops 17179869184 | bytes 6291456 | tf_op jit(solution)/shard_map/pallas_call | solution.py:213
  143.6 7.9 %shard_map.332 = (f32[1024,1024]{1,0:T(8,128)}, bf16[1024,1024]{1,0:T(8,128)(2,1)}, bf16[1024,1024]{1,0:T(8,128)(2,1)}) custom-call(bf16[1024,1024]{1,0:T(8,128)(2,1)} %get-tuple-element.329.refs_0_.x_ref, f32[1,1024]{1,0:T(1,128)} %bitcast.169, f32[1,1024]{1,0:T(1,128)} %bitcast.165, f32[1,1024]{1,0:T(1,128)} %bitcast.168, ...), custom_call_target="tpu_custom_call" | custom-call | flops 2147483648 | bytes 14680064 | tf_op jit(solution)/shard_map/pallas_call | solution.py:452
  151.6 11.8 %shard_map.333 = (bf16[1024,2048]{1,0:T(8,128)(2,1)}, bf16[1024,2048]{1,0:T(8,128)(2,1)}) custom-call(bf16[1024,1024]{1,0:T(8,128)(2,1)} %get-tuple-element.332.n_ref, bf16[1024,2048]{1,0:T(8,128)(2,1)} %refs_2_.1, f32[1,2048]{1,0:T(1,128)} %bitcast.162), custom_call_target="tpu_custom_call" | custom-call | flops 4294967296 | bytes 14680064 | tf_op jit(solution)/shard_map/pallas_call | solution.py:364
  163.4 11.1 %shard_map.334 = (bf16[1024,2048]{1,0:T(8,128)(2,1)}, bf16[1024,2048]{1,0:T(8,128)(2,1)}) custom-call(bf16[1024,1024]{1,0:T(8,128)(2,1)} %get-tuple-element.332.n_ref, bf16[1024,2048]{1,0:T(8,128)(2,1)} %all-gather.11.cloned.1.call-done.w_ref.refs_3_, f32[1,2048]{1,0:T(1,128)} %bitcast.163), custom_call_target="tpu_custom_call" | custom-call | flops 4294967296 | bytes 14680064 | tf_op jit(solution)/shard_map/pallas_call | solution.py:364
  174.5 2.2 all-gather.13.cloned.1.call-done
  176.6 15.3 %shard_map.335 = bf16[1024,1024]{1,0:T(8,128)(2,1)} custom-call(f32[1024,1024]{1,0:T(8,128)} %get-tuple-element.330.r_ref, f32[1,1024]{1,0:T(1,128)} %bitcast.167, bf16[1024,2048]{1,0:T(8,128)(2,1)} %get-tuple-element.338.refs_0_, bf16[1024,2048]{1,0:T(8,128)(2,1)} %get-tuple-element.340.refs_1_, bf16[1,2048,1024]{2,1,0:T(8,128)(2,1)} %bitcast.157, ...), custom_call_target="tpu_custom_call" | custom-call | flops 8589934592 | bytes 23068672 | tf_op jit(solution)/shard_map/pallas_call | solution.py:482
  192.1 1.9 copy-done.64
  194.1 4.9 convolution_convert_fusion.2
  199.0 4.9 convolution_convert_fusion.3
  204.0 1.8 dynamic-slice_bitcast_fusion.2
  209.7 9.7 %shard_map.336 = (bf16[1024,2048]{1,0:T(8,128)(2,1)}, f32[1,2048]{1,0:T(1,128)}) custom-call(bf16[1024,1024]{1,0:T(8,128)(2,1)} %copy-done.14, bf16[1,2048,1024]{2,1,0:T(8,128)(2,1)} %bitcast.158, bf16[1024,2048]{1,0:T(8,128)(2,1)} %get-tuple-element.344.slope_ref), custom_call_target="tpu_custom_call" | custom-call | flops 4294967296 | bytes 14680064 | tf_op jit(solution)/shard_map/pallas_call | solution.py:399
  220.8 6.5 %shard_map.337 = (bf16[4,128,1024]{2,1,0:T(8,128)(2,1)}, bf16[4,128,1024]{2,1,0:T(8,128)(2,1)}, bf16[2,4,128,1024]{3,2,1,0:T(8,128)(2,1)}) custom-call(s32[9]{0:T(128)} %pad_add_fusion.1.t_ref, bf16[8,2,128,1024]{3,2,1,0:T(8,128)(2,1)} %bitcast.123, bf16[8,2,128,1024]{3,2,1,0:T(8,128)(2,1)} %bitcast.124, bf16[8,2,128,1024]{3,2,1,0:T(8,128)(2,1)} %bitcast.120, ...), custom_call_target="tpu_custom_call" | custom-call | flops 2097152 | bytes 12582912 | tf_op jit(solution)/shard_map/pallas_call | solution.py:731
  227.3 1.7 collective-permute-start.10
  229.0 10.0 %shard_map.338 = (bf16[1024,2048]{1,0:T(8,128)(2,1)}, f32[1,2048]{1,0:T(1,128)}) custom-call(bf16[1024,1024]{1,0:T(8,128)(2,1)} %copy-done.14, bf16[1,2048,1024]{2,1,0:T(8,128)(2,1)} %bitcast.171, bf16[1024,2048]{1,0:T(8,128)(2,1)} %get-tuple-element.354.slope_ref), custom_call_target="tpu_custom_call" | custom-call | flops 4294967296 | bytes 14680064 | tf_op jit(solution)/shard_map/pallas_call | solution.py:399
  239.1 7.1 %convolution_convert_fusion = bf16[1024,2048]{1,0:T(8,128)(2,1)S(1)} fusion(bf16[1024,1024]{1,0:T(8,128)(2,1)S(1)} %copy-done.61, bf16[1024,2048]{1,0:T(8,128)(2,1)} %get-tuple-element.366.refs_1_), kind=kOutput, calls=%fused_computation | convolution fusion | flops 4297064448 | bytes 10485760 | tf_op jit(solution)/shard_map/dot_general | solution.py:32
  246.1 4.8 convolution_convert_fusion.1
  250.9 2.6 collective-permute-done.10
  257.9 2.0 collective-permute-start.15
  259.9 17.6 %shard_map.339 = (bf16[1024,1024]{1,0:T(8,128)(2,1)}, f32[8,1024]{1,0:T(8,128)}) custom-call(f32[1024,1024]{1,0:T(8,128)} %get-tuple-element.330.r_ref, bf16[1024,1024]{1,0:T(8,128)(2,1)} %copy-done.14, f32[1,1024]{1,0:T(1,128)} %bitcast.166, bf16[1024,2048]{1,0:T(8,128)(2,1)} %get-tuple-element.365.refs_0_, bf16[1024,2048]{1,0:T(8,128)(2,1)} %get-tuple-element.366.refs_1_, ...), custom_call_target="tpu_custom_call" | custom-call | flops 8589934592 | bytes 25165824 | tf_op jit(solution)/shard_map/pallas_call | solution.py:521
  278.4 2.9 fusion.1
  288.1 2.3 convolution_convert_fusion.4.refs_1_
  291.1 6.6 %shard_map.340 = (bf16[4,64,2048]{2,1,0:T(8,128)(2,1)}, bf16[4,64,2048]{2,1,0:T(8,128)(2,1)}, bf16[2,4,64,2048]{3,2,1,0:T(8,128)(2,1)}) custom-call(s32[9]{0:T(128)} %pad_add_fusion.1.t_ref, bf16[8,2,64,2048]{3,2,1,0:T(8,128)(2,1)} %bitcast.129, bf16[8,2,64,2048]{3,2,1,0:T(8,128)(2,1)} %bitcast.130, bf16[8,2,64,2048]{3,2,1,0:T(8,128)(2,1)} %bitcast.126, ...), custom_call_target="tpu_custom_call" | custom-call | flops 2097152 | bytes 12582912 | tf_op jit(solution)/shard_map/pallas_call | solution.py:731
  301.2 2.5 collective-permute-start.16
  305.0 24.3 %shard_map.341 = (bf16[1024,256]{1,0:T(8,128)(2,1)}, bf16[2,1024,256]{2,1,0:T(8,128)(2,1)}, bf16[2,1024,256]{2,1,0:T(8,128)(2,1)}) custom-call(bf16[1024,512]{1,0:T(8,128)(2,1)} %get-tuple-element.419.refs_0_, bf16[1024,512]{1,0:T(8,128)(2,1)} %convolution_convert_fusion.4.refs_1_, bf16[1024,512]{1,0:T(8,128)(2,1)} %get-tuple-element.421.refs_6_.refs_2_, ...), custom_call_target="tpu_custom_call" | custom-call | flops 21474836480 | bytes 6291456 | tf_op jit(solution)/shard_map/pallas_call | solution.py:305
  330.4 4.4 shard_map.342
  336.5 24.6 %shard_map.343 = (bf16[1024,256]{1,0:T(8,128)(2,1)}, bf16[2,1024,256]{2,1,0:T(8,128)(2,1)}, bf16[2,1024,256]{2,1,0:T(8,128)(2,1)}) custom-call(bf16[1024,512]{1,0:T(8,128)(2,1)} %get-tuple-element.419.refs_0_, bf16[1024,512]{1,0:T(8,128)(2,1)} %convolution_convert_fusion.4.refs_1_, bf16[1024,512]{1,0:T(8,128)(2,1)} %get-tuple-element.421.refs_6_.refs_2_, ...), custom_call_target="tpu_custom_call" | custom-call | flops 21474836480 | bytes 6291456 | tf_op jit(solution)/shard_map/pallas_call | solution.py:305
  366.2 24.3 %shard_map.344 = (bf16[1024,256]{1,0:T(8,128)(2,1)}, bf16[2,1024,256]{2,1,0:T(8,128)(2,1)}, bf16[2,1024,256]{2,1,0:T(8,128)(2,1)}) custom-call(bf16[1024,512]{1,0:T(8,128)(2,1)} %get-tuple-element.489.refs_0_, bf16[1024,256]{1,0:T(8,128)(2,1)} %convolution_convert_fusion.7.refs_1_, bf16[1024,256]{1,0:T(8,128)(2,1)} %get-tuple-element.438.refs_4_.refs_2_, ...), custom_call_target="tpu_custom_call" | custom-call | flops 21474836480 | bytes 6291456 | tf_op jit(solution)/shard_map/pallas_call | solution.py:305
  390.5 4.4 collective-permute-done.24
  397.0 2.3 collective-permute-start.28
  399.3 10.7 %shard_map.345 = (bf16[8,3,64,512]{3,2,1,0:T(8,128)(2,1)}, bf16[8,3,64,512]{3,2,1,0:T(8,128)(2,1)}, bf16[1024,1536]{1,0:T(8,128)(2,1)}, f32[8,1536]{1,0:T(8,128)}) custom-call(s32[16]{0:T(128)} %pad_add_fusion.t_ref, bf16[1024,1024]{1,0:T(8,128)(2,1)} %get-tuple-element.299.nt_ref, f32[1024,128]{1,0:T(8,128)} %get-tuple-element.616.c_ref.refs_4_, ...), custom_call_target="tpu_custom_call" | custom-call | flops 3221225472 | bytes 13631488 | tf_op jit(solution)/shard_map/pallas_call | solution.py:657
  413.2 7.5 %shard_map.346 = (bf16[8,3,64,256]{3,2,1,0:T(8,128)(2,1)}, bf16[8,3,64,256]{3,2,1,0:T(8,128)(2,1)}, bf16[1024,768]{1,0:T(8,128)(2,1)}, f32[8,768]{1,0:T(8,128)}) custom-call(s32[16]{0:T(128)} %pad_add_fusion.t_ref, bf16[1024,1024]{1,0:T(8,128)(2,1)} %get-tuple-element.299.nt_ref, f32[1024,128]{1,0:T(8,128)} %get-tuple-element.616.c_ref.refs_4_, ...), custom_call_target="tpu_custom_call" | custom-call | flops 1610612736 | bytes 7864320 | tf_op jit(solution)/shard_map/pallas_call | solution.py:657
  423.2 24.5 %shard_map.347 = (bf16[1024,256]{1,0:T(8,128)(2,1)}, bf16[2,1024,256]{2,1,0:T(8,128)(2,1)}, bf16[2,1024,256]{2,1,0:T(8,128)(2,1)}) custom-call(bf16[1024,512]{1,0:T(8,128)(2,1)} %get-tuple-element.489.refs_0_, bf16[1024,256]{1,0:T(8,128)(2,1)} %convolution_convert_fusion.6.refs_1_, bf16[1024,256]{1,0:T(8,128)(2,1)} %get-tuple-element.491.refs_5_.refs_2_, ...), custom_call_target="tpu_custom_call" | custom-call | flops 21474836480 | bytes 6291456 | tf_op jit(solution)/shard_map/pallas_call | solution.py:305
  450.6 7.4 %shard_map.348.refs_2_ = f32[1024,1024]{1,0:T(8,128)} custom-call(bf16[16,4,64,512]{3,2,1,0:T(8,128)(2,1)} %bitcast.152, bf16[1024,1536]{1,0:T(8,128)(2,1)} %get-tuple-element.513.refs_1_), custom_call_target="tpu_custom_call" | custom-call | flops 3221225472 | bytes 10485760 | tf_op jit(solution)/shard_map/pallas_call | solution.py:574
  458.9 7.6 %shard_map.349 = (bf16[8,3,64,256]{3,2,1,0:T(8,128)(2,1)}, bf16[8,3,64,256]{3,2,1,0:T(8,128)(2,1)}, bf16[1024,768]{1,0:T(8,128)(2,1)}, f32[8,768]{1,0:T(8,128)}) custom-call(s32[16]{0:T(128)} %pad_add_fusion.t_ref, bf16[1024,1024]{1,0:T(8,128)(2,1)} %get-tuple-element.299.nt_ref, f32[1024,128]{1,0:T(8,128)} %get-tuple-element.616.c_ref.refs_4_, ...), custom_call_target="tpu_custom_call" | custom-call | flops 1610612736 | bytes 7864320 | tf_op jit(solution)/shard_map/pallas_call | solution.py:657
  466.5 2.5 collective-permute-done.35
  469.7 2.7 collective-permute-start.37
  474.2 5.7 shard_map.350.part_ref
  479.9 2.9 collective-permute-done.37
  482.8 3.6 collective-permute-done.39
  490.5 9.0 %shard_map.351 = (bf16[1024,1024]{1,0:T(8,128)(2,1)}, f32[8,1024]{1,0:T(8,128)}) custom-call(bf16[1024,1024]{1,0:T(8,128)(2,1)} %get-tuple-element.329.refs_0_.x_ref, bf16[1024,1024]{1,0:T(8,128)(2,1)} %get-tuple-element.376.g_ref, f32[1,1024]{1,0:T(1,128)} %bitcast.156, f32[1024,1024]{1,0:T(8,128)} %shard_map.350.part_ref, ...), custom_call_target="tpu_custom_call" | custom-call | flops 1610612736 | bytes 13631488 | tf_op jit(solution)/shard_map/pallas_call | solution.py:594
  499.5 2.5 collective-permute-done.40
  503.3 3.2 collective-permute-start.43
  508.2 1.9 collective-permute-start.50
  510.0 3.3 broadcast_select_fusion.1
  514.7 1.9 collective-permute-start.44
  517.0 2.1 collective-permute-start.46
  519.9 12.7 %collective-permute-done.52 = f32[2,52,128]{2,1,0:T(8,128)S(1)} collective-permute-done((f32[2,52,128]{2,1,0:T(8,128)S(1)}, f32[2,52,128]{2,1,0:T(8,128)S(1)}, u32[]{:S(2)}, u32[]{:S(2)}) %collective-permute-start.52) | collective-permute-done | bytes 53280 | tf_op jit(solution)/shard_map/ppermute | solution.py:771
  532.6 2.1 collective-permute-start.53
  534.7 4.4 convert_element_type.83
  539.1 4.4 convert_element_type.84
  547.6 2.5 collective-permute-done.54
  557.6 3.1 broadcast_select_fusion
  561.7 5.5 shard_map.352
  (339 shorter events, 89.9 us)
Async XLA Ops:
  7.3 78.9 %all-gather.15.cloned.1.call-start = ((), (), s32[]{:S(2)}) async-start(), calls=%async_computation.2 | async-start | bytes 4456448 | tf_op jit(solution)/shard_map/all_gather | solution.py:1032
  9.1 9.3 %collective-permute-start.3 = (bf16[4,64,512]{2,1,0:T(8,128)(2,1)S(1)}, bf16[4,64,512]{2,1,0:T(8,128)(2,1)S(1)}, u32[]{:S(2)}, u32[]{:S(2)}) collective-permute-start(bf16[4,64,512]{2,1,0:T(8,128)(2,1)S(1)} %pad_maximum_fusion.2), channel_id=1, source_target_pairs={{0,1},{1,0},{2,3},{3,2},{4,5},{5,4},{6,7},{7,6},{8,9},{9,8},{10,11... | collective-permute-start | bytes 786440 | tf_op jit(solution)/shard_map/ppermute | solution.py:771
  19.2 144.2 %all-gather.11.cloned.1.call-start = ((), (), s32[]{:S(2)}) async-start(), calls=%async_computation | async-start | bytes 4456448 | tf_op jit(solution)/shard_map/all_gather | solution.py:823
  19.2 10.4 %collective-permute-start = (bf16[1024,1024]{1,0:T(8,128)(2,1)}, bf16[1024,1024]{1,0:T(8,128)(2,1)S(1)}, u32[]{:S(2)}, u32[]{:S(2)}) collective-permute-start(bf16[1024,1024]{1,0:T(8,128)(2,1)} %x_ref.1), channel_id=1, source_target_pairs={{1,2},{2,1},{5,6},{6,5},{9,10},{10,9},{13,14},{14,13},{17,18},{18,... | collective-permute-start | bytes 6291464 | tf_op jit(solution)/shard_map/ppermute | solution.py:771
  36.7 29.6 %collective-permute-start.1 = (bf16[64,2048]{1,0:T(8,128)(2,1)S(1)}, bf16[64,2048]{1,0:T(8,128)(2,1)S(1)}, u32[]{:S(2)}, u32[]{:S(2)}) collective-permute-start(bf16[64,2048]{1,0:T(8,128)(2,1)S(1)} %constant_dynamic-slice_fusion.4), channel_id=1, source_target_pairs={{0,1},{1,0},{2,3},{3,2},{4,5},{5,4},{6,7},{7,6},{8,9},{9,8},{10,11... | collective-permute-start | bytes 786440 | tf_op jit(solution)/shard_map/ppermute | solution.py:771
  55.7 12.2 %collective-permute-start.2 = (bf16[128,1024]{1,0:T(8,128)(2,1)S(1)}, bf16[128,1024]{1,0:T(8,128)(2,1)S(1)}, u32[]{:S(2)}, u32[]{:S(2)}) collective-permute-start(bf16[128,1024]{1,0:T(8,128)(2,1)S(1)} %constant_dynamic-slice_fusion.3), channel_id=1, source_target_pairs={{0,1},{1,0},{2,3},{3,2},{4,5},{5,4},{6,7},{7,6},{8,9},{9,8},{10,11... | collective-permute-start | bytes 786440 | tf_op jit(solution)/shard_map/ppermute | solution.py:771
  67.9 108.7 %all-gather.13.cloned.1.call-start = ((), (), s32[]{:S(2)}) async-start(), calls=%async_computation.1 | async-start | bytes 4456448 | tf_op jit(solution)/shard_map/all_gather | solution.py:823
  68.0 5.6 collective-permute-start.4
  68.7 352.1 %all-gather.17.cloned.1.call-start = ((), (), s32[]{:S(2)}) async-start(), calls=%async_computation.3 | async-start | bytes 4456448 | tf_op jit(solution)/shard_map/all_gather | solution.py:823
  69.2 3.7 collective-permute-start.5
  97.0 23.2 %collective-permute-start.6 = (bf16[1024,1024]{1,0:T(8,128)(2,1)}, bf16[1024,1024]{1,0:T(8,128)(2,1)}, u32[]{:S(2)}, u32[]{:S(2)}) collective-permute-start(bf16[1024,1024]{1,0:T(8,128)(2,1)} %get-tuple-element.423.refs_1_.refs_3_.refs_7_.refs_9_), channel_id=1, source_target_pairs={{0,2},{1,3},{2,0},{3,1},{4,6},{5,7},{6,4},{7,5},{8,10},{9,11},{10,... | collective-permute-start | bytes 6291464 | tf_op jit(solution)/shard_map/ppermute | solution.py:771
  105.3 86.6 %collective-permute-start.7 = (bf16[1024,1024]{1,0:T(8,128)(2,1)S(1)}, bf16[1024,1024]{1,0:T(8,128)(2,1)}, u32[]{:S(2)}, u32[]{:S(2)}) collective-permute-start(bf16[1024,1024]{1,0:T(8,128)(2,1)S(1)} %copy-done.12), channel_id=1, source_target_pairs={{1,2},{2,1},{5,6},{6,5},{9,10},{10,9},{13,14},{14,13},{17,18},{18,... | collective-permute-start | bytes 6291464 | tf_op jit(solution)/shard_map/ppermute | solution.py:771
  208.2 11.2 %collective-permute-start.8 = (bf16[8,128,1024]{2,1,0:T(8,128)(2,1)}, bf16[8,128,1024]{2,1,0:T(8,128)(2,1)S(1)}, u32[]{:S(2)}, u32[]{:S(2)}) collective-permute-start(bf16[8,128,1024]{2,1,0:T(8,128)(2,1)} %dynamic-slice_bitcast_fusion.3), channel_id=1, source_target_pairs={{0,2},{1,3},{2,0},{3,1},{4,6},{5,7},{6,4},{7,5},{8,10},{9,11},{10,... | collective-permute-start | bytes 6291464 | tf_op jit(solution)/shard_map/ppermute | solution.py:771
  209.1 10.4 %collective-permute-start.9 = (bf16[8,128,1024]{2,1,0:T(8,128)(2,1)}, bf16[8,128,1024]{2,1,0:T(8,128)(2,1)}, u32[]{:S(2)}, u32[]{:S(2)}) collective-permute-start(bf16[8,128,1024]{2,1,0:T(8,128)(2,1)} %dynamic-slice_bitcast_fusion.2), channel_id=1, source_target_pairs={{0,2},{1,3},{2,0},{3,1},{4,6},{5,7},{6,4},{7,5},{8,10},{9,11},{10,... | collective-permute-start | bytes 6291464 | tf_op jit(solution)/shard_map/ppermute | solution.py:771
  227.3 26.2 %collective-permute-start.10 = (bf16[2,4,128,1024]{3,2,1,0:T(8,128)(2,1)}, bf16[2,4,128,1024]{3,2,1,0:T(8,128)(2,1)S(1)}, u32[]{:S(2)}, u32[]{:S(2)}) collective-permute-start(bf16[2,4,128,1024]{3,2,1,0:T(8,128)(2,1)} %get-tuple-element.359), channel_id=1, source_target_pairs={{0,1},{1,0},{2,6},{3,7},{4,5},{5,4},{6,2},{7,3},{8,9},{9,8},{10,14... | collective-permute-start | bytes 6291464 | tf_op jit(solution)/shard_map/ppermute | solution.py:771
  256.8 20.6 %collective-permute-start.11 = (bf16[8,64,2048]{2,1,0:T(8,128)(2,1)}, bf16[8,64,2048]{2,1,0:T(8,128)(2,1)S(1)}, u32[]{:S(2)}, u32[]{:S(2)}) collective-permute-start(bf16[8,64,2048]{2,1,0:T(8,128)(2,1)} %dynamic-slice_bitcast_fusion.1), channel_id=1, source_target_pairs={{0,2},{1,3},{2,0},{3,1},{4,6},{5,7},{6,4},{7,5},{8,10},{9,11},{10,... | collective-permute-start | bytes 6291464 | tf_op jit(solution)/shard_map/ppermute | solution.py:771
  256.8 20.7 %collective-permute-start.12 = (bf16[8,64,2048]{2,1,0:T(8,128)(2,1)S(1)}, bf16[8,64,2048]{2,1,0:T(8,128)(2,1)S(1)}, u32[]{:S(2)}, u32[]{:S(2)}) collective-permute-start(bf16[8,64,2048]{2,1,0:T(8,128)(2,1)S(1)} %dynamic-slice_bitcast_fusion), channel_id=1, source_target_pairs={{0,2},{1,3},{2,0},{3,1},{4,6},{5,7},{6,4},{7,5},{8,10},{9,11},{10,... | collective-permute-start | bytes 6291464 | tf_op jit(solution)/shard_map/ppermute | solution.py:771
  257.3 20.1 %collective-permute-start.13 = (bf16[4,128,1024]{2,1,0:T(8,128)(2,1)}, bf16[4,128,1024]{2,1,0:T(8,128)(2,1)S(1)}, u32[]{:S(2)}, u32[]{:S(2)}) collective-permute-start(bf16[4,128,1024]{2,1,0:T(8,128)(2,1)} %bitcast_add_fusion.3), channel_id=1, source_target_pairs={{0,4},{1,5},{2,3},{3,2},{4,0},{5,1},{6,7},{7,6},{8,12},{9,13},{10,... | collective-permute-start | bytes 3145736 | tf_op jit(solution)/shard_map/ppermute | solution.py:771
  257.9 42.4 %collective-permute-start.15 = (bf16[1024,1024]{1,0:T(8,128)(2,1)}, bf16[1024,1024]{1,0:T(8,128)(2,1)}, u32[]{:S(2)}, u32[]{:S(2)}) collective-permute-start(bf16[1024,1024]{1,0:T(8,128)(2,1)} %shard_map.335), channel_id=1, source_target_pairs={{1,2},{2,1},{5,6},{6,5},{9,10},{10,9},{13,14},{14,13},{17,18},{18,... | collective-permute-start | bytes 6291464 | tf_op jit(solution)/shard_map/ppermute | solution.py:771
  282.2 18.0 %collective-permute-start.14 = (bf16[2,128,1024]{2,1,0:T(8,128)(2,1)}, bf16[2,128,1024]{2,1,0:T(8,128)(2,1)S(1)}, u32[]{:S(2)}, u32[]{:S(2)}) collective-permute-start(bf16[2,128,1024]{2,1,0:T(8,128)(2,1)} %slice.253), channel_id=1, source_target_pairs={{0,8},{1,9},{2,10},{3,11},{4,12},{5,13},{6,14},{7,15},{8,0},{9,1},... | collective-permute-start | bytes 1572872 | tf_op jit(solution)/shard_map/ppermute | solution.py:771
  301.2 28.3 %collective-permute-start.16 = (bf16[2,4,64,2048]{3,2,1,0:T(8,128)(2,1)}, bf16[2,4,64,2048]{3,2,1,0:T(8,128)(2,1)S(1)}, u32[]{:S(2)}, u32[]{:S(2)}) collective-permute-start(bf16[2,4,64,2048]{3,2,1,0:T(8,128)(2,1)} %get-tuple-element.405), channel_id=1, source_target_pairs={{0,1},{1,0},{2,6},{3,7},{4,5},{5,4},{6,2},{7,3},{8,9},{9,8},{10,14... | collective-permute-start | bytes 6291464 | tf_op jit(solution)/shard_map/ppermute | solution.py:771
  303.6 25.8 %collective-permute-start.18 = (bf16[8,32,1024]{2,1,0:T(8,128)(2,1)S(1)}, bf16[8,32,1024]{2,1,0:T(8,128)(2,1)S(1)}, u32[]{:S(2)}, u32[]{:S(2)}) collective-permute-start(bf16[8,32,1024]{2,1,0:T(8,128)(2,1)S(1)} %dynamic-slice_bitcast_fusion.5), channel_id=1, source_target_pairs={{0,2},{1,3},{2,0},{3,1},{4,6},{5,7},{6,4},{7,5},{8,10},{9,11},{10,... | collective-permute-start | bytes 1572872 | tf_op jit(solution)/shard_map/ppermute | solution.py:771
  303.8 25.6 %collective-permute-start.19 = (bf16[8,32,1024]{2,1,0:T(8,128)(2,1)S(1)}, bf16[8,32,1024]{2,1,0:T(8,128)(2,1)S(1)}, u32[]{:S(2)}, u32[]{:S(2)}) collective-permute-start(bf16[8,32,1024]{2,1,0:T(8,128)(2,1)S(1)} %dynamic-slice_bitcast_fusion.4), channel_id=1, source_target_pairs={{0,2},{1,3},{2,0},{3,1},{4,6},{5,7},{6,4},{7,5},{8,10},{9,11},{10,... | collective-permute-start | bytes 1572872 | tf_op jit(solution)/shard_map/ppermute | solution.py:771
  304.1 25.2 %collective-permute-start.17 = (bf16[1,128,1024]{2,1,0:T(8,128)(2,1)S(1)}, bf16[1,128,1024]{2,1,0:T(8,128)(2,1)S(1)}, u32[]{:S(2)}, u32[]{:S(2)}) collective-permute-start(bf16[1,128,1024]{2,1,0:T(8,128)(2,1)S(1)} %slice.256), channel_id=1, source_target_pairs={{0,16},{1,17},{2,18},{3,19},{4,20},{5,21},{6,22},{7,23},{8,24},{9,... | collective-permute-start | bytes 786440 | tf_op jit(solution)/shard_map/ppermute | solution.py:771
  335.0 26.1 %collective-permute-start.20 = (bf16[2,1024,256]{2,1,0:T(8,128)(2,1)}, bf16[2,1024,256]{2,1,0:T(8,128)(2,1)}, u32[]{:S(2)}, u32[]{:S(2)}) collective-permute-start(bf16[2,1024,256]{2,1,0:T(8,128)(2,1)} %get-tuple-element.428), channel_id=1, source_target_pairs={{0,2},{1,3},{2,0},{3,1},{4,6},{5,7},{6,4},{7,5},{8,10},{9,11},{10,... | collective-permute-start | bytes 3145736 | tf_op jit(solution)/shard_map/ppermute | solution.py:771
  335.1 26.0 %collective-permute-start.21 = (bf16[4,64,2048]{2,1,0:T(8,128)(2,1)S(1)}, bf16[4,64,2048]{2,1,0:T(8,128)(2,1)}, u32[]{:S(2)}, u32[]{:S(2)}) collective-permute-start(bf16[4,64,2048]{2,1,0:T(8,128)(2,1)S(1)} %bitcast_add_fusion.1), channel_id=1, source_target_pairs={{0,4},{1,5},{2,3},{3,2},{4,0},{5,1},{6,7},{7,6},{8,12},{9,13},{10,... | collective-permute-start | bytes 3145736 | tf_op jit(solution)/shard_map/ppermute | solution.py:771
  336.4 24.7 %collective-permute-start.22 = (bf16[2,4,32,1024]{3,2,1,0:T(8,128)(2,1)}, bf16[2,4,32,1024]{3,2,1,0:T(8,128)(2,1)}, u32[]{:S(2)}, u32[]{:S(2)}) collective-permute-start(bf16[2,4,32,1024]{3,2,1,0:T(8,128)(2,1)} %get-tuple-element.430), channel_id=1, source_target_pairs={{0,1},{1,0},{2,6},{3,7},{4,5},{5,4},{6,2},{7,3},{8,9},{9,8},{10,14... | collective-permute-start | bytes 1572872 | tf_op jit(solution)/shard_map/ppermute | solution.py:771
  336.4 150.7 %all-gather.19.cloned.1.call-start = ((), (), s32[]{:S(2)}) async-start(), calls=%async_computation.4 | async-start | bytes 4456448 | tf_op jit(solution)/shard_map/all_gather | solution.py:823
  363.7 31.3 %copy-start.38 = (bf16[4,32,1024]{2,1,0:T(8,128)(2,1)S(1)}, bf16[4,32,1024]{2,1,0:T(8,128)(2,1)}, u32[]{:S(2)}) copy-start(bf16[4,32,1024]{2,1,0:T(8,128)(2,1)} %get-tuple-element.458) | copy-start | bytes 786436
  363.7 31.2 %collective-permute-start.23 = (bf16[2,1024,256]{2,1,0:T(8,128)(2,1)S(1)}, bf16[2,1024,256]{2,1,0:T(8,128)(2,1)S(1)}, u32[]{:S(2)}, u32[]{:S(2)}) collective-permute-start(bf16[2,1024,256]{2,1,0:T(8,128)(2,1)S(1)} %copy-done.59), channel_id=1, source_target_pairs={{0,2},{1,3},{2,0},{3,1},{4,6},{5,7},{6,4},{7,5},{8,10},{9,11},{10,... | collective-permute-start | bytes 3145736 | tf_op jit(solution)/shard_map/ppermute | solution.py:771
  363.9 31.0 %collective-permute-start.24 = (bf16[2,64,2048]{2,1,0:T(8,128)(2,1)S(1)}, bf16[2,64,2048]{2,1,0:T(8,128)(2,1)S(1)}, u32[]{:S(2)}, u32[]{:S(2)}) collective-permute-start(bf16[2,64,2048]{2,1,0:T(8,128)(2,1)S(1)} %slice.257), channel_id=1, source_target_pairs={{0,8},{1,9},{2,10},{3,11},{4,12},{5,13},{6,14},{7,15},{8,0},{9,1},... | collective-permute-start | bytes 1572872 | tf_op jit(solution)/shard_map/ppermute | solution.py:771
  365.1 25.4 %collective-permute-start.25 = (bf16[4,32,1024]{2,1,0:T(8,128)(2,1)S(1)}, bf16[4,32,1024]{2,1,0:T(8,128)(2,1)S(1)}, u32[]{:S(2)}, u32[]{:S(2)}) collective-permute-start(bf16[4,32,1024]{2,1,0:T(8,128)(2,1)S(1)} %bitcast_add_fusion.5), channel_id=1, source_target_pairs={{0,4},{1,5},{2,3},{3,2},{4,0},{5,1},{6,7},{7,6},{8,12},{9,13},{10,... | collective-permute-start | bytes 786440 | tf_op jit(solution)/shard_map/ppermute | solution.py:771
  396.2 15.1 %collective-permute-start.26 = (bf16[2,1024,256]{2,1,0:T(8,128)(2,1)S(1)}, bf16[2,1024,256]{2,1,0:T(8,128)(2,1)S(1)}, u32[]{:S(2)}, u32[]{:S(2)}) collective-permute-start(bf16[2,1024,256]{2,1,0:T(8,128)(2,1)S(1)} %copy-done.58), channel_id=1, source_target_pairs={{0,2},{1,3},{2,0},{3,1},{4,6},{5,7},{6,4},{7,5},{8,10},{9,11},{10,... | collective-permute-start | bytes 3145736 | tf_op jit(solution)/shard_map/ppermute | solution.py:771
  397.0 14.3 %collective-permute-start.27 = (bf16[1,64,2048]{2,1,0:T(8,128)(2,1)S(1)}, bf16[1,64,2048]{2,1,0:T(8,128)(2,1)S(1)}, u32[]{:S(2)}, u32[]{:S(2)}) collective-permute-start(bf16[1,64,2048]{2,1,0:T(8,128)(2,1)S(1)} %slice.259), channel_id=1, source_target_pairs={{0,16},{1,17},{2,18},{3,19},{4,20},{5,21},{6,22},{7,23},{8,24},{9,... | collective-permute-start | bytes 786440 | tf_op jit(solution)/shard_map/ppermute | solution.py:771
  397.0 13.0 %collective-permute-start.28 = (bf16[2,32,1024]{2,1,0:T(8,128)(2,1)S(1)}, bf16[2,32,1024]{2,1,0:T(8,128)(2,1)S(1)}, u32[]{:S(2)}, u32[]{:S(2)}) collective-permute-start(bf16[2,32,1024]{2,1,0:T(8,128)(2,1)S(1)} %slice.260), channel_id=1, source_target_pairs={{0,8},{1,9},{2,10},{3,11},{4,12},{5,13},{6,14},{7,15},{8,0},{9,1},... | collective-permute-start | bytes 393224 | tf_op jit(solution)/shard_map/ppermute | solution.py:771
  412.4 8.4 %collective-permute-start.29 = (bf16[8,3,64,512]{3,2,1,0:T(8,128)(2,1)}, bf16[8,3,64,512]{3,2,1,0:T(8,128)(2,1)S(1)}, u32[]{:S(2)}, u32[]{:S(2)}) collective-permute-start(bf16[8,3,64,512]{3,2,1,0:T(8,128)(2,1)} %get-tuple-element.483), channel_id=1, source_target_pairs={{0,2},{1,3},{2,0},{3,1},{4,6},{5,7},{6,4},{7,5},{8,10},{9,11},{10,... | collective-permute-start | bytes 4718600 | tf_op jit(solution)/shard_map/ppermute | solution.py:771
  412.4 8.3 %collective-permute-start.30 = (bf16[1,32,1024]{2,1,0:T(8,128)(2,1)S(1)}, bf16[1,32,1024]{2,1,0:T(8,128)(2,1)S(1)}, u32[]{:S(2)}, u32[]{:S(2)}) collective-permute-start(bf16[1,32,1024]{2,1,0:T(8,128)(2,1)S(1)} %slice.262), channel_id=1, source_target_pairs={{0,16},{1,17},{2,18},{3,19},{4,20},{5,21},{6,22},{7,23},{8,24},{9,... | collective-permute-start | bytes 196616 | tf_op jit(solution)/shard_map/ppermute | solution.py:771
  420.8 131.5 %all-gather.21.cloned.1.call-start = ((), (), s32[]{:S(2)}) async-start(), calls=%async_computation.5 | async-start | bytes 2785280 | tf_op jit(solution)/shard_map/all_gather | solution.py:1164
  421.0 26.8 %copy-start.31 = (bf16[8,3,64,256]{3,2,1,0:T(8,128)(2,1)S(1)}, bf16[8,3,64,256]{3,2,1,0:T(8,128)(2,1)}, u32[]{:S(2)}) copy-start(bf16[8,3,64,256]{3,2,1,0:T(8,128)(2,1)} %get-tuple-element.509) | copy-start | bytes 2359300
  421.1 26.7 %collective-permute-start.32 = (bf16[8,3,64,256]{3,2,1,0:T(8,128)(2,1)}, bf16[8,3,64,256]{3,2,1,0:T(8,128)(2,1)S(1)}, u32[]{:S(2)}, u32[]{:S(2)}) collective-permute-start(bf16[8,3,64,256]{3,2,1,0:T(8,128)(2,1)} %get-tuple-element.498), channel_id=1, source_target_pairs={{0,2},{1,3},{2,0},{3,1},{4,6},{5,7},{6,4},{7,5},{8,10},{9,11},{10,... | collective-permute-start | bytes 2359304 | tf_op jit(solution)/shard_map/ppermute | solution.py:771
  421.5 26.2 %collective-permute-start.31 = (bf16[8,3,64,256]{3,2,1,0:T(8,128)(2,1)S(1)}, bf16[8,3,64,256]{3,2,1,0:T(8,128)(2,1)S(1)}, u32[]{:S(2)}, u32[]{:S(2)}) collective-permute-start(bf16[8,3,64,256]{3,2,1,0:T(8,128)(2,1)S(1)} %get-tuple-element.488), channel_id=1, source_target_pairs={{0,1},{1,0},{2,3},{3,2},{4,5},{5,4},{6,7},{7,6},{8,9},{9,8},{10,11... | collective-permute-start | bytes 2359304 | tf_op jit(solution)/shard_map/ppermute | solution.py:771
  449.1 8.8 %collective-permute-start.33 = (bf16[2,1024,256]{2,1,0:T(8,128)(2,1)S(1)}, bf16[2,1024,256]{2,1,0:T(8,128)(2,1)S(1)}, u32[]{:S(2)}, u32[]{:S(2)}) collective-permute-start(bf16[2,1024,256]{2,1,0:T(8,128)(2,1)S(1)} %copy-done.60), channel_id=1, source_target_pairs={{0,2},{1,3},{2,0},{3,1},{4,6},{5,7},{6,4},{7,5},{8,10},{9,11},{10,... | collective-permute-start | bytes 3145736 | tf_op jit(solution)/shard_map/ppermute | solution.py:771
  449.1 20.0 %collective-permute-start.35 = (bf16[8,3,64,256]{3,2,1,0:T(8,128)(2,1)S(1)}, bf16[8,3,64,256]{3,2,1,0:T(8,128)(2,1)S(1)}, u32[]{:S(2)}, u32[]{:S(2)}) collective-permute-start(bf16[8,3,64,256]{3,2,1,0:T(8,128)(2,1)S(1)} %get-tuple-element.521), channel_id=1, source_target_pairs={{0,1},{1,0},{2,3},{3,2},{4,5},{5,4},{6,7},{7,6},{8,9},{9,8},{10,11... | collective-permute-start | bytes 2359304 | tf_op jit(solution)/shard_map/ppermute | solution.py:771
  449.3 20.1 %collective-permute-start.34 = (bf16[4,3,64,256]{3,2,1,0:T(8,128)(2,1)S(1)}, bf16[4,3,64,256]{3,2,1,0:T(8,128)(2,1)S(1)}, u32[]{:S(2)}, u32[]{:S(2)}) collective-permute-start(bf16[4,3,64,256]{3,2,1,0:T(8,128)(2,1)S(1)} %slice.264), channel_id=1, source_target_pairs={{0,4},{1,5},{2,6},{3,7},{4,0},{5,1},{6,2},{7,3},{8,12},{9,13},{10,... | collective-permute-start | bytes 1179656 | tf_op jit(solution)/shard_map/ppermute | solution.py:771
  469.6 16.8 %collective-permute-start.36 = (bf16[8,3,64,256]{3,2,1,0:T(8,128)(2,1)}, bf16[8,3,64,256]{3,2,1,0:T(8,128)(2,1)S(1)}, u32[]{:S(2)}, u32[]{:S(2)}) collective-permute-start(bf16[8,3,64,256]{3,2,1,0:T(8,128)(2,1)} %get-tuple-element.530), channel_id=1, source_target_pairs={{0,2},{1,3},{2,0},{3,1},{4,6},{5,7},{6,4},{7,5},{8,10},{9,11},{10,... | collective-permute-start | bytes 2359304 | tf_op jit(solution)/shard_map/ppermute | solution.py:771
  469.7 13.0 %collective-permute-start.37 = (bf16[1,3,64,256]{3,2,1,0:T(8,128)(2,1)S(1)}, bf16[1,3,64,256]{3,2,1,0:T(8,128)(2,1)S(1)}, u32[]{:S(2)}, u32[]{:S(2)}) collective-permute-start(bf16[1,3,64,256]{3,2,1,0:T(8,128)(2,1)S(1)} %get-tuple-element.531), channel_id=1, source_target_pairs={{0,16},{1,17},{2,18},{3,19},{4,20},{5,21},{6,22},{7,23},{8,24},{9,... | collective-permute-start | bytes 294920 | tf_op jit(solution)/shard_map/ppermute | solution.py:771
  472.5 10.3 %collective-permute-start.38 = (bf16[1,3,64,256]{3,2,1,0:T(8,128)(2,1)S(1)}, bf16[1,3,64,256]{3,2,1,0:T(8,128)(2,1)S(1)}, u32[]{:S(2)}, u32[]{:S(2)}) collective-permute-start(bf16[1,3,64,256]{3,2,1,0:T(8,128)(2,1)S(1)} %get-tuple-element.532), channel_id=1, source_target_pairs={{0,8},{1,9},{2,10},{3,11},{4,12},{5,13},{6,14},{7,15},{8,0},{9,1},... | collective-permute-start | bytes 294920 | tf_op jit(solution)/shard_map/ppermute | solution.py:771
  472.5 13.9 %collective-permute-start.39 = (bf16[1,3,64,256]{3,2,1,0:T(8,128)(2,1)S(1)}, bf16[1,3,64,256]{3,2,1,0:T(8,128)(2,1)S(1)}, u32[]{:S(2)}, u32[]{:S(2)}) collective-permute-start(bf16[1,3,64,256]{3,2,1,0:T(8,128)(2,1)S(1)} %get-tuple-element.533), channel_id=1, source_target_pairs={{0,24},{1,25},{2,26},{3,27},{4,28},{5,29},{6,30},{7,31},{8,16},{9,... | collective-permute-start | bytes 294920 | tf_op jit(solution)/shard_map/ppermute | solution.py:771
  488.9 13.1 %collective-permute-start.40 = (bf16[4,3,64,256]{3,2,1,0:T(8,128)(2,1)S(1)}, bf16[4,3,64,256]{3,2,1,0:T(8,128)(2,1)S(1)}, u32[]{:S(2)}, u32[]{:S(2)}) collective-permute-start(bf16[4,3,64,256]{3,2,1,0:T(8,128)(2,1)S(1)} %slice.271), channel_id=1, source_target_pairs={{0,4},{1,5},{2,6},{3,7},{4,0},{5,1},{6,2},{7,3},{8,12},{9,13},{10,... | collective-permute-start | bytes 1179656 | tf_op jit(solution)/shard_map/ppermute | solution.py:771
  502.0 11.9 %collective-permute-start.41 = (bf16[1,3,64,256]{3,2,1,0:T(8,128)(2,1)S(1)}, bf16[1,3,64,256]{3,2,1,0:T(8,128)(2,1)S(1)}, u32[]{:S(2)}, u32[]{:S(2)}) collective-permute-start(bf16[1,3,64,256]{3,2,1,0:T(8,128)(2,1)S(1)} %get-tuple-element.596), channel_id=1, source_target_pairs={{0,16},{1,17},{2,18},{3,19},{4,20},{5,21},{6,22},{7,23},{8,24},{9,... | collective-permute-start | bytes 294920 | tf_op jit(solution)/shard_map/ppermute | solution.py:771
  502.1 11.9 %collective-permute-start.42 = (bf16[1,3,64,256]{3,2,1,0:T(8,128)(2,1)S(1)}, bf16[1,3,64,256]{3,2,1,0:T(8,128)(2,1)S(1)}, u32[]{:S(2)}, u32[]{:S(2)}) collective-permute-start(bf16[1,3,64,256]{3,2,1,0:T(8,128)(2,1)S(1)} %get-tuple-element.594), channel_id=1, source_target_pairs={{0,8},{1,9},{2,10},{3,11},{4,12},{5,13},{6,14},{7,15},{8,0},{9,1},... | collective-permute-start | bytes 294920 | tf_op jit(solution)/shard_map/ppermute | solution.py:771
  503.3 10.6 %collective-permute-start.43 = (bf16[1,3,64,256]{3,2,1,0:T(8,128)(2,1)S(1)}, bf16[1,3,64,256]{3,2,1,0:T(8,128)(2,1)S(1)}, u32[]{:S(2)}, u32[]{:S(2)}) collective-permute-start(bf16[1,3,64,256]{3,2,1,0:T(8,128)(2,1)S(1)} %get-tuple-element.595), channel_id=1, source_target_pairs={{0,24},{1,25},{2,26},{3,27},{4,28},{5,29},{6,30},{7,31},{8,16},{9,... | collective-permute-start | bytes 294920 | tf_op jit(solution)/shard_map/ppermute | solution.py:771
  506.5 45.9 %collective-permute-start.48 = (bf16[1024,1024]{1,0:T(8,128)(2,1)}, bf16[1024,1024]{1,0:T(8,128)(2,1)S(1)}, u32[]{:S(2)}, u32[]{:S(2)}) collective-permute-start(bf16[1024,1024]{1,0:T(8,128)(2,1)} %get-tuple-element.569), channel_id=1, source_target_pairs={{1,2},{2,1},{5,6},{6,5},{9,10},{10,9},{13,14},{14,13},{17,18},{18,... | collective-permute-start | bytes 6291464 | tf_op jit(solution)/shard_map/ppermute | solution.py:771
  508.2 5.1 collective-permute-start.50
  510.0 24.7 %copy-start.10 = (bf16[1,2048,1024]{2,1,0:T(8,128)(2,1)S(1)}, bf16[1,2048,1024]{2,1,0:T(8,128)(2,1)}, u32[]{:S(2)}) copy-start(bf16[1,2048,1024]{2,1,0:T(8,128)(2,1)} %all-gather.17.cloned.1.call-done) | copy-start | bytes 12582916
  513.3 5.7 collective-permute-start.51
  514.7 20.0 %collective-permute-start.44 = (bf16[1,3,64,256]{3,2,1,0:T(8,128)(2,1)S(1)}, bf16[1,3,64,256]{3,2,1,0:T(8,128)(2,1)S(1)}, u32[]{:S(2)}, u32[]{:S(2)}) collective-permute-start(bf16[1,3,64,256]{3,2,1,0:T(8,128)(2,1)S(1)} %get-tuple-element.585), channel_id=1, source_target_pairs={{0,16},{1,17},{2,18},{3,19},{4,20},{5,21},{6,22},{7,23},{8,24},{9,... | collective-permute-start | bytes 294920 | tf_op jit(solution)/shard_map/ppermute | solution.py:771
  516.6 27.0 %collective-permute-start.45 = (bf16[1,3,64,256]{3,2,1,0:T(8,128)(2,1)S(1)}, bf16[1,3,64,256]{3,2,1,0:T(8,128)(2,1)S(1)}, u32[]{:S(2)}, u32[]{:S(2)}) collective-permute-start(bf16[1,3,64,256]{3,2,1,0:T(8,128)(2,1)S(1)} %get-tuple-element.585), channel_id=1, source_target_pairs={{0,8},{1,9},{2,10},{3,11},{4,12},{5,13},{6,14},{7,15},{8,0},{9,1},... | collective-permute-start | bytes 294920 | tf_op jit(solution)/shard_map/ppermute | solution.py:771
  517.0 26.6 %collective-permute-start.46 = (bf16[1,3,64,256]{3,2,1,0:T(8,128)(2,1)S(1)}, bf16[1,3,64,256]{3,2,1,0:T(8,128)(2,1)S(1)}, u32[]{:S(2)}, u32[]{:S(2)}) collective-permute-start(bf16[1,3,64,256]{3,2,1,0:T(8,128)(2,1)S(1)} %get-tuple-element.585), channel_id=1, source_target_pairs={{0,24},{1,25},{2,26},{3,27},{4,28},{5,29},{6,30},{7,31},{8,16},{9,... | collective-permute-start | bytes 294920 | tf_op jit(solution)/shard_map/ppermute | solution.py:771
  519.1 13.5 %collective-permute-start.52 = (f32[2,52,128]{2,1,0:T(8,128)S(1)}, f32[2,52,128]{2,1,0:T(8,128)S(1)}, u32[]{:S(2)}, u32[]{:S(2)}) collective-permute-start(f32[2,52,128]{2,1,0:T(8,128)S(1)} %fusion.40), channel_id=1, source_target_pairs={{0,8},{1,9},{2,10},{3,11},{4,12},{5,13},{6,14},{7,15},{8,0},{9,1},... | collective-permute-start | bytes 159752 | tf_op jit(solution)/shard_map/ppermute | solution.py:771
  532.6 13.5 %collective-permute-start.53 = (f32[2,52,128]{2,1,0:T(8,128)S(1)}, f32[2,52,128]{2,1,0:T(8,128)S(1)}, u32[]{:S(2)}, u32[]{:S(2)}) collective-permute-start(f32[2,52,128]{2,1,0:T(8,128)S(1)} %add.261), channel_id=1, source_target_pairs={{0,16},{1,17},{2,18},{3,19},{4,20},{5,21},{6,22},{7,23},{8,24},{9,... | collective-permute-start | bytes 159752 | tf_op jit(solution)/shard_map/ppermute | solution.py:771
  543.7 7.8 %collective-permute-start.47 = (bf16[4,3,64,256]{3,2,1,0:T(8,128)(2,1)S(1)}, bf16[4,3,64,256]{3,2,1,0:T(8,128)(2,1)S(1)}, u32[]{:S(2)}, u32[]{:S(2)}) collective-permute-start(bf16[4,3,64,256]{3,2,1,0:T(8,128)(2,1)S(1)} %pad_maximum_fusion.1), channel_id=1, source_target_pairs={{0,4},{1,5},{2,6},{3,7},{4,0},{5,1},{6,2},{7,3},{8,12},{9,13},{10,... | collective-permute-start | bytes 1179656 | tf_op jit(solution)/shard_map/ppermute | solution.py:771
  546.2 3.9 collective-permute-start.54
  553.2 7.5 %collective-permute-start.49 = (bf16[8,3,64,256]{3,2,1,0:T(8,128)(2,1)}, bf16[8,3,64,256]{3,2,1,0:T(8,128)(2,1)S(1)}, u32[]{:S(2)}, u32[]{:S(2)}) collective-permute-start(bf16[8,3,64,256]{3,2,1,0:T(8,128)(2,1)} %copy-done.41), channel_id=1, source_target_pairs={{0,2},{1,3},{2,0},{3,1},{4,6},{5,7},{6,4},{7,5},{8,10},{9,11},{10,... | collective-permute-start | bytes 2359304 | tf_op jit(solution)/shard_map/ppermute | solution.py:771
  (62 other events, 432.6 us)
Sparse Core Ops, SparseCore 0:
  19.3 53.5 all-gather.14
  75.0 50.1 all-gather.10
  127.4 49.1 all-gather.12
  336.5 59.0 all-gather.16
  420.9 66.1 all-gather.18
  489.3 50.5 all-gather.20
